TPU v7x, 32 devices: a whole 2x2x4 slice. The times are simulated.
32 devices in a mesh: dp: 4 (over z), fsdp: 8 (over y, x, core).
Axes of the slice: x: 2, y: 2, z: 4, core: 2. Of those that a mesh axis runs over, the one named last changes fastest.
Arguments:
- features: bfloat16 [12544, 512], P(('dp', 'fsdp')), may hold values from -6 to 6
- shortcut: bfloat16 [12544, 2048], P(('dp', 'fsdp')), may hold values from -6 to 6
- conv_weight: bfloat16 [2048, 512], P('fsdp'), may hold values from -0.25 to 0.25
- proj_weight: bfloat16 [2048, 256], P('fsdp'), may hold values from -0.125 to 0.125
- partner: int32 [256], P(('dp', 'fsdp')), may hold values from 0 to 31, as said below
Outputs:
- grad_conv: float32 [2048, 512], P('fsdp')
- grad_proj: float32 [2048, 256], P('fsdp')
- group_loss: float32 [8], P('fsdp')
Inputs may be any that keep to these rules, and one draw needn't show every extreme that they name: Each image's partner is another image of its group, given as its member index, and the pairing is mutual: the partner of the partner is the image itself.
All inputs are finite; a program needn't handle non-finite values.
Results may differ from a plain program's by a relative error of at most 0.035.
Values may be sent and summed in bfloat16 or wider, within the bound.
No kernel may reach another device: no remote copies, remote signals or barrier semaphores. Data moves between devices by JAX's collectives and lax.ppermute only.
A program may use at most 64 MiB of HBM per device.

v0:
```python
import jax
import jax.numpy as jnp
from jax import lax
from jax.sharding import PartitionSpec as P

POS = 49


gamma_weight = 3.0
epsilon = 1e-06


def pool_rows(hidden, images):
    return jnp.mean(hidden.reshape(images, POS, hidden.shape[-1]), axis=1)


def forward_cols(features, short_cols, conv_rows):
    preact = lax.dot_general(
        features, conv_rows, (((1,), (1,)), ((), ())), preferred_element_type=jnp.float32
    )
    return jnp.maximum(preact + short_cols.astype(jnp.float32), 0.0)


def grad_block(features, hidden_cols, proj_rows, pooled_cols, grad_embed, images):
    count = proj_rows.shape[0]
    grad_pool = (
        lax.dot_general(
            grad_embed, proj_rows, (((1,), (1,)), ((), ())), preferred_element_type=jnp.float32
        )
        / POS
    )
    spread_rows = jnp.broadcast_to(grad_pool[:, None, :], (images, POS, count)).reshape(
        images * POS, count
    )
    grad_hidden = jnp.where(hidden_cols > 0, spread_rows, 0.0).astype(jnp.bfloat16)
    conv_part = lax.dot_general(
        grad_hidden, features, (((0,), (0,)), ((), ())), preferred_element_type=jnp.float32
    )
    proj_part = lax.dot_general(
        pooled_cols, grad_embed, (((0,), (0,)), ((), ())), preferred_element_type=jnp.float32
    )
    return jnp.concatenate([conv_part, proj_part], axis=1)


def local(features, shortcut, conv_weight, proj_weight, partner):
    images = features.shape[0] // POS
    width_in = features.shape[1]
    conv_all, proj_all = (
        lax.all_gather(conv_weight, "fsdp", axis=0, tiled=True),
        lax.all_gather(proj_weight, "fsdp", axis=0, tiled=True),
    )
    hidden = forward_cols(features, shortcut, conv_all)
    pooled = pool_rows(hidden, images).astype(jnp.bfloat16)
    embed_own = jnp.dot(pooled, proj_all, preferred_element_type=jnp.float32)
    all_embed = lax.all_gather(embed_own, "dp", axis=0, tiled=True)
    count = all_embed.shape[0]
    center = jnp.mean(all_embed, axis=0)
    spread = 2.0 * jnp.mean(jnp.sum((all_embed - center) ** 2, axis=1))
    squares_all = jnp.sum(all_embed * all_embed, axis=1)
    squares_own = jnp.sum(embed_own * embed_own, axis=1)
    inner = jnp.dot(embed_own, all_embed.T, precision=lax.Precision.HIGHEST)
    kernel = jnp.exp(-(squares_own[:, None] + squares_all[None, :] - 2.0 * inner) / (2.0 * spread))
    row_own = jnp.mean(kernel, axis=1)
    onehot = (partner[:, None] == jnp.arange(count, dtype=jnp.int32)[None, :]).astype(jnp.float32)
    positive_own = jnp.sum(kernel * onehot)
    scale_sq = float(count - 1) ** 2
    row_all = lax.all_gather(row_own, "dp", axis=0, tiled=True)
    total_mean = jnp.mean(row_all)
    centered = kernel - row_own[:, None] - row_all[None, :] + total_mean
    square_sum, positive_sum = lax.psum((jnp.sum(centered * centered), positive_own), "dp")
    root = jnp.sqrt(square_sum / scale_sq + epsilon)
    loss_value = -(positive_sum / count - total_mean) + gamma_weight * root
    groups_count = lax.axis_size("fsdp")
    coeff = (
        -onehot / count + 1.0 / (count * count) + gamma_weight * centered / (scale_sq * root)
    ) / groups_count
    weighted = coeff * kernel
    grad_embed = -(2.0 / spread) * (
        jnp.sum(weighted, axis=1)[:, None] * embed_own
        - jnp.dot(weighted, all_embed, precision=lax.Precision.HIGHEST)
    )
    grad_embed = grad_embed.astype(jnp.bfloat16)
    shard_term = lax.psum_scatter(
        grad_block(features, hidden, proj_all, pooled, grad_embed, images).astype(jnp.bfloat16),
        "fsdp",
        scatter_dimension=0,
        tiled=True,
    ).astype(jnp.float32)
    total = lax.psum(shard_term, "dp")
    return (total[:, :width_in], total[:, width_in:], jnp.reshape(loss_value, (1,)))


def solution(mesh):
    return jax.shard_map(
        local,
        mesh=mesh,
        in_specs=(
            P(("dp", "fsdp"), None),
            P(("dp", "fsdp"), None),
            P("fsdp", None),
            P("fsdp", None),
            P(("dp", "fsdp")),
        ),
        out_specs=(P("fsdp", None), P("fsdp", None), P("fsdp")),
        check_vma=False,
    )
```

profile of v0, /device:TPU:0, one launch (start us, length us, event | category | flops | bytes accessed | tf_op | source)
XLA Modules:
  0.0 208.5 jit_solution(18332078456634999875)
XLA Ops:
  7.2 0.0 copy-start
  7.2 0.0 all-gather.3.cloned.1.call-start
  7.2 0.7 all-gather.3.cloned.1.call-update
  7.9 0.0 all-gather.5.cloned.1.call-start
  8.0 0.7 all-gather.5.cloned.1.call-update
  8.7 0.0 reduce-scatter.2.cloned.1.call-start
  8.7 1.2 dynamic-slice
  10.6 29.9 %all-gather.3.cloned.1.call-done = bf16[2048,512]{1,0:T(8,128)(2,1)} async-done(((bf16[256,512]{1,0:T(8,128)(2,1)}), bf16[2048,512]{1,0:T(8,128)(2,1)}) %all-gather.3.cloned.1.call-update) | async-done | bytes 2097168 | tf_op jit(solution)/shard_map/all_gather | solution.py:49
  40.5 0.0 copy-done
  40.5 5.8 %broadcast_maximum_fusion = (f32[392,2048]{1,0:T(8,128)}, f32[392,2048]{1,0:T(8,128)}) fusion(bf16[392,2048]{1,0:T(8,128)(2,1)} %param.6, bf16[392,512]{1,0:T(8,128)(2,1)S(1)} %copy-done, bf16[2048,512]{1,0:T(8,128)(2,1)} %all-gather.3.cloned.1.call-done), kind=kOutput, calls=%fused_computation.6 | convolution fusion | flops 824492032 | bytes 10526720 | tf_op jit(solution)/shard_map/dot_general | solution.py:18
  46.3 4.1 %reshape.27 = f32[8,49,2048]{2,1,0:T(8,128)} reshape(f32[392,2048]{1,0:T(8,128)} %get-tuple-element.19) | data formatting | bytes 6422528 | tf_op jit(solution)/shard_map/reshape | solution.py:14
  50.4 0.0 copy-start.1
  50.4 2.5 %reduce_sum.94 = f32[8,2048]{1,0:T(8,128)S(1)} reduce(f32[8,49,2048]{2,1,0:T(8,128)} %reshape.27, f32[]{:T(128)} %constant.13.clone.1), dimensions={1}, to_apply=%region_0.0 | reduce | flops 786432 | bytes 3276804 | tf_op jit(solution)/shard_map/reduce_sum | solution.py:14
  52.9 13.0 %all-gather.5.cloned.1.call-done = bf16[2048,256]{1,0:T(8,128)(2,1)} async-done(((bf16[256,256]{1,0:T(8,128)(2,1)}), bf16[2048,256]{1,0:T(8,128)(2,1)}) %all-gather.5.cloned.1.call-update) | async-done | bytes 1048592 | tf_op jit(solution)/shard_map/all_gather | solution.py:50
  65.9 1.6 multiply_reduce_fusion.2
  67.5 13.2 %all_gather.14 = f32[32,256]{1,0:T(8,128)S(1)} all-gather(f32[8,256]{1,0:T(8,128)S(1)} %get-tuple-element.22), channel_id=1, replica_groups=mesh['dp'=4,'fsdp'=8] {'dp'}, dimensions={0}, use_global_device_ids=true | all-gather | bytes 40960 | tf_op jit(solution)/shard_map/all_gather | solution.py:55
  80.7 0.6 multiply_reduce_fusion
  82.0 0.3 fusion.13
  82.2 0.1 broadcast_multiply_fusion.1
  82.3 11.6 %all-reduce = f32[32]{0:T(128)S(1)} all-reduce(f32[32]{0:T(128)S(1)} %get-tuple-element.18), channel_id=1, replica_groups=mesh['dp'=4,'fsdp'=8] {'dp'}, use_global_device_ids=true, to_apply=%add | all-reduce | flops 32 | bytes 256
  94.0 0.6 reduce_sum.100
  95.2 0.0 copy-done.1
  95.2 0.7 select_reduce_fusion
  95.9 9.0 %psum.21 = f32[]{:T(128)} all-reduce(f32[]{:T(128)} %get-tuple-element.12), channel_id=1, replica_groups=mesh['dp'=4,'fsdp'=8] {'dp'}, use_global_device_ids=true, to_apply=%region_8.0 | all-reduce | flops 1 | bytes 8 | tf_op jit(solution)/shard_map/psum | solution.py:70
  105.6 0.2 fusion.12
  106.5 0.1 fusion.2
  106.6 0.5 convolution_convert_fusion.1
  107.1 1.6 convolution_multiply_fusion
  108.7 0.2 broadcast_in_dim.3
  108.9 1.7 reshape.28
  110.6 3.7 %convolution_convert_fusion = bf16[2048,512]{0,1:T(8,128)(2,1)S(1)} fusion(bf16[392,512]{1,0:T(8,128)(2,1)S(1)} %copy-done, bf16[392,2048]{1,0:T(8,128)(2,1)} %reshape.28, f32[392,2048]{1,0:T(8,128)} %get-tuple-element.20), kind=kOutput, calls=%fused_computation.3 | convolution fusion | flops 824737792 | bytes 7315456 | tf_op jit(solution)/shard_map/dot_general | solution.py:36
  114.3 1.9 pad_maximum_fusion
  116.2 0.0 reduce-scatter.2.cloned.1.call-update
  116.2 45.1 %reduce-scatter.2.cloned.1.call-done = bf16[256,768]{0,1:T(8,128)(2,1)} async-done(((bf16[2048,768]{0,1:T(8,128)(2,1)}), bf16[256,768]{0,1:T(8,128)(2,1)}) %reduce-scatter.2.cloned.1.call-update) | async-done | bytes 393232 | tf_op jit(solution)/shard_map/reduce_scatter | solution.py:83
  161.3 37.0 %all-reduce.3 = (f32[256,768]{0,1:T(8,128)S(1)}, f32[]{:T(128)}) all-reduce(bf16[256,768]{0,1:T(8,128)(2,1)} %reduce-scatter.2.cloned.1.call-done, f32[]{:T(128)} %get-tuple-element.11), channel_id=1, replica_groups=mesh['dp'=4,'fsdp'=8] {'dp'}, use_global_device_ids=true, to_apply=%region_11.0 | all-reduce | flops 196609 | bytes 1179656 | tf_op jit(solution)/shard_map/psum | solution.py:89
  199.0 1.0 copy.10
  200.0 0.8 copy.11
  (5 shorter events, 0.1 us)
Async XLA Ops:
  7.2 33.4 %copy-start = (bf16[392,512]{1,0:T(8,128)(2,1)S(1)}, bf16[392,512]{1,0:T(8,128)(2,1)}, u32[]{:S(2)}) copy-start(bf16[392,512]{1,0:T(8,128)(2,1)} %param.5) | copy-start | bytes 1204228
  7.2 33.4 %all-gather.3.cloned.1.call-start = ((), (), s32[]{:S(2)}) async-start(), calls=%async_computation.1 | async-start | bytes 2359296 | tf_op jit(solution)/shard_map/all_gather | solution.py:49
  7.9 58.0 %all-gather.5.cloned.1.call-start = ((), (), s32[]{:S(2)}) async-start(), calls=%async_computation.2 | async-start | bytes 1179648 | tf_op jit(solution)/shard_map/all_gather | solution.py:50
  8.7 152.7 %reduce-scatter.2.cloned.1.call-start = ((), (), s32[]{:S(2)}) async-start(), calls=%async_computation.3 | async-start | bytes 3538944 | tf_op jit(solution)/shard_map/reduce_scatter | solution.py:83
  50.4 44.8 %copy-start.1 = (s32[8]{0:T(128)S(1)}, s32[8]{0:T(128)}, u32[]{:S(2)}) copy-start(s32[8]{0:T(128)} %param.9) | copy-start | bytes 100
Sparse Core Ops, SparseCore 0:
  9.9 30.5 all-gather.2
  42.4 23.4 all-gather.4
  116.4 44.9 reduce-scatter.1
where the time goes:
time: 209 us
  waiting for transfers between devices  89.4 us (43%)
  blocking collectives  70.7 us (34%)
  between operations  19 us (9%)
  matrix products  13.5 us (6%)
  local copies, waits for them, and re-layouts  9.17 us (4%)
  other arithmetic  6.57 us (3%)
    reduce_scatter x1, waiting for transfers between devices, local(): lax.psum_scatter(grad_block(features, hidden, proj_all, pooled, grad_embe...  45.1 us
    psum x1, blocking collectives, local(): total = lax.psum(shard_term, 'dp')  37 us
    all_gather x1, waiting for transfers between devices, local(): lax.all_gather(conv_weight, 'fsdp', axis=0, tiled=True)  29.9 us
    all_gather x1, blocking collectives, local(): all_embed = lax.all_gather(embed_own, 'dp', axis=0, tiled=True)  13.2 us
    all_gather x1, waiting for transfers between devices, local(): lax.all_gather(proj_weight, 'fsdp', axis=0, tiled=True)  13 us
    unnamed x1, blocking collectives  11.6 us
    psum x1, blocking collectives, local(): lax.psum((jnp.sum(centered * centered), positive_own), 'dp')  8.97 us
    dot_general x1, matrix products, forward_cols(): lax.dot_general(features, conv_rows, (((1,), (1,)), ((), ())), preferred_...  5.77 us
  transfers between devices with their start and end apart: 3, of which 3 were waited for; matrix products, arithmetic and copies ran while one was open for 7% of the time, Pallas kernels for 0%

commit v1 on v0

v1 whole, which is shorter than its diff:
```python
import functools

import jax
import jax.numpy as jnp
from jax import lax
from jax.experimental import pallas as pl
from jax.experimental.pallas import tpu as pltpu
from jax.sharding import PartitionSpec as P

POS = 49
GAMMA = 3.0
EPSILON = 1e-06
BF = jnp.bfloat16
F32 = jnp.float32
NT = (((1,), (1,)), ((), ()))
TN = (((0,), (0,)), ((), ()))
VMEM_LIMIT = 24 * 1024 * 1024


def dot(a, b, dims=(((1,), (0,)), ((), ()))):
    return lax.dot_general(a, b, dims, preferred_element_type=F32)


def vspec():
    return pl.BlockSpec(memory_space=pltpu.VMEM)


def params():
    return pltpu.CompilerParams(vmem_limit_bytes=VMEM_LIMIT)


def image_of_row(shape, row_dim, image_dim):
    row = lax.broadcasted_iota(jnp.int32, shape, row_dim)
    first = lax.broadcasted_iota(jnp.int32, shape, image_dim) * POS
    return jnp.where((row >= first) & (row < first + POS), 1.0, 0.0).astype(BF)


def forward_block(feat, short, conv, pick):
    hidden = jnp.maximum(dot(feat, conv, NT) + short.astype(F32), 0.0)
    mask = jnp.where(hidden > 0, 1.0, 0.0).astype(BF)
    pooled = dot(pick, hidden.astype(BF)) / POS
    return mask, pooled


def forward_kernel(blocks, images, cols_ref, f_own, f_sib, *refs):
    shorts, convs = refs[: 2 * blocks], refs[2 * blocks : 3 * blocks]
    outs = refs[3 * blocks :]
    pick = image_of_row((images, f_own.shape[0]), 1, 0)
    for j in range(blocks):
        conv = convs[j][...]
        m_own, p_own = forward_block(f_own[...], shorts[2 * j][...], conv, pick)
        m_sib, p_sib = forward_block(f_sib[...], shorts[2 * j + 1][...], conv, pick)
        outs[3 * j][...] = m_own
        outs[3 * j + 1][...] = m_sib
        outs[3 * j + 2][...] = jnp.concatenate([p_own, p_sib], axis=0).astype(BF)


def last_forward_kernel(total, images, cols_ref, f_own, f_sib, s_own, s_sib, conv_ref, partner, *refs):
    pooled, projs = refs[: total - 1], refs[total - 1 : 2 * total - 1]
    m_own_ref, m_sib_ref, pooled_ref, mine_ref, send_ref = refs[2 * total - 1 :]
    pick = image_of_row((images, f_own.shape[0]), 1, 0)
    embed = jnp.zeros((2 * images, projs[0].shape[1]), F32)
    for j in range(total - 1):
        embed = embed + dot(pooled[j][...], projs[j][...])
    conv = conv_ref[...]
    m_own, p_own = forward_block(f_own[...], s_own[...], conv, pick)
    m_sib, p_sib = forward_block(f_sib[...], s_sib[...], conv, pick)
    m_own_ref[...] = m_own
    m_sib_ref[...] = m_sib
    last = jnp.concatenate([p_own, p_sib], axis=0).astype(BF)
    pooled_ref[...] = last
    embed = embed + dot(last, projs[total - 1][...])
    half = embed.shape[1] // 2
    whole = jnp.broadcast_to(partner[...], (images, half))
    none = jnp.zeros((images, half), F32)
    mine_ref[0 : 2 * images] = embed
    mine_ref[2 * images :] = jnp.concatenate([whole, none], axis=1)
    send_ref[0:images] = embed[images:]
    send_ref[images : 2 * images] = embed[:images]
    send_ref[2 * images :] = jnp.concatenate([none, whole], axis=1)


def column_block(j, side, i, cols):
    return (0, cols[j])


def forward_specs(rows, width, count, picks):
    return [pl.BlockSpec((rows, width), lambda i, cols: (0, 0))] * 2, [
        pl.BlockSpec((rows, count), functools.partial(column_block, j, side))
        for j in picks
        for side in (0, 1)
    ]


def whole_spec(shape):
    return pl.BlockSpec(shape, lambda i, cols: (0,) * len(shape))


def forward(cols, f_own, f_sib, s_own, s_sib, convs, images):
    rows, width = f_own.shape
    count = convs[0].shape[0]
    blocks = len(convs)
    feat_specs, short_specs = forward_specs(rows, width, count, range(blocks))
    shapes = [(rows, count), (rows, count), (2 * images, count)] * blocks
    outs = pl.pallas_call(
        functools.partial(forward_kernel, blocks, images),
        grid_spec=pltpu.PrefetchScalarGridSpec(
            num_scalar_prefetch=1,
            grid=(1,),
            in_specs=feat_specs + short_specs + [whole_spec(c.shape) for c in convs],
            out_specs=[whole_spec(s) for s in shapes],
        ),
        out_shape=[jax.ShapeDtypeStruct(s, BF) for s in shapes],
        compiler_params=params(),
        cost_estimate=pl.CostEstimate(
            flops=4 * blocks * rows * width * count, bytes_accessed=8 * blocks * rows * count, transcendentals=0
        ),
        name="forward_blocks",
    )(cols, f_own, f_sib, *([s_own, s_sib] * blocks), *convs)
    return [outs[3 * j : 3 * j + 3] for j in range(blocks)]


def last_forward(cols, f_own, f_sib, s_own, s_sib, conv, partner, pooled, projs, images):
    rows, width = f_own.shape
    count = conv.shape[0]
    total = len(projs)
    embed = projs[0].shape[1]
    feat_specs, short_specs = forward_specs(rows, width, count, [total - 1])
    shapes = [(rows, count), (rows, count), (2 * images, count)]
    packed = (3 * images, embed)
    return pl.pallas_call(
        functools.partial(last_forward_kernel, total, images),
        grid_spec=pltpu.PrefetchScalarGridSpec(
            num_scalar_prefetch=1,
            grid=(1,),
            in_specs=feat_specs
            + short_specs
            + [whole_spec(a.shape) for a in (conv, partner, *pooled, *projs)],
            out_specs=[whole_spec(s) for s in shapes] + [whole_spec(packed)] * 2,
        ),
        out_shape=[jax.ShapeDtypeStruct(s, BF) for s in shapes] + [jax.ShapeDtypeStruct(packed, F32)] * 2,
        compiler_params=params(),
        cost_estimate=pl.CostEstimate(
            flops=4 * rows * width * count, bytes_accessed=8 * rows * count, transcendentals=0
        ),
        name="forward_last",
    )(cols, f_own, f_sib, s_own, s_sib, conv, partner, *pooled, *projs)


def group_terms(z, partner, groups):
    count = z.shape[0]
    z = z - jnp.mean(z, axis=0, keepdims=True)
    squares = jnp.sum(z * z, axis=1, keepdims=True)
    spread = 2.0 * jnp.mean(squares)
    inner = lax.dot_general(z, z, NT, precision=lax.Precision.HIGHEST, preferred_element_type=F32)
    row = lax.broadcasted_iota(jnp.int32, (count, count), 0)
    col = lax.broadcasted_iota(jnp.int32, (count, count), 1)
    across = jnp.sum(jnp.where(row == col, squares, 0.0), axis=0, keepdims=True)
    kernel = jnp.exp(-(squares + across - 2.0 * inner) / (2.0 * spread))
    r_col = jnp.mean(kernel, axis=1, keepdims=True)
    r_row = jnp.mean(kernel, axis=0, keepdims=True)
    t = jnp.mean(r_col)
    centered = kernel - r_col - r_row + t
    scale_sq = float(count - 1) ** 2
    root = jnp.sqrt(jnp.sum(centered * centered, keepdims=True) / scale_sq + EPSILON)
    onehot = jnp.where(partner == col.astype(F32), 1.0, 0.0)
    positive = jnp.sum(kernel * onehot, keepdims=True) / count
    loss = -(positive - t) + GAMMA * root
    coeff = (-onehot / count + 1.0 / (count * count) + GAMMA * centered / (scale_sq * root)) / groups
    weighted = coeff * kernel
    moved = lax.dot_general(
        weighted, z, (((1,), (0,)), ((), ())), precision=lax.Precision.HIGHEST, preferred_element_type=F32
    )
    return loss, -(2.0 / spread) * (jnp.sum(weighted, axis=1, keepdims=True) * z - moved)


def hsic_kernel(slabs, images, groups, place_ref, *refs):
    chunks = refs[:-4]
    ge_ref, loss_ref, z_ref, p_ref = refs[-4:]
    place = place_ref[0]
    count = slabs * images
    half = z_ref.shape[1] // 2
    for g in (0, 1):
        for j in range(slabs):
            if len(chunks) == 1:
                block = chunks[0].at[j]
            else:
                block = chunks[j]
            at = pl.ds(pl.multiple_of((place ^ j) * images, images), images)
            z_ref[at] = block[g * images : (g + 1) * images]
            p_ref[at] = block[2 * images :, g * half : g * half + 128]
        partner = jnp.max(p_ref[...], axis=1, keepdims=True)
        loss, grad = group_terms(z_ref[...], partner, groups)
        if g == 0:
            loss_ref[...] = loss
        z_ref[...] = grad
        for j in range(slabs):
            at = pl.ds(pl.multiple_of((place ^ j) * images, images), images)
            ge_ref[j, g * images : (g + 1) * images] = z_ref[at]


def hsic(place, chunks, slabs, images, groups):
    embed = chunks[0].shape[-1]
    return pl.pallas_call(
        functools.partial(hsic_kernel, slabs, images, groups),
        in_specs=[pl.BlockSpec(memory_space=pltpu.SMEM)] + [vspec()] * len(chunks),
        out_specs=[vspec()] * 2,
        out_shape=[
            jax.ShapeDtypeStruct((slabs, 2 * images, embed), F32),
            jax.ShapeDtypeStruct((1, 1), F32),
        ],
        scratch_shapes=[pltpu.VMEM((slabs * images, embed), F32), pltpu.VMEM((slabs * images, 128), F32)],
        compiler_params=params(),
        name="hsic_groups",
    )(place, *chunks)


def backward_kernel(blocks, images, packed, f_own, f_sib, ge_ref, *refs):
    ins, outs = refs[: 4 * blocks], refs[4 * blocks :]
    spread = image_of_row((f_own.shape[0], images), 0, 1)
    mine = ge_ref[0].astype(BF)
    for j in range(blocks):
        m_own, m_sib, pooled, proj = ins[4 * j : 4 * j + 4]
        out = outs[j]
        count, width = proj.shape[0], f_own.shape[1]
        grad_pool = dot(mine, proj[...], NT) / POS
        total = jnp.zeros((count, width), F32)
        for mask, feat, part in (
            (m_own, f_own, grad_pool[:images]),
            (m_sib, f_sib, grad_pool[images:]),
        ):
            grad_hidden = dot(spread, part.astype(BF)).astype(BF) * mask[...]
            total = total + dot(grad_hidden, feat[...], TN)
        out[0:count] = total.astype(out.dtype)
        if packed:
            slabs = ge_ref.shape[0]
            flat = ge_ref[...].reshape(slabs * 2 * images, ge_ref.shape[2]).astype(BF)
            half = slabs * images
            out[count : count + half] = jnp.concatenate([flat[:half], flat[half:]], axis=1)
            extra = pooled[...]
            rest = jnp.zeros((2 * images, width - extra.shape[1]), BF)
            out[count + half :] = jnp.concatenate([extra, rest], axis=1)


def backward(f_own, f_sib, ge, blocks, images, packed):
    width = f_own.shape[1]
    rows = f_own.shape[0]
    count = blocks[0][3].shape[0]
    high = count + (ge.shape[0] + 2) * images if packed else count
    return pl.pallas_call(
        functools.partial(backward_kernel, len(blocks), images, packed),
        in_specs=[vspec()] * (3 + 4 * len(blocks)),
        out_specs=[vspec()] * len(blocks),
        out_shape=[jax.ShapeDtypeStruct((high, width), BF if packed else F32)] * len(blocks),
        compiler_params=params(),
        cost_estimate=pl.CostEstimate(
            flops=4 * len(blocks) * rows * width * count,
            bytes_accessed=4 * len(blocks) * rows * count,
            transcendentals=0,
        ),
        name="backward_blocks",
    )(f_own, f_sib, ge, *[a for block in blocks for a in block])


def proj_kernel(peers, slabs, images, count, own_ge, *refs):
    msgs, pooled, out = refs[: peers - 1], refs[peers - 1 : -1], refs[-1]
    embed = own_ge.shape[2]
    half = slabs * images
    parts = []
    for j in range(slabs):
        rows = [own_ge[j].astype(BF)]
        start, left = j * 2 * images, 0
        if start >= half:
            start, left = start - half, embed
        for msg in msgs:
            rows.append(msg[count + start : count + start + 2 * images, left : left + embed])
        slab = pooled[0][j] if len(pooled) == 1 else pooled[j][...]
        parts.append(dot(slab, jnp.concatenate(rows, axis=0), TN))
    while len(parts) > 1:
        parts = [parts[k] + parts[k + 1] for k in range(0, len(parts), 2)]
    out[...] = parts[0]


def proj_grad(own_ge, msgs, pooled, slabs, images, count):
    embed = own_ge.shape[2]
    return pl.pallas_call(
        functools.partial(proj_kernel, len(msgs) + 1, slabs, images, count),
        in_specs=[vspec()] * (1 + len(msgs) + len(pooled)),
        out_specs=vspec(),
        out_shape=jax.ShapeDtypeStruct((count, embed), F32),
        compiler_params=params(),
        name="proj_grad",
    )(own_ge, *msgs, *pooled)


def swap(x, axis, bit):
    size = lax.axis_size(axis)
    return lax.ppermute(x, axis, [(i, i ^ bit) for i in range(size)])


def gather_slabs(x, slabs):
    if slabs <= 4:
        return [x] + [swap(x, "dp", j) for j in range(1, slabs)]
    whole = lax.all_gather(x, "dp", axis=0, tiled=False)
    return [jnp.take(whole, lax.axis_index("dp") ^ jnp.arange(slabs), axis=0)]


def local(features, shortcut, conv_weight, proj_weight, partner):
    slabs, groups = lax.axis_size("dp"), lax.axis_size("fsdp")
    peers = groups // 2
    images = features.shape[0] // POS
    count, width = conv_weight.shape
    place = lax.axis_index("dp").astype(jnp.int32)
    index = lax.axis_index("fsdp").astype(jnp.int32)
    cols = index ^ (2 * jnp.arange(peers, dtype=jnp.int32))

    convs, projs = [conv_weight], [proj_weight]
    if peers == 4:
        conv_y, conv_x = swap(conv_weight, "fsdp", 4), swap(conv_weight, "fsdp", 2)
        proj_x, proj_y = swap(proj_weight, "fsdp", 2), swap(proj_weight, "fsdp", 4)
        convs += [conv_x, conv_y, swap(conv_y, "fsdp", 2)]
        projs += [proj_x, proj_y, swap(proj_x, "fsdp", 4)]
    else:
        convs += [swap(conv_weight, "fsdp", 2 * j) for j in range(1, peers)]
        projs += [swap(proj_weight, "fsdp", 2 * j) for j in range(1, peers)]
    f_sib = swap(features, "fsdp", 1)
    s_sib = swap(shortcut, "fsdp", 1)

    blocks = forward(cols, features, f_sib, shortcut, s_sib, convs[:-1], images)
    member = partner.astype(F32).reshape(images, 1)
    *last, mine, send = last_forward(
        cols, features, f_sib, shortcut, s_sib, convs[-1], member, [b[2] for b in blocks], projs, images
    )
    blocks = [(*b, p) for b, p in zip(blocks + [last], projs)]
    embeds = mine + swap(send, "fsdp", 1)
    ge, loss = hsic(place.reshape(1), gather_slabs(embeds, slabs), slabs, images, groups)

    (far,) = backward(features, f_sib, ge, blocks[-1:], images, True)
    msgs = [swap(far, "fsdp", 2 * (peers - 1))]
    near = backward(features, f_sib, ge, blocks[1:-1], images, True)
    msgs = [swap(m, "fsdp", 2 * j) for j, m in enumerate(near, 1)] + msgs
    (own,) = backward(features, f_sib, ge, blocks[:1], images, False)

    half = slabs * images
    pooled = jnp.concatenate([blocks[0][2]] + [m[count + half :, :count] for m in msgs], axis=0)
    total = own
    for m in msgs:
        total = total + m[:count].astype(F32)
    bit = 1
    while bit < slabs:
        total = total.astype(BF)
        total = total.astype(F32) + swap(total, "dp", bit).astype(F32)
        bit *= 2
    grad_proj = proj_grad(ge, msgs, gather_slabs(pooled, slabs), slabs, images, count)
    return total, grad_proj, loss.reshape(1)


def solution(mesh):
    return jax.shard_map(
        local,
        mesh=mesh,
        in_specs=(
            P(("dp", "fsdp"), None),
            P(("dp", "fsdp"), None),
            P("fsdp", None),
            P("fsdp", None),
            P(("dp", "fsdp")),
        ),
        out_specs=(P("fsdp", None), P("fsdp", None), P("fsdp")),
        check_vma=False,
    )
```

time: 209 us -> 80.5 us (0.39)
  blocking collectives: 70.7 us -> 0 us
  waiting for transfers between devices: 89.4 us -> 36.3 us
  starting transfers between devices: 0.11 us -> 23 us
  between operations: 19 us -> 0.84 us
  matrix products: 13.5 us -> 0 us
  Pallas kernels: 0 us -> 10 us
  other arithmetic: 6.57 us -> 1.75 us
    psum x2 -> x0, blocking collectives: 46 us -> none  [the longest x1 37 us: local(): total = lax.psum(shard_term, 'dp')]
    reduce_scatter x1 -> x0, waiting for transfers between devices: 45.1 us -> none  [local(): lax.psum_scatter(grad_block(features, hidden, proj_all, pooled, grad_embe...]
    all_gather x2 -> x0, waiting for transfers between devices: 43 us -> none  [the longest x1 29.9 us: local(): lax.all_gather(conv_weight, 'fsdp', axis=0, tiled=True)]
    ppermute x0 -> x20, waiting for transfers between devices: none -> 36.3 us  [swap(): return lax.ppermute(x, axis, [(i, i ^ bit) for i in range(size)])]
    ppermute x0 -> x20, starting transfers between devices: none -> 23 us  [swap(): return lax.ppermute(x, axis, [(i, i ^ bit) for i in range(size)])]
    dot_general x7 -> x0, matrix products: 13.5 us -> none  [the longest x1 5.77 us: forward_cols(): lax.dot_general(features, conv_rows, (((1,), (1,)), ((), ())), preferred_...]
    all_gather x1 -> x0, blocking collectives: 13.2 us -> none  [local(): all_embed = lax.all_gather(embed_own, 'dp', axis=0, tiled=True)]
    unnamed x1 -> x0, blocking collectives: 11.6 us -> none
  transfers between devices with their start and end apart: 3 -> 20, of which waited for: 3 -> 9; matrix products, arithmetic and copies ran while one was open for 7% -> 1% of each run, Pallas kernels for 0% -> 7%
where the time goes in v1:
time: 80.5 us; the launch traced here: 80.2 us
  waiting for transfers between devices  36.3 us (45%)
  starting transfers between devices  23 us (29%)
  Pallas kernels  10 us (12%)
  local copies, waits for them, and re-layouts  8.32 us (10%)
  other arithmetic  1.75 us (2%)
  between operations  0.84 us (1%)
    ppermute x20, waiting for transfers between devices, swap(): return lax.ppermute(x, axis, [(i, i ^ bit) for i in range(size)])  36.3 us
    ppermute x20, starting transfers between devices, swap(): return lax.ppermute(x, axis, [(i, i ^ bit) for i in range(size)])  23 us
    unnamed x42, local copies, waits for them, and re-layouts  8.23 us
    pallas_call x3, Pallas kernels, backward(): pl.pallas_call(functools.partial(backward_kernel, len(blocks), images, pa...  3.28 us
    pallas_call x1, Pallas kernels, forward(): pl.pallas_call(functools.partial(forward_kernel, blocks, images), grid_sp...  2.66 us
  transfers between devices with their start and end apart: 20, of which 9 were waited for; matrix products, arithmetic and copies ran while one was open for 1% of the time, Pallas kernels for 7%

profile of v1, /device:TPU:0, one launch (start us, length us, event | category | flops | bytes accessed | tf_op | source)
XLA Modules:
  0.0 80.2 jit_solution(5338158137876236678)
XLA Ops:
  0.6 0.5 collective-permute-start.1
  1.1 2.6 %collective-permute-start.2 = (bf16[256,512]{1,0:T(8,128)(2,1)}, bf16[256,512]{1,0:T(8,128)(2,1)S(1)}, u32[]{:S(2)}, u32[]{:S(2)}) collective-permute-start(bf16[256,512]{1,0:T(8,128)(2,1)} %refs_6_.1), channel_id=1, source_target_pairs={{0,4},{1,5},{2,6},{3,7},{4,0},{5,1},{6,2},{7,3},{8,12},{9,13},{10,... | collective-permute-start | bytes 786440 | tf_op jit(solution)/shard_map/ppermute | solution.py:298
  3.7 0.2 collective-permute-start
  3.9 1.5 %collective-permute-start.4 = (bf16[256,512]{1,0:T(8,128)(2,1)}, bf16[256,512]{1,0:T(8,128)(2,1)S(1)}, u32[]{:S(2)}, u32[]{:S(2)}) collective-permute-start(bf16[256,512]{1,0:T(8,128)(2,1)} %refs_6_.1), channel_id=1, source_target_pairs={{0,2},{1,3},{2,0},{3,1},{4,6},{5,7},{6,4},{7,5},{8,10},{9,11},{10,... | collective-permute-start | bytes 786440 | tf_op jit(solution)/shard_map/ppermute | solution.py:298
  5.4 0.5 collective-permute-start.5
  5.9 4.9 %collective-permute-done.2.refs_8_ = bf16[256,512]{1,0:T(8,128)(2,1)S(1)} collective-permute-done((bf16[256,512]{1,0:T(8,128)(2,1)}, bf16[256,512]{1,0:T(8,128)(2,1)S(1)}, u32[]{:S(2)}, u32[]{:S(2)}) %collective-permute-start.2) | collective-permute-done | bytes 262176 | tf_op jit(solution)/shard_map/ppermute | solution.py:298
  10.9 1.7 %collective-permute-start.3 = (bf16[256,512]{1,0:T(8,128)(2,1)S(1)}, bf16[256,512]{1,0:T(8,128)(2,1)S(1)}, u32[]{:S(2)}, u32[]{:S(2)}) collective-permute-start(bf16[256,512]{1,0:T(8,128)(2,1)S(1)} %collective-permute-done.2.refs_8_), channel_id=1, source_target_pairs={{0,2},{1,3},{2,0},{3,1},{4,6},{5,7},{6,4},{7,5},{8,10},{9,11},{10,... | collective-permute-start | bytes 786440 | tf_op jit(solution)/shard_map/ppermute | solution.py:298
  12.6 0.7 convert_bitcast_fusion
  13.2 0.1 copy.8.partner
  13.3 2.7 %collective-permute-done.5.refs_4_.refs_3_ = bf16[256,256]{1,0:T(8,128)(2,1)S(1)} collective-permute-done((bf16[256,256]{1,0:T(8,128)(2,1)}, bf16[256,256]{1,0:T(8,128)(2,1)S(1)}, u32[]{:S(2)}, u32[]{:S(2)}) %collective-permute-start.5) | collective-permute-done | bytes 131104 | tf_op jit(solution)/shard_map/ppermute | solution.py:298
  16.1 0.3 collective-permute-start.6
  16.3 0.0 collective-permute-done.4.refs_7_
  16.3 1.8 %collective-permute-start.7 = (bf16[256,256]{1,0:T(8,128)(2,1)S(1)}, bf16[256,256]{1,0:T(8,128)(2,1)S(1)}, u32[]{:S(2)}, u32[]{:S(2)}) collective-permute-start(bf16[256,256]{1,0:T(8,128)(2,1)S(1)} %collective-permute-done.5.refs_4_.refs_3_), channel_id=1, source_target_pairs={{0,4},{1,5},{2,6},{3,7},{4,0},{5,1},{6,2},{7,3},{8,12},{9,13},{10,... | collective-permute-start | bytes 393224 | tf_op jit(solution)/shard_map/ppermute | solution.py:298
  18.1 0.0 collective-permute-done.f_sib
  18.1 0.0 collective-permute-done.1.refs_1_.refs_3_.refs_5_.s_sib
  18.1 0.0 copy-start
  18.1 1.4 %copy-done = bf16[392,2048]{1,0:T(8,128)(2,1)S(1)} copy-done((bf16[392,2048]{1,0:T(8,128)(2,1)S(1)}, bf16[392,2048]{1,0:T(8,128)(2,1)}, u32[]{:S(2)}) %copy-start) | copy-done | bytes 1605656
  19.5 1.0 %copy-done.1 = bf16[392,512]{1,0:T(8,128)(2,1)S(1)} copy-done((bf16[392,512]{1,0:T(8,128)(2,1)S(1)}, bf16[392,512]{1,0:T(8,128)(2,1)}, u32[]{:S(2)}) %copy-start.1) | copy-done | bytes 401432
  20.5 0.9 %copy-done.4 = bf16[256,512]{1,0:T(8,128)(2,1)S(1)} copy-done((bf16[256,512]{1,0:T(8,128)(2,1)S(1)}, bf16[256,512]{1,0:T(8,128)(2,1)}, u32[]{:S(2)}) %copy-start.4) | copy-done | bytes 262168
  21.5 2.7 %forward_blocks.1 = (bf16[392,256]{1,0:T(8,128)(2,1)S(1)}, bf16[392,256]{1,0:T(8,128)(2,1)S(1)}, bf16[16,256]{1,0:T(8,128)(2,1)S(1)}, bf16[392,256]{1,0:T(8,128)...) custom-call(s32[4]{0:T(128)S(1)} %multiply_xor_fusion.cols_ref, ...), custom_call_target="tpu_custom_call" | custom-call | flops 616562688 | bytes 2408448 | tf_op jit(solution)/shard_map/forward_blocks/pallas_call | solution.py:105
  24.1 0.7 copy-done.9
  24.8 0.0 collective-permute-done.6.refs_5_.refs_7_
  24.8 0.0 collective-permute-done.7.refs_6_.refs_3_
  24.9 0.0 collective-permute-done.3.conv_ref
  24.9 0.0 copy-start.2
  24.9 1.5 %forward_last.1 = (bf16[392,256]{1,0:T(8,128)(2,1)S(1)}, bf16[392,256]{1,0:T(8,128)(2,1)S(1)}, bf16[16,256]{1,0:T(8,128)(2,1)S(1)}, f32[24,256]{1,0:T(8,128)S(1)}, f32[24,256]{1,0:T(8,128)S(1)}) custom-call(s32[4]{0:T(128)S(1)} %multiply_xor_fusion.cols_ref, bf16[392,512]{1,0:T(8,128)(2,1)S(1)} %copy-done.1, ...), custom_call_target="tpu_custom_call" | custom-call | flops 205520896 | bytes 802816 | tf_op jit(solution)/shard_map/forward_last/pallas_call | solution.py:131
  26.4 0.0 copy-done.11
  26.5 0.7 copy-done.17
  27.2 0.7 copy-done.19
  27.8 0.0 collective-permute-start.8
  27.9 1.2 %collective-permute-done.8 = f32[24,256]{1,0:T(8,128)S(1)} collective-permute-done((f32[24,256]{1,0:T(8,128)S(1)}, f32[24,256]{1,0:T(8,128)S(1)}, u32[]{:S(2)}, u32[]{:S(2)}) %collective-permute-start.8) | collective-permute-done | bytes 24608 | tf_op jit(solution)/shard_map/ppermute | solution.py:298
  29.1 2.6 %collective-permute-start.10 = (f32[24,256]{1,0:T(8,128)S(1)}, f32[24,256]{1,0:T(8,128)S(1)}, u32[]{:S(2)}, u32[]{:S(2)}) collective-permute-start(f32[24,256]{1,0:T(8,128)S(1)} %add.18.refs_0_), channel_id=1, source_target_pairs={{0,16},{8,24},{16,0},{24,8},{1,17},{9,25},{17,1},{25,9},{2,18},{10... | collective-permute-start | bytes 73736 | tf_op jit(solution)/shard_map/ppermute | solution.py:298
  31.6 1.3 %collective-permute-start.11 = (f32[24,256]{1,0:T(8,128)S(1)}, f32[24,256]{1,0:T(8,128)S(1)}, u32[]{:S(2)}, u32[]{:S(2)}) collective-permute-start(f32[24,256]{1,0:T(8,128)S(1)} %add.18.refs_0_), channel_id=1, source_target_pairs={{0,24},{8,16},{16,8},{24,0},{1,25},{9,17},{17,9},{25,1},{2,26},{10... | collective-permute-start | bytes 73736 | tf_op jit(solution)/shard_map/ppermute | solution.py:298
  33.0 0.2 collective-permute-start.9
  33.2 0.6 collective-permute-done.10.refs_2_
  33.8 3.5 %collective-permute-done.11.refs_3_ = f32[24,256]{1,0:T(8,128)S(1)} collective-permute-done((f32[24,256]{1,0:T(8,128)S(1)}, f32[24,256]{1,0:T(8,128)S(1)}, u32[]{:S(2)}, u32[]{:S(2)}) %collective-permute-start.11) | collective-permute-done | bytes 24608 | tf_op jit(solution)/shard_map/ppermute | solution.py:298
  37.3 0.0 collective-permute-done.9.refs_1_
  37.3 1.5 %hsic_groups.1 = (f32[4,16,256]{2,1,0:T(8,128)S(1)}, f32[1,1]{1,0:T(1,128)}) custom-call(s32[1]{0:T(128)} %bitcast.place_ref, f32[24,256]{1,0:T(8,128)S(1)} %add.18.refs_0_, f32[24,256]{1,0:T(8,128)S(1)} %collective-permute-done.9.refs_1_, f32[24,256]{1,0:T(8,128)S(1)} %collective-permute-done.10.refs_2_, f32[24,256]{1,0:T(8,128)S(1)} %collective-permute-done.11.refs_3_), custom_call_target="tpu_custom_call" | custom-call | tf_op jit(solution)/shard_map/hsic_groups/pallas_call | solution.py:204
  38.8 0.9 %copy-done.12 = bf16[392,256]{1,0:T(8,128)(2,1)S(1)} copy-done((bf16[392,256]{1,0:T(8,128)(2,1)S(1)}, bf16[392,256]{1,0:T(8,128)(2,1)}, u32[]{:S(2)}) %copy-start.12) | copy-done | bytes 200728
  39.7 0.9 %copy-done.14 = bf16[392,256]{1,0:T(8,128)(2,1)S(1)} copy-done((bf16[392,256]{1,0:T(8,128)(2,1)S(1)}, bf16[392,256]{1,0:T(8,128)(2,1)}, u32[]{:S(2)}) %copy-start.14) | copy-done | bytes 200728
  40.7 0.9 %copy-done.16 = bf16[392,256]{1,0:T(8,128)(2,1)S(1)} copy-done((bf16[392,256]{1,0:T(8,128)(2,1)S(1)}, bf16[392,256]{1,0:T(8,128)(2,1)}, u32[]{:S(2)}) %copy-start.16) | copy-done | bytes 200728
  41.6 1.5 %backward_blocks.4 = (bf16[304,512]{1,0:T(8,128)(2,1)S(1)}, bf16[304,512]{1,0:T(8,128)(2,1)S(1)}) custom-call(bf16[392,512]{1,0:T(8,128)(2,1)S(1)} %copy-done.2, bf16[392,512]{1,0:T(8,128)(2,1)S(1)} %collective-permute-done.f_sib, f32[4,16,256]{2,1,0:T(8,128)S(1)} %get-tuple-element.26.ge_ref.own_ge, bf16[392,256]{1,0:T(8,128)(2,1)S(1)} %copy-done.10, ...), custom_call_target="tpu_custom_call" | custom-call | flops 411041792 | bytes 802816 | tf_op jit(solution)/shard_map/backward_blocks/pallas_call | solution.py:250
  43.1 1.5 %collective-permute-start.12 = (bf16[304,512]{1,0:T(8,128)(2,1)S(1)}, bf16[304,512]{1,0:T(8,128)(2,1)S(1)}, u32[]{:S(2)}, u32[]{:S(2)}) collective-permute-start(bf16[304,512]{1,0:T(8,128)(2,1)S(1)} %get-tuple-element.33), channel_id=1, source_target_pairs={{0,2},{1,3},{2,0},{3,1},{4,6},{5,7},{6,4},{7,5},{8,10},{9,11},{10,... | collective-permute-start | bytes 933896 | tf_op jit(solution)/shard_map/ppermute | solution.py:298
  44.7 0.5 collective-permute-start.13
  45.2 0.9 %backward_blocks.5 = bf16[304,512]{1,0:T(8,128)(2,1)S(1)} custom-call(bf16[392,512]{1,0:T(8,128)(2,1)S(1)} %copy-done.2, bf16[392,512]{1,0:T(8,128)(2,1)S(1)} %collective-permute-done.f_sib, f32[4,16,256]{2,1,0:T(8,128)S(1)} %get-tuple-element.26.ge_ref.own_ge, bf16[392,256]{1,0:T(8,128)(2,1)S(1)} %copy-done.18, bf16[392,256]{1,0:T(8,128)(2,1)S(1)} %copy-done.20, ...), custom_call_target="tpu_custom_call" | custom-call | flops 205520896 | bytes 401408 | tf_op jit(solution)/shard_map/backward_blocks/pallas_call | solution.py:250
  46.1 1.6 %collective-permute-start.14 = (bf16[304,512]{1,0:T(8,128)(2,1)S(1)}, bf16[304,512]{1,0:T(8,128)(2,1)S(1)}, u32[]{:S(2)}, u32[]{:S(2)}) collective-permute-start(bf16[304,512]{1,0:T(8,128)(2,1)S(1)} %backward_blocks.5), channel_id=1, source_target_pairs={{0,6},{1,7},{2,4},{3,5},{4,2},{5,3},{6,0},{7,1},{8,14},{9,15},{10,... | collective-permute-start | bytes 933896 | tf_op jit(solution)/shard_map/ppermute | solution.py:298
  47.6 0.9 %backward_blocks.3 = f32[256,512]{1,0:T(8,128)S(1)} custom-call(bf16[392,512]{1,0:T(8,128)(2,1)S(1)} %copy-done.2, bf16[392,512]{1,0:T(8,128)(2,1)S(1)} %collective-permute-done.f_sib, f32[4,16,256]{2,1,0:T(8,128)S(1)} %get-tuple-element.26.ge_ref.own_ge, bf16[392,256]{1,0:T(8,128)(2,1)S(1)} %copy-done.6, bf16[392,256]{1,0:T(8,128)(2,1)S(1)} %copy-done.8, ...), custom_call_target="tpu_custom_call" | custom-call | flops 205520896 | bytes 401408 | tf_op jit(solution)/shard_map/backward_blocks/pallas_call | solution.py:250
  48.5 5.0 %collective-permute-done.12.refs_0_ = bf16[304,512]{1,0:T(8,128)(2,1)S(1)} collective-permute-done((bf16[304,512]{1,0:T(8,128)(2,1)S(1)}, bf16[304,512]{1,0:T(8,128)(2,1)S(1)}, u32[]{:S(2)}, u32[]{:S(2)}) %collective-permute-start.12) | collective-permute-done | bytes 311328 | tf_op jit(solution)/shard_map/ppermute | solution.py:298
  53.5 5.6 %collective-permute-done.13.refs_1_ = bf16[304,512]{1,0:T(8,128)(2,1)S(1)} collective-permute-done((bf16[304,512]{1,0:T(8,128)(2,1)S(1)}, bf16[304,512]{1,0:T(8,128)(2,1)S(1)}, u32[]{:S(2)}, u32[]{:S(2)}) %collective-permute-start.13) | collective-permute-done | bytes 311328 | tf_op jit(solution)/shard_map/ppermute | solution.py:298
  59.1 0.0 collective-permute-done.14.refs_2_
  59.1 0.1 add_convert_fusion.1
  59.2 0.1 collective-permute-start.15
  59.3 8.0 %collective-permute-done.15 = bf16[256,512]{1,0:T(8,128)(2,1)S(1)} collective-permute-done((bf16[256,512]{1,0:T(8,128)(2,1)S(1)}, bf16[256,512]{1,0:T(8,128)(2,1)S(1)}, u32[]{:S(2)}, u32[]{:S(2)}) %collective-permute-start.15) | collective-permute-done | bytes 262176 | tf_op jit(solution)/shard_map/ppermute | solution.py:298
  67.3 0.1 add_convert_fusion
  67.4 1.6 %collective-permute-start.16 = (bf16[256,512]{1,0:T(8,128)(2,1)S(1)}, bf16[256,512]{1,0:T(8,128)(2,1)S(1)}, u32[]{:S(2)}, u32[]{:S(2)}) collective-permute-start(bf16[256,512]{1,0:T(8,128)(2,1)S(1)} %add_convert_fusion), channel_id=1, source_target_pairs={{0,16},{8,24},{16,0},{24,8},{1,17},{9,25},{17,1},{25,9},{2,18},{10... | collective-permute-start | bytes 786440 | tf_op jit(solution)/shard_map/ppermute | solution.py:298
  69.0 0.5 collective-permute-start.17
  69.5 1.0 %collective-permute-start.18 = (bf16[64,256]{1,0:T(8,128)(2,1)S(1)}, bf16[64,256]{1,0:T(8,128)(2,1)S(1)}, u32[]{:S(2)}, u32[]{:S(2)}) collective-permute-start(bf16[64,256]{1,0:T(8,128)(2,1)S(1)} %pad_maximum_fusion.refs_3_), channel_id=1, source_target_pairs={{0,16},{8,24},{16,0},{24,8},{1,17},{9,25},{17,1},{25,9},{2,18},{10... | collective-permute-start | bytes 98312 | tf_op jit(solution)/shard_map/ppermute | solution.py:298
  70.5 2.9 %collective-permute-start.19 = (bf16[64,256]{1,0:T(8,128)(2,1)S(1)}, bf16[64,256]{1,0:T(8,128)(2,1)S(1)}, u32[]{:S(2)}, u32[]{:S(2)}) collective-permute-start(bf16[64,256]{1,0:T(8,128)(2,1)S(1)} %pad_maximum_fusion.refs_3_), channel_id=1, source_target_pairs={{0,24},{8,16},{16,8},{24,0},{1,25},{9,17},{17,9},{25,1},{2,26},{10... | collective-permute-start | bytes 98312 | tf_op jit(solution)/shard_map/ppermute | solution.py:298
  73.4 0.0 collective-permute-done.17.refs_4_
  73.4 4.8 %collective-permute-done.18.refs_5_ = bf16[64,256]{1,0:T(8,128)(2,1)S(1)} collective-permute-done((bf16[64,256]{1,0:T(8,128)(2,1)S(1)}, bf16[64,256]{1,0:T(8,128)(2,1)S(1)}, u32[]{:S(2)}, u32[]{:S(2)}) %collective-permute-start.18) | collective-permute-done | bytes 32800 | tf_op jit(solution)/shard_map/ppermute | solution.py:298
  78.3 0.0 collective-permute-done.19.refs_6_
  78.3 1.0 %proj_grad.1 = f32[256,256]{1,0:T(8,128)} custom-call(f32[4,16,256]{2,1,0:T(8,128)S(1)} %get-tuple-element.26.ge_ref.own_ge, bf16[304,512]{1,0:T(8,128)(2,1)S(1)} %collective-permute-done.12.refs_0_, bf16[304,512]{1,0:T(8,128)(2,1)S(1)} %collective-permute-done.13.refs_1_, bf16[304,512]{1,0:T(8,128)(2,1)S(1)} %collective-permute-done.14.refs_2_, ...), custom_call_target="tpu_custom_call" | custom-call | tf_op jit(solution)/shard_map/proj_grad/pallas_call | solution.py:286
  79.3 0.0 collective-permute-done.16
  79.3 0.9 %convert_add_fusion = f32[256,512]{1,0:T(8,128)} fusion(bf16[256,512]{1,0:T(8,128)(2,1)S(1)} %collective-permute-done.16, bf16[256,512]{1,0:T(8,128)(2,1)S(1)} %add_convert_fusion), kind=kLoop, calls=%fused_computation | loop fusion | flops 393216 | bytes 1048576 | tf_op jit(solution)/shard_map/add | solution.py:352
  (36 shorter events, 0.1 us)
Async XLA Ops:
  0.6 17.5 %collective-permute-start.1 = (bf16[392,2048]{1,0:T(8,128)(2,1)}, bf16[392,2048]{1,0:T(8,128)(2,1)S(1)}, u32[]{:S(2)}, u32[]{:S(2)}) collective-permute-start(bf16[392,2048]{1,0:T(8,128)(2,1)} %s_own.1), channel_id=1, source_target_pairs={{0,1},{1,0},{2,3},{3,2},{4,5},{5,4},{6,7},{7,6},{8,9},{9,8},{10,11... | collective-permute-start | bytes 4816904 | tf_op jit(solution)/shard_map/ppermute | solution.py:298
  1.1 9.7 %collective-permute-start.2 = (bf16[256,512]{1,0:T(8,128)(2,1)}, bf16[256,512]{1,0:T(8,128)(2,1)S(1)}, u32[]{:S(2)}, u32[]{:S(2)}) collective-permute-start(bf16[256,512]{1,0:T(8,128)(2,1)} %refs_6_.1), channel_id=1, source_target_pairs={{0,4},{1,5},{2,6},{3,7},{4,0},{5,1},{6,2},{7,3},{8,12},{9,13},{10,... | collective-permute-start | bytes 786440 | tf_op jit(solution)/shard_map/ppermute | solution.py:298
  3.7 14.3 %collective-permute-start = (bf16[392,512]{1,0:T(8,128)(2,1)}, bf16[392,512]{1,0:T(8,128)(2,1)S(1)}, u32[]{:S(2)}, u32[]{:S(2)}) collective-permute-start(bf16[392,512]{1,0:T(8,128)(2,1)} %f_own.9), channel_id=1, source_target_pairs={{0,1},{1,0},{2,3},{3,2},{4,5},{5,4},{6,7},{7,6},{8,9},{9,8},{10,11... | collective-permute-start | bytes 1204232 | tf_op jit(solution)/shard_map/ppermute | solution.py:298
  3.9 12.4 %collective-permute-start.4 = (bf16[256,512]{1,0:T(8,128)(2,1)}, bf16[256,512]{1,0:T(8,128)(2,1)S(1)}, u32[]{:S(2)}, u32[]{:S(2)}) collective-permute-start(bf16[256,512]{1,0:T(8,128)(2,1)} %refs_6_.1), channel_id=1, source_target_pairs={{0,2},{1,3},{2,0},{3,1},{4,6},{5,7},{6,4},{7,5},{8,10},{9,11},{10,... | collective-permute-start | bytes 786440 | tf_op jit(solution)/shard_map/ppermute | solution.py:298
  5.4 10.7 %collective-permute-start.5 = (bf16[256,256]{1,0:T(8,128)(2,1)}, bf16[256,256]{1,0:T(8,128)(2,1)S(1)}, u32[]{:S(2)}, u32[]{:S(2)}) collective-permute-start(bf16[256,256]{1,0:T(8,128)(2,1)} %refs_3_.3), channel_id=1, source_target_pairs={{0,2},{1,3},{2,0},{3,1},{4,6},{5,7},{6,4},{7,5},{8,10},{9,11},{10,... | collective-permute-start | bytes 393224 | tf_op jit(solution)/shard_map/ppermute | solution.py:298
  10.9 14.0 %collective-permute-start.3 = (bf16[256,512]{1,0:T(8,128)(2,1)S(1)}, bf16[256,512]{1,0:T(8,128)(2,1)S(1)}, u32[]{:S(2)}, u32[]{:S(2)}) collective-permute-start(bf16[256,512]{1,0:T(8,128)(2,1)S(1)} %collective-permute-done.2.refs_8_), channel_id=1, source_target_pairs={{0,2},{1,3},{2,0},{3,1},{4,6},{5,7},{6,4},{7,5},{8,10},{9,11},{10,... | collective-permute-start | bytes 786440 | tf_op jit(solution)/shard_map/ppermute | solution.py:298
  16.1 8.8 %collective-permute-start.6 = (bf16[256,256]{1,0:T(8,128)(2,1)}, bf16[256,256]{1,0:T(8,128)(2,1)S(1)}, u32[]{:S(2)}, u32[]{:S(2)}) collective-permute-start(bf16[256,256]{1,0:T(8,128)(2,1)} %refs_3_.3), channel_id=1, source_target_pairs={{0,4},{1,5},{2,6},{3,7},{4,0},{5,1},{6,2},{7,3},{8,12},{9,13},{10,... | collective-permute-start | bytes 393224 | tf_op jit(solution)/shard_map/ppermute | solution.py:298
  16.3 8.5 %collective-permute-start.7 = (bf16[256,256]{1,0:T(8,128)(2,1)S(1)}, bf16[256,256]{1,0:T(8,128)(2,1)S(1)}, u32[]{:S(2)}, u32[]{:S(2)}) collective-permute-start(bf16[256,256]{1,0:T(8,128)(2,1)S(1)} %collective-permute-done.5.refs_4_.refs_3_), channel_id=1, source_target_pairs={{0,4},{1,5},{2,6},{3,7},{4,0},{5,1},{6,2},{7,3},{8,12},{9,13},{10,... | collective-permute-start | bytes 393224 | tf_op jit(solution)/shard_map/ppermute | solution.py:298
  18.1 1.4 %copy-start = (bf16[392,2048]{1,0:T(8,128)(2,1)S(1)}, bf16[392,2048]{1,0:T(8,128)(2,1)}, u32[]{:S(2)}) copy-start(bf16[392,2048]{1,0:T(8,128)(2,1)} %s_own.1) | copy-start | bytes 4816900
  19.5 1.0 %copy-start.1 = (bf16[392,512]{1,0:T(8,128)(2,1)S(1)}, bf16[392,512]{1,0:T(8,128)(2,1)}, u32[]{:S(2)}) copy-start(bf16[392,512]{1,0:T(8,128)(2,1)} %f_own.9) | copy-start | bytes 1204228
  20.5 0.9 %copy-start.4 = (bf16[256,512]{1,0:T(8,128)(2,1)S(1)}, bf16[256,512]{1,0:T(8,128)(2,1)}, u32[]{:S(2)}) copy-start(bf16[256,512]{1,0:T(8,128)(2,1)} %refs_6_.1) | copy-start | bytes 786436
  21.5 3.4 %copy-start.3 = (bf16[256,256]{1,0:T(8,128)(2,1)S(1)}, bf16[256,256]{1,0:T(8,128)(2,1)}, u32[]{:S(2)}) copy-start(bf16[256,256]{1,0:T(8,128)(2,1)} %refs_3_.3) | copy-start | bytes 393220
  24.1 0.7 copy-start.9
  24.8 1.6 %copy-start.5 = (bf16[392,256]{1,0:T(8,128)(2,1)}, bf16[392,256]{1,0:T(8,128)(2,1)S(1)}, u32[]{:S(2)}) copy-start(bf16[392,256]{1,0:T(8,128)(2,1)S(1)} %get-tuple-element.27.refs_0_) | copy-start | bytes 602116
  24.8 1.6 %copy-start.7 = (bf16[392,256]{1,0:T(8,128)(2,1)}, bf16[392,256]{1,0:T(8,128)(2,1)S(1)}, u32[]{:S(2)}) copy-start(bf16[392,256]{1,0:T(8,128)(2,1)S(1)} %get-tuple-element.28.refs_1_) | copy-start | bytes 602116
  24.8 1.6 %copy-start.11 = (bf16[392,256]{1,0:T(8,128)(2,1)}, bf16[392,256]{1,0:T(8,128)(2,1)S(1)}, u32[]{:S(2)}) copy-start(bf16[392,256]{1,0:T(8,128)(2,1)S(1)} %get-tuple-element.30.refs_1_) | copy-start | bytes 602116
  24.8 1.6 %copy-start.13 = (bf16[392,256]{1,0:T(8,128)(2,1)}, bf16[392,256]{1,0:T(8,128)(2,1)S(1)}, u32[]{:S(2)}) copy-start(bf16[392,256]{1,0:T(8,128)(2,1)S(1)} %get-tuple-element.31.refs_4_) | copy-start | bytes 602116
  24.8 1.6 %copy-start.15 = (bf16[392,256]{1,0:T(8,128)(2,1)}, bf16[392,256]{1,0:T(8,128)(2,1)S(1)}, u32[]{:S(2)}) copy-start(bf16[392,256]{1,0:T(8,128)(2,1)S(1)} %get-tuple-element.32.refs_5_) | copy-start | bytes 602116
  24.9 13.9 %copy-start.2 = (bf16[392,512]{1,0:T(8,128)(2,1)S(1)}, bf16[392,512]{1,0:T(8,128)(2,1)}, u32[]{:S(2)}) copy-start(bf16[392,512]{1,0:T(8,128)(2,1)} %f_own.9) | copy-start | bytes 1204228
  24.9 13.9 %copy-start.10 = (bf16[392,256]{1,0:T(8,128)(2,1)S(1)}, bf16[392,256]{1,0:T(8,128)(2,1)}, u32[]{:S(2)}) copy-start(bf16[392,256]{1,0:T(8,128)(2,1)} %copy-done.9) | copy-start | bytes 602116
  26.5 0.7 copy-start.17
  27.2 0.7 copy-start.19
  27.8 1.2 %collective-permute-start.8 = (f32[24,256]{1,0:T(8,128)S(1)}, f32[24,256]{1,0:T(8,128)S(1)}, u32[]{:S(2)}, u32[]{:S(2)}) collective-permute-start(f32[24,256]{1,0:T(8,128)S(1)} %get-tuple-element.25), channel_id=1, source_target_pairs={{0,1},{1,0},{2,3},{3,2},{4,5},{5,4},{6,7},{7,6},{8,9},{9,8},{10,11... | collective-permute-start | bytes 73736 | tf_op jit(solution)/shard_map/ppermute | solution.py:298
  29.1 4.7 %collective-permute-start.10 = (f32[24,256]{1,0:T(8,128)S(1)}, f32[24,256]{1,0:T(8,128)S(1)}, u32[]{:S(2)}, u32[]{:S(2)}) collective-permute-start(f32[24,256]{1,0:T(8,128)S(1)} %add.18.refs_0_), channel_id=1, source_target_pairs={{0,16},{8,24},{16,0},{24,8},{1,17},{9,25},{17,1},{25,9},{2,18},{10... | collective-permute-start | bytes 73736 | tf_op jit(solution)/shard_map/ppermute | solution.py:298
  31.6 5.6 %collective-permute-start.11 = (f32[24,256]{1,0:T(8,128)S(1)}, f32[24,256]{1,0:T(8,128)S(1)}, u32[]{:S(2)}, u32[]{:S(2)}) collective-permute-start(f32[24,256]{1,0:T(8,128)S(1)} %add.18.refs_0_), channel_id=1, source_target_pairs={{0,24},{8,16},{16,8},{24,0},{1,25},{9,17},{17,9},{25,1},{2,26},{10... | collective-permute-start | bytes 73736 | tf_op jit(solution)/shard_map/ppermute | solution.py:298
  33.0 4.3 %collective-permute-start.9 = (f32[24,256]{1,0:T(8,128)S(1)}, f32[24,256]{1,0:T(8,128)S(1)}, u32[]{:S(2)}, u32[]{:S(2)}) collective-permute-start(f32[24,256]{1,0:T(8,128)S(1)} %add.18.refs_0_), channel_id=1, source_target_pairs={{0,8},{8,0},{16,24},{24,16},{1,9},{9,1},{17,25},{25,17},{2,10},{10... | collective-permute-start | bytes 73736 | tf_op jit(solution)/shard_map/ppermute | solution.py:298
  38.8 0.9 %copy-start.12 = (bf16[392,256]{1,0:T(8,128)(2,1)S(1)}, bf16[392,256]{1,0:T(8,128)(2,1)}, u32[]{:S(2)}) copy-start(bf16[392,256]{1,0:T(8,128)(2,1)} %copy-done.11) | copy-start | bytes 602116
  39.7 0.9 %copy-start.14 = (bf16[392,256]{1,0:T(8,128)(2,1)S(1)}, bf16[392,256]{1,0:T(8,128)(2,1)}, u32[]{:S(2)}) copy-start(bf16[392,256]{1,0:T(8,128)(2,1)} %copy-done.13) | copy-start | bytes 602116
  40.6 0.9 %copy-start.16 = (bf16[392,256]{1,0:T(8,128)(2,1)S(1)}, bf16[392,256]{1,0:T(8,128)(2,1)}, u32[]{:S(2)}) copy-start(bf16[392,256]{1,0:T(8,128)(2,1)} %copy-done.15) | copy-start | bytes 602116
  41.6 3.6 %copy-start.18 = (bf16[392,256]{1,0:T(8,128)(2,1)S(1)}, bf16[392,256]{1,0:T(8,128)(2,1)}, u32[]{:S(2)}) copy-start(bf16[392,256]{1,0:T(8,128)(2,1)} %copy-done.17) | copy-start | bytes 602116
  41.6 3.6 %copy-start.20 = (bf16[392,256]{1,0:T(8,128)(2,1)S(1)}, bf16[392,256]{1,0:T(8,128)(2,1)}, u32[]{:S(2)}) copy-start(bf16[392,256]{1,0:T(8,128)(2,1)} %copy-done.19) | copy-start | bytes 602116
  41.6 6.1 %copy-start.6 = (bf16[392,256]{1,0:T(8,128)(2,1)S(1)}, bf16[392,256]{1,0:T(8,128)(2,1)}, u32[]{:S(2)}) copy-start(bf16[392,256]{1,0:T(8,128)(2,1)} %copy-done.5) | copy-start | bytes 602116
  41.6 6.1 %copy-start.8 = (bf16[392,256]{1,0:T(8,128)(2,1)S(1)}, bf16[392,256]{1,0:T(8,128)(2,1)}, u32[]{:S(2)}) copy-start(bf16[392,256]{1,0:T(8,128)(2,1)} %copy-done.7) | copy-start | bytes 602116
  43.1 10.4 %collective-permute-start.12 = (bf16[304,512]{1,0:T(8,128)(2,1)S(1)}, bf16[304,512]{1,0:T(8,128)(2,1)S(1)}, u32[]{:S(2)}, u32[]{:S(2)}) collective-permute-start(bf16[304,512]{1,0:T(8,128)(2,1)S(1)} %get-tuple-element.33), channel_id=1, source_target_pairs={{0,2},{1,3},{2,0},{3,1},{4,6},{5,7},{6,4},{7,5},{8,10},{9,11},{10,... | collective-permute-start | bytes 933896 | tf_op jit(solution)/shard_map/ppermute | solution.py:298
  44.7 14.4 %collective-permute-start.13 = (bf16[304,512]{1,0:T(8,128)(2,1)S(1)}, bf16[304,512]{1,0:T(8,128)(2,1)S(1)}, u32[]{:S(2)}, u32[]{:S(2)}) collective-permute-start(bf16[304,512]{1,0:T(8,128)(2,1)S(1)} %get-tuple-element.34), channel_id=1, source_target_pairs={{0,4},{1,5},{2,6},{3,7},{4,0},{5,1},{6,2},{7,3},{8,12},{9,13},{10,... | collective-permute-start | bytes 933896 | tf_op jit(solution)/shard_map/ppermute | solution.py:298
  46.1 13.0 %collective-permute-start.14 = (bf16[304,512]{1,0:T(8,128)(2,1)S(1)}, bf16[304,512]{1,0:T(8,128)(2,1)S(1)}, u32[]{:S(2)}, u32[]{:S(2)}) collective-permute-start(bf16[304,512]{1,0:T(8,128)(2,1)S(1)} %backward_blocks.5), channel_id=1, source_target_pairs={{0,6},{1,7},{2,4},{3,5},{4,2},{5,3},{6,0},{7,1},{8,14},{9,15},{10,... | collective-permute-start | bytes 933896 | tf_op jit(solution)/shard_map/ppermute | solution.py:298
  59.2 8.1 %collective-permute-start.15 = (bf16[256,512]{1,0:T(8,128)(2,1)S(1)}, bf16[256,512]{1,0:T(8,128)(2,1)S(1)}, u32[]{:S(2)}, u32[]{:S(2)}) collective-permute-start(bf16[256,512]{1,0:T(8,128)(2,1)S(1)} %add_convert_fusion.1), channel_id=1, source_target_pairs={{0,8},{8,0},{16,24},{24,16},{1,9},{9,1},{17,25},{25,17},{2,10},{10... | collective-permute-start | bytes 786440 | tf_op jit(solution)/shard_map/ppermute | solution.py:298
  67.4 11.9 %collective-permute-start.16 = (bf16[256,512]{1,0:T(8,128)(2,1)S(1)}, bf16[256,512]{1,0:T(8,128)(2,1)S(1)}, u32[]{:S(2)}, u32[]{:S(2)}) collective-permute-start(bf16[256,512]{1,0:T(8,128)(2,1)S(1)} %add_convert_fusion), channel_id=1, source_target_pairs={{0,16},{8,24},{16,0},{24,8},{1,17},{9,25},{17,1},{25,9},{2,18},{10... | collective-permute-start | bytes 786440 | tf_op jit(solution)/shard_map/ppermute | solution.py:298
  69.0 4.5 %collective-permute-start.17 = (bf16[64,256]{1,0:T(8,128)(2,1)S(1)}, bf16[64,256]{1,0:T(8,128)(2,1)S(1)}, u32[]{:S(2)}, u32[]{:S(2)}) collective-permute-start(bf16[64,256]{1,0:T(8,128)(2,1)S(1)} %pad_maximum_fusion.refs_3_), channel_id=1, source_target_pairs={{0,8},{8,0},{16,24},{24,16},{1,9},{9,1},{17,25},{25,17},{2,10},{10... | collective-permute-start | bytes 98312 | tf_op jit(solution)/shard_map/ppermute | solution.py:298
  69.5 8.7 %collective-permute-start.18 = (bf16[64,256]{1,0:T(8,128)(2,1)S(1)}, bf16[64,256]{1,0:T(8,128)(2,1)S(1)}, u32[]{:S(2)}, u32[]{:S(2)}) collective-permute-start(bf16[64,256]{1,0:T(8,128)(2,1)S(1)} %pad_maximum_fusion.refs_3_), channel_id=1, source_target_pairs={{0,16},{8,24},{16,0},{24,8},{1,17},{9,25},{17,1},{25,9},{2,18},{10... | collective-permute-start | bytes 98312 | tf_op jit(solution)/shard_map/ppermute | solution.py:298
  70.5 7.8 %collective-permute-start.19 = (bf16[64,256]{1,0:T(8,128)(2,1)S(1)}, bf16[64,256]{1,0:T(8,128)(2,1)S(1)}, u32[]{:S(2)}, u32[]{:S(2)}) collective-permute-start(bf16[64,256]{1,0:T(8,128)(2,1)S(1)} %pad_maximum_fusion.refs_3_), channel_id=1, source_target_pairs={{0,24},{8,16},{16,8},{24,0},{1,25},{9,17},{17,9},{25,1},{2,26},{10... | collective-permute-start | bytes 98312 | tf_op jit(solution)/shard_map/ppermute | solution.py:298

commit v2 on v0

v2 whole, which is shorter than its diff:
```python
import functools

import jax
import jax.numpy as jnp
from jax import lax
from jax.experimental import pallas as pl
from jax.experimental.pallas import tpu as pltpu
from jax.sharding import PartitionSpec as P

POS = 49
GAMMA = 3.0
EPSILON = 1e-06
BF = jnp.bfloat16
F32 = jnp.float32
NT = (((1,), (1,)), ((), ()))
TN = (((0,), (0,)), ((), ()))
VMEM_LIMIT = 8 * 1024 * 1024
SPLIT = 4


def dot(a, b, dims=(((1,), (0,)), ((), ()))):
    return lax.dot_general(a, b, dims, preferred_element_type=F32)


def vspec():
    return pl.BlockSpec(memory_space=pltpu.VMEM)


def params(more=0):
    return pltpu.CompilerParams(vmem_limit_bytes=VMEM_LIMIT + more)


def image_of_row(shape, row_dim, image_dim):
    row = lax.broadcasted_iota(jnp.int32, shape, row_dim)
    first = lax.broadcasted_iota(jnp.int32, shape, image_dim) * POS
    return jnp.where((row >= first) & (row < first + POS), 1.0, 0.0).astype(BF)


def forward_block(feat, short, conv, pick):
    hidden = jnp.maximum(dot(feat, conv, NT) + short.astype(F32), 0.0)
    mask = jnp.where(hidden > 0, 1.0, 0.0).astype(BF)
    pooled = dot(pick, hidden.astype(BF)) / POS
    return mask, pooled


def forward_blocks(picks, feats, shorts, convs, projs, embed, outs, ready=None):
    images = outs[2].shape[0] // 2
    pick_rows = image_of_row((images, feats[0].shape[0]), 1, 0)
    for j in range(picks):
        pooled = []
        for side in (0, 1):
            if ready is not None:
                ready(j, side)
            mask, mean = forward_block(feats[side][...], shorts[2 * j + side][...], convs[j][...], pick_rows)
            outs[3 * j + side][...] = mask
            pooled.append(mean)
        pooled = jnp.concatenate(pooled, axis=0).astype(BF)
        outs[3 * j + 2][...] = pooled
        embed = embed + dot(pooled, projs[j][...])
    return embed


def first_kernel(peers, images, index_ref, partner, f_sib, f_own, s_own, s_sib, conv, proj, *refs):
    blocks, embed_ref, feat, proj_out, member_ref = refs[:3], refs[3], refs[4], refs[5], refs[6]
    ahead, (short, conv_buf, sems) = refs[7 : 5 + 2 * peers], refs[5 + 2 * peers :]
    index = index_ref[0]
    count = conv_buf.shape[0]
    copies = []

    def fetch(source, target):
        copies.append(pltpu.make_async_copy(source, target, sems.at[len(copies)]))
        copies[-1].start()

    fetch(f_own, feat)
    fetch(conv, conv_buf)
    shorts = [short.at[0], short.at[1], *ahead]
    for k, target in enumerate(shorts):
        at = pl.ds(pl.multiple_of((index ^ (k // 2 * 2)) * count, count), count)
        fetch((s_own, s_sib)[k % 2].at[:, at], target)
        if k == 1:
            fetch(proj, proj_out)
    member = lax.broadcasted_iota(jnp.int32, member_ref.shape, 0)
    whole = jnp.zeros(member_ref.shape, F32)
    for i in range(images):
        whole = jnp.where(member == i, partner[i].astype(F32), whole)
    member_ref[...] = whole
    for copy in copies[:5]:
        copy.wait()
    embed = jnp.zeros(embed_ref.shape, F32)
    embed_ref[...] = forward_blocks(1, (feat, f_sib), shorts, [conv_buf], [proj_out], embed, blocks)
    for copy in copies[5:]:
        copy.wait()


def middle_kernel(blocks, f_own, f_sib, before, *refs):
    shorts, convs, projs = refs[: 2 * blocks], refs[2 * blocks : 3 * blocks], refs[3 * blocks : 4 * blocks]
    outs = refs[4 * blocks :]
    outs[-1][...] = forward_blocks(blocks, (f_own, f_sib), shorts, convs, projs, before[...], outs)


def last_kernel(images, f_own, f_sib, before, member, s_own, s_sib, conv, proj, *outs):
    embed = forward_blocks(1, (f_own, f_sib), (s_own, s_sib), [conv], [proj], before[...], outs)
    mine_ref, send_ref = outs[-2:]
    half = embed.shape[1] // 2
    whole = jnp.concatenate([member[...]] * (half // member.shape[1]), axis=1)
    none = jnp.zeros((images, half), F32)
    mine_ref[0 : 2 * images] = embed
    mine_ref[2 * images :] = jnp.concatenate([whole, none], axis=1)
    send_ref[0:images] = embed[images:]
    send_ref[images : 2 * images] = embed[:images]
    send_ref[2 * images :] = jnp.concatenate([none, whole], axis=1)


def forward_call(kernel, in_specs, shapes, scratch, busy, name, *arrays):
    rows, width, count = busy
    return pl.pallas_call(
        kernel,
        in_specs=in_specs,
        out_specs=[vspec()] * len(shapes),
        out_shape=[jax.ShapeDtypeStruct(shape, kind) for shape, kind in shapes],
        scratch_shapes=scratch,
        compiler_params=params(),
        cost_estimate=pl.CostEstimate(
            flops=16 * rows * width * count, bytes_accessed=8 * rows * count, transcendentals=0
        ),
        name=name,
    )(*arrays)


def block_shapes(rows, count, images):
    return [((rows, count), BF), ((rows, count), BF), ((2 * images, count), BF)]


def forward_first(index, partner, feats, shorts, conv, proj, peers, images):
    rows, width = feats[0].shape
    count, embed = proj.shape
    hbm = [pltpu.with_memory_space_constraint(a, pltpu.HBM) for a in (feats[0], shorts[0], conv, proj)]
    hbm.insert(2, shorts[1])
    shapes = block_shapes(rows, count, images)
    shapes += [((2 * images, embed), F32), ((rows, width), BF), ((count, embed), BF), ((images, 128), F32)]
    shapes += [((rows, count), BF)] * (2 * peers - 2)
    outs = forward_call(
        functools.partial(first_kernel, peers, images),
        [pl.BlockSpec(memory_space=pltpu.SMEM)] * 2 + [vspec()] + [pl.BlockSpec(memory_space=pl.ANY)] * 5,
        shapes,
        [
            pltpu.VMEM((2, rows, count), BF),
            pltpu.VMEM((count, width), BF),
            pltpu.SemaphoreType.DMA((3 + 2 * peers,)),
        ],
        (rows, width, count),
        "forward_first",
        *(index, pltpu.with_memory_space_constraint(partner, pltpu.HBM), feats[1], *hbm),
    )
    return outs[:3], outs[3], outs[4], outs[5], outs[6], outs[7:]


def forward_middle(feats, shorts, convs, projs, images, before):
    rows, width = feats[0].shape
    count, blocks = convs[0].shape[0], len(convs)
    arrays = (*feats, before, *shorts, *convs, *projs)
    outs = forward_call(
        functools.partial(middle_kernel, blocks),
        [vspec()] * len(arrays),
        block_shapes(rows, count, images) * blocks + [(before.shape, F32)],
        [],
        (rows, width, blocks * count),
        "forward_middle",
        *arrays,
    )
    return [outs[3 * j : 3 * j + 3] for j in range(blocks)], outs[-1]


def forward_last(feats, shorts, conv, proj, images, before, member):
    rows, width = feats[0].shape
    count, embed = proj.shape
    arrays = (*feats, before, member, *shorts, conv, proj)
    outs = forward_call(
        functools.partial(last_kernel, images),
        [vspec()] * len(arrays),
        block_shapes(rows, count, images) + [((3 * images, embed), F32)] * 2,
        [],
        (rows, width, count),
        "forward_last",
        *arrays,
    )
    return outs[:3], outs[3], outs[4]


def group_terms(z, partner, groups):
    count = z.shape[0]
    z = z - jnp.mean(z, axis=0, keepdims=True)
    squares = jnp.sum(z * z, axis=1, keepdims=True)
    spread = 2.0 * jnp.mean(squares)
    inner = lax.dot_general(z, z, NT, precision=lax.Precision.HIGHEST, preferred_element_type=F32)
    row = lax.broadcasted_iota(jnp.int32, (count, count), 0)
    col = lax.broadcasted_iota(jnp.int32, (count, count), 1)
    across = jnp.sum(jnp.where(row == col, squares, 0.0), axis=0, keepdims=True)
    kernel = jnp.exp(-(squares + across - 2.0 * inner) / (2.0 * spread))
    r_col = jnp.mean(kernel, axis=1, keepdims=True)
    r_row = jnp.mean(kernel, axis=0, keepdims=True)
    t = jnp.mean(r_col)
    centered = kernel - r_col - r_row + t
    scale_sq = float(count - 1) ** 2
    root = jnp.sqrt(jnp.sum(centered * centered, keepdims=True) / scale_sq + EPSILON)
    onehot = jnp.where(partner == col.astype(F32), 1.0, 0.0)
    positive = jnp.sum(kernel * onehot, keepdims=True) / count
    loss = -(positive - t) + GAMMA * root
    coeff = (-onehot / count + 1.0 / (count * count) + GAMMA * centered / (scale_sq * root)) / groups
    weighted = coeff * kernel
    moved = lax.dot_general(
        weighted, z, (((1,), (0,)), ((), ())), precision=lax.Precision.HIGHEST, preferred_element_type=F32
    )
    return loss, -(2.0 / spread) * (jnp.sum(weighted, axis=1, keepdims=True) * z - moved)


def hsic_kernel(slabs, images, groups, place_ref, *refs):
    chunks = refs[:-5]
    ge_ref, loss_ref, z_ref, p_ref, g_ref = refs[-5:]
    place = place_ref[0]
    half = z_ref.shape[2] // 2
    for j in range(slabs):
        block = chunks[0].at[j] if len(chunks) == 1 else chunks[j]
        at = pl.ds(pl.multiple_of((place ^ j) * images, images), images)
        for g in (0, 1):
            z_ref[g, at] = block[g * images : (g + 1) * images]
            p_ref[g, at] = block[2 * images :, g * half : g * half + 128]
    for g in (0, 1):
        partner = jnp.max(p_ref[g], axis=1, keepdims=True)
        loss, grad = group_terms(z_ref[g], partner, groups)
        if g == 0:
            loss_ref[...] = loss
        g_ref[g] = grad
    for j in range(slabs):
        at = pl.ds(pl.multiple_of((place ^ j) * images, images), images)
        for g in (0, 1):
            ge_ref[j, g * images : (g + 1) * images] = g_ref[g, at]


def hsic(place, chunks, slabs, images, groups):
    embed = chunks[0].shape[-1]
    return pl.pallas_call(
        functools.partial(hsic_kernel, slabs, images, groups),
        in_specs=[pl.BlockSpec(memory_space=pltpu.SMEM)] + [vspec()] * len(chunks),
        out_specs=[vspec()] * 2,
        out_shape=[
            jax.ShapeDtypeStruct((slabs, 2 * images, embed), F32),
            jax.ShapeDtypeStruct((1, 1), F32),
        ],
        scratch_shapes=[pltpu.VMEM((2, slabs * images, width), F32) for width in (embed, 128, embed)],
        compiler_params=params(80 * (slabs * images) ** 2),
        cost_estimate=pl.CostEstimate(flops=10**9, bytes_accessed=0, transcendentals=0),
        name="hsic_groups",
    )(place, *chunks)


def backward_kernel(blocks, images, part, extra, after, f_own, f_sib, ge_ref, *refs):
    ins, outs = refs[: 4 * blocks], refs[4 * blocks + after :]
    spread = image_of_row((f_own.shape[0], images), 0, 1)
    mine = ge_ref[0].astype(BF)
    start, rows = part
    width = f_own.shape[1]
    for j in range(blocks):
        m_own, m_sib, pooled, proj = ins[4 * j : 4 * j + 4]
        out = outs[j]
        grad_pool = dot(mine, proj[start : start + rows], NT) / POS
        total = jnp.zeros((rows, width), F32)
        for mask, feat, piece in (
            (m_own, f_own, grad_pool[:images]),
            (m_sib, f_sib, grad_pool[images:]),
        ):
            grad_hidden = dot(spread, piece.astype(BF)).astype(BF) * mask[:, start : start + rows]
            total = total + dot(grad_hidden, feat[...], TN)
        out[0:rows] = total.astype(out.dtype)
        if extra == "pooled":
            rest = jnp.zeros((2 * images, width - pooled.shape[1]), BF)
            out[rows:] = jnp.concatenate([pooled[...], rest], axis=1)
        if extra == "embed":
            slabs = ge_ref.shape[0]
            flat = ge_ref[...].reshape(slabs * 2 * images, ge_ref.shape[2]).astype(BF)
            half = slabs * images
            out[rows:] = jnp.concatenate([flat[:half], flat[half:]], axis=1)


def backward(feats, ge, blocks, images, part, extra=None, after=()):
    length, width = feats[0].shape
    rows = part[1]
    high = rows + {None: 0, "pooled": 2 * images, "embed": ge.shape[0] * images}[extra]
    return pl.pallas_call(
        functools.partial(backward_kernel, len(blocks), images, part, extra, len(after)),
        in_specs=[vspec()] * (3 + 4 * len(blocks)) + [pl.BlockSpec(memory_space=pl.ANY)] * len(after),
        out_specs=[vspec()] * len(blocks),
        out_shape=[jax.ShapeDtypeStruct((high, width), BF if extra else F32)] * len(blocks),
        compiler_params=params(),
        cost_estimate=pl.CostEstimate(
            flops=16 * len(blocks) * length * width * rows,
            bytes_accessed=4 * len(blocks) * length * rows,
            transcendentals=0,
        ),
        name="backward_blocks",
    )(*feats, ge, *[a for block in blocks for a in block], *after)


def small_call(kernel, shapes, name, *arrays, tokens=()):
    return pl.pallas_call(
        kernel,
        in_specs=[vspec()] * len(arrays) + [pl.BlockSpec(memory_space=pl.ANY)] * len(tokens),
        out_specs=[vspec()] * len(shapes),
        out_shape=[jax.ShapeDtypeStruct(shape, kind) for shape, kind in shapes],
        compiler_params=params(),
        cost_estimate=pl.CostEstimate(flops=0, bytes_accessed=0, transcendentals=0),
        name=name,
    )(*arrays, *tokens)


def sum_kernel(*refs):
    total = refs[0][...].astype(F32)
    for ref in refs[1:-1]:
        total = total + ref[...].astype(F32)
    refs[-1][...] = total.astype(refs[-1].dtype)


def sum_of(kind, *arrays):
    return small_call(sum_kernel, [(arrays[0].shape, kind)], "sum_arrays", *arrays)[0]


def collect_kernel(start, rows, count_msgs, own, pooled, *refs):
    msgs, out = refs[:count_msgs], refs[-1]
    total = own[start : start + rows]
    for msg in msgs:
        total = total + msg[0:rows].astype(F32)
    out[0:rows] = total.astype(BF)
    if out.shape[0] == rows:
        return
    high, count = pooled.shape
    slab = [pooled[...]] + [msg[rows : rows + high, 0:count] for msg in msgs]
    tall = (out.shape[0] - rows) // high
    for k, piece in enumerate(slab):
        at = rows + k % tall * high
        out[at : at + high, k // tall * count : (k // tall + 1) * count] = piece


def collect(own, pooled, msgs, part, with_pooled, token):
    start, rows = part
    width = own.shape[1]
    more = (len(msgs) + 1) * pooled.size // width if with_pooled else 0
    kernel = functools.partial(collect_kernel, start, rows, len(msgs))
    return small_call(kernel, [((rows + more, width), BF)], "collect_terms", own, pooled, *msgs, tokens=token)[0]


def merge_kernel(rows, mine, other, *refs):
    out = refs[-1]
    out[0:rows] = (mine[0:rows].astype(F32) + other[0:rows].astype(F32)).astype(BF)
    more = mine.shape[0] - rows
    if more:
        out[rows : rows + more] = mine[rows:]
        out[rows + more :] = other[rows:]


def merge(rows, mine, other, *token):
    high, width = mine.shape
    shape = (2 * high - rows, width)
    return small_call(functools.partial(merge_kernel, rows), [(shape, BF)], "merge_slabs", mine, other, tokens=token)[0]


def final_kernel(*refs):
    pieces, out = refs[:-1], refs[-1]
    tail = pieces[2].shape[0]
    head = out.shape[0] - tail
    out[0:head] = pieces[0][0:head].astype(F32) + pieces[1][0:head].astype(F32)
    out[head:] = pieces[2][...].astype(F32) + pieces[3][...].astype(F32)


def proj_kernel(slabs, images, rows, msg_rows, own_ge, mine, other, *refs):
    msgs, (out, token) = refs[:-2], refs[-2:]
    token[...] = jnp.zeros(token.shape, F32)
    count, embed = out.shape
    groups = mine.shape[1] // count
    half = slabs * images
    per = (mine.shape[0] - rows) // (slabs // 2)
    together = per // (2 * images)
    parts = []
    for j in range(slabs):
        pieces = [own_ge[j].astype(BF)]
        start, left = j * 2 * images, 0
        if start >= half:
            start, left = start - half, embed
        for msg in msgs:
            pieces.append(msg[msg_rows + start : msg_rows + start + 2 * images, left : left + embed])
        ref, at = (mine, j) if j < slabs // 2 else (other, j - slabs // 2)
        total = jnp.zeros((count, embed), F32)
        for g in range(groups):
            pooled = ref[rows + at * per : rows + (at + 1) * per, g * count : (g + 1) * count]
            grads = jnp.concatenate(pieces[g * together : (g + 1) * together], axis=0)
            total = total + dot(pooled, grads, TN)
        parts.append(total)
    while len(parts) > 1:
        parts = [parts[k] + parts[k + 1] for k in range(0, len(parts), 2)]
    out[...] = parts[0]


def gate_kernel(x, token, out):
    out[...] = x[...]


def after(x, token):
    return small_call(gate_kernel, [(x.shape, x.dtype)], "gate", x, tokens=(token,))[0]


def pack_kernel(start, conv, proj, token, out):
    half = conv.shape[0] // 2
    fold = conv.shape[1] // proj.shape[1]
    out[0:half] = conv[start : start + half]
    rows = half // fold
    for k in range(fold):
        piece = proj[start + k * rows : start + (k + 1) * rows]
        out[half:, k * proj.shape[1] : (k + 1) * proj.shape[1]] = piece


def pack_half(start, conv, proj, token):
    half, fold = conv.shape[0] // 2, conv.shape[1] // proj.shape[1]
    shape = (half + half // fold, conv.shape[1])
    return small_call(functools.partial(pack_kernel, start), [(shape, BF)], "pack_half", conv, proj, tokens=(token,))[0]


def unpack_kernel(*refs):
    conv, proj = refs[-2:]
    half = conv.shape[0] // 2
    fold = conv.shape[1] // proj.shape[1]
    rows = half // fold
    for k, ref in enumerate(refs[:-2]):
        conv[k * half : (k + 1) * half] = ref[0:half]
        for j in range(fold):
            at = k * half + j * rows
            proj[at : at + rows] = ref[half:, j * proj.shape[1] : (j + 1) * proj.shape[1]]


def swap(x, axis, bit):
    size = lax.axis_size(axis)
    return lax.ppermute(x, axis, [(i, i ^ bit) for i in range(size)])


def gather_slabs(x, slabs):
    if slabs <= 4:
        return [x] + [swap(x, "dp", j) for j in range(1, slabs)]
    whole = lax.all_gather(x, "dp", axis=0, tiled=False)
    return [jnp.take(whole, lax.axis_index("dp") ^ jnp.arange(slabs), axis=0)]


def local(features, shortcut, conv_weight, proj_weight, partner):
    slabs, groups = lax.axis_size("dp"), lax.axis_size("fsdp")
    peers = groups // 2
    images = features.shape[0] // POS
    count, width = conv_weight.shape
    place = lax.axis_index("dp").astype(jnp.int32).reshape(1)
    index = lax.axis_index("fsdp").astype(jnp.int32).reshape(1)

    f_sib = swap(features, "fsdp", 1)
    s_sib = swap(shortcut, "fsdp", 1)
    first, embed, f_own, proj_own, member, ahead = forward_first(
        index, partner, (features, f_sib), (shortcut, s_sib), conv_weight, proj_weight, peers, images
    )
    feats = (f_own, f_sib)
    if peers == 4:
        conv_y = swap(conv_weight, "fsdp", 4)
        proj_x = swap(proj_weight, "fsdp", 2)
        conv_x = swap(conv_weight, "fsdp", 2)
        proj_y = swap(proj_weight, "fsdp", 4)
        halves = [
            swap(pack_half(0, conv_y, proj_y, embed), "fsdp", 2),
            swap(pack_half(count // 2, conv_x, proj_x, embed), "fsdp", 4),
        ]
        conv_far, proj_far = small_call(
            unpack_kernel, [(conv_weight.shape, BF), (proj_weight.shape, BF)], "unpack_halves", *halves
        )
        convs, projs = [conv_x, conv_y, conv_far], [proj_x, proj_y, proj_far]
    else:
        convs = [swap(conv_weight, "fsdp", 2 * j) for j in range(1, peers)]
        projs = [swap(proj_weight, "fsdp", 2 * j) for j in range(1, peers)]
    middle, embed = forward_middle(feats, ahead[:-2], convs[:-1], projs[:-1], images, embed)
    last, mine, send = forward_last(feats, ahead[-2:], convs[-1], projs[-1], images, embed, member)
    blocks, projs = [first, *middle, last], [proj_own, *projs]
    blocks = [(*b, p) for b, p in zip(blocks, projs)]
    embeds = sum_of(F32, mine, swap(send, "fsdp", 1))
    ge, loss = hsic(place, gather_slabs(embeds, slabs), slabs, images, groups)

    first_rows = count * SPLIT // 8
    parts = [(0, first_rows), (first_rows, count - first_rows)]
    terms, done = [], ()
    for part, extra in zip(parts, ("pooled", "embed")):
        far = backward(feats, ge, blocks[-1:], images, part, extra, done)
        near = backward(feats, ge, blocks[1:-1], images, part, extra, tuple(far))
        done = tuple(near)
        terms.append([*near, *far])
    (own,) = backward(feats, ge, blocks[:1], images, (0, count), None, done)

    pieces, token = [], ()
    for k, part in enumerate(parts):
        if k:
            terms[k] = [after(m, total) for m in terms[k]]
        msgs = [swap(m, "fsdp", 2 * j) for j, m in enumerate(terms[k], 1)]
        total = collect(own, blocks[0][2], msgs, part, k == 0, pieces[:1])
        if k:
            grad_proj, token = small_call(
                functools.partial(proj_kernel, slabs, images, parts[0][1], part[1]),
                [(proj_weight.shape, F32), ((8, 128), F32)],
                "proj_grad",
                *(ge, *pieces, *msgs),
            )
            token = (token,)
        piece, bit = total, 1
        while 2 * bit < slabs:
            piece = merge(part[1], piece, swap(piece, "dp", bit), *token)
            bit *= 2
        pieces += [piece, swap(piece, "dp", bit)]
    (grad_conv,) = small_call(
        final_kernel, [((count, width), F32)], "sum_slabs", *pieces
    )
    return grad_conv, grad_proj, loss.reshape(1)


def solution(mesh):
    return jax.shard_map(
        local,
        mesh=mesh,
        in_specs=(
            P(("dp", "fsdp"), None),
            P(("dp", "fsdp"), None),
            P("fsdp", None),
            P("fsdp", None),
            P(("dp", "fsdp")),
        ),
        out_specs=(P("fsdp", None), P("fsdp", None), P("fsdp")),
        check_vma=False,
    )
```

time: 209 us -> 68.8 us (0.33)
  blocking collectives: 70.7 us -> 0 us
  waiting for transfers between devices: 89.4 us -> 28.5 us
  starting transfers between devices: 0.11 us -> 25.3 us
  between operations: 19 us -> 0.8 us
  Pallas kernels: 0 us -> 14 us
  matrix products: 13.5 us -> 0 us
  local copies, waits for them, and re-layouts: 9.17 us -> 0.01 us
  other arithmetic: 6.57 us -> 0 us
    psum x2 -> x0, blocking collectives: 46 us -> none  [the longest x1 37 us: local(): total = lax.psum(shard_term, 'dp')]
    reduce_scatter x1 -> x0, waiting for transfers between devices: 45.1 us -> none  [local(): lax.psum_scatter(grad_block(features, hidden, proj_all, pooled, grad_embe...]
    all_gather x2 -> x0, waiting for transfers between devices: 43 us -> none  [the longest x1 29.9 us: local(): lax.all_gather(conv_weight, 'fsdp', axis=0, tiled=True)]
    ppermute x0 -> x22, waiting for transfers between devices: none -> 28.5 us  [swap(): return lax.ppermute(x, axis, [(i, i ^ bit) for i in range(size)])]
    ppermute x0 -> x22, starting transfers between devices: none -> 25.3 us  [swap(): return lax.ppermute(x, axis, [(i, i ^ bit) for i in range(size)])]
    pallas_call x0 -> x22, Pallas kernels: none -> 14 us  [the longest x3 5.58 us: forward_call(): pl.pallas_call(kernel, in_specs=in_specs, out_specs=[vspec()] * len(shape...]
    dot_general x7 -> x0, matrix products: 13.5 us -> none  [the longest x1 5.77 us: forward_cols(): lax.dot_general(features, conv_rows, (((1,), (1,)), ((), ())), preferred_...]
    all_gather x1 -> x0, blocking collectives: 13.2 us -> none  [local(): all_embed = lax.all_gather(embed_own, 'dp', axis=0, tiled=True)]
  transfers between devices with their start and end apart: 3 -> 22, of which waited for: 3 -> 14; matrix products, arithmetic and copies ran while one was open for 7% -> 0% of each run, Pallas kernels for 0% -> 15%
where the time goes in v2:
time: 68.8 us; the launch traced here: 68.6 us
  waiting for transfers between devices  28.5 us (41%)
  starting transfers between devices  25.3 us (37%)
  Pallas kernels  14 us (20%)
  between operations  0.8 us (1%)
    ppermute x22, waiting for transfers between devices, swap(): return lax.ppermute(x, axis, [(i, i ^ bit) for i in range(size)])  28.5 us
    ppermute x22, starting transfers between devices, swap(): return lax.ppermute(x, axis, [(i, i ^ bit) for i in range(size)])  25.3 us
    pallas_call x3, Pallas kernels, forward_call(): pl.pallas_call(kernel, in_specs=in_specs, out_specs=[vspec()] * len(shape...  5.58 us
    pallas_call x5, Pallas kernels, backward(): pl.pallas_call(functools.partial(backward_kernel, len(blocks), images, pa...  4.82 us
    pallas_call x13, Pallas kernels, small_call(): pl.pallas_call(kernel, in_specs=[vspec()] * len(arrays) + [pl.BlockSpec(m...  2.31 us
  transfers between devices with their start and end apart: 22, of which 14 were waited for; matrix products, arithmetic and copies ran while one was open for 0% of the time, Pallas kernels for 15%

profile of v2, /device:TPU:0, one launch (start us, length us, event | category | flops | bytes accessed | tf_op | source)
XLA Modules:
  0.0 68.6 jit_solution(9937633068231589283)
XLA Ops:
  0.6 0.5 collective-permute-start.1
  1.1 0.1 collective-permute-start
  1.2 2.9 %collective-permute-start.3 = (bf16[256,512]{1,0:T(8,128)(2,1)}, bf16[256,512]{1,0:T(8,128)(2,1)S(1)}, u32[]{:S(2)}, u32[]{:S(2)}) collective-permute-start(bf16[256,512]{1,0:T(8,128)(2,1)} %conv.1), channel_id=1, source_target_pairs={{0,4},{1,5},{2,6},{3,7},{4,0},{5,1},{6,2},{7,3},{8,12},{9,13},{10,... | collective-permute-start | bytes 786440 | tf_op jit(solution)/shard_map/ppermute | solution.py:440
  4.2 1.5 %collective-permute-start.2 = (bf16[256,512]{1,0:T(8,128)(2,1)}, bf16[256,512]{1,0:T(8,128)(2,1)S(1)}, u32[]{:S(2)}, u32[]{:S(2)}) collective-permute-start(bf16[256,512]{1,0:T(8,128)(2,1)} %conv.1), channel_id=1, source_target_pairs={{0,2},{1,3},{2,0},{3,1},{4,6},{5,7},{6,4},{7,5},{8,10},{9,11},{10,... | collective-permute-start | bytes 786440 | tf_op jit(solution)/shard_map/ppermute | solution.py:440
  5.7 0.5 collective-permute-start.5
  6.2 0.0 collective-permute-done.f_sib
  6.2 1.7 %collective-permute-start.4 = (bf16[256,256]{1,0:T(8,128)(2,1)}, bf16[256,256]{1,0:T(8,128)(2,1)S(1)}, u32[]{:S(2)}, u32[]{:S(2)}) collective-permute-start(bf16[256,256]{1,0:T(8,128)(2,1)} %proj.1), channel_id=1, source_target_pairs={{0,2},{1,3},{2,0},{3,1},{4,6},{5,7},{6,4},{7,5},{8,10},{9,11},{10,... | collective-permute-start | bytes 393224 | tf_op jit(solution)/shard_map/ppermute | solution.py:440
  7.9 0.0 collective-permute-done.1.s_sib
  7.9 3.0 %forward_first.1 = (bf16[392,256]{1,0:T(8,128)(2,1)S(1)}, bf16[392,256]{1,0:T(8,128)(2,1)S(1)}, bf16[16,256]{1,0:T(8,128)(2,1)S(1)}, f32[16,256]{1,0:T(8,128)S(1...) custom-call(s32[1]{0:T(128)} %bitcast.index_ref, ...), custom_call_target="tpu_custom_call" | custom-call | flops 822083584 | bytes 802816 | tf_op jit(solution)/shard_map/forward_first/pallas_call | solution.py:116
  10.9 0.0 copy-start
  10.9 2.9 %collective-permute-done.5.refs_7_.proj = bf16[256,256]{1,0:T(8,128)(2,1)S(1)} collective-permute-done((bf16[256,256]{1,0:T(8,128)(2,1)}, bf16[256,256]{1,0:T(8,128)(2,1)S(1)}, u32[]{:S(2)}, u32[]{:S(2)}) %collective-permute-start.5) | collective-permute-done | bytes 131104 | tf_op jit(solution)/shard_map/ppermute | solution.py:440
  13.7 0.0 collective-permute-done.3.refs_5_.conv
  13.8 1.8 %collective-permute-start.6 = (bf16[192,512]{1,0:T(8,128)(2,1)S(1)}, bf16[192,512]{1,0:T(8,128)(2,1)S(1)}, u32[]{:S(2)}, u32[]{:S(2)}) collective-permute-start(bf16[192,512]{1,0:T(8,128)(2,1)S(1)} %pack_half.2), channel_id=1, source_target_pairs={{0,2},{1,3},{2,0},{3,1},{4,6},{5,7},{6,4},{7,5},{8,10},{9,11},{10,... | collective-permute-start | bytes 589832 | tf_op jit(solution)/shard_map/ppermute | solution.py:440
  15.5 0.0 collective-permute-done.4.refs_6_.proj.refs_3_
  15.5 0.0 collective-permute-done.2.refs_4_.conv
  15.5 0.0 copy-done
  15.6 1.6 %collective-permute-start.7 = (bf16[192,512]{1,0:T(8,128)(2,1)S(1)}, bf16[192,512]{1,0:T(8,128)(2,1)S(1)}, u32[]{:S(2)}, u32[]{:S(2)}) collective-permute-start(bf16[192,512]{1,0:T(8,128)(2,1)S(1)} %pack_half.3), channel_id=1, source_target_pairs={{0,4},{1,5},{2,6},{3,7},{4,0},{5,1},{6,2},{7,3},{8,12},{9,13},{10,... | collective-permute-start | bytes 589832 | tf_op jit(solution)/shard_map/ppermute | solution.py:440
  17.2 1.6 %forward_middle.1 = (bf16[392,256]{1,0:T(8,128)(2,1)S(1)}, bf16[392,256]{1,0:T(8,128)(2,1)S(1)}, bf16[16,256]{1,0:T(8,128)(2,1)S(1)}, bf16[392,256]{1,0:T(8,128)...) custom-call(bf16[392,512]{1,0:T(8,128)(2,1)S(1)} %get-tuple-element.38.f_own, ...), custom_call_target="tpu_custom_call" | custom-call | flops 1644167168 | bytes 1605632 | tf_op jit(solution)/shard_map/forward_middle/pallas_call | solution.py:116
  18.8 1.4 %collective-permute-done.6.refs_0_ = bf16[192,512]{1,0:T(8,128)(2,1)S(1)} collective-permute-done((bf16[192,512]{1,0:T(8,128)(2,1)S(1)}, bf16[192,512]{1,0:T(8,128)(2,1)S(1)}, u32[]{:S(2)}, u32[]{:S(2)}) %collective-permute-start.6) | collective-permute-done | bytes 196640 | tf_op jit(solution)/shard_map/ppermute | solution.py:440
  20.2 1.2 %collective-permute-done.7.refs_1_ = bf16[192,512]{1,0:T(8,128)(2,1)S(1)} collective-permute-done((bf16[192,512]{1,0:T(8,128)(2,1)S(1)}, bf16[192,512]{1,0:T(8,128)(2,1)S(1)}, u32[]{:S(2)}, u32[]{:S(2)}) %collective-permute-start.7) | collective-permute-done | bytes 196640 | tf_op jit(solution)/shard_map/ppermute | solution.py:440
  21.4 1.0 %forward_last.1 = (bf16[392,256]{1,0:T(8,128)(2,1)S(1)}, bf16[392,256]{1,0:T(8,128)(2,1)S(1)}, bf16[16,256]{1,0:T(8,128)(2,1)S(1)}, f32[24,256]{1,0:T(8,128)S(1)}, f32[24,256]{1,0:T(8,128)S(1)}) custom-call(bf16[392,512]{1,0:T(8,128)(2,1)S(1)} %get-tuple-element.38.f_own, bf16[392,512]{1,0:T(8,128)(2,1)S(1)} %collective-permute-done.f_sib, ...), custom_call_target="tpu_custom_call" | custom-call | flops 822083584 | bytes 802816 | tf_op jit(solution)/shard_map/forward_last/pallas_call | solution.py:116
  22.5 0.0 collective-permute-start.8
  22.5 1.2 %collective-permute-done.8.refs_1_ = f32[24,256]{1,0:T(8,128)S(1)} collective-permute-done((f32[24,256]{1,0:T(8,128)S(1)}, f32[24,256]{1,0:T(8,128)S(1)}, u32[]{:S(2)}, u32[]{:S(2)}) %collective-permute-start.8) | collective-permute-done | bytes 24608 | tf_op jit(solution)/shard_map/ppermute | solution.py:440
  23.7 2.6 %collective-permute-start.10 = (f32[24,256]{1,0:T(8,128)S(1)}, f32[24,256]{1,0:T(8,128)S(1)}, u32[]{:S(2)}, u32[]{:S(2)}) collective-permute-start(f32[24,256]{1,0:T(8,128)S(1)} %sum_arrays.1.refs_0_), channel_id=1, source_target_pairs={{0,16},{8,24},{16,0},{24,8},{1,17},{9,25},{17,1},{25,9},{2,18},{10... | collective-permute-start | bytes 73736 | tf_op jit(solution)/shard_map/ppermute | solution.py:440
  26.3 1.3 %collective-permute-start.11 = (f32[24,256]{1,0:T(8,128)S(1)}, f32[24,256]{1,0:T(8,128)S(1)}, u32[]{:S(2)}, u32[]{:S(2)}) collective-permute-start(f32[24,256]{1,0:T(8,128)S(1)} %sum_arrays.1.refs_0_), channel_id=1, source_target_pairs={{0,24},{8,16},{16,8},{24,0},{1,25},{9,17},{17,9},{25,1},{2,26},{10... | collective-permute-start | bytes 73736 | tf_op jit(solution)/shard_map/ppermute | solution.py:440
  27.6 0.2 collective-permute-start.9
  27.8 0.6 collective-permute-done.10.refs_2_
  28.4 3.5 %collective-permute-done.11.refs_3_ = f32[24,256]{1,0:T(8,128)S(1)} collective-permute-done((f32[24,256]{1,0:T(8,128)S(1)}, f32[24,256]{1,0:T(8,128)S(1)}, u32[]{:S(2)}, u32[]{:S(2)}) %collective-permute-start.11) | collective-permute-done | bytes 24608 | tf_op jit(solution)/shard_map/ppermute | solution.py:440
  31.9 0.0 collective-permute-done.9.refs_1_
  31.9 1.3 %hsic_groups.1 = (f32[4,16,256]{2,1,0:T(8,128)S(1)}, f32[1,1]{1,0:T(1,128)}) custom-call(s32[1]{0:T(128)} %bitcast.1.place_ref, f32[24,256]{1,0:T(8,128)S(1)} %sum_arrays.1.refs_0_, f32[24,256]{1,0:T(8,128)S(1)} %collective-permute-done.9.refs_1_, f32[24,256]{1,0:T(8,128)S(1)} %collective-permute-done.10.refs_2_, f32[24,256]{1,0:T(8,128)S(1)} %collective-permute-done.11.refs_3_), custom_call_target="tpu_custom_call" | custom-call | flops 1000000000 | tf_op jit(solution)/shard_map/hsic_groups/pallas_call | solution.py:242
  33.2 0.7 %backward_blocks.5.refs_8_ = bf16[144,512]{1,0:T(8,128)(2,1)S(1)} custom-call(bf16[392,512]{1,0:T(8,128)(2,1)S(1)} %get-tuple-element.38.f_own, bf16[392,512]{1,0:T(8,128)(2,1)S(1)} %collective-permute-done.f_sib, f32[4,16,256]{2,1,0:T(8,128)S(1)} %get-tuple-element.52.ge_ref.own_ge, bf16[392,256]{1,0:T(8,128)(2,1)S(1)} %get-tuple-element.63.refs_0_, ...), custom_call_target="tpu_custom_call" | custom-call | flops 411041792 | bytes 200704 | tf_op jit(solution)/shard_map/backward_blocks/pallas_call | solution.py:289
  33.9 1.6 %collective-permute-start.14 = (bf16[144,512]{1,0:T(8,128)(2,1)S(1)}, bf16[144,512]{1,0:T(8,128)(2,1)S(1)}, u32[]{:S(2)}, u32[]{:S(2)}) collective-permute-start(bf16[144,512]{1,0:T(8,128)(2,1)S(1)} %backward_blocks.5.refs_8_), channel_id=1, source_target_pairs={{0,6},{1,7},{2,4},{3,5},{4,2},{5,3},{6,0},{7,1},{8,14},{9,15},{10,... | collective-permute-start | bytes 442376 | tf_op jit(solution)/shard_map/ppermute | solution.py:440
  35.5 1.3 %backward_blocks.6 = (bf16[144,512]{1,0:T(8,128)(2,1)S(1)}, bf16[144,512]{1,0:T(8,128)(2,1)S(1)}) custom-call(bf16[392,512]{1,0:T(8,128)(2,1)S(1)} %get-tuple-element.38.f_own, bf16[392,512]{1,0:T(8,128)(2,1)S(1)} %collective-permute-done.f_sib, f32[4,16,256]{2,1,0:T(8,128)S(1)} %get-tuple-element.52.ge_ref.own_ge, ...), custom_call_target="tpu_custom_call" | custom-call | flops 822083584 | bytes 401408 | tf_op jit(solution)/shard_map/backward_blocks/pallas_call | solution.py:289
  36.8 1.6 %collective-permute-start.12 = (bf16[144,512]{1,0:T(8,128)(2,1)S(1)}, bf16[144,512]{1,0:T(8,128)(2,1)S(1)}, u32[]{:S(2)}, u32[]{:S(2)}) collective-permute-start(bf16[144,512]{1,0:T(8,128)(2,1)S(1)} %get-tuple-element.66.refs_4_), channel_id=1, source_target_pairs={{0,2},{1,3},{2,0},{3,1},{4,6},{5,7},{6,4},{7,5},{8,10},{9,11},{10,... | collective-permute-start | bytes 442376 | tf_op jit(solution)/shard_map/ppermute | solution.py:440
  38.3 0.5 collective-permute-start.13
  38.8 0.7 %backward_blocks.7.refs_8_.x = bf16[160,512]{1,0:T(8,128)(2,1)S(1)} custom-call(bf16[392,512]{1,0:T(8,128)(2,1)S(1)} %get-tuple-element.38.f_own, bf16[392,512]{1,0:T(8,128)(2,1)S(1)} %collective-permute-done.f_sib, f32[4,16,256]{2,1,0:T(8,128)S(1)} %get-tuple-element.52.ge_ref.own_ge, bf16[392,256]{1,0:T(8,128)(2,1)S(1)} %get-tuple-element.63.refs_0_, ...), custom_call_target="tpu_custom_call" | custom-call | flops 411041792 | bytes 200704 | tf_op jit(solution)/shard_map/backward_blocks/pallas_call | solution.py:289
  39.5 0.0 copy-start.1
  39.5 1.3 %backward_blocks.8 = (bf16[160,512]{1,0:T(8,128)(2,1)S(1)}, bf16[160,512]{1,0:T(8,128)(2,1)S(1)}) custom-call(bf16[392,512]{1,0:T(8,128)(2,1)S(1)} %get-tuple-element.38.f_own, bf16[392,512]{1,0:T(8,128)(2,1)S(1)} %collective-permute-done.f_sib, f32[4,16,256]{2,1,0:T(8,128)S(1)} %get-tuple-element.52.ge_ref.own_ge, ...), custom_call_target="tpu_custom_call" | custom-call | flops 822083584 | bytes 401408 | tf_op jit(solution)/shard_map/backward_blocks/pallas_call | solution.py:289
  40.8 0.0 copy-done.1
  40.8 0.9 %backward_blocks.9.own = f32[256,512]{1,0:T(8,128)S(1)} custom-call(bf16[392,512]{1,0:T(8,128)(2,1)S(1)} %get-tuple-element.38.f_own, bf16[392,512]{1,0:T(8,128)(2,1)S(1)} %collective-permute-done.f_sib, f32[4,16,256]{2,1,0:T(8,128)S(1)} %get-tuple-element.52.ge_ref.own_ge, bf16[392,256]{1,0:T(8,128)(2,1)S(1)} %get-tuple-element.53.refs_0_, ...), custom_call_target="tpu_custom_call" | custom-call | flops 822083584 | bytes 401408 | tf_op jit(solution)/shard_map/backward_blocks/pallas_call | solution.py:289
  41.7 0.9 %collective-permute-done.12.refs_0_ = bf16[144,512]{1,0:T(8,128)(2,1)S(1)} collective-permute-done((bf16[144,512]{1,0:T(8,128)(2,1)S(1)}, bf16[144,512]{1,0:T(8,128)(2,1)S(1)}, u32[]{:S(2)}, u32[]{:S(2)}) %collective-permute-start.12) | collective-permute-done | bytes 147488 | tf_op jit(solution)/shard_map/ppermute | solution.py:440
  42.6 0.9 %collective-permute-done.13.refs_1_ = bf16[144,512]{1,0:T(8,128)(2,1)S(1)} collective-permute-done((bf16[144,512]{1,0:T(8,128)(2,1)S(1)}, bf16[144,512]{1,0:T(8,128)(2,1)S(1)}, u32[]{:S(2)}, u32[]{:S(2)}) %collective-permute-start.13) | collective-permute-done | bytes 147488 | tf_op jit(solution)/shard_map/ppermute | solution.py:440
  43.5 0.0 collective-permute-done.14.refs_2_
  43.5 0.1 collect_terms.2.mine.token
  43.6 0.1 collective-permute-start.15
  43.7 1.2 %collective-permute-start.19 = (bf16[160,512]{1,0:T(8,128)(2,1)S(1)}, bf16[160,512]{1,0:T(8,128)(2,1)S(1)}, u32[]{:S(2)}, u32[]{:S(2)}) collective-permute-start(bf16[160,512]{1,0:T(8,128)(2,1)S(1)} %gate.5), channel_id=1, source_target_pairs={{0,6},{1,7},{2,4},{3,5},{4,2},{5,3},{6,0},{7,1},{8,14},{9,15},{10,... | collective-permute-start | bytes 491528 | tf_op jit(solution)/shard_map/ppermute | solution.py:440
  45.0 1.1 %collective-permute-start.18 = (bf16[160,512]{1,0:T(8,128)(2,1)S(1)}, bf16[160,512]{1,0:T(8,128)(2,1)S(1)}, u32[]{:S(2)}, u32[]{:S(2)}) collective-permute-start(bf16[160,512]{1,0:T(8,128)(2,1)S(1)} %gate.4), channel_id=1, source_target_pairs={{0,4},{1,5},{2,6},{3,7},{4,0},{5,1},{6,2},{7,3},{8,12},{9,13},{10,... | collective-permute-start | bytes 491528 | tf_op jit(solution)/shard_map/ppermute | solution.py:440
  46.1 1.2 %collective-permute-start.17 = (bf16[160,512]{1,0:T(8,128)(2,1)S(1)}, bf16[160,512]{1,0:T(8,128)(2,1)S(1)}, u32[]{:S(2)}, u32[]{:S(2)}) collective-permute-start(bf16[160,512]{1,0:T(8,128)(2,1)S(1)} %gate.3), channel_id=1, source_target_pairs={{0,2},{1,3},{2,0},{3,1},{4,6},{5,7},{6,4},{7,5},{8,10},{9,11},{10,... | collective-permute-start | bytes 491528 | tf_op jit(solution)/shard_map/ppermute | solution.py:440
  47.3 1.7 %collective-permute-done.15.other = bf16[160,512]{1,0:T(8,128)(2,1)S(1)} collective-permute-done((bf16[160,512]{1,0:T(8,128)(2,1)S(1)}, bf16[160,512]{1,0:T(8,128)(2,1)S(1)}, u32[]{:S(2)}, u32[]{:S(2)}) %collective-permute-start.15) | collective-permute-done | bytes 163872 | tf_op jit(solution)/shard_map/ppermute | solution.py:440
  49.0 1.3 %collective-permute-start.16 = (bf16[192,512]{1,0:T(8,128)(2,1)S(1)}, bf16[192,512]{1,0:T(8,128)(2,1)S(1)}, u32[]{:S(2)}, u32[]{:S(2)}) collective-permute-start(bf16[192,512]{1,0:T(8,128)(2,1)S(1)} %merge_slabs.2.refs_3_.mine.refs_0_), channel_id=1, source_target_pairs={{0,16},{8,24},{16,0},{24,8},{1,17},{9,25},{17,1},{25,9},{2,18},{10... | collective-permute-start | bytes 589832 | tf_op jit(solution)/shard_map/ppermute | solution.py:440
  50.3 0.9 %collective-permute-done.19.refs_2_ = bf16[160,512]{1,0:T(8,128)(2,1)S(1)} collective-permute-done((bf16[160,512]{1,0:T(8,128)(2,1)S(1)}, bf16[160,512]{1,0:T(8,128)(2,1)S(1)}, u32[]{:S(2)}, u32[]{:S(2)}) %collective-permute-start.19) | collective-permute-done | bytes 163872 | tf_op jit(solution)/shard_map/ppermute | solution.py:440
  51.2 1.6 %collective-permute-done.18.refs_1_ = bf16[160,512]{1,0:T(8,128)(2,1)S(1)} collective-permute-done((bf16[160,512]{1,0:T(8,128)(2,1)S(1)}, bf16[160,512]{1,0:T(8,128)(2,1)S(1)}, u32[]{:S(2)}, u32[]{:S(2)}) %collective-permute-start.18) | collective-permute-done | bytes 163872 | tf_op jit(solution)/shard_map/ppermute | solution.py:440
  52.8 0.0 collective-permute-done.17.refs_0_
  52.8 0.1 collect_terms.3.mine
  52.9 1.8 %collective-permute-start.20 = (bf16[128,512]{1,0:T(8,128)(2,1)S(1)}, bf16[128,512]{1,0:T(8,128)(2,1)S(1)}, u32[]{:S(2)}, u32[]{:S(2)}) collective-permute-start(bf16[128,512]{1,0:T(8,128)(2,1)S(1)} %collect_terms.3.mine), channel_id=1, source_target_pairs={{0,8},{8,0},{16,24},{24,16},{1,9},{9,1},{17,25},{25,17},{2,10},{10... | collective-permute-start | bytes 393224 | tf_op jit(solution)/shard_map/ppermute | solution.py:440
  54.7 3.6 %collective-permute-done.16.other.refs_1_ = bf16[192,512]{1,0:T(8,128)(2,1)S(1)} collective-permute-done((bf16[192,512]{1,0:T(8,128)(2,1)S(1)}, bf16[192,512]{1,0:T(8,128)(2,1)S(1)}, u32[]{:S(2)}, u32[]{:S(2)}) %collective-permute-start.16) | collective-permute-done | bytes 196640 | tf_op jit(solution)/shard_map/ppermute | solution.py:440
  58.3 1.2 %proj_grad.1 = (f32[256,256]{1,0:T(8,128)}, f32[8,128]{1,0:T(8,128)S(1)}) custom-call(f32[4,16,256]{2,1,0:T(8,128)S(1)} %get-tuple-element.52.ge_ref.own_ge, bf16[192,512]{1,0:T(8,128)(2,1)S(1)} %merge_slabs.2.refs_3_.mine.refs_0_, bf16[192,512]{1,0:T(8,128)(2,1)S(1)} %collective-permute-done.16.other.refs_1_, ...), custom_call_target="tpu_custom_call" | custom-call | tf_op jit(solution)/shard_map/proj_grad/pallas_call | solution.py:305
  59.5 0.8 %collective-permute-done.20.other = bf16[128,512]{1,0:T(8,128)(2,1)S(1)} collective-permute-done((bf16[128,512]{1,0:T(8,128)(2,1)S(1)}, bf16[128,512]{1,0:T(8,128)(2,1)S(1)}, u32[]{:S(2)}, u32[]{:S(2)}) %collective-permute-start.20) | collective-permute-done | bytes 131104 | tf_op jit(solution)/shard_map/ppermute | solution.py:440
  60.3 0.2 collective-permute-start.21
  60.5 7.3 %collective-permute-done.21.refs_3_ = bf16[128,512]{1,0:T(8,128)(2,1)S(1)} collective-permute-done((bf16[128,512]{1,0:T(8,128)(2,1)S(1)}, bf16[128,512]{1,0:T(8,128)(2,1)S(1)}, u32[]{:S(2)}, u32[]{:S(2)}) %collective-permute-start.21) | collective-permute-done | bytes 131104 | tf_op jit(solution)/shard_map/ppermute | solution.py:440
  67.8 0.8 %sum_slabs.1 = f32[256,512]{1,0:T(8,128)} custom-call(bf16[192,512]{1,0:T(8,128)(2,1)S(1)} %merge_slabs.2.refs_3_.mine.refs_0_, bf16[192,512]{1,0:T(8,128)(2,1)S(1)} %collective-permute-done.16.other.refs_1_, bf16[128,512]{1,0:T(8,128)(2,1)S(1)} %merge_slabs.3.refs_2_, bf16[128,512]{1,0:T(8,128)(2,1)S(1)} %collective-permute-done.21.refs_3_), custom_call_target="tpu_custom_call" | custom-call | tf_op jit(solution)/shard_map/sum_slabs/pallas_call | solution.py:305
  (9 shorter events, 0.2 us)
Async XLA Ops:
  0.6 7.2 %collective-permute-start.1 = (bf16[392,2048]{1,0:T(8,128)(2,1)}, bf16[392,2048]{1,0:T(8,128)(2,1)S(1)}, u32[]{:S(2)}, u32[]{:S(2)}) collective-permute-start(bf16[392,2048]{1,0:T(8,128)(2,1)} %s_own.1), channel_id=1, source_target_pairs={{0,1},{1,0},{2,3},{3,2},{4,5},{5,4},{6,7},{7,6},{8,9},{9,8},{10,11... | collective-permute-start | bytes 4816904 | tf_op jit(solution)/shard_map/ppermute | solution.py:440
  1.1 5.0 %collective-permute-start = (bf16[392,512]{1,0:T(8,128)(2,1)}, bf16[392,512]{1,0:T(8,128)(2,1)S(1)}, u32[]{:S(2)}, u32[]{:S(2)}) collective-permute-start(bf16[392,512]{1,0:T(8,128)(2,1)} %f_own.1), channel_id=1, source_target_pairs={{0,1},{1,0},{2,3},{3,2},{4,5},{5,4},{6,7},{7,6},{8,9},{9,8},{10,11... | collective-permute-start | bytes 1204232 | tf_op jit(solution)/shard_map/ppermute | solution.py:440
  1.2 12.5 %collective-permute-start.3 = (bf16[256,512]{1,0:T(8,128)(2,1)}, bf16[256,512]{1,0:T(8,128)(2,1)S(1)}, u32[]{:S(2)}, u32[]{:S(2)}) collective-permute-start(bf16[256,512]{1,0:T(8,128)(2,1)} %conv.1), channel_id=1, source_target_pairs={{0,4},{1,5},{2,6},{3,7},{4,0},{5,1},{6,2},{7,3},{8,12},{9,13},{10,... | collective-permute-start | bytes 786440 | tf_op jit(solution)/shard_map/ppermute | solution.py:440
  4.2 11.4 %collective-permute-start.2 = (bf16[256,512]{1,0:T(8,128)(2,1)}, bf16[256,512]{1,0:T(8,128)(2,1)S(1)}, u32[]{:S(2)}, u32[]{:S(2)}) collective-permute-start(bf16[256,512]{1,0:T(8,128)(2,1)} %conv.1), channel_id=1, source_target_pairs={{0,2},{1,3},{2,0},{3,1},{4,6},{5,7},{6,4},{7,5},{8,10},{9,11},{10,... | collective-permute-start | bytes 786440 | tf_op jit(solution)/shard_map/ppermute | solution.py:440
  5.7 8.1 %collective-permute-start.5 = (bf16[256,256]{1,0:T(8,128)(2,1)}, bf16[256,256]{1,0:T(8,128)(2,1)S(1)}, u32[]{:S(2)}, u32[]{:S(2)}) collective-permute-start(bf16[256,256]{1,0:T(8,128)(2,1)} %proj.1), channel_id=1, source_target_pairs={{0,4},{1,5},{2,6},{3,7},{4,0},{5,1},{6,2},{7,3},{8,12},{9,13},{10,... | collective-permute-start | bytes 393224 | tf_op jit(solution)/shard_map/ppermute | solution.py:440
  6.2 9.4 %collective-permute-start.4 = (bf16[256,256]{1,0:T(8,128)(2,1)}, bf16[256,256]{1,0:T(8,128)(2,1)S(1)}, u32[]{:S(2)}, u32[]{:S(2)}) collective-permute-start(bf16[256,256]{1,0:T(8,128)(2,1)} %proj.1), channel_id=1, source_target_pairs={{0,2},{1,3},{2,0},{3,1},{4,6},{5,7},{6,4},{7,5},{8,10},{9,11},{10,... | collective-permute-start | bytes 393224 | tf_op jit(solution)/shard_map/ppermute | solution.py:440
  10.9 4.7 %copy-start = (bf16[392,256]{1,0:T(8,128)(2,1)}, bf16[392,256]{1,0:T(8,128)(2,1)S(1)}, u32[]{:S(2)}) copy-start(bf16[392,256]{1,0:T(8,128)(2,1)S(1)} %get-tuple-element.54.refs_1_) | copy-start | bytes 602116
  13.8 6.4 %collective-permute-start.6 = (bf16[192,512]{1,0:T(8,128)(2,1)S(1)}, bf16[192,512]{1,0:T(8,128)(2,1)S(1)}, u32[]{:S(2)}, u32[]{:S(2)}) collective-permute-start(bf16[192,512]{1,0:T(8,128)(2,1)S(1)} %pack_half.2), channel_id=1, source_target_pairs={{0,2},{1,3},{2,0},{3,1},{4,6},{5,7},{6,4},{7,5},{8,10},{9,11},{10,... | collective-permute-start | bytes 589832 | tf_op jit(solution)/shard_map/ppermute | solution.py:440
  15.6 5.8 %collective-permute-start.7 = (bf16[192,512]{1,0:T(8,128)(2,1)S(1)}, bf16[192,512]{1,0:T(8,128)(2,1)S(1)}, u32[]{:S(2)}, u32[]{:S(2)}) collective-permute-start(bf16[192,512]{1,0:T(8,128)(2,1)S(1)} %pack_half.3), channel_id=1, source_target_pairs={{0,4},{1,5},{2,6},{3,7},{4,0},{5,1},{6,2},{7,3},{8,12},{9,13},{10,... | collective-permute-start | bytes 589832 | tf_op jit(solution)/shard_map/ppermute | solution.py:440
  22.5 1.2 %collective-permute-start.8 = (f32[24,256]{1,0:T(8,128)S(1)}, f32[24,256]{1,0:T(8,128)S(1)}, u32[]{:S(2)}, u32[]{:S(2)}) collective-permute-start(f32[24,256]{1,0:T(8,128)S(1)} %get-tuple-element.51), channel_id=1, source_target_pairs={{0,1},{1,0},{2,3},{3,2},{4,5},{5,4},{6,7},{7,6},{8,9},{9,8},{10,11... | collective-permute-start | bytes 73736 | tf_op jit(solution)/shard_map/ppermute | solution.py:440
  23.7 4.7 %collective-permute-start.10 = (f32[24,256]{1,0:T(8,128)S(1)}, f32[24,256]{1,0:T(8,128)S(1)}, u32[]{:S(2)}, u32[]{:S(2)}) collective-permute-start(f32[24,256]{1,0:T(8,128)S(1)} %sum_arrays.1.refs_0_), channel_id=1, source_target_pairs={{0,16},{8,24},{16,0},{24,8},{1,17},{9,25},{17,1},{25,9},{2,18},{10... | collective-permute-start | bytes 73736 | tf_op jit(solution)/shard_map/ppermute | solution.py:440
  26.3 5.6 %collective-permute-start.11 = (f32[24,256]{1,0:T(8,128)S(1)}, f32[24,256]{1,0:T(8,128)S(1)}, u32[]{:S(2)}, u32[]{:S(2)}) collective-permute-start(f32[24,256]{1,0:T(8,128)S(1)} %sum_arrays.1.refs_0_), channel_id=1, source_target_pairs={{0,24},{8,16},{16,8},{24,0},{1,25},{9,17},{17,9},{25,1},{2,26},{10... | collective-permute-start | bytes 73736 | tf_op jit(solution)/shard_map/ppermute | solution.py:440
  27.6 4.3 %collective-permute-start.9 = (f32[24,256]{1,0:T(8,128)S(1)}, f32[24,256]{1,0:T(8,128)S(1)}, u32[]{:S(2)}, u32[]{:S(2)}) collective-permute-start(f32[24,256]{1,0:T(8,128)S(1)} %sum_arrays.1.refs_0_), channel_id=1, source_target_pairs={{0,8},{8,0},{16,24},{24,16},{1,9},{9,1},{17,25},{25,17},{2,10},{10... | collective-permute-start | bytes 73736 | tf_op jit(solution)/shard_map/ppermute | solution.py:440
  33.9 9.6 %collective-permute-start.14 = (bf16[144,512]{1,0:T(8,128)(2,1)S(1)}, bf16[144,512]{1,0:T(8,128)(2,1)S(1)}, u32[]{:S(2)}, u32[]{:S(2)}) collective-permute-start(bf16[144,512]{1,0:T(8,128)(2,1)S(1)} %backward_blocks.5.refs_8_), channel_id=1, source_target_pairs={{0,6},{1,7},{2,4},{3,5},{4,2},{5,3},{6,0},{7,1},{8,14},{9,15},{10,... | collective-permute-start | bytes 442376 | tf_op jit(solution)/shard_map/ppermute | solution.py:440
  36.8 5.9 %collective-permute-start.12 = (bf16[144,512]{1,0:T(8,128)(2,1)S(1)}, bf16[144,512]{1,0:T(8,128)(2,1)S(1)}, u32[]{:S(2)}, u32[]{:S(2)}) collective-permute-start(bf16[144,512]{1,0:T(8,128)(2,1)S(1)} %get-tuple-element.66.refs_4_), channel_id=1, source_target_pairs={{0,2},{1,3},{2,0},{3,1},{4,6},{5,7},{6,4},{7,5},{8,10},{9,11},{10,... | collective-permute-start | bytes 442376 | tf_op jit(solution)/shard_map/ppermute | solution.py:440
  38.3 5.2 %collective-permute-start.13 = (bf16[144,512]{1,0:T(8,128)(2,1)S(1)}, bf16[144,512]{1,0:T(8,128)(2,1)S(1)}, u32[]{:S(2)}, u32[]{:S(2)}) collective-permute-start(bf16[144,512]{1,0:T(8,128)(2,1)S(1)} %get-tuple-element.67.refs_5_), channel_id=1, source_target_pairs={{0,4},{1,5},{2,6},{3,7},{4,0},{5,1},{6,2},{7,3},{8,12},{9,13},{10,... | collective-permute-start | bytes 442376 | tf_op jit(solution)/shard_map/ppermute | solution.py:440
  39.5 1.3 %copy-start.1 = (bf16[392,256]{1,0:T(8,128)(2,1)S(1)}, bf16[392,256]{1,0:T(8,128)(2,1)}, u32[]{:S(2)}) copy-start(bf16[392,256]{1,0:T(8,128)(2,1)} %copy-done) | copy-start | bytes 602116
  43.6 5.4 %collective-permute-start.15 = (bf16[160,512]{1,0:T(8,128)(2,1)S(1)}, bf16[160,512]{1,0:T(8,128)(2,1)S(1)}, u32[]{:S(2)}, u32[]{:S(2)}) collective-permute-start(bf16[160,512]{1,0:T(8,128)(2,1)S(1)} %collect_terms.2.mine.token), channel_id=1, source_target_pairs={{0,8},{8,0},{16,24},{24,16},{1,9},{9,1},{17,25},{25,17},{2,10},{10... | collective-permute-start | bytes 491528 | tf_op jit(solution)/shard_map/ppermute | solution.py:440
  43.7 7.5 %collective-permute-start.19 = (bf16[160,512]{1,0:T(8,128)(2,1)S(1)}, bf16[160,512]{1,0:T(8,128)(2,1)S(1)}, u32[]{:S(2)}, u32[]{:S(2)}) collective-permute-start(bf16[160,512]{1,0:T(8,128)(2,1)S(1)} %gate.5), channel_id=1, source_target_pairs={{0,6},{1,7},{2,4},{3,5},{4,2},{5,3},{6,0},{7,1},{8,14},{9,15},{10,... | collective-permute-start | bytes 491528 | tf_op jit(solution)/shard_map/ppermute | solution.py:440
  45.0 7.9 %collective-permute-start.18 = (bf16[160,512]{1,0:T(8,128)(2,1)S(1)}, bf16[160,512]{1,0:T(8,128)(2,1)S(1)}, u32[]{:S(2)}, u32[]{:S(2)}) collective-permute-start(bf16[160,512]{1,0:T(8,128)(2,1)S(1)} %gate.4), channel_id=1, source_target_pairs={{0,4},{1,5},{2,6},{3,7},{4,0},{5,1},{6,2},{7,3},{8,12},{9,13},{10,... | collective-permute-start | bytes 491528 | tf_op jit(solution)/shard_map/ppermute | solution.py:440
  46.1 6.8 %collective-permute-start.17 = (bf16[160,512]{1,0:T(8,128)(2,1)S(1)}, bf16[160,512]{1,0:T(8,128)(2,1)S(1)}, u32[]{:S(2)}, u32[]{:S(2)}) collective-permute-start(bf16[160,512]{1,0:T(8,128)(2,1)S(1)} %gate.3), channel_id=1, source_target_pairs={{0,2},{1,3},{2,0},{3,1},{4,6},{5,7},{6,4},{7,5},{8,10},{9,11},{10,... | collective-permute-start | bytes 491528 | tf_op jit(solution)/shard_map/ppermute | solution.py:440
  49.0 9.3 %collective-permute-start.16 = (bf16[192,512]{1,0:T(8,128)(2,1)S(1)}, bf16[192,512]{1,0:T(8,128)(2,1)S(1)}, u32[]{:S(2)}, u32[]{:S(2)}) collective-permute-start(bf16[192,512]{1,0:T(8,128)(2,1)S(1)} %merge_slabs.2.refs_3_.mine.refs_0_), channel_id=1, source_target_pairs={{0,16},{8,24},{16,0},{24,8},{1,17},{9,25},{17,1},{25,9},{2,18},{10... | collective-permute-start | bytes 589832 | tf_op jit(solution)/shard_map/ppermute | solution.py:440
  52.9 7.3 %collective-permute-start.20 = (bf16[128,512]{1,0:T(8,128)(2,1)S(1)}, bf16[128,512]{1,0:T(8,128)(2,1)S(1)}, u32[]{:S(2)}, u32[]{:S(2)}) collective-permute-start(bf16[128,512]{1,0:T(8,128)(2,1)S(1)} %collect_terms.3.mine), channel_id=1, source_target_pairs={{0,8},{8,0},{16,24},{24,16},{1,9},{9,1},{17,25},{25,17},{2,10},{10... | collective-permute-start | bytes 393224 | tf_op jit(solution)/shard_map/ppermute | solution.py:440
  60.3 7.5 %collective-permute-start.21 = (bf16[128,512]{1,0:T(8,128)(2,1)S(1)}, bf16[128,512]{1,0:T(8,128)(2,1)S(1)}, u32[]{:S(2)}, u32[]{:S(2)}) collective-permute-start(bf16[128,512]{1,0:T(8,128)(2,1)S(1)} %merge_slabs.3.refs_2_), channel_id=1, source_target_pairs={{0,16},{8,24},{16,0},{24,8},{1,17},{9,25},{17,1},{25,9},{2,18},{10... | collective-permute-start | bytes 393224 | tf_op jit(solution)/shard_map/ppermute | solution.py:440

commit v3 on v2

--- a/solution.py
+++ b/solution.py
@@ -16,6 +16,7 @@
 TN = (((0,), (0,)), ((), ()))
 VMEM_LIMIT = 8 * 1024 * 1024
 SPLIT = 4
+ORDER = (0, 3, 1, 2)
 
 
 def dot(a, b, dims=(((1,), (0,)), ((), ()))):
@@ -36,8 +37,10 @@
     return jnp.where((row >= first) & (row < first + POS), 1.0, 0.0).astype(BF)
 
 
-def forward_block(feat, short, conv, pick):
-    hidden = jnp.maximum(dot(feat, conv, NT) + short.astype(F32), 0.0)
+def forward_block(feat, short, convs, pick):
+    preact = [dot(feat, conv[...], NT) for conv in convs]
+    preact = preact[0] if len(preact) == 1 else jnp.concatenate(preact, axis=1)
+    hidden = jnp.maximum(preact + short.astype(F32), 0.0)
     mask = jnp.where(hidden > 0, 1.0, 0.0).astype(BF)
     pooled = dot(pick, hidden.astype(BF)) / POS
     return mask, pooled
@@ -47,59 +50,82 @@
     images = outs[2].shape[0] // 2
     pick_rows = image_of_row((images, feats[0].shape[0]), 1, 0)
     for j in range(picks):
-        pooled = []
-        for side in (0, 1):
+        pooled = [None, None]
+        for side in (1, 0):
             if ready is not None:
                 ready(j, side)
-            mask, mean = forward_block(feats[side][...], shorts[2 * j + side][...], convs[j][...], pick_rows)
+            mask, pooled[side] = forward_block(feats[side][...], shorts[2 * j + side][...], convs[j], pick_rows)
             outs[3 * j + side][...] = mask
-            pooled.append(mean)
         pooled = jnp.concatenate(pooled, axis=0).astype(BF)
         outs[3 * j + 2][...] = pooled
         embed = embed + dot(pooled, projs[j][...])
     return embed
 
 
-def first_kernel(peers, images, index_ref, partner, f_sib, f_own, s_own, s_sib, conv, proj, *refs):
-    blocks, embed_ref, feat, proj_out, member_ref = refs[:3], refs[3], refs[4], refs[5], refs[6]
-    ahead, (short, conv_buf, sems) = refs[7 : 5 + 2 * peers], refs[5 + 2 * peers :]
-    index = index_ref[0]
-    count = conv_buf.shape[0]
+def fetcher(sems):
     copies = []
 
     def fetch(source, target):
         copies.append(pltpu.make_async_copy(source, target, sems.at[len(copies)]))
         copies[-1].start()
-
-    fetch(f_own, feat)
-    fetch(conv, conv_buf)
-    shorts = [short.at[0], short.at[1], *ahead]
-    for k, target in enumerate(shorts):
-        at = pl.ds(pl.multiple_of((index ^ (k // 2 * 2)) * count, count), count)
-        fetch((s_own, s_sib)[k % 2].at[:, at], target)
-        if k == 1:
-            fetch(proj, proj_out)
+        return copies[-1]
+
+    return fetch
+
+
+def columns(index_ref, pick, count):
+    return pl.ds(pl.multiple_of((index_ref[0] ^ (2 * pick)) * count, count), count)
+
+
+def first_kernel(images, index_ref, f_sib, partner_ref, f_own, s_own, s_sib, conv, proj, *refs):
+    blocks, embed_ref, feat, proj_out, member_ref = refs[:3], refs[3], refs[4], refs[5], refs[6]
+    short, conv_buf, partner, sems = refs[7:]
+    fetch = fetcher(sems)
+    at = columns(index_ref, 0, conv_buf.shape[0])
+    shorts = [short.at[0], short.at[1]]
+    waits = [
+        [fetch(conv, conv_buf), fetch(s_sib.at[:, at], shorts[1])],
+        [fetch(f_own, feat), fetch(s_own.at[:, at], shorts[0]), fetch(proj, proj_out)],
+    ]
+    partner_copy = fetch(partner_ref, partner)
+
+    def ready(j, side):
+        for copy in waits[1 - side]:
+            copy.wait()
+
+    embed = jnp.zeros(embed_ref.shape, F32)
+    embed_ref[...] = forward_blocks(1, (feat, f_sib), shorts, [[conv_buf]], [proj_out], embed, blocks, ready)
+    partner_copy.wait()
     member = lax.broadcasted_iota(jnp.int32, member_ref.shape, 0)
     whole = jnp.zeros(member_ref.shape, F32)
     for i in range(images):
         whole = jnp.where(member == i, partner[i].astype(F32), whole)
     member_ref[...] = whole
-    for copy in copies[:5]:
-        copy.wait()
-    embed = jnp.zeros(embed_ref.shape, F32)
-    embed_ref[...] = forward_blocks(1, (feat, f_sib), shorts, [conv_buf], [proj_out], embed, blocks)
-    for copy in copies[5:]:
-        copy.wait()
-
-
-def middle_kernel(blocks, f_own, f_sib, before, *refs):
-    shorts, convs, projs = refs[: 2 * blocks], refs[2 * blocks : 3 * blocks], refs[3 * blocks : 4 * blocks]
-    outs = refs[4 * blocks :]
-    outs[-1][...] = forward_blocks(blocks, (f_own, f_sib), shorts, convs, projs, before[...], outs)
-
-
-def last_kernel(images, f_own, f_sib, before, member, s_own, s_sib, conv, proj, *outs):
-    embed = forward_blocks(1, (f_own, f_sib), (s_own, s_sib), [conv], [proj], before[...], outs)
+
+
+def middle_kernel(blocks, index_ref, f_own, f_sib, before, s_own, s_sib, *refs):
+    convs, projs, refs = refs[:blocks], refs[blocks : 2 * blocks], refs[2 * blocks :]
+    *outs, embed_ref, ahead_own, ahead_sib, short, sems = refs
+    fetch = fetcher(sems)
+    targets = [short.at[k] for k in range(2 * blocks)] + [ahead_own, ahead_sib]
+    copies = [None] * len(targets)
+    for j in range(blocks + 1):
+        at = columns(index_ref, j + 1, short.shape[2])
+        for side in (1, 0):
+            copies[2 * j + side] = fetch((s_own, s_sib)[side].at[:, at], targets[2 * j + side])
+
+    def ready(j, side):
+        copies[2 * j + side].wait()
+
+    feats, weights = (f_own, f_sib), [[c] for c in convs]
+    embed_ref[...] = forward_blocks(blocks, feats, targets, weights, projs, before[...], outs, ready)
+    ready(blocks, 1)
+    ready(blocks, 0)
+
+
+def last_kernel(images, f_own, f_sib, before, member, s_own, s_sib, proj, *refs):
+    convs, outs = refs[:-5], refs[-5:]
+    embed = forward_blocks(1, (f_own, f_sib), (s_own, s_sib), [convs], [proj], before[...], outs)
     mine_ref, send_ref = outs[-2:]
     half = embed.shape[1] // 2
     whole = jnp.concatenate([member[...]] * (half // member.shape[1]), axis=1)
@@ -131,50 +157,55 @@
     return [((rows, count), BF), ((rows, count), BF), ((2 * images, count), BF)]
 
 
-def forward_first(index, partner, feats, shorts, conv, proj, peers, images):
+def from_hbm(x):
+    return pltpu.with_memory_space_constraint(x, pltpu.HBM)
+
+
+def forward_first(index, partner, feats, shorts, conv, proj, images):
     rows, width = feats[0].shape
     count, embed = proj.shape
-    hbm = [pltpu.with_memory_space_constraint(a, pltpu.HBM) for a in (feats[0], shorts[0], conv, proj)]
-    hbm.insert(2, shorts[1])
     shapes = block_shapes(rows, count, images)
     shapes += [((2 * images, embed), F32), ((rows, width), BF), ((count, embed), BF), ((images, 128), F32)]
-    shapes += [((rows, count), BF)] * (2 * peers - 2)
     outs = forward_call(
-        functools.partial(first_kernel, peers, images),
-        [pl.BlockSpec(memory_space=pltpu.SMEM)] * 2 + [vspec()] + [pl.BlockSpec(memory_space=pl.ANY)] * 5,
+        functools.partial(first_kernel, images),
+        [pl.BlockSpec(memory_space=pltpu.SMEM)] + [vspec()] + [pl.BlockSpec(memory_space=pl.ANY)] * 6,
         shapes,
         [
             pltpu.VMEM((2, rows, count), BF),
             pltpu.VMEM((count, width), BF),
-            pltpu.SemaphoreType.DMA((3 + 2 * peers,)),
+            pltpu.SMEM((images,), jnp.int32),
+            pltpu.SemaphoreType.DMA((6,)),
         ],
         (rows, width, count),
         "forward_first",
-        *(index, pltpu.with_memory_space_constraint(partner, pltpu.HBM), feats[1], *hbm),
-    )
-    return outs[:3], outs[3], outs[4], outs[5], outs[6], outs[7:]
-
-
-def forward_middle(feats, shorts, convs, projs, images, before):
+        *(index, feats[1], from_hbm(partner), from_hbm(feats[0]), from_hbm(shorts[0]), from_hbm(shorts[1])),
+        *(from_hbm(conv), from_hbm(proj)),
+    )
+    return outs[:3], outs[3], outs[4], outs[5], outs[6]
+
+
+def forward_middle(index, feats, shorts, convs, projs, images, before):
     rows, width = feats[0].shape
     count, blocks = convs[0].shape[0], len(convs)
-    arrays = (*feats, before, *shorts, *convs, *projs)
     outs = forward_call(
         functools.partial(middle_kernel, blocks),
-        [vspec()] * len(arrays),
-        block_shapes(rows, count, images) * blocks + [(before.shape, F32)],
-        [],
+        [pl.BlockSpec(memory_space=pltpu.SMEM)]
+        + [vspec()] * 3
+        + [pl.BlockSpec(memory_space=pl.ANY)] * 2
+        + [vspec()] * (2 * blocks),
+        block_shapes(rows, count, images) * blocks + [(before.shape, F32)] + [((rows, count), BF)] * 2,
+        [pltpu.VMEM((2 * blocks, rows, count), BF), pltpu.SemaphoreType.DMA((2 * blocks + 2,))],
         (rows, width, blocks * count),
         "forward_middle",
-        *arrays,
-    )
-    return [outs[3 * j : 3 * j + 3] for j in range(blocks)], outs[-1]
-
-
-def forward_last(feats, shorts, conv, proj, images, before, member):
+        *(index, *feats, before, from_hbm(shorts[0]), from_hbm(shorts[1]), *convs, *projs),
+    )
+    return [outs[3 * j : 3 * j + 3] for j in range(blocks)], outs[-3], outs[-2:]
+
+
+def forward_last(feats, shorts, convs, proj, images, before, member):
     rows, width = feats[0].shape
     count, embed = proj.shape
-    arrays = (*feats, before, member, *shorts, conv, proj)
+    arrays = (*feats, before, member, *shorts, proj, *convs)
     outs = forward_call(
         functools.partial(last_kernel, images),
         [vspec()] * len(arrays),
@@ -220,7 +251,7 @@
     place = place_ref[0]
     half = z_ref.shape[2] // 2
     for j in range(slabs):
-        block = chunks[0].at[j] if len(chunks) == 1 else chunks[j]
+        block = chunks[0].at[j] if len(chunks) == 1 else chunks[ORDER.index(j)]
         at = pl.ds(pl.multiple_of((place ^ j) * images, images), images)
         for g in (0, 1):
             z_ref[g, at] = block[g * images : (g + 1) * images]
@@ -251,7 +282,7 @@
         compiler_params=params(80 * (slabs * images) ** 2),
         cost_estimate=pl.CostEstimate(flops=10**9, bytes_accessed=0, transcendentals=0),
         name="hsic_groups",
-    )(place, *chunks)
+    )(place, *([chunks[j] for j in ORDER] if len(chunks) > 1 else chunks))
 
 
 def backward_kernel(blocks, images, part, extra, after, f_own, f_sib, ge_ref, *refs):
@@ -407,32 +438,13 @@
     return small_call(gate_kernel, [(x.shape, x.dtype)], "gate", x, tokens=(token,))[0]
 
 
-def pack_kernel(start, conv, proj, token, out):
-    half = conv.shape[0] // 2
-    fold = conv.shape[1] // proj.shape[1]
-    out[0:half] = conv[start : start + half]
-    rows = half // fold
-    for k in range(fold):
-        piece = proj[start + k * rows : start + (k + 1) * rows]
-        out[half:, k * proj.shape[1] : (k + 1) * proj.shape[1]] = piece
-
-
-def pack_half(start, conv, proj, token):
-    half, fold = conv.shape[0] // 2, conv.shape[1] // proj.shape[1]
-    shape = (half + half // fold, conv.shape[1])
-    return small_call(functools.partial(pack_kernel, start), [(shape, BF)], "pack_half", conv, proj, tokens=(token,))[0]
-
-
-def unpack_kernel(*refs):
-    conv, proj = refs[-2:]
-    half = conv.shape[0] // 2
-    fold = conv.shape[1] // proj.shape[1]
-    rows = half // fold
-    for k, ref in enumerate(refs[:-2]):
-        conv[k * half : (k + 1) * half] = ref[0:half]
-        for j in range(fold):
-            at = k * half + j * rows
-            proj[at : at + rows] = ref[half:, j * proj.shape[1] : (j + 1) * proj.shape[1]]
+def part_kernel(start, x, token, out):
+    out[...] = x[start : start + out.shape[0]]
+
+
+def half_of(start, x, token):
+    shape = (x.shape[0] // 2, x.shape[1])
+    return small_call(functools.partial(part_kernel, start), [(shape, x.dtype)], "half_of", x, tokens=(token,))[0]
 
 
 def swap(x, axis, bit):
@@ -457,28 +469,25 @@
 
     f_sib = swap(features, "fsdp", 1)
     s_sib = swap(shortcut, "fsdp", 1)
-    first, embed, f_own, proj_own, member, ahead = forward_first(
-        index, partner, (features, f_sib), (shortcut, s_sib), conv_weight, proj_weight, peers, images
+    shorts = (shortcut, s_sib)
+    first, embed, f_own, proj_own, member = forward_first(
+        index, partner, (features, f_sib), shorts, conv_weight, proj_weight, images
     )
     feats = (f_own, f_sib)
+    projs = [swap(proj_weight, "fsdp", 2 * j) for j in range(1, peers)]
     if peers == 4:
         conv_y = swap(conv_weight, "fsdp", 4)
-        proj_x = swap(proj_weight, "fsdp", 2)
         conv_x = swap(conv_weight, "fsdp", 2)
-        proj_y = swap(proj_weight, "fsdp", 4)
         halves = [
-            swap(pack_half(0, conv_y, proj_y, embed), "fsdp", 2),
-            swap(pack_half(count // 2, conv_x, proj_x, embed), "fsdp", 4),
+            swap(half_of(0, conv_y, embed), "fsdp", 2),
+            swap(half_of(count // 2, conv_x, embed), "fsdp", 4),
         ]
-        conv_far, proj_far = small_call(
-            unpack_kernel, [(conv_weight.shape, BF), (proj_weight.shape, BF)], "unpack_halves", *halves
-        )
-        convs, projs = [conv_x, conv_y, conv_far], [proj_x, proj_y, proj_far]
+        convs = [conv_x, conv_y, halves]
     else:
         convs = [swap(conv_weight, "fsdp", 2 * j) for j in range(1, peers)]
-        projs = [swap(proj_weight, "fsdp", 2 * j) for j in range(1, peers)]
-    middle, embed = forward_middle(feats, ahead[:-2], convs[:-1], projs[:-1], images, embed)
-    last, mine, send = forward_last(feats, ahead[-2:], convs[-1], projs[-1], images, embed, member)
+        convs[-1] = [convs[-1]]
+    middle, embed, ahead = forward_middle(index, feats, shorts, convs[:-1], projs[:-1], images, embed)
+    last, mine, send = forward_last(feats, ahead, convs[-1], projs[-1], images, embed, member)
     blocks, projs = [first, *middle, last], [proj_own, *projs]
     blocks = [(*b, p) for b, p in zip(blocks, projs)]
     embeds = sum_of(F32, mine, swap(send, "fsdp", 1))

time: 68.8 us -> 66.6 us (0.968)
  waiting for transfers between devices: 28.5 us -> 23.5 us
  starting transfers between devices: 25.3 us -> 27.3 us
  Pallas kernels: 14 us -> 14.8 us
    ppermute x22 -> x23, waiting for transfers between devices: 28.5 us -> 23.5 us  [swap(): return lax.ppermute(x, axis, [(i, i ^ bit) for i in range(size)])]
    ppermute x22 -> x23, starting transfers between devices: 25.3 us -> 27.3 us  [swap(): return lax.ppermute(x, axis, [(i, i ^ bit) for i in range(size)])]
    pallas_call x3, Pallas kernels: 5.58 us -> 6.36 us  [forward_call(): pl.pallas_call(kernel, in_specs=in_specs, out_specs=[vspec()] * len(shape...]
    pallas_call x13 -> x12, Pallas kernels: 2.31 us -> 2.28 us  [small_call(): pl.pallas_call(kernel, in_specs=[vspec()] * len(arrays) + [pl.BlockSpec(m...]
  transfers between devices with their start and end apart: 22 -> 23, of which waited for: 14 -> 15; matrix products, arithmetic and copies ran while one was open for 0% -> 0% of each run, Pallas kernels for 15% -> 16%
where the time goes in v3:
time: 66.6 us; the launch traced here: 66.4 us
  starting transfers between devices  27.3 us (41%)
  waiting for transfers between devices  23.5 us (35%)
  Pallas kernels  14.8 us (22%)
  between operations  0.77 us (1%)
    ppermute x23, starting transfers between devices, swap(): return lax.ppermute(x, axis, [(i, i ^ bit) for i in range(size)])  27.3 us
    ppermute x23, waiting for transfers between devices, swap(): return lax.ppermute(x, axis, [(i, i ^ bit) for i in range(size)])  23.5 us
    pallas_call x3, Pallas kernels, forward_call(): pl.pallas_call(kernel, in_specs=in_specs, out_specs=[vspec()] * len(shape...  6.36 us
    pallas_call x5, Pallas kernels, backward(): pl.pallas_call(functools.partial(backward_kernel, len(blocks), images, pa...  4.84 us
    pallas_call x12, Pallas kernels, small_call(): pl.pallas_call(kernel, in_specs=[vspec()] * len(arrays) + [pl.BlockSpec(m...  2.28 us
  transfers between devices with their start and end apart: 23, of which 15 were waited for; matrix products, arithmetic and copies ran while one was open for 0% of the time, Pallas kernels for 16%

profile of v3, /device:TPU:0, one launch (start us, length us, event | category | flops | bytes accessed | tf_op | source)
XLA Modules:
  0.0 66.4 jit_solution(5330753210058261952)
XLA Ops:
  0.6 0.5 collective-permute-start.1
  1.1 0.1 collective-permute-start
  1.2 2.9 %collective-permute-start.3 = (bf16[256,512]{1,0:T(8,128)(2,1)}, bf16[256,512]{1,0:T(8,128)(2,1)S(1)}, u32[]{:S(2)}, u32[]{:S(2)}) collective-permute-start(bf16[256,512]{1,0:T(8,128)(2,1)} %conv.1), channel_id=1, source_target_pairs={{0,4},{1,5},{2,6},{3,7},{4,0},{5,1},{6,2},{7,3},{8,12},{9,13},{10,... | collective-permute-start | bytes 786440 | tf_op jit(solution)/shard_map/ppermute | solution.py:452
  4.2 1.5 %collective-permute-start.2 = (bf16[256,512]{1,0:T(8,128)(2,1)}, bf16[256,512]{1,0:T(8,128)(2,1)S(1)}, u32[]{:S(2)}, u32[]{:S(2)}) collective-permute-start(bf16[256,512]{1,0:T(8,128)(2,1)} %conv.1), channel_id=1, source_target_pairs={{0,2},{1,3},{2,0},{3,1},{4,6},{5,7},{6,4},{7,5},{8,10},{9,11},{10,... | collective-permute-start | bytes 786440 | tf_op jit(solution)/shard_map/ppermute | solution.py:452
  5.7 0.5 collective-permute-start.4
  6.2 0.0 collective-permute-done.f_sib
  6.2 1.4 %collective-permute-start.5 = (bf16[256,256]{1,0:T(8,128)(2,1)}, bf16[256,256]{1,0:T(8,128)(2,1)S(1)}, u32[]{:S(2)}, u32[]{:S(2)}) collective-permute-start(bf16[256,256]{1,0:T(8,128)(2,1)} %proj.1), channel_id=1, source_target_pairs={{0,4},{1,5},{2,6},{3,7},{4,0},{5,1},{6,2},{7,3},{8,12},{9,13},{10,... | collective-permute-start | bytes 393224 | tf_op jit(solution)/shard_map/ppermute | solution.py:452
  7.6 0.0 collective-permute-done.1.s_sib
  7.6 1.6 %collective-permute-start.6 = (bf16[256,256]{1,0:T(8,128)(2,1)}, bf16[256,256]{1,0:T(8,128)(2,1)S(1)}, u32[]{:S(2)}, u32[]{:S(2)}) collective-permute-start(bf16[256,256]{1,0:T(8,128)(2,1)} %proj.1), channel_id=1, source_target_pairs={{0,6},{1,7},{2,4},{3,5},{4,2},{5,3},{6,0},{7,1},{8,14},{9,15},{10,... | collective-permute-start | bytes 393224 | tf_op jit(solution)/shard_map/ppermute | solution.py:452
  9.2 2.2 %forward_first.1 = (bf16[392,256]{1,0:T(8,128)(2,1)S(1)}, bf16[392,256]{1,0:T(8,128)(2,1)S(1)}, bf16[16,256]{1,0:T(8,128)(2,1)S(1)}, f32[16,256]{1,0:T(8,128)S(1...) custom-call(s32[1]{0:T(128)} %bitcast.index_ref, ...), custom_call_target="tpu_custom_call" | custom-call | flops 822083584 | bytes 802816 | tf_op jit(solution)/shard_map/forward_first/pallas_call | solution.py:142
  11.4 0.1 collective-permute-done.3.refs_1_.x
  11.5 2.1 %collective-permute-start.7 = (bf16[128,512]{1,0:T(8,128)(2,1)S(1)}, bf16[128,512]{1,0:T(8,128)(2,1)S(1)}, u32[]{:S(2)}, u32[]{:S(2)}) collective-permute-start(bf16[128,512]{1,0:T(8,128)(2,1)S(1)} %half_of.2), channel_id=1, source_target_pairs={{0,2},{1,3},{2,0},{3,1},{4,6},{5,7},{6,4},{7,5},{8,10},{9,11},{10,... | collective-permute-start | bytes 393224 | tf_op jit(solution)/shard_map/ppermute | solution.py:452
  13.6 0.0 collective-permute-done.2.refs_0_.x
  13.6 1.6 %collective-permute-start.8 = (bf16[128,512]{1,0:T(8,128)(2,1)S(1)}, bf16[128,512]{1,0:T(8,128)(2,1)S(1)}, u32[]{:S(2)}, u32[]{:S(2)}) collective-permute-start(bf16[128,512]{1,0:T(8,128)(2,1)S(1)} %half_of.3), channel_id=1, source_target_pairs={{0,4},{1,5},{2,6},{3,7},{4,0},{5,1},{6,2},{7,3},{8,12},{9,13},{10,... | collective-permute-start | bytes 393224 | tf_op jit(solution)/shard_map/ppermute | solution.py:452
  15.2 1.2 %collective-permute-done.4.refs_2_.refs_3_ = bf16[256,256]{1,0:T(8,128)(2,1)S(1)} collective-permute-done((bf16[256,256]{1,0:T(8,128)(2,1)}, bf16[256,256]{1,0:T(8,128)(2,1)S(1)}, u32[]{:S(2)}, u32[]{:S(2)}) %collective-permute-start.4) | collective-permute-done | bytes 131104 | tf_op jit(solution)/shard_map/ppermute | solution.py:452
  16.4 0.0 collective-permute-done.5.refs_3_.refs_7_
  16.4 3.1 %forward_middle.1 = (bf16[392,256]{1,0:T(8,128)(2,1)S(1)}, bf16[392,256]{1,0:T(8,128)(2,1)S(1)}, bf16[16,256]{1,0:T(8,128)(2,1)S(1)}, bf16[392,256]{1,0:T(8,128)...) custom-call(s32[1]{0:T(128)} %bitcast.index_ref, ...), custom_call_target="tpu_custom_call" | custom-call | flops 1644167168 | bytes 1605632 | tf_op jit(solution)/shard_map/forward_middle/pallas_call | solution.py:142
  19.5 0.0 collective-permute-done.6.proj.refs_3_
  19.6 1.3 %collective-permute-done.7.refs_0_ = bf16[128,512]{1,0:T(8,128)(2,1)S(1)} collective-permute-done((bf16[128,512]{1,0:T(8,128)(2,1)S(1)}, bf16[128,512]{1,0:T(8,128)(2,1)S(1)}, u32[]{:S(2)}, u32[]{:S(2)}) %collective-permute-start.7) | collective-permute-done | bytes 131104 | tf_op jit(solution)/shard_map/ppermute | solution.py:452
  20.8 0.0 collective-permute-done.8.refs_1_
  20.8 1.0 %forward_last.1 = (bf16[392,256]{1,0:T(8,128)(2,1)S(1)}, bf16[392,256]{1,0:T(8,128)(2,1)S(1)}, bf16[16,256]{1,0:T(8,128)(2,1)S(1)}, f32[24,256]{1,0:T(8,128)S(1)}, f32[24,256]{1,0:T(8,128)S(1)}) custom-call(bf16[392,512]{1,0:T(8,128)(2,1)S(1)} %get-tuple-element.32.f_own, bf16[392,512]{1,0:T(8,128)(2,1)S(1)} %collective-permute-done.f_sib, ...), custom_call_target="tpu_custom_call" | custom-call | flops 822083584 | bytes 802816 | tf_op jit(solution)/shard_map/forward_last/pallas_call | solution.py:142
  21.8 0.0 collective-permute-start.9
  21.8 1.2 %collective-permute-done.9.refs_1_ = f32[24,256]{1,0:T(8,128)S(1)} collective-permute-done((f32[24,256]{1,0:T(8,128)S(1)}, f32[24,256]{1,0:T(8,128)S(1)}, u32[]{:S(2)}, u32[]{:S(2)}) %collective-permute-start.9) | collective-permute-done | bytes 24608 | tf_op jit(solution)/shard_map/ppermute | solution.py:452
  23.0 3.6 %collective-permute-start.10 = (f32[24,256]{1,0:T(8,128)S(1)}, f32[24,256]{1,0:T(8,128)S(1)}, u32[]{:S(2)}, u32[]{:S(2)}) collective-permute-start(f32[24,256]{1,0:T(8,128)S(1)} %sum_arrays.1.refs_0_), channel_id=1, source_target_pairs={{0,24},{8,16},{16,8},{24,0},{1,25},{9,17},{17,9},{25,1},{2,26},{10... | collective-permute-start | bytes 73736 | tf_op jit(solution)/shard_map/ppermute | solution.py:452
  26.6 0.0 collective-permute-start.11
  26.6 0.8 %collective-permute-start.12 = (f32[24,256]{1,0:T(8,128)S(1)}, f32[24,256]{1,0:T(8,128)S(1)}, u32[]{:S(2)}, u32[]{:S(2)}) collective-permute-start(f32[24,256]{1,0:T(8,128)S(1)} %sum_arrays.1.refs_0_), channel_id=1, source_target_pairs={{0,16},{8,24},{16,0},{24,8},{1,17},{9,25},{17,1},{25,9},{2,18},{10... | collective-permute-start | bytes 73736 | tf_op jit(solution)/shard_map/ppermute | solution.py:452
  27.4 1.2 %collective-permute-done.10.refs_1_ = f32[24,256]{1,0:T(8,128)S(1)} collective-permute-done((f32[24,256]{1,0:T(8,128)S(1)}, f32[24,256]{1,0:T(8,128)S(1)}, u32[]{:S(2)}, u32[]{:S(2)}) %collective-permute-start.10) | collective-permute-done | bytes 24608 | tf_op jit(solution)/shard_map/ppermute | solution.py:452
  28.7 1.9 %collective-permute-done.11.refs_2_ = f32[24,256]{1,0:T(8,128)S(1)} collective-permute-done((f32[24,256]{1,0:T(8,128)S(1)}, f32[24,256]{1,0:T(8,128)S(1)}, u32[]{:S(2)}, u32[]{:S(2)}) %collective-permute-start.11) | collective-permute-done | bytes 24608 | tf_op jit(solution)/shard_map/ppermute | solution.py:452
  30.5 1.1 %collective-permute-done.12.refs_3_ = f32[24,256]{1,0:T(8,128)S(1)} collective-permute-done((f32[24,256]{1,0:T(8,128)S(1)}, f32[24,256]{1,0:T(8,128)S(1)}, u32[]{:S(2)}, u32[]{:S(2)}) %collective-permute-start.12) | collective-permute-done | bytes 24608 | tf_op jit(solution)/shard_map/ppermute | solution.py:452
  31.6 1.3 %hsic_groups.1 = (f32[4,16,256]{2,1,0:T(8,128)S(1)}, f32[1,1]{1,0:T(1,128)}) custom-call(s32[1]{0:T(128)} %bitcast.1.place_ref, f32[24,256]{1,0:T(8,128)S(1)} %sum_arrays.1.refs_0_, f32[24,256]{1,0:T(8,128)S(1)} %collective-permute-done.10.refs_1_, f32[24,256]{1,0:T(8,128)S(1)} %collective-permute-done.11.refs_2_, f32[24,256]{1,0:T(8,128)S(1)} %collective-permute-done.12.refs_3_), custom_call_target="tpu_custom_call" | custom-call | flops 1000000000 | tf_op jit(solution)/shard_map/hsic_groups/pallas_call | solution.py:273
  33.0 0.7 %backward_blocks.5.refs_8_ = bf16[144,512]{1,0:T(8,128)(2,1)S(1)} custom-call(bf16[392,512]{1,0:T(8,128)(2,1)S(1)} %get-tuple-element.32.f_own, bf16[392,512]{1,0:T(8,128)(2,1)S(1)} %collective-permute-done.f_sib, f32[4,16,256]{2,1,0:T(8,128)S(1)} %get-tuple-element.40.ge_ref.own_ge, bf16[392,256]{1,0:T(8,128)(2,1)S(1)} %get-tuple-element.51.refs_0_, ...), custom_call_target="tpu_custom_call" | custom-call | flops 411041792 | bytes 200704 | tf_op jit(solution)/shard_map/backward_blocks/pallas_call | solution.py:320
  33.7 1.5 %collective-permute-start.15 = (bf16[144,512]{1,0:T(8,128)(2,1)S(1)}, bf16[144,512]{1,0:T(8,128)(2,1)S(1)}, u32[]{:S(2)}, u32[]{:S(2)}) collective-permute-start(bf16[144,512]{1,0:T(8,128)(2,1)S(1)} %backward_blocks.5.refs_8_), channel_id=1, source_target_pairs={{0,6},{1,7},{2,4},{3,5},{4,2},{5,3},{6,0},{7,1},{8,14},{9,15},{10,... | collective-permute-start | bytes 442376 | tf_op jit(solution)/shard_map/ppermute | solution.py:452
  35.2 1.3 %backward_blocks.6 = (bf16[144,512]{1,0:T(8,128)(2,1)S(1)}, bf16[144,512]{1,0:T(8,128)(2,1)S(1)}) custom-call(bf16[392,512]{1,0:T(8,128)(2,1)S(1)} %get-tuple-element.32.f_own, bf16[392,512]{1,0:T(8,128)(2,1)S(1)} %collective-permute-done.f_sib, f32[4,16,256]{2,1,0:T(8,128)S(1)} %get-tuple-element.40.ge_ref.own_ge, ...), custom_call_target="tpu_custom_call" | custom-call | flops 822083584 | bytes 401408 | tf_op jit(solution)/shard_map/backward_blocks/pallas_call | solution.py:320
  36.4 0.6 collective-permute-start.13
  37.0 1.5 %collective-permute-start.14 = (bf16[144,512]{1,0:T(8,128)(2,1)S(1)}, bf16[144,512]{1,0:T(8,128)(2,1)S(1)}, u32[]{:S(2)}, u32[]{:S(2)}) collective-permute-start(bf16[144,512]{1,0:T(8,128)(2,1)S(1)} %get-tuple-element.55.refs_5_), channel_id=1, source_target_pairs={{0,4},{1,5},{2,6},{3,7},{4,0},{5,1},{6,2},{7,3},{8,12},{9,13},{10,... | collective-permute-start | bytes 442376 | tf_op jit(solution)/shard_map/ppermute | solution.py:452
  38.6 0.7 %backward_blocks.7.refs_8_.x = bf16[160,512]{1,0:T(8,128)(2,1)S(1)} custom-call(bf16[392,512]{1,0:T(8,128)(2,1)S(1)} %get-tuple-element.32.f_own, bf16[392,512]{1,0:T(8,128)(2,1)S(1)} %collective-permute-done.f_sib, f32[4,16,256]{2,1,0:T(8,128)S(1)} %get-tuple-element.40.ge_ref.own_ge, bf16[392,256]{1,0:T(8,128)(2,1)S(1)} %get-tuple-element.51.refs_0_, ...), custom_call_target="tpu_custom_call" | custom-call | flops 411041792 | bytes 200704 | tf_op jit(solution)/shard_map/backward_blocks/pallas_call | solution.py:320
  39.3 1.3 %backward_blocks.8 = (bf16[160,512]{1,0:T(8,128)(2,1)S(1)}, bf16[160,512]{1,0:T(8,128)(2,1)S(1)}) custom-call(bf16[392,512]{1,0:T(8,128)(2,1)S(1)} %get-tuple-element.32.f_own, bf16[392,512]{1,0:T(8,128)(2,1)S(1)} %collective-permute-done.f_sib, f32[4,16,256]{2,1,0:T(8,128)S(1)} %get-tuple-element.40.ge_ref.own_ge, ...), custom_call_target="tpu_custom_call" | custom-call | flops 822083584 | bytes 401408 | tf_op jit(solution)/shard_map/backward_blocks/pallas_call | solution.py:320
  40.6 0.9 %backward_blocks.9.own = f32[256,512]{1,0:T(8,128)S(1)} custom-call(bf16[392,512]{1,0:T(8,128)(2,1)S(1)} %get-tuple-element.32.f_own, bf16[392,512]{1,0:T(8,128)(2,1)S(1)} %collective-permute-done.f_sib, f32[4,16,256]{2,1,0:T(8,128)S(1)} %get-tuple-element.40.ge_ref.own_ge, bf16[392,256]{1,0:T(8,128)(2,1)S(1)} %get-tuple-element.41.refs_0_, ...), custom_call_target="tpu_custom_call" | custom-call | flops 822083584 | bytes 401408 | tf_op jit(solution)/shard_map/backward_blocks/pallas_call | solution.py:320
  41.5 0.5 collective-permute-done.13.refs_0_
  42.0 0.6 collective-permute-done.14.refs_1_
  42.5 0.0 collective-permute-done.15.refs_2_
  42.5 0.1 collect_terms.2.mine.token
  42.6 1.8 %collective-permute-start.16 = (bf16[160,512]{1,0:T(8,128)(2,1)S(1)}, bf16[160,512]{1,0:T(8,128)(2,1)S(1)}, u32[]{:S(2)}, u32[]{:S(2)}) collective-permute-start(bf16[160,512]{1,0:T(8,128)(2,1)S(1)} %collect_terms.2.mine.token), channel_id=1, source_target_pairs={{0,8},{8,0},{16,24},{24,16},{1,9},{9,1},{17,25},{25,17},{2,10},{10... | collective-permute-start | bytes 491528 | tf_op jit(solution)/shard_map/ppermute | solution.py:452
  44.4 2.2 %collective-permute-start.20 = (bf16[160,512]{1,0:T(8,128)(2,1)S(1)}, bf16[160,512]{1,0:T(8,128)(2,1)S(1)}, u32[]{:S(2)}, u32[]{:S(2)}) collective-permute-start(bf16[160,512]{1,0:T(8,128)(2,1)S(1)} %gate.5), channel_id=1, source_target_pairs={{0,6},{1,7},{2,4},{3,5},{4,2},{5,3},{6,0},{7,1},{8,14},{9,15},{10,... | collective-permute-start | bytes 491528 | tf_op jit(solution)/shard_map/ppermute | solution.py:452
  46.7 0.7 %collective-permute-start.19 = (bf16[160,512]{1,0:T(8,128)(2,1)S(1)}, bf16[160,512]{1,0:T(8,128)(2,1)S(1)}, u32[]{:S(2)}, u32[]{:S(2)}) collective-permute-start(bf16[160,512]{1,0:T(8,128)(2,1)S(1)} %gate.4), channel_id=1, source_target_pairs={{0,4},{1,5},{2,6},{3,7},{4,0},{5,1},{6,2},{7,3},{8,12},{9,13},{10,... | collective-permute-start | bytes 491528 | tf_op jit(solution)/shard_map/ppermute | solution.py:452
  47.4 0.6 collective-permute-start.18
  48.0 0.2 collective-permute-done.16.other
  48.3 0.4 collective-permute-start.17
  48.7 3.3 %collective-permute-done.20.refs_2_ = bf16[160,512]{1,0:T(8,128)(2,1)S(1)} collective-permute-done((bf16[160,512]{1,0:T(8,128)(2,1)S(1)}, bf16[160,512]{1,0:T(8,128)(2,1)S(1)}, u32[]{:S(2)}, u32[]{:S(2)}) %collective-permute-start.20) | collective-permute-done | bytes 163872 | tf_op jit(solution)/shard_map/ppermute | solution.py:452
  51.9 1.2 %collective-permute-done.19.refs_1_ = bf16[160,512]{1,0:T(8,128)(2,1)S(1)} collective-permute-done((bf16[160,512]{1,0:T(8,128)(2,1)S(1)}, bf16[160,512]{1,0:T(8,128)(2,1)S(1)}, u32[]{:S(2)}, u32[]{:S(2)}) %collective-permute-start.19) | collective-permute-done | bytes 163872 | tf_op jit(solution)/shard_map/ppermute | solution.py:452
  53.1 0.0 collective-permute-done.18.refs_0_
  53.1 0.1 collect_terms.3.mine
  53.2 0.4 collective-permute-start.21
  53.5 1.9 %collective-permute-done.17.other.refs_1_ = bf16[192,512]{1,0:T(8,128)(2,1)S(1)} collective-permute-done((bf16[192,512]{1,0:T(8,128)(2,1)S(1)}, bf16[192,512]{1,0:T(8,128)(2,1)S(1)}, u32[]{:S(2)}, u32[]{:S(2)}) %collective-permute-start.17) | collective-permute-done | bytes 196640 | tf_op jit(solution)/shard_map/ppermute | solution.py:452
  55.4 1.2 %proj_grad.1 = (f32[256,256]{1,0:T(8,128)}, f32[8,128]{1,0:T(8,128)S(1)}) custom-call(f32[4,16,256]{2,1,0:T(8,128)S(1)} %get-tuple-element.40.ge_ref.own_ge, bf16[192,512]{1,0:T(8,128)(2,1)S(1)} %merge_slabs.2.refs_3_.mine.refs_0_, bf16[192,512]{1,0:T(8,128)(2,1)S(1)} %collective-permute-done.17.other.refs_1_, ...), custom_call_target="tpu_custom_call" | custom-call | tf_op jit(solution)/shard_map/proj_grad/pallas_call | solution.py:336
  56.6 1.6 %collective-permute-done.21.other = bf16[128,512]{1,0:T(8,128)(2,1)S(1)} collective-permute-done((bf16[128,512]{1,0:T(8,128)(2,1)S(1)}, bf16[128,512]{1,0:T(8,128)(2,1)S(1)}, u32[]{:S(2)}, u32[]{:S(2)}) %collective-permute-start.21) | collective-permute-done | bytes 131104 | tf_op jit(solution)/shard_map/ppermute | solution.py:452
  58.2 1.0 %collective-permute-start.22 = (bf16[128,512]{1,0:T(8,128)(2,1)S(1)}, bf16[128,512]{1,0:T(8,128)(2,1)S(1)}, u32[]{:S(2)}, u32[]{:S(2)}) collective-permute-start(bf16[128,512]{1,0:T(8,128)(2,1)S(1)} %merge_slabs.3.refs_2_), channel_id=1, source_target_pairs={{0,16},{8,24},{16,0},{24,8},{1,17},{9,25},{17,1},{25,9},{2,18},{10... | collective-permute-start | bytes 393224 | tf_op jit(solution)/shard_map/ppermute | solution.py:452
  59.2 6.3 %collective-permute-done.22.refs_3_ = bf16[128,512]{1,0:T(8,128)(2,1)S(1)} collective-permute-done((bf16[128,512]{1,0:T(8,128)(2,1)S(1)}, bf16[128,512]{1,0:T(8,128)(2,1)S(1)}, u32[]{:S(2)}, u32[]{:S(2)}) %collective-permute-start.22) | collective-permute-done | bytes 131104 | tf_op jit(solution)/shard_map/ppermute | solution.py:452
  65.6 0.8 %sum_slabs.1 = f32[256,512]{1,0:T(8,128)} custom-call(bf16[192,512]{1,0:T(8,128)(2,1)S(1)} %merge_slabs.2.refs_3_.mine.refs_0_, bf16[192,512]{1,0:T(8,128)(2,1)S(1)} %collective-permute-done.17.other.refs_1_, bf16[128,512]{1,0:T(8,128)(2,1)S(1)} %merge_slabs.3.refs_2_, bf16[128,512]{1,0:T(8,128)(2,1)S(1)} %collective-permute-done.22.refs_3_), custom_call_target="tpu_custom_call" | custom-call | tf_op jit(solution)/shard_map/sum_slabs/pallas_call | solution.py:336
  (8 shorter events, 0.1 us)
Async XLA Ops:
  0.6 6.9 %collective-permute-start.1 = (bf16[392,2048]{1,0:T(8,128)(2,1)}, bf16[392,2048]{1,0:T(8,128)(2,1)}, u32[]{:S(2)}, u32[]{:S(2)}) collective-permute-start(bf16[392,2048]{1,0:T(8,128)(2,1)} %s_own.3), channel_id=1, source_target_pairs={{0,1},{1,0},{2,3},{3,2},{4,5},{5,4},{6,7},{7,6},{8,9},{9,8},{10,11... | collective-permute-start | bytes 4816904 | tf_op jit(solution)/shard_map/ppermute | solution.py:452
  1.1 5.1 %collective-permute-start = (bf16[392,512]{1,0:T(8,128)(2,1)}, bf16[392,512]{1,0:T(8,128)(2,1)S(1)}, u32[]{:S(2)}, u32[]{:S(2)}) collective-permute-start(bf16[392,512]{1,0:T(8,128)(2,1)} %f_own.1), channel_id=1, source_target_pairs={{0,1},{1,0},{2,3},{3,2},{4,5},{5,4},{6,7},{7,6},{8,9},{9,8},{10,11... | collective-permute-start | bytes 1204232 | tf_op jit(solution)/shard_map/ppermute | solution.py:452
  1.2 10.3 %collective-permute-start.3 = (bf16[256,512]{1,0:T(8,128)(2,1)}, bf16[256,512]{1,0:T(8,128)(2,1)S(1)}, u32[]{:S(2)}, u32[]{:S(2)}) collective-permute-start(bf16[256,512]{1,0:T(8,128)(2,1)} %conv.1), channel_id=1, source_target_pairs={{0,4},{1,5},{2,6},{3,7},{4,0},{5,1},{6,2},{7,3},{8,12},{9,13},{10,... | collective-permute-start | bytes 786440 | tf_op jit(solution)/shard_map/ppermute | solution.py:452
  4.2 9.4 %collective-permute-start.2 = (bf16[256,512]{1,0:T(8,128)(2,1)}, bf16[256,512]{1,0:T(8,128)(2,1)S(1)}, u32[]{:S(2)}, u32[]{:S(2)}) collective-permute-start(bf16[256,512]{1,0:T(8,128)(2,1)} %conv.1), channel_id=1, source_target_pairs={{0,2},{1,3},{2,0},{3,1},{4,6},{5,7},{6,4},{7,5},{8,10},{9,11},{10,... | collective-permute-start | bytes 786440 | tf_op jit(solution)/shard_map/ppermute | solution.py:452
  5.7 10.7 %collective-permute-start.4 = (bf16[256,256]{1,0:T(8,128)(2,1)}, bf16[256,256]{1,0:T(8,128)(2,1)S(1)}, u32[]{:S(2)}, u32[]{:S(2)}) collective-permute-start(bf16[256,256]{1,0:T(8,128)(2,1)} %proj.1), channel_id=1, source_target_pairs={{0,2},{1,3},{2,0},{3,1},{4,6},{5,7},{6,4},{7,5},{8,10},{9,11},{10,... | collective-permute-start | bytes 393224 | tf_op jit(solution)/shard_map/ppermute | solution.py:452
  6.2 10.2 %collective-permute-start.5 = (bf16[256,256]{1,0:T(8,128)(2,1)}, bf16[256,256]{1,0:T(8,128)(2,1)S(1)}, u32[]{:S(2)}, u32[]{:S(2)}) collective-permute-start(bf16[256,256]{1,0:T(8,128)(2,1)} %proj.1), channel_id=1, source_target_pairs={{0,4},{1,5},{2,6},{3,7},{4,0},{5,1},{6,2},{7,3},{8,12},{9,13},{10,... | collective-permute-start | bytes 393224 | tf_op jit(solution)/shard_map/ppermute | solution.py:452
  7.6 12.0 %collective-permute-start.6 = (bf16[256,256]{1,0:T(8,128)(2,1)}, bf16[256,256]{1,0:T(8,128)(2,1)S(1)}, u32[]{:S(2)}, u32[]{:S(2)}) collective-permute-start(bf16[256,256]{1,0:T(8,128)(2,1)} %proj.1), channel_id=1, source_target_pairs={{0,6},{1,7},{2,4},{3,5},{4,2},{5,3},{6,0},{7,1},{8,14},{9,15},{10,... | collective-permute-start | bytes 393224 | tf_op jit(solution)/shard_map/ppermute | solution.py:452
  11.5 9.3 %collective-permute-start.7 = (bf16[128,512]{1,0:T(8,128)(2,1)S(1)}, bf16[128,512]{1,0:T(8,128)(2,1)S(1)}, u32[]{:S(2)}, u32[]{:S(2)}) collective-permute-start(bf16[128,512]{1,0:T(8,128)(2,1)S(1)} %half_of.2), channel_id=1, source_target_pairs={{0,2},{1,3},{2,0},{3,1},{4,6},{5,7},{6,4},{7,5},{8,10},{9,11},{10,... | collective-permute-start | bytes 393224 | tf_op jit(solution)/shard_map/ppermute | solution.py:452
  13.6 7.2 %collective-permute-start.8 = (bf16[128,512]{1,0:T(8,128)(2,1)S(1)}, bf16[128,512]{1,0:T(8,128)(2,1)S(1)}, u32[]{:S(2)}, u32[]{:S(2)}) collective-permute-start(bf16[128,512]{1,0:T(8,128)(2,1)S(1)} %half_of.3), channel_id=1, source_target_pairs={{0,4},{1,5},{2,6},{3,7},{4,0},{5,1},{6,2},{7,3},{8,12},{9,13},{10,... | collective-permute-start | bytes 393224 | tf_op jit(solution)/shard_map/ppermute | solution.py:452
  21.8 1.2 %collective-permute-start.9 = (f32[24,256]{1,0:T(8,128)S(1)}, f32[24,256]{1,0:T(8,128)S(1)}, u32[]{:S(2)}, u32[]{:S(2)}) collective-permute-start(f32[24,256]{1,0:T(8,128)S(1)} %get-tuple-element.39), channel_id=1, source_target_pairs={{0,1},{1,0},{2,3},{3,2},{4,5},{5,4},{6,7},{7,6},{8,9},{9,8},{10,11... | collective-permute-start | bytes 73736 | tf_op jit(solution)/shard_map/ppermute | solution.py:452
  23.0 5.6 %collective-permute-start.10 = (f32[24,256]{1,0:T(8,128)S(1)}, f32[24,256]{1,0:T(8,128)S(1)}, u32[]{:S(2)}, u32[]{:S(2)}) collective-permute-start(f32[24,256]{1,0:T(8,128)S(1)} %sum_arrays.1.refs_0_), channel_id=1, source_target_pairs={{0,24},{8,16},{16,8},{24,0},{1,25},{9,17},{17,9},{25,1},{2,26},{10... | collective-permute-start | bytes 73736 | tf_op jit(solution)/shard_map/ppermute | solution.py:452
  26.6 3.9 %collective-permute-start.11 = (f32[24,256]{1,0:T(8,128)S(1)}, f32[24,256]{1,0:T(8,128)S(1)}, u32[]{:S(2)}, u32[]{:S(2)}) collective-permute-start(f32[24,256]{1,0:T(8,128)S(1)} %sum_arrays.1.refs_0_), channel_id=1, source_target_pairs={{0,8},{8,0},{16,24},{24,16},{1,9},{9,1},{17,25},{25,17},{2,10},{10... | collective-permute-start | bytes 73736 | tf_op jit(solution)/shard_map/ppermute | solution.py:452
  26.6 5.0 %collective-permute-start.12 = (f32[24,256]{1,0:T(8,128)S(1)}, f32[24,256]{1,0:T(8,128)S(1)}, u32[]{:S(2)}, u32[]{:S(2)}) collective-permute-start(f32[24,256]{1,0:T(8,128)S(1)} %sum_arrays.1.refs_0_), channel_id=1, source_target_pairs={{0,16},{8,24},{16,0},{24,8},{1,17},{9,25},{17,1},{25,9},{2,18},{10... | collective-permute-start | bytes 73736 | tf_op jit(solution)/shard_map/ppermute | solution.py:452
  33.7 8.9 %collective-permute-start.15 = (bf16[144,512]{1,0:T(8,128)(2,1)S(1)}, bf16[144,512]{1,0:T(8,128)(2,1)S(1)}, u32[]{:S(2)}, u32[]{:S(2)}) collective-permute-start(bf16[144,512]{1,0:T(8,128)(2,1)S(1)} %backward_blocks.5.refs_8_), channel_id=1, source_target_pairs={{0,6},{1,7},{2,4},{3,5},{4,2},{5,3},{6,0},{7,1},{8,14},{9,15},{10,... | collective-permute-start | bytes 442376 | tf_op jit(solution)/shard_map/ppermute | solution.py:452
  36.4 5.5 %collective-permute-start.13 = (bf16[144,512]{1,0:T(8,128)(2,1)S(1)}, bf16[144,512]{1,0:T(8,128)(2,1)S(1)}, u32[]{:S(2)}, u32[]{:S(2)}) collective-permute-start(bf16[144,512]{1,0:T(8,128)(2,1)S(1)} %get-tuple-element.54.refs_4_), channel_id=1, source_target_pairs={{0,2},{1,3},{2,0},{3,1},{4,6},{5,7},{6,4},{7,5},{8,10},{9,11},{10,... | collective-permute-start | bytes 442376 | tf_op jit(solution)/shard_map/ppermute | solution.py:452
  37.0 5.5 %collective-permute-start.14 = (bf16[144,512]{1,0:T(8,128)(2,1)S(1)}, bf16[144,512]{1,0:T(8,128)(2,1)S(1)}, u32[]{:S(2)}, u32[]{:S(2)}) collective-permute-start(bf16[144,512]{1,0:T(8,128)(2,1)S(1)} %get-tuple-element.55.refs_5_), channel_id=1, source_target_pairs={{0,4},{1,5},{2,6},{3,7},{4,0},{5,1},{6,2},{7,3},{8,12},{9,13},{10,... | collective-permute-start | bytes 442376 | tf_op jit(solution)/shard_map/ppermute | solution.py:452
  42.6 5.6 %collective-permute-start.16 = (bf16[160,512]{1,0:T(8,128)(2,1)S(1)}, bf16[160,512]{1,0:T(8,128)(2,1)S(1)}, u32[]{:S(2)}, u32[]{:S(2)}) collective-permute-start(bf16[160,512]{1,0:T(8,128)(2,1)S(1)} %collect_terms.2.mine.token), channel_id=1, source_target_pairs={{0,8},{8,0},{16,24},{24,16},{1,9},{9,1},{17,25},{25,17},{2,10},{10... | collective-permute-start | bytes 491528 | tf_op jit(solution)/shard_map/ppermute | solution.py:452
  44.4 7.5 %collective-permute-start.20 = (bf16[160,512]{1,0:T(8,128)(2,1)S(1)}, bf16[160,512]{1,0:T(8,128)(2,1)S(1)}, u32[]{:S(2)}, u32[]{:S(2)}) collective-permute-start(bf16[160,512]{1,0:T(8,128)(2,1)S(1)} %gate.5), channel_id=1, source_target_pairs={{0,6},{1,7},{2,4},{3,5},{4,2},{5,3},{6,0},{7,1},{8,14},{9,15},{10,... | collective-permute-start | bytes 491528 | tf_op jit(solution)/shard_map/ppermute | solution.py:452
  46.7 6.4 %collective-permute-start.19 = (bf16[160,512]{1,0:T(8,128)(2,1)S(1)}, bf16[160,512]{1,0:T(8,128)(2,1)S(1)}, u32[]{:S(2)}, u32[]{:S(2)}) collective-permute-start(bf16[160,512]{1,0:T(8,128)(2,1)S(1)} %gate.4), channel_id=1, source_target_pairs={{0,4},{1,5},{2,6},{3,7},{4,0},{5,1},{6,2},{7,3},{8,12},{9,13},{10,... | collective-permute-start | bytes 491528 | tf_op jit(solution)/shard_map/ppermute | solution.py:452
  47.4 5.7 %collective-permute-start.18 = (bf16[160,512]{1,0:T(8,128)(2,1)S(1)}, bf16[160,512]{1,0:T(8,128)(2,1)S(1)}, u32[]{:S(2)}, u32[]{:S(2)}) collective-permute-start(bf16[160,512]{1,0:T(8,128)(2,1)S(1)} %gate.3), channel_id=1, source_target_pairs={{0,2},{1,3},{2,0},{3,1},{4,6},{5,7},{6,4},{7,5},{8,10},{9,11},{10,... | collective-permute-start | bytes 491528 | tf_op jit(solution)/shard_map/ppermute | solution.py:452
  48.3 7.2 %collective-permute-start.17 = (bf16[192,512]{1,0:T(8,128)(2,1)S(1)}, bf16[192,512]{1,0:T(8,128)(2,1)S(1)}, u32[]{:S(2)}, u32[]{:S(2)}) collective-permute-start(bf16[192,512]{1,0:T(8,128)(2,1)S(1)} %merge_slabs.2.refs_3_.mine.refs_0_), channel_id=1, source_target_pairs={{0,16},{8,24},{16,0},{24,8},{1,17},{9,25},{17,1},{25,9},{2,18},{10... | collective-permute-start | bytes 589832 | tf_op jit(solution)/shard_map/ppermute | solution.py:452
  53.2 5.0 %collective-permute-start.21 = (bf16[128,512]{1,0:T(8,128)(2,1)S(1)}, bf16[128,512]{1,0:T(8,128)(2,1)S(1)}, u32[]{:S(2)}, u32[]{:S(2)}) collective-permute-start(bf16[128,512]{1,0:T(8,128)(2,1)S(1)} %collect_terms.3.mine), channel_id=1, source_target_pairs={{0,8},{8,0},{16,24},{24,16},{1,9},{9,1},{17,25},{25,17},{2,10},{10... | collective-permute-start | bytes 393224 | tf_op jit(solution)/shard_map/ppermute | solution.py:452
  58.2 7.3 %collective-permute-start.22 = (bf16[128,512]{1,0:T(8,128)(2,1)S(1)}, bf16[128,512]{1,0:T(8,128)(2,1)S(1)}, u32[]{:S(2)}, u32[]{:S(2)}) collective-permute-start(bf16[128,512]{1,0:T(8,128)(2,1)S(1)} %merge_slabs.3.refs_2_), channel_id=1, source_target_pairs={{0,16},{8,24},{16,0},{24,8},{1,17},{9,25},{17,1},{25,9},{2,18},{10... | collective-permute-start | bytes 393224 | tf_op jit(solution)/shard_map/ppermute | solution.py:452

commit v4 on v3

--- a/solution.py
+++ b/solution.py
@@ -16,7 +16,7 @@
 TN = (((0,), (0,)), ((), ()))
 VMEM_LIMIT = 8 * 1024 * 1024
 SPLIT = 4
-ORDER = (0, 3, 1, 2)
+ORDER = (0, 2, 3, 1)
 
 
 def dot(a, b, dims=(((1,), (0,)), ((), ()))):
@@ -31,30 +31,55 @@
     return pltpu.CompilerParams(vmem_limit_bytes=VMEM_LIMIT + more)
 
 
-def image_of_row(shape, row_dim, image_dim):
-    row = lax.broadcasted_iota(jnp.int32, shape, row_dim)
-    first = lax.broadcasted_iota(jnp.int32, shape, image_dim) * POS
-    return jnp.where((row >= first) & (row < first + POS), 1.0, 0.0).astype(BF)
-
-
-def forward_block(feat, short, convs, pick):
+def tile_iota(width):
+    return lax.broadcasted_iota(jnp.int32, (8, width), 0)
+
+
+def pool_rows(hidden, images):
+    width = hidden.shape[1]
+    row = tile_iota(width)
+    pooled = jnp.zeros((images, width), F32)
+    for i in range(images):
+        first, last = i * POS, i * POS + POS - 1
+        total = jnp.zeros((8, width), F32)
+        for t in range(first // 8, last // 8 + 1):
+            tile = hidden[8 * t : 8 * t + 8]
+            if 8 * t < first:
+                tile = jnp.where(row >= first - 8 * t, tile, 0.0)
+            if 8 * t + 7 > last:
+                tile = jnp.where(row <= last - 8 * t, tile, 0.0)
+            total = total + tile
+        pooled = jnp.where(row == i, jnp.sum(total, axis=0, keepdims=True) / POS, pooled)
+    return pooled
+
+
+def spread_rows(values, images):
+    width = values.shape[1]
+    row = tile_iota(width)
+    whole = [jnp.broadcast_to(values[i : i + 1], (8, width)) for i in range(images)]
+    tiles = []
+    for t in range(images * POS // 8):
+        low, high = 8 * t // POS, (8 * t + 7) // POS
+        tiles.append(whole[low] if low == high else jnp.where(row < high * POS - 8 * t, whole[low], whole[high]))
+    return jnp.concatenate(tiles, axis=0)
+
+
+def forward_block(feat, short, convs, images):
     preact = [dot(feat, conv[...], NT) for conv in convs]
     preact = preact[0] if len(preact) == 1 else jnp.concatenate(preact, axis=1)
     hidden = jnp.maximum(preact + short.astype(F32), 0.0)
     mask = jnp.where(hidden > 0, 1.0, 0.0).astype(BF)
-    pooled = dot(pick, hidden.astype(BF)) / POS
-    return mask, pooled
+    return mask, pool_rows(hidden, images)
 
 
 def forward_blocks(picks, feats, shorts, convs, projs, embed, outs, ready=None):
     images = outs[2].shape[0] // 2
-    pick_rows = image_of_row((images, feats[0].shape[0]), 1, 0)
     for j in range(picks):
         pooled = [None, None]
         for side in (1, 0):
             if ready is not None:
                 ready(j, side)
-            mask, pooled[side] = forward_block(feats[side][...], shorts[2 * j + side][...], convs[j], pick_rows)
+            mask, pooled[side] = forward_block(feats[side][...], shorts[2 * j + side][...], convs[j], images)
             outs[3 * j + side][...] = mask
         pooled = jnp.concatenate(pooled, axis=0).astype(BF)
         outs[3 * j + 2][...] = pooled
@@ -287,22 +312,20 @@
 
 def backward_kernel(blocks, images, part, extra, after, f_own, f_sib, ge_ref, *refs):
     ins, outs = refs[: 4 * blocks], refs[4 * blocks + after :]
-    spread = image_of_row((f_own.shape[0], images), 0, 1)
     mine = ge_ref[0].astype(BF)
     start, rows = part
     width = f_own.shape[1]
+    grad_pool = [dot(mine, ins[4 * j + 3][start : start + rows], NT) / POS for j in range(blocks)]
+    total = jnp.zeros((blocks * rows, width), F32)
+    for side, feat in enumerate((f_own, f_sib)):
+        grad_hidden = []
+        for j in range(blocks):
+            spread = spread_rows(grad_pool[j][side * images : (side + 1) * images], images)
+            grad_hidden.append(spread.astype(BF) * ins[4 * j + side][:, start : start + rows])
+        total = total + dot(jnp.concatenate(grad_hidden, axis=1), feat[...], TN)
     for j in range(blocks):
-        m_own, m_sib, pooled, proj = ins[4 * j : 4 * j + 4]
-        out = outs[j]
-        grad_pool = dot(mine, proj[start : start + rows], NT) / POS
-        total = jnp.zeros((rows, width), F32)
-        for mask, feat, piece in (
-            (m_own, f_own, grad_pool[:images]),
-            (m_sib, f_sib, grad_pool[images:]),
-        ):
-            grad_hidden = dot(spread, piece.astype(BF)).astype(BF) * mask[:, start : start + rows]
-            total = total + dot(grad_hidden, feat[...], TN)
-        out[0:rows] = total.astype(out.dtype)
+        out, pooled = outs[j], ins[4 * j + 2]
+        out[0:rows] = total[j * rows : (j + 1) * rows].astype(out.dtype)
         if extra == "pooled":
             rest = jnp.zeros((2 * images, width - pooled.shape[1]), BF)
             out[rows:] = jnp.concatenate([pooled[...], rest], axis=1)
@@ -497,10 +520,8 @@
     parts = [(0, first_rows), (first_rows, count - first_rows)]
     terms, done = [], ()
     for part, extra in zip(parts, ("pooled", "embed")):
-        far = backward(feats, ge, blocks[-1:], images, part, extra, done)
-        near = backward(feats, ge, blocks[1:-1], images, part, extra, tuple(far))
-        done = tuple(near)
-        terms.append([*near, *far])
+        done = tuple(backward(feats, ge, blocks[1:], images, part, extra, done))
+        terms.append(done)
     (own,) = backward(feats, ge, blocks[:1], images, (0, count), None, done)
 
     pieces, token = [], ()
@@ -516,7 +537,7 @@
                 "proj_grad",
                 *(ge, *pieces, *msgs),
             )
-            token = (token,)
+            token = (pieces[1],)
         piece, bit = total, 1
         while 2 * bit < slabs:
             piece = merge(part[1], piece, swap(piece, "dp", bit), *token)

time: 66.6 us -> 65.5 us (0.983)
  Pallas kernels: 14.8 us -> 11.3 us
  starting transfers between devices: 27.3 us -> 28.6 us
  waiting for transfers between devices: 23.5 us -> 24.7 us
    pallas_call x5 -> x3, Pallas kernels: 4.84 us -> 2.27 us  [backward(): pl.pallas_call(functools.partial(backward_kernel, len(blocks), images, pa...]
    ppermute x23, starting transfers between devices: 27.3 us -> 28.6 us  [swap(): return lax.ppermute(x, axis, [(i, i ^ bit) for i in range(size)])]
    ppermute x23, waiting for transfers between devices: 23.5 us -> 24.7 us  [swap(): return lax.ppermute(x, axis, [(i, i ^ bit) for i in range(size)])]
    pallas_call x3, Pallas kernels: 6.36 us -> 5.42 us  [forward_call(): pl.pallas_call(kernel, in_specs=in_specs, out_specs=[vspec()] * len(shape...]
  transfers between devices with their start and end apart: 23 -> 23, of which waited for: 15 -> 13; matrix products, arithmetic and copies ran while one was open for 0% -> 0% of each run, Pallas kernels for 16% -> 11%
where the time goes in v4:
time: 65.5 us; the launch traced here: 65.4 us
  starting transfers between devices  28.6 us (44%)
  waiting for transfers between devices  24.7 us (38%)
  Pallas kernels  11.3 us (17%)
  between operations  0.75 us (1%)
    ppermute x23, starting transfers between devices, swap(): return lax.ppermute(x, axis, [(i, i ^ bit) for i in range(size)])  28.6 us
    ppermute x23, waiting for transfers between devices, swap(): return lax.ppermute(x, axis, [(i, i ^ bit) for i in range(size)])  24.7 us
    pallas_call x3, Pallas kernels, forward_call(): pl.pallas_call(kernel, in_specs=in_specs, out_specs=[vspec()] * len(shape...  5.42 us
    pallas_call x12, Pallas kernels, small_call(): pl.pallas_call(kernel, in_specs=[vspec()] * len(arrays) + [pl.BlockSpec(m...  2.27 us
    pallas_call x3, Pallas kernels, backward(): pl.pallas_call(functools.partial(backward_kernel, len(blocks), images, pa...  2.27 us
    pallas_call x1, Pallas kernels, hsic(): pl.pallas_call(functools.partial(hsic_kernel, slabs, images, groups), in_...  1.33 us
  transfers between devices with their start and end apart: 23, of which 13 were waited for; matrix products, arithmetic and copies ran while one was open for 0% of the time, Pallas kernels for 11%

profile of v4, /device:TPU:0, one launch (start us, length us, event | category | flops | bytes accessed | tf_op | source)
XLA Modules:
  0.0 65.4 jit_solution(2481784395022960170)
XLA Ops:
  0.6 0.5 collective-permute-start.1
  1.1 0.1 collective-permute-start
  1.2 2.9 %collective-permute-start.3 = (bf16[256,512]{1,0:T(8,128)(2,1)}, bf16[256,512]{1,0:T(8,128)(2,1)S(1)}, u32[]{:S(2)}, u32[]{:S(2)}) collective-permute-start(bf16[256,512]{1,0:T(8,128)(2,1)} %conv.1), channel_id=1, source_target_pairs={{0,4},{1,5},{2,6},{3,7},{4,0},{5,1},{6,2},{7,3},{8,12},{9,13},{10,... | collective-permute-start | bytes 786440 | tf_op jit(solution)/shard_map/ppermute | solution.py:475
  4.2 1.5 %collective-permute-start.2 = (bf16[256,512]{1,0:T(8,128)(2,1)}, bf16[256,512]{1,0:T(8,128)(2,1)S(1)}, u32[]{:S(2)}, u32[]{:S(2)}) collective-permute-start(bf16[256,512]{1,0:T(8,128)(2,1)} %conv.1), channel_id=1, source_target_pairs={{0,2},{1,3},{2,0},{3,1},{4,6},{5,7},{6,4},{7,5},{8,10},{9,11},{10,... | collective-permute-start | bytes 786440 | tf_op jit(solution)/shard_map/ppermute | solution.py:475
  5.7 0.5 collective-permute-start.4
  6.2 0.0 collective-permute-done.f_sib
  6.2 1.4 %collective-permute-start.5 = (bf16[256,256]{1,0:T(8,128)(2,1)}, bf16[256,256]{1,0:T(8,128)(2,1)S(1)}, u32[]{:S(2)}, u32[]{:S(2)}) collective-permute-start(bf16[256,256]{1,0:T(8,128)(2,1)} %proj.1), channel_id=1, source_target_pairs={{0,4},{1,5},{2,6},{3,7},{4,0},{5,1},{6,2},{7,3},{8,12},{9,13},{10,... | collective-permute-start | bytes 393224 | tf_op jit(solution)/shard_map/ppermute | solution.py:475
  7.6 0.0 collective-permute-done.1.s_sib
  7.6 1.6 %collective-permute-start.6 = (bf16[256,256]{1,0:T(8,128)(2,1)}, bf16[256,256]{1,0:T(8,128)(2,1)S(1)}, u32[]{:S(2)}, u32[]{:S(2)}) collective-permute-start(bf16[256,256]{1,0:T(8,128)(2,1)} %proj.1), channel_id=1, source_target_pairs={{0,6},{1,7},{2,4},{3,5},{4,2},{5,3},{6,0},{7,1},{8,14},{9,15},{10,... | collective-permute-start | bytes 393224 | tf_op jit(solution)/shard_map/ppermute | solution.py:475
  9.2 2.0 %forward_first.1 = (bf16[392,256]{1,0:T(8,128)(2,1)S(1)}, bf16[392,256]{1,0:T(8,128)(2,1)S(1)}, bf16[16,256]{1,0:T(8,128)(2,1)S(1)}, f32[16,256]{1,0:T(8,128)S(1...) custom-call(s32[1]{0:T(128)} %bitcast.index_ref, ...), custom_call_target="tpu_custom_call" | custom-call | flops 822083584 | bytes 802816 | tf_op jit(solution)/shard_map/forward_first/pallas_call | solution.py:167
  11.2 0.3 collective-permute-done.3.refs_1_.x
  11.5 2.1 %collective-permute-start.7 = (bf16[128,512]{1,0:T(8,128)(2,1)S(1)}, bf16[128,512]{1,0:T(8,128)(2,1)S(1)}, u32[]{:S(2)}, u32[]{:S(2)}) collective-permute-start(bf16[128,512]{1,0:T(8,128)(2,1)S(1)} %half_of.2), channel_id=1, source_target_pairs={{0,2},{1,3},{2,0},{3,1},{4,6},{5,7},{6,4},{7,5},{8,10},{9,11},{10,... | collective-permute-start | bytes 393224 | tf_op jit(solution)/shard_map/ppermute | solution.py:475
  13.6 0.0 collective-permute-done.2.refs_0_.x
  13.6 1.6 %collective-permute-start.8 = (bf16[128,512]{1,0:T(8,128)(2,1)S(1)}, bf16[128,512]{1,0:T(8,128)(2,1)S(1)}, u32[]{:S(2)}, u32[]{:S(2)}) collective-permute-start(bf16[128,512]{1,0:T(8,128)(2,1)S(1)} %half_of.3), channel_id=1, source_target_pairs={{0,4},{1,5},{2,6},{3,7},{4,0},{5,1},{6,2},{7,3},{8,12},{9,13},{10,... | collective-permute-start | bytes 393224 | tf_op jit(solution)/shard_map/ppermute | solution.py:475
  15.2 1.2 %collective-permute-done.4.refs_2_.refs_3_ = bf16[256,256]{1,0:T(8,128)(2,1)S(1)} collective-permute-done((bf16[256,256]{1,0:T(8,128)(2,1)}, bf16[256,256]{1,0:T(8,128)(2,1)S(1)}, u32[]{:S(2)}, u32[]{:S(2)}) %collective-permute-start.4) | collective-permute-done | bytes 131104 | tf_op jit(solution)/shard_map/ppermute | solution.py:475
  16.4 0.0 collective-permute-done.5.refs_3_.refs_7_
  16.4 2.7 %forward_middle.1 = (bf16[392,256]{1,0:T(8,128)(2,1)S(1)}, bf16[392,256]{1,0:T(8,128)(2,1)S(1)}, bf16[16,256]{1,0:T(8,128)(2,1)S(1)}, bf16[392,256]{1,0:T(8,128)...) custom-call(s32[1]{0:T(128)} %bitcast.index_ref, ...), custom_call_target="tpu_custom_call" | custom-call | flops 1644167168 | bytes 1605632 | tf_op jit(solution)/shard_map/forward_middle/pallas_call | solution.py:167
  19.1 0.0 collective-permute-done.6.proj.refs_11_
  19.1 1.7 %collective-permute-done.7.refs_0_ = bf16[128,512]{1,0:T(8,128)(2,1)S(1)} collective-permute-done((bf16[128,512]{1,0:T(8,128)(2,1)S(1)}, bf16[128,512]{1,0:T(8,128)(2,1)S(1)}, u32[]{:S(2)}, u32[]{:S(2)}) %collective-permute-start.7) | collective-permute-done | bytes 131104 | tf_op jit(solution)/shard_map/ppermute | solution.py:475
  20.8 0.0 collective-permute-done.8.refs_1_
  20.8 0.7 %forward_last.1 = (bf16[392,256]{1,0:T(8,128)(2,1)S(1)}, bf16[392,256]{1,0:T(8,128)(2,1)S(1)}, bf16[16,256]{1,0:T(8,128)(2,1)S(1)}, f32[24,256]{1,0:T(8,128)S(1)}, f32[24,256]{1,0:T(8,128)S(1)}) custom-call(bf16[392,512]{1,0:T(8,128)(2,1)S(1)} %get-tuple-element.33.f_own, bf16[392,512]{1,0:T(8,128)(2,1)S(1)} %collective-permute-done.f_sib, ...), custom_call_target="tpu_custom_call" | custom-call | flops 822083584 | bytes 802816 | tf_op jit(solution)/shard_map/forward_last/pallas_call | solution.py:167
  21.5 0.0 collective-permute-start.9
  21.5 1.2 %collective-permute-done.9.refs_1_ = f32[24,256]{1,0:T(8,128)S(1)} collective-permute-done((f32[24,256]{1,0:T(8,128)S(1)}, f32[24,256]{1,0:T(8,128)S(1)}, u32[]{:S(2)}, u32[]{:S(2)}) %collective-permute-start.9) | collective-permute-done | bytes 24608 | tf_op jit(solution)/shard_map/ppermute | solution.py:475
  22.8 2.6 %collective-permute-start.10 = (f32[24,256]{1,0:T(8,128)S(1)}, f32[24,256]{1,0:T(8,128)S(1)}, u32[]{:S(2)}, u32[]{:S(2)}) collective-permute-start(f32[24,256]{1,0:T(8,128)S(1)} %sum_arrays.1.refs_0_), channel_id=1, source_target_pairs={{0,16},{8,24},{16,0},{24,8},{1,17},{9,25},{17,1},{25,9},{2,18},{10... | collective-permute-start | bytes 73736 | tf_op jit(solution)/shard_map/ppermute | solution.py:475
  25.3 1.3 %collective-permute-start.11 = (f32[24,256]{1,0:T(8,128)S(1)}, f32[24,256]{1,0:T(8,128)S(1)}, u32[]{:S(2)}, u32[]{:S(2)}) collective-permute-start(f32[24,256]{1,0:T(8,128)S(1)} %sum_arrays.1.refs_0_), channel_id=1, source_target_pairs={{0,24},{8,16},{16,8},{24,0},{1,25},{9,17},{17,9},{25,1},{2,26},{10... | collective-permute-start | bytes 73736 | tf_op jit(solution)/shard_map/ppermute | solution.py:475
  26.7 0.2 collective-permute-start.12
  26.9 0.6 collective-permute-done.10.refs_1_
  27.5 3.5 %collective-permute-done.11.refs_2_ = f32[24,256]{1,0:T(8,128)S(1)} collective-permute-done((f32[24,256]{1,0:T(8,128)S(1)}, f32[24,256]{1,0:T(8,128)S(1)}, u32[]{:S(2)}, u32[]{:S(2)}) %collective-permute-start.11) | collective-permute-done | bytes 24608 | tf_op jit(solution)/shard_map/ppermute | solution.py:475
  31.0 0.0 collective-permute-done.12.refs_3_
  31.0 1.3 %hsic_groups.1 = (f32[4,16,256]{2,1,0:T(8,128)S(1)}, f32[1,1]{1,0:T(1,128)}) custom-call(s32[1]{0:T(128)} %bitcast.1.place_ref, f32[24,256]{1,0:T(8,128)S(1)} %sum_arrays.1.refs_0_, f32[24,256]{1,0:T(8,128)S(1)} %collective-permute-done.10.refs_1_, f32[24,256]{1,0:T(8,128)S(1)} %collective-permute-done.11.refs_2_, f32[24,256]{1,0:T(8,128)S(1)} %collective-permute-done.12.refs_3_), custom_call_target="tpu_custom_call" | custom-call | flops 1000000000 | tf_op jit(solution)/shard_map/hsic_groups/pallas_call | solution.py:298
  32.3 0.8 %backward_blocks.3 = (bf16[144,512]{1,0:T(8,128)(2,1)S(1)}, bf16[144,512]{1,0:T(8,128)(2,1)S(1)}, bf16[144,512]{1,0:T(8,128)(2,1)S(1)}) custom-call(bf16[392,512]{1,0:T(8,128)(2,1)S(1)} %get-tuple-element.33.f_own, bf16[392,512]{1,0:T(8,128)(2,1)S(1)} %collective-permute-done.f_sib, f32[4,16,256]{2,1,0:T(8,128)S(1)} %get-tuple-element.41.ge_ref.own_ge, ...), custom_call_target="tpu_custom_call" | custom-call | flops 1233125376 | bytes 602112 | tf_op jit(solution)/shard_map/backward_blocks/pallas_call | solution.py:343
  33.1 1.6 %collective-permute-start.13 = (bf16[144,512]{1,0:T(8,128)(2,1)S(1)}, bf16[144,512]{1,0:T(8,128)(2,1)S(1)}, u32[]{:S(2)}, u32[]{:S(2)}) collective-permute-start(bf16[144,512]{1,0:T(8,128)(2,1)S(1)} %get-tuple-element.55.refs_12_), channel_id=1, source_target_pairs={{0,2},{1,3},{2,0},{3,1},{4,6},{5,7},{6,4},{7,5},{8,10},{9,11},{10,... | collective-permute-start | bytes 442376 | tf_op jit(solution)/shard_map/ppermute | solution.py:475
  34.7 0.5 collective-permute-start.14
  35.2 1.5 %collective-permute-start.15 = (bf16[144,512]{1,0:T(8,128)(2,1)S(1)}, bf16[144,512]{1,0:T(8,128)(2,1)S(1)}, u32[]{:S(2)}, u32[]{:S(2)}) collective-permute-start(bf16[144,512]{1,0:T(8,128)(2,1)S(1)} %get-tuple-element.57.refs_14_), channel_id=1, source_target_pairs={{0,6},{1,7},{2,4},{3,5},{4,2},{5,3},{6,0},{7,1},{8,14},{9,15},{10,... | collective-permute-start | bytes 442376 | tf_op jit(solution)/shard_map/ppermute | solution.py:475
  36.7 0.8 %backward_blocks.4 = (bf16[160,512]{1,0:T(8,128)(2,1)S(1)}, bf16[160,512]{1,0:T(8,128)(2,1)S(1)}, bf16[160,512]{1,0:T(8,128)(2,1)S(1)}) custom-call(bf16[392,512]{1,0:T(8,128)(2,1)S(1)} %get-tuple-element.33.f_own, bf16[392,512]{1,0:T(8,128)(2,1)S(1)} %collective-permute-done.f_sib, f32[4,16,256]{2,1,0:T(8,128)S(1)} %get-tuple-element.41.ge_ref.own_ge, ...), custom_call_target="tpu_custom_call" | custom-call | flops 1233125376 | bytes 602112 | tf_op jit(solution)/shard_map/backward_blocks/pallas_call | solution.py:343
  37.4 0.7 %backward_blocks.5.own = f32[256,512]{1,0:T(8,128)S(1)} custom-call(bf16[392,512]{1,0:T(8,128)(2,1)S(1)} %get-tuple-element.33.f_own, bf16[392,512]{1,0:T(8,128)(2,1)S(1)} %collective-permute-done.f_sib, f32[4,16,256]{2,1,0:T(8,128)S(1)} %get-tuple-element.41.ge_ref.own_ge, bf16[392,256]{1,0:T(8,128)(2,1)S(1)} %get-tuple-element.42.refs_0_, ...), custom_call_target="tpu_custom_call" | custom-call | flops 822083584 | bytes 401408 | tf_op jit(solution)/shard_map/backward_blocks/pallas_call | solution.py:343
  38.1 1.6 %collective-permute-done.13.refs_0_ = bf16[144,512]{1,0:T(8,128)(2,1)S(1)} collective-permute-done((bf16[144,512]{1,0:T(8,128)(2,1)S(1)}, bf16[144,512]{1,0:T(8,128)(2,1)S(1)}, u32[]{:S(2)}, u32[]{:S(2)}) %collective-permute-start.13) | collective-permute-done | bytes 147488 | tf_op jit(solution)/shard_map/ppermute | solution.py:475
  39.7 2.5 %collective-permute-done.14.refs_1_ = bf16[144,512]{1,0:T(8,128)(2,1)S(1)} collective-permute-done((bf16[144,512]{1,0:T(8,128)(2,1)S(1)}, bf16[144,512]{1,0:T(8,128)(2,1)S(1)}, u32[]{:S(2)}, u32[]{:S(2)}) %collective-permute-start.14) | collective-permute-done | bytes 147488 | tf_op jit(solution)/shard_map/ppermute | solution.py:475
  42.3 0.0 collective-permute-done.15.refs_2_
  42.3 0.1 collect_terms.2.mine.token
  42.3 0.1 collective-permute-start.16
  42.5 1.0 %collective-permute-start.20 = (bf16[160,512]{1,0:T(8,128)(2,1)S(1)}, bf16[160,512]{1,0:T(8,128)(2,1)S(1)}, u32[]{:S(2)}, u32[]{:S(2)}) collective-permute-start(bf16[160,512]{1,0:T(8,128)(2,1)S(1)} %gate.5), channel_id=1, source_target_pairs={{0,6},{1,7},{2,4},{3,5},{4,2},{5,3},{6,0},{7,1},{8,14},{9,15},{10,... | collective-permute-start | bytes 491528 | tf_op jit(solution)/shard_map/ppermute | solution.py:475
  43.5 0.8 %collective-permute-start.19 = (bf16[160,512]{1,0:T(8,128)(2,1)S(1)}, bf16[160,512]{1,0:T(8,128)(2,1)S(1)}, u32[]{:S(2)}, u32[]{:S(2)}) collective-permute-start(bf16[160,512]{1,0:T(8,128)(2,1)S(1)} %gate.4), channel_id=1, source_target_pairs={{0,4},{1,5},{2,6},{3,7},{4,0},{5,1},{6,2},{7,3},{8,12},{9,13},{10,... | collective-permute-start | bytes 491528 | tf_op jit(solution)/shard_map/ppermute | solution.py:475
  44.3 1.7 %collective-permute-start.18 = (bf16[160,512]{1,0:T(8,128)(2,1)S(1)}, bf16[160,512]{1,0:T(8,128)(2,1)S(1)}, u32[]{:S(2)}, u32[]{:S(2)}) collective-permute-start(bf16[160,512]{1,0:T(8,128)(2,1)S(1)} %gate.3), channel_id=1, source_target_pairs={{0,2},{1,3},{2,0},{3,1},{4,6},{5,7},{6,4},{7,5},{8,10},{9,11},{10,... | collective-permute-start | bytes 491528 | tf_op jit(solution)/shard_map/ppermute | solution.py:475
  46.0 1.7 %collective-permute-done.16.other = bf16[160,512]{1,0:T(8,128)(2,1)S(1)} collective-permute-done((bf16[160,512]{1,0:T(8,128)(2,1)S(1)}, bf16[160,512]{1,0:T(8,128)(2,1)S(1)}, u32[]{:S(2)}, u32[]{:S(2)}) %collective-permute-start.16) | collective-permute-done | bytes 163872 | tf_op jit(solution)/shard_map/ppermute | solution.py:475
  47.8 1.9 %collective-permute-start.17 = (bf16[192,512]{1,0:T(8,128)(2,1)S(1)}, bf16[192,512]{1,0:T(8,128)(2,1)S(1)}, u32[]{:S(2)}, u32[]{:S(2)}) collective-permute-start(bf16[192,512]{1,0:T(8,128)(2,1)S(1)} %merge_slabs.2.refs_3_.refs_0_.mine), channel_id=1, source_target_pairs={{0,16},{8,24},{16,0},{24,8},{1,17},{9,25},{17,1},{25,9},{2,18},{10... | collective-permute-start | bytes 589832 | tf_op jit(solution)/shard_map/ppermute | solution.py:475
  49.7 0.0 collective-permute-done.20.refs_2_
  49.7 0.9 %collective-permute-done.19.refs_1_ = bf16[160,512]{1,0:T(8,128)(2,1)S(1)} collective-permute-done((bf16[160,512]{1,0:T(8,128)(2,1)S(1)}, bf16[160,512]{1,0:T(8,128)(2,1)S(1)}, u32[]{:S(2)}, u32[]{:S(2)}) %collective-permute-start.19) | collective-permute-done | bytes 163872 | tf_op jit(solution)/shard_map/ppermute | solution.py:475
  50.5 0.4 collective-permute-done.18.refs_0_
  51.0 0.1 collect_terms.3.mine
  51.1 1.8 %collective-permute-start.21 = (bf16[128,512]{1,0:T(8,128)(2,1)S(1)}, bf16[128,512]{1,0:T(8,128)(2,1)S(1)}, u32[]{:S(2)}, u32[]{:S(2)}) collective-permute-start(bf16[128,512]{1,0:T(8,128)(2,1)S(1)} %collect_terms.3.mine), channel_id=1, source_target_pairs={{0,8},{8,0},{16,24},{24,16},{1,9},{9,1},{17,25},{25,17},{2,10},{10... | collective-permute-start | bytes 393224 | tf_op jit(solution)/shard_map/ppermute | solution.py:475
  52.9 4.2 %collective-permute-done.21.other = bf16[128,512]{1,0:T(8,128)(2,1)S(1)} collective-permute-done((bf16[128,512]{1,0:T(8,128)(2,1)S(1)}, bf16[128,512]{1,0:T(8,128)(2,1)S(1)}, u32[]{:S(2)}, u32[]{:S(2)}) %collective-permute-start.21) | collective-permute-done | bytes 131104 | tf_op jit(solution)/shard_map/ppermute | solution.py:475
  57.1 0.0 collective-permute-done.17.refs_0_.refs_1_.other
  57.2 1.3 %collective-permute-start.22 = (bf16[128,512]{1,0:T(8,128)(2,1)S(1)}, bf16[128,512]{1,0:T(8,128)(2,1)S(1)}, u32[]{:S(2)}, u32[]{:S(2)}) collective-permute-start(bf16[128,512]{1,0:T(8,128)(2,1)S(1)} %merge_slabs.3.refs_2_), channel_id=1, source_target_pairs={{0,16},{8,24},{16,0},{24,8},{1,17},{9,25},{17,1},{25,9},{2,18},{10... | collective-permute-start | bytes 393224 | tf_op jit(solution)/shard_map/ppermute | solution.py:475
  58.5 1.2 %proj_grad.1 = (f32[256,256]{1,0:T(8,128)}, f32[8,128]{1,0:T(8,128)}) custom-call(f32[4,16,256]{2,1,0:T(8,128)S(1)} %get-tuple-element.41.ge_ref.own_ge, bf16[192,512]{1,0:T(8,128)(2,1)S(1)} %merge_slabs.2.refs_3_.refs_0_.mine, bf16[192,512]{1,0:T(8,128)(2,1)S(1)} %collective-permute-done.17.refs_0_.refs_1_.other, ...), custom_call_target="tpu_custom_call" | custom-call | tf_op jit(solution)/shard_map/proj_grad/pallas_call | solution.py:359
  59.7 4.8 %collective-permute-done.22.refs_3_ = bf16[128,512]{1,0:T(8,128)(2,1)S(1)} collective-permute-done((bf16[128,512]{1,0:T(8,128)(2,1)S(1)}, bf16[128,512]{1,0:T(8,128)(2,1)S(1)}, u32[]{:S(2)}, u32[]{:S(2)}) %collective-permute-start.22) | collective-permute-done | bytes 131104 | tf_op jit(solution)/shard_map/ppermute | solution.py:475
  64.5 0.8 %sum_slabs.1 = f32[256,512]{1,0:T(8,128)} custom-call(bf16[192,512]{1,0:T(8,128)(2,1)S(1)} %merge_slabs.2.refs_3_.refs_0_.mine, bf16[192,512]{1,0:T(8,128)(2,1)S(1)} %collective-permute-done.17.refs_0_.refs_1_.other, bf16[128,512]{1,0:T(8,128)(2,1)S(1)} %merge_slabs.3.refs_2_, bf16[128,512]{1,0:T(8,128)(2,1)S(1)} %collective-permute-done.22.refs_3_), custom_call_target="tpu_custom_call" | custom-call | tf_op jit(solution)/shard_map/sum_slabs/pallas_call | solution.py:359
  (8 shorter events, 0.1 us)
Async XLA Ops:
  0.6 6.9 %collective-permute-start.1 = (bf16[392,2048]{1,0:T(8,128)(2,1)}, bf16[392,2048]{1,0:T(8,128)(2,1)}, u32[]{:S(2)}, u32[]{:S(2)}) collective-permute-start(bf16[392,2048]{1,0:T(8,128)(2,1)} %s_own.3), channel_id=1, source_target_pairs={{0,1},{1,0},{2,3},{3,2},{4,5},{5,4},{6,7},{7,6},{8,9},{9,8},{10,11... | collective-permute-start | bytes 4816904 | tf_op jit(solution)/shard_map/ppermute | solution.py:475
  1.1 5.1 %collective-permute-start = (bf16[392,512]{1,0:T(8,128)(2,1)}, bf16[392,512]{1,0:T(8,128)(2,1)S(1)}, u32[]{:S(2)}, u32[]{:S(2)}) collective-permute-start(bf16[392,512]{1,0:T(8,128)(2,1)} %f_own.1), channel_id=1, source_target_pairs={{0,1},{1,0},{2,3},{3,2},{4,5},{5,4},{6,7},{7,6},{8,9},{9,8},{10,11... | collective-permute-start | bytes 1204232 | tf_op jit(solution)/shard_map/ppermute | solution.py:475
  1.2 10.3 %collective-permute-start.3 = (bf16[256,512]{1,0:T(8,128)(2,1)}, bf16[256,512]{1,0:T(8,128)(2,1)S(1)}, u32[]{:S(2)}, u32[]{:S(2)}) collective-permute-start(bf16[256,512]{1,0:T(8,128)(2,1)} %conv.1), channel_id=1, source_target_pairs={{0,4},{1,5},{2,6},{3,7},{4,0},{5,1},{6,2},{7,3},{8,12},{9,13},{10,... | collective-permute-start | bytes 786440 | tf_op jit(solution)/shard_map/ppermute | solution.py:475
  4.2 9.4 %collective-permute-start.2 = (bf16[256,512]{1,0:T(8,128)(2,1)}, bf16[256,512]{1,0:T(8,128)(2,1)S(1)}, u32[]{:S(2)}, u32[]{:S(2)}) collective-permute-start(bf16[256,512]{1,0:T(8,128)(2,1)} %conv.1), channel_id=1, source_target_pairs={{0,2},{1,3},{2,0},{3,1},{4,6},{5,7},{6,4},{7,5},{8,10},{9,11},{10,... | collective-permute-start | bytes 786440 | tf_op jit(solution)/shard_map/ppermute | solution.py:475
  5.7 10.7 %collective-permute-start.4 = (bf16[256,256]{1,0:T(8,128)(2,1)}, bf16[256,256]{1,0:T(8,128)(2,1)S(1)}, u32[]{:S(2)}, u32[]{:S(2)}) collective-permute-start(bf16[256,256]{1,0:T(8,128)(2,1)} %proj.1), channel_id=1, source_target_pairs={{0,2},{1,3},{2,0},{3,1},{4,6},{5,7},{6,4},{7,5},{8,10},{9,11},{10,... | collective-permute-start | bytes 393224 | tf_op jit(solution)/shard_map/ppermute | solution.py:475
  6.2 10.2 %collective-permute-start.5 = (bf16[256,256]{1,0:T(8,128)(2,1)}, bf16[256,256]{1,0:T(8,128)(2,1)S(1)}, u32[]{:S(2)}, u32[]{:S(2)}) collective-permute-start(bf16[256,256]{1,0:T(8,128)(2,1)} %proj.1), channel_id=1, source_target_pairs={{0,4},{1,5},{2,6},{3,7},{4,0},{5,1},{6,2},{7,3},{8,12},{9,13},{10,... | collective-permute-start | bytes 393224 | tf_op jit(solution)/shard_map/ppermute | solution.py:475
  7.6 11.5 %collective-permute-start.6 = (bf16[256,256]{1,0:T(8,128)(2,1)}, bf16[256,256]{1,0:T(8,128)(2,1)S(1)}, u32[]{:S(2)}, u32[]{:S(2)}) collective-permute-start(bf16[256,256]{1,0:T(8,128)(2,1)} %proj.1), channel_id=1, source_target_pairs={{0,6},{1,7},{2,4},{3,5},{4,2},{5,3},{6,0},{7,1},{8,14},{9,15},{10,... | collective-permute-start | bytes 393224 | tf_op jit(solution)/shard_map/ppermute | solution.py:475
  11.5 9.3 %collective-permute-start.7 = (bf16[128,512]{1,0:T(8,128)(2,1)S(1)}, bf16[128,512]{1,0:T(8,128)(2,1)S(1)}, u32[]{:S(2)}, u32[]{:S(2)}) collective-permute-start(bf16[128,512]{1,0:T(8,128)(2,1)S(1)} %half_of.2), channel_id=1, source_target_pairs={{0,2},{1,3},{2,0},{3,1},{4,6},{5,7},{6,4},{7,5},{8,10},{9,11},{10,... | collective-permute-start | bytes 393224 | tf_op jit(solution)/shard_map/ppermute | solution.py:475
  13.6 7.2 %collective-permute-start.8 = (bf16[128,512]{1,0:T(8,128)(2,1)S(1)}, bf16[128,512]{1,0:T(8,128)(2,1)S(1)}, u32[]{:S(2)}, u32[]{:S(2)}) collective-permute-start(bf16[128,512]{1,0:T(8,128)(2,1)S(1)} %half_of.3), channel_id=1, source_target_pairs={{0,4},{1,5},{2,6},{3,7},{4,0},{5,1},{6,2},{7,3},{8,12},{9,13},{10,... | collective-permute-start | bytes 393224 | tf_op jit(solution)/shard_map/ppermute | solution.py:475
  21.5 1.2 %collective-permute-start.9 = (f32[24,256]{1,0:T(8,128)S(1)}, f32[24,256]{1,0:T(8,128)S(1)}, u32[]{:S(2)}, u32[]{:S(2)}) collective-permute-start(f32[24,256]{1,0:T(8,128)S(1)} %get-tuple-element.40), channel_id=1, source_target_pairs={{0,1},{1,0},{2,3},{3,2},{4,5},{5,4},{6,7},{7,6},{8,9},{9,8},{10,11... | collective-permute-start | bytes 73736 | tf_op jit(solution)/shard_map/ppermute | solution.py:475
  22.8 4.7 %collective-permute-start.10 = (f32[24,256]{1,0:T(8,128)S(1)}, f32[24,256]{1,0:T(8,128)S(1)}, u32[]{:S(2)}, u32[]{:S(2)}) collective-permute-start(f32[24,256]{1,0:T(8,128)S(1)} %sum_arrays.1.refs_0_), channel_id=1, source_target_pairs={{0,16},{8,24},{16,0},{24,8},{1,17},{9,25},{17,1},{25,9},{2,18},{10... | collective-permute-start | bytes 73736 | tf_op jit(solution)/shard_map/ppermute | solution.py:475
  25.3 5.6 %collective-permute-start.11 = (f32[24,256]{1,0:T(8,128)S(1)}, f32[24,256]{1,0:T(8,128)S(1)}, u32[]{:S(2)}, u32[]{:S(2)}) collective-permute-start(f32[24,256]{1,0:T(8,128)S(1)} %sum_arrays.1.refs_0_), channel_id=1, source_target_pairs={{0,24},{8,16},{16,8},{24,0},{1,25},{9,17},{17,9},{25,1},{2,26},{10... | collective-permute-start | bytes 73736 | tf_op jit(solution)/shard_map/ppermute | solution.py:475
  26.7 4.3 %collective-permute-start.12 = (f32[24,256]{1,0:T(8,128)S(1)}, f32[24,256]{1,0:T(8,128)S(1)}, u32[]{:S(2)}, u32[]{:S(2)}) collective-permute-start(f32[24,256]{1,0:T(8,128)S(1)} %sum_arrays.1.refs_0_), channel_id=1, source_target_pairs={{0,8},{8,0},{16,24},{24,16},{1,9},{9,1},{17,25},{25,17},{2,10},{10... | collective-permute-start | bytes 73736 | tf_op jit(solution)/shard_map/ppermute | solution.py:475
  33.1 6.6 %collective-permute-start.13 = (bf16[144,512]{1,0:T(8,128)(2,1)S(1)}, bf16[144,512]{1,0:T(8,128)(2,1)S(1)}, u32[]{:S(2)}, u32[]{:S(2)}) collective-permute-start(bf16[144,512]{1,0:T(8,128)(2,1)S(1)} %get-tuple-element.55.refs_12_), channel_id=1, source_target_pairs={{0,2},{1,3},{2,0},{3,1},{4,6},{5,7},{6,4},{7,5},{8,10},{9,11},{10,... | collective-permute-start | bytes 442376 | tf_op jit(solution)/shard_map/ppermute | solution.py:475
  34.7 7.6 %collective-permute-start.14 = (bf16[144,512]{1,0:T(8,128)(2,1)S(1)}, bf16[144,512]{1,0:T(8,128)(2,1)S(1)}, u32[]{:S(2)}, u32[]{:S(2)}) collective-permute-start(bf16[144,512]{1,0:T(8,128)(2,1)S(1)} %get-tuple-element.56.refs_13_), channel_id=1, source_target_pairs={{0,4},{1,5},{2,6},{3,7},{4,0},{5,1},{6,2},{7,3},{8,12},{9,13},{10,... | collective-permute-start | bytes 442376 | tf_op jit(solution)/shard_map/ppermute | solution.py:475
  35.2 7.1 %collective-permute-start.15 = (bf16[144,512]{1,0:T(8,128)(2,1)S(1)}, bf16[144,512]{1,0:T(8,128)(2,1)S(1)}, u32[]{:S(2)}, u32[]{:S(2)}) collective-permute-start(bf16[144,512]{1,0:T(8,128)(2,1)S(1)} %get-tuple-element.57.refs_14_), channel_id=1, source_target_pairs={{0,6},{1,7},{2,4},{3,5},{4,2},{5,3},{6,0},{7,1},{8,14},{9,15},{10,... | collective-permute-start | bytes 442376 | tf_op jit(solution)/shard_map/ppermute | solution.py:475
  42.3 5.4 %collective-permute-start.16 = (bf16[160,512]{1,0:T(8,128)(2,1)S(1)}, bf16[160,512]{1,0:T(8,128)(2,1)S(1)}, u32[]{:S(2)}, u32[]{:S(2)}) collective-permute-start(bf16[160,512]{1,0:T(8,128)(2,1)S(1)} %collect_terms.2.mine.token), channel_id=1, source_target_pairs={{0,8},{8,0},{16,24},{24,16},{1,9},{9,1},{17,25},{25,17},{2,10},{10... | collective-permute-start | bytes 491528 | tf_op jit(solution)/shard_map/ppermute | solution.py:475
  42.5 7.2 %collective-permute-start.20 = (bf16[160,512]{1,0:T(8,128)(2,1)S(1)}, bf16[160,512]{1,0:T(8,128)(2,1)S(1)}, u32[]{:S(2)}, u32[]{:S(2)}) collective-permute-start(bf16[160,512]{1,0:T(8,128)(2,1)S(1)} %gate.5), channel_id=1, source_target_pairs={{0,6},{1,7},{2,4},{3,5},{4,2},{5,3},{6,0},{7,1},{8,14},{9,15},{10,... | collective-permute-start | bytes 491528 | tf_op jit(solution)/shard_map/ppermute | solution.py:475
  43.5 7.1 %collective-permute-start.19 = (bf16[160,512]{1,0:T(8,128)(2,1)S(1)}, bf16[160,512]{1,0:T(8,128)(2,1)S(1)}, u32[]{:S(2)}, u32[]{:S(2)}) collective-permute-start(bf16[160,512]{1,0:T(8,128)(2,1)S(1)} %gate.4), channel_id=1, source_target_pairs={{0,4},{1,5},{2,6},{3,7},{4,0},{5,1},{6,2},{7,3},{8,12},{9,13},{10,... | collective-permute-start | bytes 491528 | tf_op jit(solution)/shard_map/ppermute | solution.py:475
  44.3 6.7 %collective-permute-start.18 = (bf16[160,512]{1,0:T(8,128)(2,1)S(1)}, bf16[160,512]{1,0:T(8,128)(2,1)S(1)}, u32[]{:S(2)}, u32[]{:S(2)}) collective-permute-start(bf16[160,512]{1,0:T(8,128)(2,1)S(1)} %gate.3), channel_id=1, source_target_pairs={{0,2},{1,3},{2,0},{3,1},{4,6},{5,7},{6,4},{7,5},{8,10},{9,11},{10,... | collective-permute-start | bytes 491528 | tf_op jit(solution)/shard_map/ppermute | solution.py:475
  47.8 9.4 %collective-permute-start.17 = (bf16[192,512]{1,0:T(8,128)(2,1)S(1)}, bf16[192,512]{1,0:T(8,128)(2,1)S(1)}, u32[]{:S(2)}, u32[]{:S(2)}) collective-permute-start(bf16[192,512]{1,0:T(8,128)(2,1)S(1)} %merge_slabs.2.refs_3_.refs_0_.mine), channel_id=1, source_target_pairs={{0,16},{8,24},{16,0},{24,8},{1,17},{9,25},{17,1},{25,9},{2,18},{10... | collective-permute-start | bytes 589832 | tf_op jit(solution)/shard_map/ppermute | solution.py:475
  51.1 6.1 %collective-permute-start.21 = (bf16[128,512]{1,0:T(8,128)(2,1)S(1)}, bf16[128,512]{1,0:T(8,128)(2,1)S(1)}, u32[]{:S(2)}, u32[]{:S(2)}) collective-permute-start(bf16[128,512]{1,0:T(8,128)(2,1)S(1)} %collect_terms.3.mine), channel_id=1, source_target_pairs={{0,8},{8,0},{16,24},{24,16},{1,9},{9,1},{17,25},{25,17},{2,10},{10... | collective-permute-start | bytes 393224 | tf_op jit(solution)/shard_map/ppermute | solution.py:475
  57.2 7.3 %collective-permute-start.22 = (bf16[128,512]{1,0:T(8,128)(2,1)S(1)}, bf16[128,512]{1,0:T(8,128)(2,1)S(1)}, u32[]{:S(2)}, u32[]{:S(2)}) collective-permute-start(bf16[128,512]{1,0:T(8,128)(2,1)S(1)} %merge_slabs.3.refs_2_), channel_id=1, source_target_pairs={{0,16},{8,24},{16,0},{24,8},{1,17},{9,25},{17,1},{25,9},{2,18},{10... | collective-permute-start | bytes 393224 | tf_op jit(solution)/shard_map/ppermute | solution.py:475

commit v5 on v4

--- a/solution.py
+++ b/solution.py
@@ -271,9 +271,10 @@
 
 
 def hsic_kernel(slabs, images, groups, place_ref, *refs):
-    chunks = refs[:-5]
-    ge_ref, loss_ref, z_ref, p_ref, g_ref = refs[-5:]
+    chunks = refs[:-6]
+    ge_ref, loss_ref, odd_ref, z_ref, p_ref, g_ref = refs[-6:]
     place = place_ref[0]
+    odd_ref[...] = jnp.full(odd_ref.shape, (place & 1).astype(F32))
     half = z_ref.shape[2] // 2
     for j in range(slabs):
         block = chunks[0].at[j] if len(chunks) == 1 else chunks[ORDER.index(j)]
@@ -298,10 +299,11 @@
     return pl.pallas_call(
         functools.partial(hsic_kernel, slabs, images, groups),
         in_specs=[pl.BlockSpec(memory_space=pltpu.SMEM)] + [vspec()] * len(chunks),
-        out_specs=[vspec()] * 2,
+        out_specs=[vspec()] * 3,
         out_shape=[
             jax.ShapeDtypeStruct((slabs, 2 * images, embed), F32),
             jax.ShapeDtypeStruct((1, 1), F32),
+            jax.ShapeDtypeStruct((8, 128), F32),
         ],
         scratch_shapes=[pltpu.VMEM((2, slabs * images, width), F32) for width in (embed, 128, embed)],
         compiler_params=params(80 * (slabs * images) ** 2),
@@ -417,17 +419,85 @@
     return small_call(functools.partial(merge_kernel, rows), [(shape, BF)], "merge_slabs", mine, other, tokens=token)[0]
 
 
-def final_kernel(*refs):
-    pieces, out = refs[:-1], refs[-1]
+def choose(odd, width):
+    return jnp.broadcast_to(odd[0:1, 0:1], (1, width)) > 0.5
+
+
+def collect_halves_kernel(start, rows, own, pooled, odd, *refs):
+    msgs, (keep, send, slab_ref) = refs[:-3], refs[-3:]
+    width, half = own.shape[1], rows // 2
+    total = own[start : start + rows]
+    for msg in msgs:
+        total = total + msg[0:rows].astype(F32)
+    total = total.astype(BF).astype(F32)
+    pick = choose(odd, width)
+    keep[...] = jnp.where(pick, total[half:], total[:half]).astype(BF)
+    send[...] = jnp.where(pick, total[:half], total[half:]).astype(BF)
+    high, count = pooled.shape
+    slab = [pooled[...]] + [msg[rows : rows + high, 0:count] for msg in msgs]
+    tall = slab_ref.shape[0] // high
+    for k, piece in enumerate(slab):
+        at = k % tall * high
+        slab_ref[at : at + high, k // tall * count : (k // tall + 1) * count] = piece
+
+
+def add_and_append_kernel(rows, count, mine, other, *refs):
+    more, out = refs[:count], refs[-1]
+    out[0:rows] = (mine[0:rows].astype(F32) + other[0:rows].astype(F32)).astype(BF)
+    at = rows
+    for ref in more:
+        tail = ref[...] if ref.shape[0] < rows else ref[rows:]
+        out[at : at + tail.shape[0]] = tail
+        at += tail.shape[0]
+
+
+def sum_by_halves(own, pooled, odd, msgs, part, token, late):
+    start, rows = part
+    width, half = own.shape[1], rows // 2
+    slab_rows = (len(msgs) + 1) * pooled.size // width
+    keep, send, slab = small_call(
+        functools.partial(collect_halves_kernel, start, rows),
+        [((half, width), BF), ((half, width), BF), ((slab_rows, width), BF)],
+        "collect_terms",
+        *(own, pooled, odd, *msgs),
+    )
+    first = small_call(
+        functools.partial(add_and_append_kernel, half, 1),
+        [((half + slab_rows, width), BF)],
+        "merge_slabs",
+        *(keep, swap(send, "dp", 1), slab),
+        tokens=token,
+    )[0]
+    far = swap(first, "dp", 2)
+    mine = small_call(
+        functools.partial(add_and_append_kernel, half, 2),
+        [((half + 2 * slab_rows, width), BF)],
+        "merge_slabs",
+        *(first, far, first, far),
+        tokens=late,
+    )[0]
+    return mine, swap(mine, "dp", 1)
+
+
+def final_halves(odd, mine, other, pieces, out):
+    tail = pieces[0].shape[0]
+    head = out.shape[0] - tail
+    half = head // 2
+    pick = choose(odd, out.shape[1])
+    left, right = mine[0:half].astype(F32), other[0:half].astype(F32)
+    out[0:half] = jnp.where(pick, right, left)
+    out[half:head] = jnp.where(pick, left, right)
+    out[head:] = pieces[0][...].astype(F32) + pieces[1][...].astype(F32)
+
+
+def final_whole(pieces, out):
     tail = pieces[2].shape[0]
     head = out.shape[0] - tail
     out[0:head] = pieces[0][0:head].astype(F32) + pieces[1][0:head].astype(F32)
     out[head:] = pieces[2][...].astype(F32) + pieces[3][...].astype(F32)
 
 
-def proj_kernel(slabs, images, rows, msg_rows, own_ge, mine, other, *refs):
-    msgs, (out, token) = refs[:-2], refs[-2:]
-    token[...] = jnp.zeros(token.shape, F32)
+def proj_sum(slabs, images, order, rows, msg_rows, own_ge, mine, other, msgs, out):
     count, embed = out.shape
     groups = mine.shape[1] // count
     half = slabs * images
@@ -441,7 +511,8 @@
             start, left = start - half, embed
         for msg in msgs:
             pieces.append(msg[msg_rows + start : msg_rows + start + 2 * images, left : left + embed])
-        ref, at = (mine, j) if j < slabs // 2 else (other, j - slabs // 2)
+        at = order.index(j)
+        ref, at = (mine, at) if at < slabs // 2 else (other, at - slabs // 2)
         total = jnp.zeros((count, embed), F32)
         for g in range(groups):
             pooled = ref[rows + at * per : rows + (at + 1) * per, g * count : (g + 1) * count]
@@ -468,6 +539,15 @@
 def half_of(start, x, token):
     shape = (x.shape[0] // 2, x.shape[1])
     return small_call(functools.partial(part_kernel, start), [(shape, x.dtype)], "half_of", x, tokens=(token,))[0]
+
+
+def last_sums_kernel(slabs, images, order, rows, msg_rows, own_ge, odd, last_mine, last_other, mine, other, *refs):
+    msgs, (conv_out, proj_out) = refs[:-2], refs[-2:]
+    proj_sum(slabs, images, order, rows, msg_rows, own_ge, mine, other, msgs, proj_out)
+    if slabs == 4:
+        final_halves(odd, mine, other, (last_mine, last_other), conv_out)
+    else:
+        final_whole((mine, other, last_mine, last_other), conv_out)
 
 
 def swap(x, axis, bit):
@@ -514,7 +594,7 @@
     blocks, projs = [first, *middle, last], [proj_own, *projs]
     blocks = [(*b, p) for b, p in zip(blocks, projs)]
     embeds = sum_of(F32, mine, swap(send, "fsdp", 1))
-    ge, loss = hsic(place, gather_slabs(embeds, slabs), slabs, images, groups)
+    ge, loss, odd = hsic(place, gather_slabs(embeds, slabs), slabs, images, groups)
 
     first_rows = count * SPLIT // 8
     parts = [(0, first_rows), (first_rows, count - first_rows)]
@@ -524,27 +604,26 @@
         terms.append(done)
     (own,) = backward(feats, ge, blocks[:1], images, (0, count), None, done)
 
-    pieces, token = [], ()
-    for k, part in enumerate(parts):
-        if k:
-            terms[k] = [after(m, total) for m in terms[k]]
-        msgs = [swap(m, "fsdp", 2 * j) for j, m in enumerate(terms[k], 1)]
-        total = collect(own, blocks[0][2], msgs, part, k == 0, pieces[:1])
-        if k:
-            grad_proj, token = small_call(
-                functools.partial(proj_kernel, slabs, images, parts[0][1], part[1]),
-                [(proj_weight.shape, F32), ((8, 128), F32)],
-                "proj_grad",
-                *(ge, *pieces, *msgs),
-            )
-            token = (pieces[1],)
-        piece, bit = total, 1
-        while 2 * bit < slabs:
-            piece = merge(part[1], piece, swap(piece, "dp", bit), *token)
-            bit *= 2
-        pieces += [piece, swap(piece, "dp", bit)]
-    (grad_conv,) = small_call(
-        final_kernel, [((count, width), F32)], "sum_slabs", *pieces
+    received = [[swap(m, "fsdp", 2 * j) for j, m in enumerate(term, 1)] for term in terms]
+    total = collect(own, blocks[0][2], received[1], parts[1], False, ())
+    if slabs == 4:
+        merged = merge(parts[1][1], total, swap(total, "dp", 1))
+        mine, other = sum_by_halves(own, blocks[0][2], odd, received[0], parts[0], (), (merged,))
+        pieces = [mine, other, merged, swap(merged, "dp", 2)]
+        order, above = [0, 2, 1, 3], parts[0][1] // 2
+    else:
+        pieces, order, above = [], list(range(slabs)), parts[0][1]
+        for piece, part in zip((collect(own, blocks[0][2], received[0], parts[0], True, ()), total), parts):
+            bit = 1
+            while 2 * bit < slabs:
+                piece = merge(part[1], piece, swap(piece, "dp", bit))
+                bit *= 2
+            pieces += [piece, swap(piece, "dp", bit)]
+    grad_conv, grad_proj = small_call(
+        functools.partial(last_sums_kernel, slabs, images, order, above, parts[1][1]),
+        [((count, width), F32), (proj_weight.shape, F32)],
+        "last_sums",
+        *(ge, odd, pieces[2], pieces[3], pieces[0], pieces[1], *received[1]),
     )
     return grad_conv, grad_proj, loss.reshape(1)
 

time: 65.5 us -> 64.5 us (0.985)
  waiting for transfers between devices: 24.7 us -> 23.6 us
  starting transfers between devices: 28.6 us -> 29.4 us
  Pallas kernels: 11.3 us -> 10.6 us
    ppermute x23 -> x24, waiting for transfers between devices: 24.7 us -> 23.6 us  [swap(): return lax.ppermute(x, axis, [(i, i ^ bit) for i in range(size)])]
    ppermute x23 -> x24, starting transfers between devices: 28.6 us -> 29.4 us  [swap(): return lax.ppermute(x, axis, [(i, i ^ bit) for i in range(size)])]
    pallas_call x12 -> x9, Pallas kernels: 2.27 us -> 1.62 us  [small_call(): pl.pallas_call(kernel, in_specs=[vspec()] * len(arrays) + [pl.BlockSpec(m...]
  transfers between devices with their start and end apart: 23 -> 24, of which waited for: 13 -> 13; matrix products, arithmetic and copies ran while one was open for 0% -> 0% of each run, Pallas kernels for 11% -> 10%
where the time goes in v5:
time: 64.5 us; the launch traced here: 64.3 us
  starting transfers between devices  29.4 us (46%)
  waiting for transfers between devices  23.6 us (37%)
  Pallas kernels  10.6 us (16%)
  between operations  0.77 us (1%)
    ppermute x24, starting transfers between devices, swap(): return lax.ppermute(x, axis, [(i, i ^ bit) for i in range(size)])  29.4 us
    ppermute x24, waiting for transfers between devices, swap(): return lax.ppermute(x, axis, [(i, i ^ bit) for i in range(size)])  23.6 us
    pallas_call x3, Pallas kernels, forward_call(): pl.pallas_call(kernel, in_specs=in_specs, out_specs=[vspec()] * len(shape...  5.42 us
    pallas_call x3, Pallas kernels, backward(): pl.pallas_call(functools.partial(backward_kernel, len(blocks), images, pa...  2.27 us
    pallas_call x9, Pallas kernels, small_call(): pl.pallas_call(kernel, in_specs=[vspec()] * len(arrays) + [pl.BlockSpec(m...  1.62 us
    pallas_call x1, Pallas kernels, hsic(): pl.pallas_call(functools.partial(hsic_kernel, slabs, images, groups), in_...  1.33 us
  transfers between devices with their start and end apart: 24, of which 13 were waited for; matrix products, arithmetic and copies ran while one was open for 0% of the time, Pallas kernels for 10%

profile of v5, /device:TPU:0, one launch (start us, length us, event | category | flops | bytes accessed | tf_op | source)
XLA Modules:
  0.0 64.3 jit_solution(2896483178580653365)
XLA Ops:
  0.6 0.5 collective-permute-start.1
  1.1 0.1 collective-permute-start
  1.2 2.9 %collective-permute-start.3 = (bf16[256,512]{1,0:T(8,128)(2,1)}, bf16[256,512]{1,0:T(8,128)(2,1)S(1)}, u32[]{:S(2)}, u32[]{:S(2)}) collective-permute-start(bf16[256,512]{1,0:T(8,128)(2,1)} %conv.1), channel_id=1, source_target_pairs={{0,4},{1,5},{2,6},{3,7},{4,0},{5,1},{6,2},{7,3},{8,12},{9,13},{10,... | collective-permute-start | bytes 786440 | tf_op jit(solution)/shard_map/ppermute | solution.py:555
  4.2 1.5 %collective-permute-start.2 = (bf16[256,512]{1,0:T(8,128)(2,1)}, bf16[256,512]{1,0:T(8,128)(2,1)S(1)}, u32[]{:S(2)}, u32[]{:S(2)}) collective-permute-start(bf16[256,512]{1,0:T(8,128)(2,1)} %conv.1), channel_id=1, source_target_pairs={{0,2},{1,3},{2,0},{3,1},{4,6},{5,7},{6,4},{7,5},{8,10},{9,11},{10,... | collective-permute-start | bytes 786440 | tf_op jit(solution)/shard_map/ppermute | solution.py:555
  5.7 0.5 collective-permute-start.4
  6.2 0.0 collective-permute-done.f_sib
  6.2 1.4 %collective-permute-start.5 = (bf16[256,256]{1,0:T(8,128)(2,1)}, bf16[256,256]{1,0:T(8,128)(2,1)S(1)}, u32[]{:S(2)}, u32[]{:S(2)}) collective-permute-start(bf16[256,256]{1,0:T(8,128)(2,1)} %proj.1), channel_id=1, source_target_pairs={{0,4},{1,5},{2,6},{3,7},{4,0},{5,1},{6,2},{7,3},{8,12},{9,13},{10,... | collective-permute-start | bytes 393224 | tf_op jit(solution)/shard_map/ppermute | solution.py:555
  7.6 0.0 collective-permute-done.1.s_sib
  7.6 1.6 %collective-permute-start.6 = (bf16[256,256]{1,0:T(8,128)(2,1)}, bf16[256,256]{1,0:T(8,128)(2,1)S(1)}, u32[]{:S(2)}, u32[]{:S(2)}) collective-permute-start(bf16[256,256]{1,0:T(8,128)(2,1)} %proj.1), channel_id=1, source_target_pairs={{0,6},{1,7},{2,4},{3,5},{4,2},{5,3},{6,0},{7,1},{8,14},{9,15},{10,... | collective-permute-start | bytes 393224 | tf_op jit(solution)/shard_map/ppermute | solution.py:555
  9.2 2.0 %forward_first.1 = (bf16[392,256]{1,0:T(8,128)(2,1)S(1)}, bf16[392,256]{1,0:T(8,128)(2,1)S(1)}, bf16[16,256]{1,0:T(8,128)(2,1)S(1)}, f32[16,256]{1,0:T(8,128)S(1...) custom-call(s32[1]{0:T(128)} %bitcast.1.index_ref, ...), custom_call_target="tpu_custom_call" | custom-call | flops 822083584 | bytes 802816 | tf_op jit(solution)/shard_map/forward_first/pallas_call | solution.py:167
  11.2 0.3 collective-permute-done.3.refs_1_.x
  11.5 2.1 %collective-permute-start.7 = (bf16[128,512]{1,0:T(8,128)(2,1)S(1)}, bf16[128,512]{1,0:T(8,128)(2,1)S(1)}, u32[]{:S(2)}, u32[]{:S(2)}) collective-permute-start(bf16[128,512]{1,0:T(8,128)(2,1)S(1)} %half_of.2), channel_id=1, source_target_pairs={{0,2},{1,3},{2,0},{3,1},{4,6},{5,7},{6,4},{7,5},{8,10},{9,11},{10,... | collective-permute-start | bytes 393224 | tf_op jit(solution)/shard_map/ppermute | solution.py:555
  13.6 0.0 collective-permute-done.2.refs_0_.x
  13.6 1.6 %collective-permute-start.8 = (bf16[128,512]{1,0:T(8,128)(2,1)S(1)}, bf16[128,512]{1,0:T(8,128)(2,1)S(1)}, u32[]{:S(2)}, u32[]{:S(2)}) collective-permute-start(bf16[128,512]{1,0:T(8,128)(2,1)S(1)} %half_of.3), channel_id=1, source_target_pairs={{0,4},{1,5},{2,6},{3,7},{4,0},{5,1},{6,2},{7,3},{8,12},{9,13},{10,... | collective-permute-start | bytes 393224 | tf_op jit(solution)/shard_map/ppermute | solution.py:555
  15.2 1.2 %collective-permute-done.4.refs_2_.refs_3_ = bf16[256,256]{1,0:T(8,128)(2,1)S(1)} collective-permute-done((bf16[256,256]{1,0:T(8,128)(2,1)}, bf16[256,256]{1,0:T(8,128)(2,1)S(1)}, u32[]{:S(2)}, u32[]{:S(2)}) %collective-permute-start.4) | collective-permute-done | bytes 131104 | tf_op jit(solution)/shard_map/ppermute | solution.py:555
  16.4 0.0 collective-permute-done.5.refs_3_.refs_7_
  16.4 2.7 %forward_middle.1 = (bf16[392,256]{1,0:T(8,128)(2,1)S(1)}, bf16[392,256]{1,0:T(8,128)(2,1)S(1)}, bf16[16,256]{1,0:T(8,128)(2,1)S(1)}, bf16[392,256]{1,0:T(8,128)...) custom-call(s32[1]{0:T(128)} %bitcast.1.index_ref, ...), custom_call_target="tpu_custom_call" | custom-call | flops 1644167168 | bytes 1605632 | tf_op jit(solution)/shard_map/forward_middle/pallas_call | solution.py:167
  19.1 0.0 collective-permute-done.6.proj.refs_11_
  19.1 1.7 %collective-permute-done.7.refs_0_ = bf16[128,512]{1,0:T(8,128)(2,1)S(1)} collective-permute-done((bf16[128,512]{1,0:T(8,128)(2,1)S(1)}, bf16[128,512]{1,0:T(8,128)(2,1)S(1)}, u32[]{:S(2)}, u32[]{:S(2)}) %collective-permute-start.7) | collective-permute-done | bytes 131104 | tf_op jit(solution)/shard_map/ppermute | solution.py:555
  20.8 0.0 collective-permute-done.8.refs_1_
  20.8 0.7 %forward_last.1 = (bf16[392,256]{1,0:T(8,128)(2,1)S(1)}, bf16[392,256]{1,0:T(8,128)(2,1)S(1)}, bf16[16,256]{1,0:T(8,128)(2,1)S(1)}, f32[24,256]{1,0:T(8,128)S(1)}, f32[24,256]{1,0:T(8,128)S(1)}) custom-call(bf16[392,512]{1,0:T(8,128)(2,1)S(1)} %get-tuple-element.38.f_own, bf16[392,512]{1,0:T(8,128)(2,1)S(1)} %collective-permute-done.f_sib, ...), custom_call_target="tpu_custom_call" | custom-call | flops 822083584 | bytes 802816 | tf_op jit(solution)/shard_map/forward_last/pallas_call | solution.py:167
  21.5 0.0 collective-permute-start.9
  21.5 1.2 %collective-permute-done.9.refs_1_ = f32[24,256]{1,0:T(8,128)S(1)} collective-permute-done((f32[24,256]{1,0:T(8,128)S(1)}, f32[24,256]{1,0:T(8,128)S(1)}, u32[]{:S(2)}, u32[]{:S(2)}) %collective-permute-start.9) | collective-permute-done | bytes 24608 | tf_op jit(solution)/shard_map/ppermute | solution.py:555
  22.8 2.6 %collective-permute-start.10 = (f32[24,256]{1,0:T(8,128)S(1)}, f32[24,256]{1,0:T(8,128)S(1)}, u32[]{:S(2)}, u32[]{:S(2)}) collective-permute-start(f32[24,256]{1,0:T(8,128)S(1)} %sum_arrays.1.refs_0_), channel_id=1, source_target_pairs={{0,16},{8,24},{16,0},{24,8},{1,17},{9,25},{17,1},{25,9},{2,18},{10... | collective-permute-start | bytes 73736 | tf_op jit(solution)/shard_map/ppermute | solution.py:555
  25.3 1.3 %collective-permute-start.11 = (f32[24,256]{1,0:T(8,128)S(1)}, f32[24,256]{1,0:T(8,128)S(1)}, u32[]{:S(2)}, u32[]{:S(2)}) collective-permute-start(f32[24,256]{1,0:T(8,128)S(1)} %sum_arrays.1.refs_0_), channel_id=1, source_target_pairs={{0,24},{8,16},{16,8},{24,0},{1,25},{9,17},{17,9},{25,1},{2,26},{10... | collective-permute-start | bytes 73736 | tf_op jit(solution)/shard_map/ppermute | solution.py:555
  26.7 0.2 collective-permute-start.12
  26.9 0.6 collective-permute-done.10.refs_1_
  27.5 3.5 %collective-permute-done.11.refs_2_ = f32[24,256]{1,0:T(8,128)S(1)} collective-permute-done((f32[24,256]{1,0:T(8,128)S(1)}, f32[24,256]{1,0:T(8,128)S(1)}, u32[]{:S(2)}, u32[]{:S(2)}) %collective-permute-start.11) | collective-permute-done | bytes 24608 | tf_op jit(solution)/shard_map/ppermute | solution.py:555
  31.0 0.0 collective-permute-done.12.refs_3_
  31.0 1.3 %hsic_groups.1 = (f32[4,16,256]{2,1,0:T(8,128)S(1)}, f32[1,1]{1,0:T(1,128)}, f32[8,128]{1,0:T(8,128)S(1)}) custom-call(s32[1]{0:T(128)} %bitcast.place_ref, f32[24,256]{1,0:T(8,128)S(1)} %sum_arrays.1.refs_0_, f32[24,256]{1,0:T(8,128)S(1)} %collective-permute-done.10.refs_1_, f32[24,256]{1,0:T(8,128)S(1)} %collective-permute-done.11.refs_2_, ...), custom_call_target="tpu_custom_call" | custom-call | flops 1000000000 | tf_op jit(solution)/shard_map/hsic_groups/pallas_call | solution.py:299
  32.3 0.8 %backward_blocks.3 = (bf16[144,512]{1,0:T(8,128)(2,1)S(1)}, bf16[144,512]{1,0:T(8,128)(2,1)S(1)}, bf16[144,512]{1,0:T(8,128)(2,1)S(1)}) custom-call(bf16[392,512]{1,0:T(8,128)(2,1)S(1)} %get-tuple-element.38.f_own, bf16[392,512]{1,0:T(8,128)(2,1)S(1)} %collective-permute-done.f_sib, f32[4,16,256]{2,1,0:T(8,128)S(1)} %get-tuple-element.46.ge_ref.own_ge, ...), custom_call_target="tpu_custom_call" | custom-call | flops 1233125376 | bytes 602112 | tf_op jit(solution)/shard_map/backward_blocks/pallas_call | solution.py:345
  33.1 1.6 %collective-permute-start.18 = (bf16[144,512]{1,0:T(8,128)(2,1)S(1)}, bf16[144,512]{1,0:T(8,128)(2,1)S(1)}, u32[]{:S(2)}, u32[]{:S(2)}) collective-permute-start(bf16[144,512]{1,0:T(8,128)(2,1)S(1)} %get-tuple-element.61.refs_12_), channel_id=1, source_target_pairs={{0,2},{1,3},{2,0},{3,1},{4,6},{5,7},{6,4},{7,5},{8,10},{9,11},{10,... | collective-permute-start | bytes 442376 | tf_op jit(solution)/shard_map/ppermute | solution.py:555
  34.7 0.5 collective-permute-start.19
  35.2 1.5 %collective-permute-start.20 = (bf16[144,512]{1,0:T(8,128)(2,1)S(1)}, bf16[144,512]{1,0:T(8,128)(2,1)S(1)}, u32[]{:S(2)}, u32[]{:S(2)}) collective-permute-start(bf16[144,512]{1,0:T(8,128)(2,1)S(1)} %get-tuple-element.63.refs_14_), channel_id=1, source_target_pairs={{0,6},{1,7},{2,4},{3,5},{4,2},{5,3},{6,0},{7,1},{8,14},{9,15},{10,... | collective-permute-start | bytes 442376 | tf_op jit(solution)/shard_map/ppermute | solution.py:555
  36.7 0.8 %backward_blocks.4 = (bf16[160,512]{1,0:T(8,128)(2,1)S(1)}, bf16[160,512]{1,0:T(8,128)(2,1)S(1)}, bf16[160,512]{1,0:T(8,128)(2,1)S(1)}) custom-call(bf16[392,512]{1,0:T(8,128)(2,1)S(1)} %get-tuple-element.38.f_own, bf16[392,512]{1,0:T(8,128)(2,1)S(1)} %collective-permute-done.f_sib, f32[4,16,256]{2,1,0:T(8,128)S(1)} %get-tuple-element.46.ge_ref.own_ge, ...), custom_call_target="tpu_custom_call" | custom-call | flops 1233125376 | bytes 602112 | tf_op jit(solution)/shard_map/backward_blocks/pallas_call | solution.py:345
  37.4 1.6 %collective-permute-start.13 = (bf16[160,512]{1,0:T(8,128)(2,1)S(1)}, bf16[160,512]{1,0:T(8,128)(2,1)S(1)}, u32[]{:S(2)}, u32[]{:S(2)}) collective-permute-start(bf16[160,512]{1,0:T(8,128)(2,1)S(1)} %get-tuple-element.64.refs_4_), channel_id=1, source_target_pairs={{0,2},{1,3},{2,0},{3,1},{4,6},{5,7},{6,4},{7,5},{8,10},{9,11},{10,... | collective-permute-start | bytes 491528 | tf_op jit(solution)/shard_map/ppermute | solution.py:555
  39.0 0.5 collective-permute-start.14
  39.5 0.2 collective-permute-done.18.refs_0_
  39.7 1.7 %collective-permute-start.15 = (bf16[160,512]{1,0:T(8,128)(2,1)S(1)}, bf16[160,512]{1,0:T(8,128)(2,1)S(1)}, u32[]{:S(2)}, u32[]{:S(2)}) collective-permute-start(bf16[160,512]{1,0:T(8,128)(2,1)S(1)} %get-tuple-element.66.refs_6_), channel_id=1, source_target_pairs={{0,6},{1,7},{2,4},{3,5},{4,2},{5,3},{6,0},{7,1},{8,14},{9,15},{10,... | collective-permute-start | bytes 491528 | tf_op jit(solution)/shard_map/ppermute | solution.py:555
  41.4 0.7 %backward_blocks.5.own = f32[256,512]{1,0:T(8,128)S(1)} custom-call(bf16[392,512]{1,0:T(8,128)(2,1)S(1)} %get-tuple-element.38.f_own, bf16[392,512]{1,0:T(8,128)(2,1)S(1)} %collective-permute-done.f_sib, f32[4,16,256]{2,1,0:T(8,128)S(1)} %get-tuple-element.46.ge_ref.own_ge, bf16[392,256]{1,0:T(8,128)(2,1)S(1)} %get-tuple-element.48.refs_0_, ...), custom_call_target="tpu_custom_call" | custom-call | flops 822083584 | bytes 401408 | tf_op jit(solution)/shard_map/backward_blocks/pallas_call | solution.py:345
  42.1 1.3 %collective-permute-done.19.refs_1_ = bf16[144,512]{1,0:T(8,128)(2,1)S(1)} collective-permute-done((bf16[144,512]{1,0:T(8,128)(2,1)S(1)}, bf16[144,512]{1,0:T(8,128)(2,1)S(1)}, u32[]{:S(2)}, u32[]{:S(2)}) %collective-permute-start.19) | collective-permute-done | bytes 147488 | tf_op jit(solution)/shard_map/ppermute | solution.py:555
  43.4 0.0 collective-permute-done.20.refs_2_
  43.4 0.1 collect_terms.3
  43.5 0.1 collective-permute-start.21
  43.5 2.9 %collective-permute-done.13.refs_0_ = bf16[160,512]{1,0:T(8,128)(2,1)S(1)} collective-permute-done((bf16[160,512]{1,0:T(8,128)(2,1)S(1)}, bf16[160,512]{1,0:T(8,128)(2,1)S(1)}, u32[]{:S(2)}, u32[]{:S(2)}) %collective-permute-start.13) | collective-permute-done | bytes 163872 | tf_op jit(solution)/shard_map/ppermute | solution.py:555
  46.4 2.9 %collective-permute-done.14.refs_1_ = bf16[160,512]{1,0:T(8,128)(2,1)S(1)} collective-permute-done((bf16[160,512]{1,0:T(8,128)(2,1)S(1)}, bf16[160,512]{1,0:T(8,128)(2,1)S(1)}, u32[]{:S(2)}, u32[]{:S(2)}) %collective-permute-start.14) | collective-permute-done | bytes 163872 | tf_op jit(solution)/shard_map/ppermute | solution.py:555
  49.3 0.0 collective-permute-done.15.refs_2_
  49.3 0.1 collect_terms.2.mine
  49.4 0.1 collective-permute-start.16
  49.4 0.0 collective-permute-done.21.other
  49.5 2.7 %collective-permute-start.22 = (bf16[96,512]{1,0:T(8,128)(2,1)S(1)}, bf16[96,512]{1,0:T(8,128)(2,1)S(1)}, u32[]{:S(2)}, u32[]{:S(2)}) collective-permute-start(bf16[96,512]{1,0:T(8,128)(2,1)S(1)} %merge_slabs.4.mine.refs_0_), channel_id=1, source_target_pairs={{0,16},{8,24},{16,0},{24,8},{1,17},{9,25},{17,1},{25,9},{2,18},{10... | collective-permute-start | bytes 294920 | tf_op jit(solution)/shard_map/ppermute | solution.py:555
  52.2 3.5 %collective-permute-done.16.other = bf16[128,512]{1,0:T(8,128)(2,1)S(1)} collective-permute-done((bf16[128,512]{1,0:T(8,128)(2,1)S(1)}, bf16[128,512]{1,0:T(8,128)(2,1)S(1)}, u32[]{:S(2)}, u32[]{:S(2)}) %collective-permute-start.16) | collective-permute-done | bytes 131104 | tf_op jit(solution)/shard_map/ppermute | solution.py:555
  55.7 0.1 collective-permute-start.17
  55.8 0.0 collective-permute-done.22.other.refs_1_
  55.8 2.8 %collective-permute-start.23 = (bf16[128,512]{1,0:T(8,128)(2,1)S(1)}, bf16[128,512]{1,0:T(8,128)(2,1)S(1)}, u32[]{:S(2)}, u32[]{:S(2)}) collective-permute-start(bf16[128,512]{1,0:T(8,128)(2,1)S(1)} %merge_slabs.5.mine), channel_id=1, source_target_pairs={{0,8},{8,0},{16,24},{24,16},{1,9},{9,1},{17,25},{25,17},{2,10},{10... | collective-permute-start | bytes 393224 | tf_op jit(solution)/shard_map/ppermute | solution.py:555
  58.6 3.4 %collective-permute-done.17.last_other = bf16[128,512]{1,0:T(8,128)(2,1)S(1)} collective-permute-done((bf16[128,512]{1,0:T(8,128)(2,1)S(1)}, bf16[128,512]{1,0:T(8,128)(2,1)S(1)}, u32[]{:S(2)}, u32[]{:S(2)}) %collective-permute-start.17) | collective-permute-done | bytes 131104 | tf_op jit(solution)/shard_map/ppermute | solution.py:555
  62.0 1.0 %collective-permute-done.23.other = bf16[128,512]{1,0:T(8,128)(2,1)S(1)} collective-permute-done((bf16[128,512]{1,0:T(8,128)(2,1)S(1)}, bf16[128,512]{1,0:T(8,128)(2,1)S(1)}, u32[]{:S(2)}, u32[]{:S(2)}) %collective-permute-start.23) | collective-permute-done | bytes 131104 | tf_op jit(solution)/shard_map/ppermute | solution.py:555
  63.0 1.4 %last_sums.1 = (f32[256,512]{1,0:T(8,128)}, f32[256,256]{1,0:T(8,128)}) custom-call(f32[4,16,256]{2,1,0:T(8,128)S(1)} %get-tuple-element.46.ge_ref.own_ge, f32[8,128]{1,0:T(8,128)S(1)} %get-tuple-element.47.odd, bf16[128,512]{1,0:T(8,128)(2,1)S(1)} %merge_slabs.3.refs_2_.last_mine, bf16[128,512]{1,0:T(8,128)(2,1)S(1)} %collective-permute-done.17.last_other, ...), custom_call_target="tpu_custom_call" | custom-call | tf_op jit(solution)/shard_map/last_sums/pallas_call | solution.py:361
  (6 shorter events, 0.1 us)
Async XLA Ops:
  0.6 6.9 %collective-permute-start.1 = (bf16[392,2048]{1,0:T(8,128)(2,1)}, bf16[392,2048]{1,0:T(8,128)(2,1)}, u32[]{:S(2)}, u32[]{:S(2)}) collective-permute-start(bf16[392,2048]{1,0:T(8,128)(2,1)} %s_own.3), channel_id=1, source_target_pairs={{0,1},{1,0},{2,3},{3,2},{4,5},{5,4},{6,7},{7,6},{8,9},{9,8},{10,11... | collective-permute-start | bytes 4816904 | tf_op jit(solution)/shard_map/ppermute | solution.py:555
  1.1 5.1 %collective-permute-start = (bf16[392,512]{1,0:T(8,128)(2,1)}, bf16[392,512]{1,0:T(8,128)(2,1)S(1)}, u32[]{:S(2)}, u32[]{:S(2)}) collective-permute-start(bf16[392,512]{1,0:T(8,128)(2,1)} %f_own.1), channel_id=1, source_target_pairs={{0,1},{1,0},{2,3},{3,2},{4,5},{5,4},{6,7},{7,6},{8,9},{9,8},{10,11... | collective-permute-start | bytes 1204232 | tf_op jit(solution)/shard_map/ppermute | solution.py:555
  1.2 10.3 %collective-permute-start.3 = (bf16[256,512]{1,0:T(8,128)(2,1)}, bf16[256,512]{1,0:T(8,128)(2,1)S(1)}, u32[]{:S(2)}, u32[]{:S(2)}) collective-permute-start(bf16[256,512]{1,0:T(8,128)(2,1)} %conv.1), channel_id=1, source_target_pairs={{0,4},{1,5},{2,6},{3,7},{4,0},{5,1},{6,2},{7,3},{8,12},{9,13},{10,... | collective-permute-start | bytes 786440 | tf_op jit(solution)/shard_map/ppermute | solution.py:555
  4.2 9.4 %collective-permute-start.2 = (bf16[256,512]{1,0:T(8,128)(2,1)}, bf16[256,512]{1,0:T(8,128)(2,1)S(1)}, u32[]{:S(2)}, u32[]{:S(2)}) collective-permute-start(bf16[256,512]{1,0:T(8,128)(2,1)} %conv.1), channel_id=1, source_target_pairs={{0,2},{1,3},{2,0},{3,1},{4,6},{5,7},{6,4},{7,5},{8,10},{9,11},{10,... | collective-permute-start | bytes 786440 | tf_op jit(solution)/shard_map/ppermute | solution.py:555
  5.7 10.7 %collective-permute-start.4 = (bf16[256,256]{1,0:T(8,128)(2,1)}, bf16[256,256]{1,0:T(8,128)(2,1)S(1)}, u32[]{:S(2)}, u32[]{:S(2)}) collective-permute-start(bf16[256,256]{1,0:T(8,128)(2,1)} %proj.1), channel_id=1, source_target_pairs={{0,2},{1,3},{2,0},{3,1},{4,6},{5,7},{6,4},{7,5},{8,10},{9,11},{10,... | collective-permute-start | bytes 393224 | tf_op jit(solution)/shard_map/ppermute | solution.py:555
  6.2 10.2 %collective-permute-start.5 = (bf16[256,256]{1,0:T(8,128)(2,1)}, bf16[256,256]{1,0:T(8,128)(2,1)S(1)}, u32[]{:S(2)}, u32[]{:S(2)}) collective-permute-start(bf16[256,256]{1,0:T(8,128)(2,1)} %proj.1), channel_id=1, source_target_pairs={{0,4},{1,5},{2,6},{3,7},{4,0},{5,1},{6,2},{7,3},{8,12},{9,13},{10,... | collective-permute-start | bytes 393224 | tf_op jit(solution)/shard_map/ppermute | solution.py:555
  7.6 11.5 %collective-permute-start.6 = (bf16[256,256]{1,0:T(8,128)(2,1)}, bf16[256,256]{1,0:T(8,128)(2,1)S(1)}, u32[]{:S(2)}, u32[]{:S(2)}) collective-permute-start(bf16[256,256]{1,0:T(8,128)(2,1)} %proj.1), channel_id=1, source_target_pairs={{0,6},{1,7},{2,4},{3,5},{4,2},{5,3},{6,0},{7,1},{8,14},{9,15},{10,... | collective-permute-start | bytes 393224 | tf_op jit(solution)/shard_map/ppermute | solution.py:555
  11.5 9.3 %collective-permute-start.7 = (bf16[128,512]{1,0:T(8,128)(2,1)S(1)}, bf16[128,512]{1,0:T(8,128)(2,1)S(1)}, u32[]{:S(2)}, u32[]{:S(2)}) collective-permute-start(bf16[128,512]{1,0:T(8,128)(2,1)S(1)} %half_of.2), channel_id=1, source_target_pairs={{0,2},{1,3},{2,0},{3,1},{4,6},{5,7},{6,4},{7,5},{8,10},{9,11},{10,... | collective-permute-start | bytes 393224 | tf_op jit(solution)/shard_map/ppermute | solution.py:555
  13.6 7.2 %collective-permute-start.8 = (bf16[128,512]{1,0:T(8,128)(2,1)S(1)}, bf16[128,512]{1,0:T(8,128)(2,1)S(1)}, u32[]{:S(2)}, u32[]{:S(2)}) collective-permute-start(bf16[128,512]{1,0:T(8,128)(2,1)S(1)} %half_of.3), channel_id=1, source_target_pairs={{0,4},{1,5},{2,6},{3,7},{4,0},{5,1},{6,2},{7,3},{8,12},{9,13},{10,... | collective-permute-start | bytes 393224 | tf_op jit(solution)/shard_map/ppermute | solution.py:555
  21.5 1.2 %collective-permute-start.9 = (f32[24,256]{1,0:T(8,128)S(1)}, f32[24,256]{1,0:T(8,128)S(1)}, u32[]{:S(2)}, u32[]{:S(2)}) collective-permute-start(f32[24,256]{1,0:T(8,128)S(1)} %get-tuple-element.45), channel_id=1, source_target_pairs={{0,1},{1,0},{2,3},{3,2},{4,5},{5,4},{6,7},{7,6},{8,9},{9,8},{10,11... | collective-permute-start | bytes 73736 | tf_op jit(solution)/shard_map/ppermute | solution.py:555
  22.8 4.7 %collective-permute-start.10 = (f32[24,256]{1,0:T(8,128)S(1)}, f32[24,256]{1,0:T(8,128)S(1)}, u32[]{:S(2)}, u32[]{:S(2)}) collective-permute-start(f32[24,256]{1,0:T(8,128)S(1)} %sum_arrays.1.refs_0_), channel_id=1, source_target_pairs={{0,16},{8,24},{16,0},{24,8},{1,17},{9,25},{17,1},{25,9},{2,18},{10... | collective-permute-start | bytes 73736 | tf_op jit(solution)/shard_map/ppermute | solution.py:555
  25.3 5.6 %collective-permute-start.11 = (f32[24,256]{1,0:T(8,128)S(1)}, f32[24,256]{1,0:T(8,128)S(1)}, u32[]{:S(2)}, u32[]{:S(2)}) collective-permute-start(f32[24,256]{1,0:T(8,128)S(1)} %sum_arrays.1.refs_0_), channel_id=1, source_target_pairs={{0,24},{8,16},{16,8},{24,0},{1,25},{9,17},{17,9},{25,1},{2,26},{10... | collective-permute-start | bytes 73736 | tf_op jit(solution)/shard_map/ppermute | solution.py:555
  26.7 4.3 %collective-permute-start.12 = (f32[24,256]{1,0:T(8,128)S(1)}, f32[24,256]{1,0:T(8,128)S(1)}, u32[]{:S(2)}, u32[]{:S(2)}) collective-permute-start(f32[24,256]{1,0:T(8,128)S(1)} %sum_arrays.1.refs_0_), channel_id=1, source_target_pairs={{0,8},{8,0},{16,24},{24,16},{1,9},{9,1},{17,25},{25,17},{2,10},{10... | collective-permute-start | bytes 73736 | tf_op jit(solution)/shard_map/ppermute | solution.py:555
  33.1 6.6 %collective-permute-start.18 = (bf16[144,512]{1,0:T(8,128)(2,1)S(1)}, bf16[144,512]{1,0:T(8,128)(2,1)S(1)}, u32[]{:S(2)}, u32[]{:S(2)}) collective-permute-start(bf16[144,512]{1,0:T(8,128)(2,1)S(1)} %get-tuple-element.61.refs_12_), channel_id=1, source_target_pairs={{0,2},{1,3},{2,0},{3,1},{4,6},{5,7},{6,4},{7,5},{8,10},{9,11},{10,... | collective-permute-start | bytes 442376 | tf_op jit(solution)/shard_map/ppermute | solution.py:555
  34.7 8.7 %collective-permute-start.19 = (bf16[144,512]{1,0:T(8,128)(2,1)S(1)}, bf16[144,512]{1,0:T(8,128)(2,1)S(1)}, u32[]{:S(2)}, u32[]{:S(2)}) collective-permute-start(bf16[144,512]{1,0:T(8,128)(2,1)S(1)} %get-tuple-element.62.refs_13_), channel_id=1, source_target_pairs={{0,4},{1,5},{2,6},{3,7},{4,0},{5,1},{6,2},{7,3},{8,12},{9,13},{10,... | collective-permute-start | bytes 442376 | tf_op jit(solution)/shard_map/ppermute | solution.py:555
  35.2 8.2 %collective-permute-start.20 = (bf16[144,512]{1,0:T(8,128)(2,1)S(1)}, bf16[144,512]{1,0:T(8,128)(2,1)S(1)}, u32[]{:S(2)}, u32[]{:S(2)}) collective-permute-start(bf16[144,512]{1,0:T(8,128)(2,1)S(1)} %get-tuple-element.63.refs_14_), channel_id=1, source_target_pairs={{0,6},{1,7},{2,4},{3,5},{4,2},{5,3},{6,0},{7,1},{8,14},{9,15},{10,... | collective-permute-start | bytes 442376 | tf_op jit(solution)/shard_map/ppermute | solution.py:555
  37.4 9.0 %collective-permute-start.13 = (bf16[160,512]{1,0:T(8,128)(2,1)S(1)}, bf16[160,512]{1,0:T(8,128)(2,1)S(1)}, u32[]{:S(2)}, u32[]{:S(2)}) collective-permute-start(bf16[160,512]{1,0:T(8,128)(2,1)S(1)} %get-tuple-element.64.refs_4_), channel_id=1, source_target_pairs={{0,2},{1,3},{2,0},{3,1},{4,6},{5,7},{6,4},{7,5},{8,10},{9,11},{10,... | collective-permute-start | bytes 491528 | tf_op jit(solution)/shard_map/ppermute | solution.py:555
  39.0 10.3 %collective-permute-start.14 = (bf16[160,512]{1,0:T(8,128)(2,1)S(1)}, bf16[160,512]{1,0:T(8,128)(2,1)S(1)}, u32[]{:S(2)}, u32[]{:S(2)}) collective-permute-start(bf16[160,512]{1,0:T(8,128)(2,1)S(1)} %get-tuple-element.65.refs_5_), channel_id=1, source_target_pairs={{0,4},{1,5},{2,6},{3,7},{4,0},{5,1},{6,2},{7,3},{8,12},{9,13},{10,... | collective-permute-start | bytes 491528 | tf_op jit(solution)/shard_map/ppermute | solution.py:555
  39.7 9.6 %collective-permute-start.15 = (bf16[160,512]{1,0:T(8,128)(2,1)S(1)}, bf16[160,512]{1,0:T(8,128)(2,1)S(1)}, u32[]{:S(2)}, u32[]{:S(2)}) collective-permute-start(bf16[160,512]{1,0:T(8,128)(2,1)S(1)} %get-tuple-element.66.refs_6_), channel_id=1, source_target_pairs={{0,6},{1,7},{2,4},{3,5},{4,2},{5,3},{6,0},{7,1},{8,14},{9,15},{10,... | collective-permute-start | bytes 491528 | tf_op jit(solution)/shard_map/ppermute | solution.py:555
  43.5 6.0 %collective-permute-start.21 = (bf16[64,512]{1,0:T(8,128)(2,1)S(1)}, bf16[64,512]{1,0:T(8,128)(2,1)S(1)}, u32[]{:S(2)}, u32[]{:S(2)}) collective-permute-start(bf16[64,512]{1,0:T(8,128)(2,1)S(1)} %get-tuple-element.68), channel_id=1, source_target_pairs={{0,8},{8,0},{16,24},{24,16},{1,9},{9,1},{17,25},{25,17},{2,10},{10... | collective-permute-start | bytes 196616 | tf_op jit(solution)/shard_map/ppermute | solution.py:555
  49.4 6.3 %collective-permute-start.16 = (bf16[128,512]{1,0:T(8,128)(2,1)S(1)}, bf16[128,512]{1,0:T(8,128)(2,1)S(1)}, u32[]{:S(2)}, u32[]{:S(2)}) collective-permute-start(bf16[128,512]{1,0:T(8,128)(2,1)S(1)} %collect_terms.2.mine), channel_id=1, source_target_pairs={{0,8},{8,0},{16,24},{24,16},{1,9},{9,1},{17,25},{25,17},{2,10},{10... | collective-permute-start | bytes 393224 | tf_op jit(solution)/shard_map/ppermute | solution.py:555
  49.5 6.3 %collective-permute-start.22 = (bf16[96,512]{1,0:T(8,128)(2,1)S(1)}, bf16[96,512]{1,0:T(8,128)(2,1)S(1)}, u32[]{:S(2)}, u32[]{:S(2)}) collective-permute-start(bf16[96,512]{1,0:T(8,128)(2,1)S(1)} %merge_slabs.4.mine.refs_0_), channel_id=1, source_target_pairs={{0,16},{8,24},{16,0},{24,8},{1,17},{9,25},{17,1},{25,9},{2,18},{10... | collective-permute-start | bytes 294920 | tf_op jit(solution)/shard_map/ppermute | solution.py:555
  55.7 6.3 %collective-permute-start.17 = (bf16[128,512]{1,0:T(8,128)(2,1)S(1)}, bf16[128,512]{1,0:T(8,128)(2,1)S(1)}, u32[]{:S(2)}, u32[]{:S(2)}) collective-permute-start(bf16[128,512]{1,0:T(8,128)(2,1)S(1)} %merge_slabs.3.refs_2_.last_mine), channel_id=1, source_target_pairs={{0,16},{8,24},{16,0},{24,8},{1,17},{9,25},{17,1},{25,9},{2,18},{10... | collective-permute-start | bytes 393224 | tf_op jit(solution)/shard_map/ppermute | solution.py:555
  55.8 7.1 %collective-permute-start.23 = (bf16[128,512]{1,0:T(8,128)(2,1)S(1)}, bf16[128,512]{1,0:T(8,128)(2,1)S(1)}, u32[]{:S(2)}, u32[]{:S(2)}) collective-permute-start(bf16[128,512]{1,0:T(8,128)(2,1)S(1)} %merge_slabs.5.mine), channel_id=1, source_target_pairs={{0,8},{8,0},{16,24},{24,16},{1,9},{9,1},{17,25},{25,17},{2,10},{10... | collective-permute-start | bytes 393224 | tf_op jit(solution)/shard_map/ppermute | solution.py:555

commit v6 on v5

--- a/solution.py
+++ b/solution.py
@@ -152,14 +152,18 @@
     convs, outs = refs[:-5], refs[-5:]
     embed = forward_blocks(1, (f_own, f_sib), (s_own, s_sib), [convs], [proj], before[...], outs)
     mine_ref, send_ref = outs[-2:]
-    half = embed.shape[1] // 2
-    whole = jnp.concatenate([member[...]] * (half // member.shape[1]), axis=1)
-    none = jnp.zeros((images, half), F32)
-    mine_ref[0 : 2 * images] = embed
-    mine_ref[2 * images :] = jnp.concatenate([whole, none], axis=1)
-    send_ref[0:images] = embed[images:]
-    send_ref[images : 2 * images] = embed[:images]
-    send_ref[2 * images :] = jnp.concatenate([none, whole], axis=1)
+    lanes = member.shape[1]
+    tiles = embed.shape[1] // lanes
+    for g in (0, 1):
+        for t in range(tiles):
+            piece = embed[g * images : (g + 1) * images, t * lanes : (t + 1) * lanes]
+            at = (g * tiles + t) * images
+            mine_ref[at : at + images] = piece
+            at = ((1 - g) * tiles + t) * images
+            send_ref[at : at + images] = piece
+    low = lax.broadcasted_iota(jnp.int32, (images, lanes), 1) < lanes // 2
+    mine_ref[2 * tiles * images :] = jnp.where(low, member[...], 0.0)
+    send_ref[2 * tiles * images :] = jnp.where(low, 0.0, member[...])
 
 
 def forward_call(kernel, in_specs, shapes, scratch, busy, name, *arrays):
@@ -234,7 +238,7 @@
     outs = forward_call(
         functools.partial(last_kernel, images),
         [vspec()] * len(arrays),
-        block_shapes(rows, count, images) + [((3 * images, embed), F32)] * 2,
+        block_shapes(rows, count, images) + [(((2 * embed // 128 + 1) * images, 128), F32)] * 2,
         [],
         (rows, width, count),
         "forward_last",
@@ -275,15 +279,18 @@
     ge_ref, loss_ref, odd_ref, z_ref, p_ref, g_ref = refs[-6:]
     place = place_ref[0]
     odd_ref[...] = jnp.full(odd_ref.shape, (place & 1).astype(F32))
-    half = z_ref.shape[2] // 2
+    tiles = z_ref.shape[2] // 128
     for j in range(slabs):
         block = chunks[0].at[j] if len(chunks) == 1 else chunks[ORDER.index(j)]
         at = pl.ds(pl.multiple_of((place ^ j) * images, images), images)
         for g in (0, 1):
-            z_ref[g, at] = block[g * images : (g + 1) * images]
-            p_ref[g, at] = block[2 * images :, g * half : g * half + 128]
+            for t in range(tiles):
+                row = (g * tiles + t) * images
+                z_ref[g, at, t * 128 : (t + 1) * 128] = block[row : row + images]
+        p_ref[at] = block[2 * tiles * images :]
+    high_lane = lax.broadcasted_iota(jnp.int32, p_ref.shape, 1) >= 64
     for g in (0, 1):
-        partner = jnp.max(p_ref[g], axis=1, keepdims=True)
+        partner = jnp.max(jnp.where(high_lane == (g == 1), p_ref[...], -1.0), axis=1, keepdims=True)
         loss, grad = group_terms(z_ref[g], partner, groups)
         if g == 0:
             loss_ref[...] = loss
@@ -294,8 +301,7 @@
             ge_ref[j, g * images : (g + 1) * images] = g_ref[g, at]
 
 
-def hsic(place, chunks, slabs, images, groups):
-    embed = chunks[0].shape[-1]
+def hsic(place, chunks, embed, slabs, images, groups):
     return pl.pallas_call(
         functools.partial(hsic_kernel, slabs, images, groups),
         in_specs=[pl.BlockSpec(memory_space=pltpu.SMEM)] + [vspec()] * len(chunks),
@@ -305,7 +311,11 @@
             jax.ShapeDtypeStruct((1, 1), F32),
             jax.ShapeDtypeStruct((8, 128), F32),
         ],
-        scratch_shapes=[pltpu.VMEM((2, slabs * images, width), F32) for width in (embed, 128, embed)],
+        scratch_shapes=[
+            pltpu.VMEM((2, slabs * images, embed), F32),
+            pltpu.VMEM((slabs * images, 128), F32),
+            pltpu.VMEM((2, slabs * images, embed), F32),
+        ],
         compiler_params=params(80 * (slabs * images) ** 2),
         cost_estimate=pl.CostEstimate(flops=10**9, bytes_accessed=0, transcendentals=0),
         name="hsic_groups",
@@ -332,16 +342,15 @@
             rest = jnp.zeros((2 * images, width - pooled.shape[1]), BF)
             out[rows:] = jnp.concatenate([pooled[...], rest], axis=1)
         if extra == "embed":
-            slabs = ge_ref.shape[0]
-            flat = ge_ref[...].reshape(slabs * 2 * images, ge_ref.shape[2]).astype(BF)
-            half = slabs * images
+            half = ge_ref.shape[0] * images // 2
+            flat = ge_ref[:, :images].reshape(2 * half, ge_ref.shape[2]).astype(BF)
             out[rows:] = jnp.concatenate([flat[:half], flat[half:]], axis=1)
 
 
 def backward(feats, ge, blocks, images, part, extra=None, after=()):
     length, width = feats[0].shape
     rows = part[1]
-    high = rows + {None: 0, "pooled": 2 * images, "embed": ge.shape[0] * images}[extra]
+    high = rows + {None: 0, "pooled": 2 * images, "embed": ge.shape[0] * images // 2}[extra]
     return pl.pallas_call(
         functools.partial(backward_kernel, len(blocks), images, part, extra, len(after)),
         in_specs=[vspec()] * (3 + 4 * len(blocks)) + [pl.BlockSpec(memory_space=pl.ANY)] * len(after),
@@ -402,6 +411,24 @@
     more = (len(msgs) + 1) * pooled.size // width if with_pooled else 0
     kernel = functools.partial(collect_kernel, start, rows, len(msgs))
     return small_call(kernel, [((rows + more, width), BF)], "collect_terms", own, pooled, *msgs, tokens=token)[0]
+
+
+def collect_grads_kernel(start, rows, own, *refs):
+    msgs, (out, tails) = refs[:-2], refs[-2:]
+    total = own[start : start + rows]
+    for msg in msgs:
+        total = total + msg[0:rows].astype(F32)
+    out[...] = total.astype(BF)
+    high = msgs[0].shape[0] - rows
+    for k, msg in enumerate(msgs):
+        tails[k * high : (k + 1) * high] = msg[rows:]
+
+
+def collect_grads(own, msgs, part):
+    start, rows = part
+    width = own.shape[1]
+    shapes = [((rows, width), BF), ((len(msgs) * (msgs[0].shape[0] - rows), width), BF)]
+    return small_call(functools.partial(collect_grads_kernel, start, rows), shapes, "collect_terms", own, *msgs)
 
 
 def merge_kernel(rows, mine, other, *refs):
@@ -497,20 +524,20 @@
     out[head:] = pieces[2][...].astype(F32) + pieces[3][...].astype(F32)
 
 
-def proj_sum(slabs, images, order, rows, msg_rows, own_ge, mine, other, msgs, out):
+def proj_sum(slabs, images, order, rows, own_ge, mine, other, tails, out):
     count, embed = out.shape
     groups = mine.shape[1] // count
-    half = slabs * images
+    half = slabs * images // 2
     per = (mine.shape[0] - rows) // (slabs // 2)
     together = per // (2 * images)
     parts = []
     for j in range(slabs):
         pieces = [own_ge[j].astype(BF)]
-        start, left = j * 2 * images, 0
-        if start >= half:
-            start, left = start - half, embed
-        for msg in msgs:
-            pieces.append(msg[msg_rows + start : msg_rows + start + 2 * images, left : left + embed])
+        start, left = j * images % half, j * images // half * embed
+        base = start // 16 * 16
+        for k in range(0, tails[0].shape[0], half):
+            pair = [t[k + base : k + base + 16, left : left + embed].astype(F32) for t in tails]
+            pieces.append(jnp.concatenate([p[start - base : start - base + images] for p in pair], axis=0).astype(BF))
         at = order.index(j)
         ref, at = (mine, at) if at < slabs // 2 else (other, at - slabs // 2)
         total = jnp.zeros((count, embed), F32)
@@ -541,9 +568,9 @@
     return small_call(functools.partial(part_kernel, start), [(shape, x.dtype)], "half_of", x, tokens=(token,))[0]
 
 
-def last_sums_kernel(slabs, images, order, rows, msg_rows, own_ge, odd, last_mine, last_other, mine, other, *refs):
-    msgs, (conv_out, proj_out) = refs[:-2], refs[-2:]
-    proj_sum(slabs, images, order, rows, msg_rows, own_ge, mine, other, msgs, proj_out)
+def last_sums_kernel(slabs, images, order, rows, own_ge, odd, last_mine, last_other, mine, other, *refs):
+    tails, (conv_out, proj_out) = refs[:-2], refs[-2:]
+    proj_sum(slabs, images, order, rows, own_ge, mine, other, tails, proj_out)
     if slabs == 4:
         final_halves(odd, mine, other, (last_mine, last_other), conv_out)
     else:
@@ -594,7 +621,7 @@
     blocks, projs = [first, *middle, last], [proj_own, *projs]
     blocks = [(*b, p) for b, p in zip(blocks, projs)]
     embeds = sum_of(F32, mine, swap(send, "fsdp", 1))
-    ge, loss, odd = hsic(place, gather_slabs(embeds, slabs), slabs, images, groups)
+    ge, loss, odd = hsic(place, gather_slabs(embeds, slabs), proj_weight.shape[1], slabs, images, groups)
 
     first_rows = count * SPLIT // 8
     parts = [(0, first_rows), (first_rows, count - first_rows)]
@@ -605,7 +632,7 @@
     (own,) = backward(feats, ge, blocks[:1], images, (0, count), None, done)
 
     received = [[swap(m, "fsdp", 2 * j) for j, m in enumerate(term, 1)] for term in terms]
-    total = collect(own, blocks[0][2], received[1], parts[1], False, ())
+    total, tails = collect_grads(own, received[1], parts[1])
     if slabs == 4:
         merged = merge(parts[1][1], total, swap(total, "dp", 1))
         mine, other = sum_by_halves(own, blocks[0][2], odd, received[0], parts[0], (), (merged,))
@@ -620,10 +647,10 @@
                 bit *= 2
             pieces += [piece, swap(piece, "dp", bit)]
     grad_conv, grad_proj = small_call(
-        functools.partial(last_sums_kernel, slabs, images, order, above, parts[1][1]),
+        functools.partial(last_sums_kernel, slabs, images, order, above),
         [((count, width), F32), (proj_weight.shape, F32)],
         "last_sums",
-        *(ge, odd, pieces[2], pieces[3], pieces[0], pieces[1], *received[1]),
+        *(ge, odd, pieces[2], pieces[3], pieces[0], pieces[1], tails, swap(tails, "fsdp", 1)),
     )
     return grad_conv, grad_proj, loss.reshape(1)
 

time: 64.5 us -> 63.3 us (0.981)
  waiting for transfers between devices: 23.6 us -> 22.7 us
    ppermute x24 -> x25, waiting for transfers between devices: 23.6 us -> 22.7 us  [swap(): return lax.ppermute(x, axis, [(i, i ^ bit) for i in range(size)])]
    ppermute x24 -> x25, starting transfers between devices: 29.4 us -> 29.1 us  [swap(): return lax.ppermute(x, axis, [(i, i ^ bit) for i in range(size)])]
  transfers between devices with their start and end apart: 24 -> 25, of which waited for: 13 -> 14; matrix products, arithmetic and copies ran while one was open for 0% -> 0% of each run, Pallas kernels for 10% -> 10%
where the time goes in v6:
time: 63.3 us; the launch traced here: 63.2 us
  starting transfers between devices  29.1 us (46%)
  waiting for transfers between devices  22.7 us (36%)
  Pallas kernels  10.6 us (17%)
  between operations  0.75 us (1%)
    ppermute x25, starting transfers between devices, swap(): return lax.ppermute(x, axis, [(i, i ^ bit) for i in range(size)])  29.1 us
    ppermute x25, waiting for transfers between devices, swap(): return lax.ppermute(x, axis, [(i, i ^ bit) for i in range(size)])  22.7 us
    pallas_call x3, Pallas kernels, forward_call(): pl.pallas_call(kernel, in_specs=in_specs, out_specs=[vspec()] * len(shape...  5.42 us
    pallas_call x3, Pallas kernels, backward(): pl.pallas_call(functools.partial(backward_kernel, len(blocks), images, pa...  2.27 us
    pallas_call x9, Pallas kernels, small_call(): pl.pallas_call(kernel, in_specs=[vspec()] * len(arrays) + [pl.BlockSpec(m...  1.62 us
    pallas_call x1, Pallas kernels, hsic(): pl.pallas_call(functools.partial(hsic_kernel, slabs, images, groups), in_...  1.33 us
  transfers between devices with their start and end apart: 25, of which 14 were waited for; matrix products, arithmetic and copies ran while one was open for 0% of the time, Pallas kernels for 10%

profile of v6, /device:TPU:0, one launch (start us, length us, event | category | flops | bytes accessed | tf_op | source)
XLA Modules:
  0.0 63.2 jit_solution(14084120624749213139)
XLA Ops:
  0.6 0.5 collective-permute-start.1
  1.1 0.1 collective-permute-start
  1.2 2.9 %collective-permute-start.3 = (bf16[256,512]{1,0:T(8,128)(2,1)}, bf16[256,512]{1,0:T(8,128)(2,1)S(1)}, u32[]{:S(2)}, u32[]{:S(2)}) collective-permute-start(bf16[256,512]{1,0:T(8,128)(2,1)} %conv.1), channel_id=1, source_target_pairs={{0,4},{1,5},{2,6},{3,7},{4,0},{5,1},{6,2},{7,3},{8,12},{9,13},{10,... | collective-permute-start | bytes 786440 | tf_op jit(solution)/shard_map/ppermute | solution.py:582
  4.2 1.5 %collective-permute-start.2 = (bf16[256,512]{1,0:T(8,128)(2,1)}, bf16[256,512]{1,0:T(8,128)(2,1)S(1)}, u32[]{:S(2)}, u32[]{:S(2)}) collective-permute-start(bf16[256,512]{1,0:T(8,128)(2,1)} %conv.1), channel_id=1, source_target_pairs={{0,2},{1,3},{2,0},{3,1},{4,6},{5,7},{6,4},{7,5},{8,10},{9,11},{10,... | collective-permute-start | bytes 786440 | tf_op jit(solution)/shard_map/ppermute | solution.py:582
  5.7 0.5 collective-permute-start.4
  6.2 0.0 collective-permute-done.f_sib
  6.2 1.4 %collective-permute-start.5 = (bf16[256,256]{1,0:T(8,128)(2,1)}, bf16[256,256]{1,0:T(8,128)(2,1)S(1)}, u32[]{:S(2)}, u32[]{:S(2)}) collective-permute-start(bf16[256,256]{1,0:T(8,128)(2,1)} %proj.1), channel_id=1, source_target_pairs={{0,4},{1,5},{2,6},{3,7},{4,0},{5,1},{6,2},{7,3},{8,12},{9,13},{10,... | collective-permute-start | bytes 393224 | tf_op jit(solution)/shard_map/ppermute | solution.py:582
  7.6 0.0 collective-permute-done.1.s_sib
  7.6 1.6 %collective-permute-start.6 = (bf16[256,256]{1,0:T(8,128)(2,1)}, bf16[256,256]{1,0:T(8,128)(2,1)S(1)}, u32[]{:S(2)}, u32[]{:S(2)}) collective-permute-start(bf16[256,256]{1,0:T(8,128)(2,1)} %proj.1), channel_id=1, source_target_pairs={{0,6},{1,7},{2,4},{3,5},{4,2},{5,3},{6,0},{7,1},{8,14},{9,15},{10,... | collective-permute-start | bytes 393224 | tf_op jit(solution)/shard_map/ppermute | solution.py:582
  9.2 2.0 %forward_first.1 = (bf16[392,256]{1,0:T(8,128)(2,1)S(1)}, bf16[392,256]{1,0:T(8,128)(2,1)S(1)}, bf16[16,256]{1,0:T(8,128)(2,1)S(1)}, f32[16,256]{1,0:T(8,128)S(1...) custom-call(s32[1]{0:T(128)} %bitcast.1.index_ref, ...), custom_call_target="tpu_custom_call" | custom-call | flops 822083584 | bytes 802816 | tf_op jit(solution)/shard_map/forward_first/pallas_call | solution.py:171
  11.2 0.3 collective-permute-done.3.refs_1_.x
  11.5 2.1 %collective-permute-start.7 = (bf16[128,512]{1,0:T(8,128)(2,1)S(1)}, bf16[128,512]{1,0:T(8,128)(2,1)S(1)}, u32[]{:S(2)}, u32[]{:S(2)}) collective-permute-start(bf16[128,512]{1,0:T(8,128)(2,1)S(1)} %half_of.2), channel_id=1, source_target_pairs={{0,2},{1,3},{2,0},{3,1},{4,6},{5,7},{6,4},{7,5},{8,10},{9,11},{10,... | collective-permute-start | bytes 393224 | tf_op jit(solution)/shard_map/ppermute | solution.py:582
  13.6 0.0 collective-permute-done.2.refs_0_.x
  13.6 1.6 %collective-permute-start.8 = (bf16[128,512]{1,0:T(8,128)(2,1)S(1)}, bf16[128,512]{1,0:T(8,128)(2,1)S(1)}, u32[]{:S(2)}, u32[]{:S(2)}) collective-permute-start(bf16[128,512]{1,0:T(8,128)(2,1)S(1)} %half_of.3), channel_id=1, source_target_pairs={{0,4},{1,5},{2,6},{3,7},{4,0},{5,1},{6,2},{7,3},{8,12},{9,13},{10,... | collective-permute-start | bytes 393224 | tf_op jit(solution)/shard_map/ppermute | solution.py:582
  15.2 1.2 %collective-permute-done.4.refs_2_.refs_3_ = bf16[256,256]{1,0:T(8,128)(2,1)S(1)} collective-permute-done((bf16[256,256]{1,0:T(8,128)(2,1)}, bf16[256,256]{1,0:T(8,128)(2,1)S(1)}, u32[]{:S(2)}, u32[]{:S(2)}) %collective-permute-start.4) | collective-permute-done | bytes 131104 | tf_op jit(solution)/shard_map/ppermute | solution.py:582
  16.4 0.0 collective-permute-done.5.refs_3_.refs_7_
  16.4 2.7 %forward_middle.1 = (bf16[392,256]{1,0:T(8,128)(2,1)S(1)}, bf16[392,256]{1,0:T(8,128)(2,1)S(1)}, bf16[16,256]{1,0:T(8,128)(2,1)S(1)}, bf16[392,256]{1,0:T(8,128)...) custom-call(s32[1]{0:T(128)} %bitcast.1.index_ref, ...), custom_call_target="tpu_custom_call" | custom-call | flops 1644167168 | bytes 1605632 | tf_op jit(solution)/shard_map/forward_middle/pallas_call | solution.py:171
  19.1 0.0 collective-permute-done.6.proj.refs_11_
  19.1 1.7 %collective-permute-done.7.refs_0_ = bf16[128,512]{1,0:T(8,128)(2,1)S(1)} collective-permute-done((bf16[128,512]{1,0:T(8,128)(2,1)S(1)}, bf16[128,512]{1,0:T(8,128)(2,1)S(1)}, u32[]{:S(2)}, u32[]{:S(2)}) %collective-permute-start.7) | collective-permute-done | bytes 131104 | tf_op jit(solution)/shard_map/ppermute | solution.py:582
  20.8 0.0 collective-permute-done.8.refs_1_
  20.8 0.7 %forward_last.1 = (bf16[392,256]{1,0:T(8,128)(2,1)S(1)}, bf16[392,256]{1,0:T(8,128)(2,1)S(1)}, bf16[16,256]{1,0:T(8,128)(2,1)S(1)}, f32[40,128]{1,0:T(8,128)S(1)}, f32[40,128]{1,0:T(8,128)S(1)}) custom-call(bf16[392,512]{1,0:T(8,128)(2,1)S(1)} %get-tuple-element.40.f_own, bf16[392,512]{1,0:T(8,128)(2,1)S(1)} %collective-permute-done.f_sib, ...), custom_call_target="tpu_custom_call" | custom-call | flops 822083584 | bytes 802816 | tf_op jit(solution)/shard_map/forward_last/pallas_call | solution.py:171
  21.5 0.0 collective-permute-start.9
  21.5 1.2 %collective-permute-done.9.refs_1_ = f32[40,128]{1,0:T(8,128)S(1)} collective-permute-done((f32[40,128]{1,0:T(8,128)S(1)}, f32[40,128]{1,0:T(8,128)S(1)}, u32[]{:S(2)}, u32[]{:S(2)}) %collective-permute-start.9) | collective-permute-done | bytes 20512 | tf_op jit(solution)/shard_map/ppermute | solution.py:582
  22.7 2.6 %collective-permute-start.10 = (f32[40,128]{1,0:T(8,128)S(1)}, f32[40,128]{1,0:T(8,128)S(1)}, u32[]{:S(2)}, u32[]{:S(2)}) collective-permute-start(f32[40,128]{1,0:T(8,128)S(1)} %sum_arrays.1.refs_0_), channel_id=1, source_target_pairs={{0,16},{8,24},{16,0},{24,8},{1,17},{9,25},{17,1},{25,9},{2,18},{10... | collective-permute-start | bytes 61448 | tf_op jit(solution)/shard_map/ppermute | solution.py:582
  25.3 1.3 %collective-permute-start.11 = (f32[40,128]{1,0:T(8,128)S(1)}, f32[40,128]{1,0:T(8,128)S(1)}, u32[]{:S(2)}, u32[]{:S(2)}) collective-permute-start(f32[40,128]{1,0:T(8,128)S(1)} %sum_arrays.1.refs_0_), channel_id=1, source_target_pairs={{0,24},{8,16},{16,8},{24,0},{1,25},{9,17},{17,9},{25,1},{2,26},{10... | collective-permute-start | bytes 61448 | tf_op jit(solution)/shard_map/ppermute | solution.py:582
  26.7 0.2 collective-permute-start.12
  26.9 0.5 collective-permute-done.10.refs_1_
  27.4 3.5 %collective-permute-done.11.refs_2_ = f32[40,128]{1,0:T(8,128)S(1)} collective-permute-done((f32[40,128]{1,0:T(8,128)S(1)}, f32[40,128]{1,0:T(8,128)S(1)}, u32[]{:S(2)}, u32[]{:S(2)}) %collective-permute-start.11) | collective-permute-done | bytes 20512 | tf_op jit(solution)/shard_map/ppermute | solution.py:582
  30.9 0.0 collective-permute-done.12.refs_3_
  30.9 1.3 %hsic_groups.1 = (f32[4,16,256]{2,1,0:T(8,128)S(1)}, f32[1,1]{1,0:T(1,128)}, f32[8,128]{1,0:T(8,128)S(1)}) custom-call(s32[1]{0:T(128)} %bitcast.place_ref, f32[40,128]{1,0:T(8,128)S(1)} %sum_arrays.1.refs_0_, f32[40,128]{1,0:T(8,128)S(1)} %collective-permute-done.10.refs_1_, f32[40,128]{1,0:T(8,128)S(1)} %collective-permute-done.11.refs_2_, ...), custom_call_target="tpu_custom_call" | custom-call | flops 1000000000 | tf_op jit(solution)/shard_map/hsic_groups/pallas_call | solution.py:305
  32.3 0.8 %backward_blocks.3 = (bf16[144,512]{1,0:T(8,128)(2,1)S(1)}, bf16[144,512]{1,0:T(8,128)(2,1)S(1)}, bf16[144,512]{1,0:T(8,128)(2,1)S(1)}) custom-call(bf16[392,512]{1,0:T(8,128)(2,1)S(1)} %get-tuple-element.40.f_own, bf16[392,512]{1,0:T(8,128)(2,1)S(1)} %collective-permute-done.f_sib, f32[4,16,256]{2,1,0:T(8,128)S(1)} %get-tuple-element.48.ge_ref.own_ge, ...), custom_call_target="tpu_custom_call" | custom-call | flops 1233125376 | bytes 602112 | tf_op jit(solution)/shard_map/backward_blocks/pallas_call | solution.py:354
  33.0 1.6 %collective-permute-start.18 = (bf16[144,512]{1,0:T(8,128)(2,1)S(1)}, bf16[144,512]{1,0:T(8,128)(2,1)S(1)}, u32[]{:S(2)}, u32[]{:S(2)}) collective-permute-start(bf16[144,512]{1,0:T(8,128)(2,1)S(1)} %get-tuple-element.63.refs_12_), channel_id=1, source_target_pairs={{0,2},{1,3},{2,0},{3,1},{4,6},{5,7},{6,4},{7,5},{8,10},{9,11},{10,... | collective-permute-start | bytes 442376 | tf_op jit(solution)/shard_map/ppermute | solution.py:582
  34.6 0.5 collective-permute-start.19
  35.1 1.5 %collective-permute-start.20 = (bf16[144,512]{1,0:T(8,128)(2,1)S(1)}, bf16[144,512]{1,0:T(8,128)(2,1)S(1)}, u32[]{:S(2)}, u32[]{:S(2)}) collective-permute-start(bf16[144,512]{1,0:T(8,128)(2,1)S(1)} %get-tuple-element.65.refs_14_), channel_id=1, source_target_pairs={{0,6},{1,7},{2,4},{3,5},{4,2},{5,3},{6,0},{7,1},{8,14},{9,15},{10,... | collective-permute-start | bytes 442376 | tf_op jit(solution)/shard_map/ppermute | solution.py:582
  36.6 0.8 %backward_blocks.4 = (bf16[144,512]{1,0:T(8,128)(2,1)S(1)}, bf16[144,512]{1,0:T(8,128)(2,1)S(1)}, bf16[144,512]{1,0:T(8,128)(2,1)S(1)}) custom-call(bf16[392,512]{1,0:T(8,128)(2,1)S(1)} %get-tuple-element.40.f_own, bf16[392,512]{1,0:T(8,128)(2,1)S(1)} %collective-permute-done.f_sib, f32[4,16,256]{2,1,0:T(8,128)S(1)} %get-tuple-element.48.ge_ref.own_ge, ...), custom_call_target="tpu_custom_call" | custom-call | flops 1233125376 | bytes 602112 | tf_op jit(solution)/shard_map/backward_blocks/pallas_call | solution.py:354
  37.4 1.6 %collective-permute-start.13 = (bf16[144,512]{1,0:T(8,128)(2,1)S(1)}, bf16[144,512]{1,0:T(8,128)(2,1)S(1)}, u32[]{:S(2)}, u32[]{:S(2)}) collective-permute-start(bf16[144,512]{1,0:T(8,128)(2,1)S(1)} %get-tuple-element.66.refs_4_), channel_id=1, source_target_pairs={{0,2},{1,3},{2,0},{3,1},{4,6},{5,7},{6,4},{7,5},{8,10},{9,11},{10,... | collective-permute-start | bytes 442376 | tf_op jit(solution)/shard_map/ppermute | solution.py:582
  38.9 0.5 collective-permute-start.14
  39.5 0.2 collective-permute-done.18.refs_0_
  39.7 1.7 %collective-permute-start.15 = (bf16[144,512]{1,0:T(8,128)(2,1)S(1)}, bf16[144,512]{1,0:T(8,128)(2,1)S(1)}, u32[]{:S(2)}, u32[]{:S(2)}) collective-permute-start(bf16[144,512]{1,0:T(8,128)(2,1)S(1)} %get-tuple-element.68.refs_6_), channel_id=1, source_target_pairs={{0,6},{1,7},{2,4},{3,5},{4,2},{5,3},{6,0},{7,1},{8,14},{9,15},{10,... | collective-permute-start | bytes 442376 | tf_op jit(solution)/shard_map/ppermute | solution.py:582
  41.3 0.7 %backward_blocks.5.own = f32[256,512]{1,0:T(8,128)S(1)} custom-call(bf16[392,512]{1,0:T(8,128)(2,1)S(1)} %get-tuple-element.40.f_own, bf16[392,512]{1,0:T(8,128)(2,1)S(1)} %collective-permute-done.f_sib, f32[4,16,256]{2,1,0:T(8,128)S(1)} %get-tuple-element.48.ge_ref.own_ge, bf16[392,256]{1,0:T(8,128)(2,1)S(1)} %get-tuple-element.50.refs_0_, ...), custom_call_target="tpu_custom_call" | custom-call | flops 822083584 | bytes 401408 | tf_op jit(solution)/shard_map/backward_blocks/pallas_call | solution.py:354
  42.0 1.5 %collective-permute-done.19.refs_1_ = bf16[144,512]{1,0:T(8,128)(2,1)S(1)} collective-permute-done((bf16[144,512]{1,0:T(8,128)(2,1)S(1)}, bf16[144,512]{1,0:T(8,128)(2,1)S(1)}, u32[]{:S(2)}, u32[]{:S(2)}) %collective-permute-start.19) | collective-permute-done | bytes 147488 | tf_op jit(solution)/shard_map/ppermute | solution.py:582
  43.5 0.0 collective-permute-done.20.refs_2_
  43.5 0.1 collect_terms.3
  43.6 0.1 collective-permute-start.21
  43.7 2.3 %collective-permute-done.13.refs_0_ = bf16[144,512]{1,0:T(8,128)(2,1)S(1)} collective-permute-done((bf16[144,512]{1,0:T(8,128)(2,1)S(1)}, bf16[144,512]{1,0:T(8,128)(2,1)S(1)}, u32[]{:S(2)}, u32[]{:S(2)}) %collective-permute-start.13) | collective-permute-done | bytes 147488 | tf_op jit(solution)/shard_map/ppermute | solution.py:582
  46.0 2.5 %collective-permute-done.14.refs_1_ = bf16[144,512]{1,0:T(8,128)(2,1)S(1)} collective-permute-done((bf16[144,512]{1,0:T(8,128)(2,1)S(1)}, bf16[144,512]{1,0:T(8,128)(2,1)S(1)}, u32[]{:S(2)}, u32[]{:S(2)}) %collective-permute-start.14) | collective-permute-done | bytes 147488 | tf_op jit(solution)/shard_map/ppermute | solution.py:582
  48.5 0.0 collective-permute-done.15.refs_2_
  48.5 0.1 collect_terms.2
  48.6 0.1 collective-permute-start.16
  48.7 0.0 collective-permute-done.21.other
  48.7 2.6 %collective-permute-start.22 = (bf16[96,512]{1,0:T(8,128)(2,1)S(1)}, bf16[96,512]{1,0:T(8,128)(2,1)S(1)}, u32[]{:S(2)}, u32[]{:S(2)}) collective-permute-start(bf16[96,512]{1,0:T(8,128)(2,1)S(1)} %merge_slabs.4.mine.refs_0_), channel_id=1, source_target_pairs={{0,16},{8,24},{16,0},{24,8},{1,17},{9,25},{17,1},{25,9},{2,18},{10... | collective-permute-start | bytes 294920 | tf_op jit(solution)/shard_map/ppermute | solution.py:582
  51.3 3.3 %collective-permute-done.16.other = bf16[128,512]{1,0:T(8,128)(2,1)S(1)} collective-permute-done((bf16[128,512]{1,0:T(8,128)(2,1)S(1)}, bf16[128,512]{1,0:T(8,128)(2,1)S(1)}, u32[]{:S(2)}, u32[]{:S(2)}) %collective-permute-start.16) | collective-permute-done | bytes 131104 | tf_op jit(solution)/shard_map/ppermute | solution.py:582
  54.7 0.2 collective-permute-start.17
  54.9 0.0 collective-permute-done.22.other.refs_1_
  55.0 2.5 %collective-permute-start.23 = (bf16[128,512]{1,0:T(8,128)(2,1)S(1)}, bf16[128,512]{1,0:T(8,128)(2,1)S(1)}, u32[]{:S(2)}, u32[]{:S(2)}) collective-permute-start(bf16[128,512]{1,0:T(8,128)(2,1)S(1)} %merge_slabs.5.mine), channel_id=1, source_target_pairs={{0,8},{8,0},{16,24},{24,16},{1,9},{9,1},{17,25},{25,17},{2,10},{10... | collective-permute-start | bytes 393224 | tf_op jit(solution)/shard_map/ppermute | solution.py:582
  57.4 0.0 collective-permute-start.24
  57.4 1.2 %collective-permute-done.24.refs_1_ = bf16[48,512]{1,0:T(8,128)(2,1)S(1)} collective-permute-done((bf16[48,512]{1,0:T(8,128)(2,1)S(1)}, bf16[48,512]{1,0:T(8,128)(2,1)S(1)}, u32[]{:S(2)}, u32[]{:S(2)}) %collective-permute-start.24) | collective-permute-done | bytes 49184 | tf_op jit(solution)/shard_map/ppermute | solution.py:582
  58.7 2.5 %collective-permute-done.17.last_other = bf16[128,512]{1,0:T(8,128)(2,1)S(1)} collective-permute-done((bf16[128,512]{1,0:T(8,128)(2,1)S(1)}, bf16[128,512]{1,0:T(8,128)(2,1)S(1)}, u32[]{:S(2)}, u32[]{:S(2)}) %collective-permute-start.17) | collective-permute-done | bytes 131104 | tf_op jit(solution)/shard_map/ppermute | solution.py:582
  61.2 0.6 collective-permute-done.23.other
  61.8 1.4 %last_sums.1 = (f32[256,512]{1,0:T(8,128)}, f32[256,256]{1,0:T(8,128)}) custom-call(f32[4,16,256]{2,1,0:T(8,128)S(1)} %get-tuple-element.48.ge_ref.own_ge, f32[8,128]{1,0:T(8,128)S(1)} %get-tuple-element.49.odd, bf16[128,512]{1,0:T(8,128)(2,1)S(1)} %merge_slabs.3.refs_2_.last_mine, bf16[128,512]{1,0:T(8,128)(2,1)S(1)} %collective-permute-done.17.last_other, ...), custom_call_target="tpu_custom_call" | custom-call | tf_op jit(solution)/shard_map/last_sums/pallas_call | solution.py:370
  (6 shorter events, 0.1 us)
Async XLA Ops:
  0.6 6.9 %collective-permute-start.1 = (bf16[392,2048]{1,0:T(8,128)(2,1)}, bf16[392,2048]{1,0:T(8,128)(2,1)}, u32[]{:S(2)}, u32[]{:S(2)}) collective-permute-start(bf16[392,2048]{1,0:T(8,128)(2,1)} %s_own.3), channel_id=1, source_target_pairs={{0,1},{1,0},{2,3},{3,2},{4,5},{5,4},{6,7},{7,6},{8,9},{9,8},{10,11... | collective-permute-start | bytes 4816904 | tf_op jit(solution)/shard_map/ppermute | solution.py:582
  1.1 5.1 %collective-permute-start = (bf16[392,512]{1,0:T(8,128)(2,1)}, bf16[392,512]{1,0:T(8,128)(2,1)S(1)}, u32[]{:S(2)}, u32[]{:S(2)}) collective-permute-start(bf16[392,512]{1,0:T(8,128)(2,1)} %f_own.1), channel_id=1, source_target_pairs={{0,1},{1,0},{2,3},{3,2},{4,5},{5,4},{6,7},{7,6},{8,9},{9,8},{10,11... | collective-permute-start | bytes 1204232 | tf_op jit(solution)/shard_map/ppermute | solution.py:582
  1.2 10.3 %collective-permute-start.3 = (bf16[256,512]{1,0:T(8,128)(2,1)}, bf16[256,512]{1,0:T(8,128)(2,1)S(1)}, u32[]{:S(2)}, u32[]{:S(2)}) collective-permute-start(bf16[256,512]{1,0:T(8,128)(2,1)} %conv.1), channel_id=1, source_target_pairs={{0,4},{1,5},{2,6},{3,7},{4,0},{5,1},{6,2},{7,3},{8,12},{9,13},{10,... | collective-permute-start | bytes 786440 | tf_op jit(solution)/shard_map/ppermute | solution.py:582
  4.2 9.4 %collective-permute-start.2 = (bf16[256,512]{1,0:T(8,128)(2,1)}, bf16[256,512]{1,0:T(8,128)(2,1)S(1)}, u32[]{:S(2)}, u32[]{:S(2)}) collective-permute-start(bf16[256,512]{1,0:T(8,128)(2,1)} %conv.1), channel_id=1, source_target_pairs={{0,2},{1,3},{2,0},{3,1},{4,6},{5,7},{6,4},{7,5},{8,10},{9,11},{10,... | collective-permute-start | bytes 786440 | tf_op jit(solution)/shard_map/ppermute | solution.py:582
  5.7 10.7 %collective-permute-start.4 = (bf16[256,256]{1,0:T(8,128)(2,1)}, bf16[256,256]{1,0:T(8,128)(2,1)S(1)}, u32[]{:S(2)}, u32[]{:S(2)}) collective-permute-start(bf16[256,256]{1,0:T(8,128)(2,1)} %proj.1), channel_id=1, source_target_pairs={{0,2},{1,3},{2,0},{3,1},{4,6},{5,7},{6,4},{7,5},{8,10},{9,11},{10,... | collective-permute-start | bytes 393224 | tf_op jit(solution)/shard_map/ppermute | solution.py:582
  6.2 10.2 %collective-permute-start.5 = (bf16[256,256]{1,0:T(8,128)(2,1)}, bf16[256,256]{1,0:T(8,128)(2,1)S(1)}, u32[]{:S(2)}, u32[]{:S(2)}) collective-permute-start(bf16[256,256]{1,0:T(8,128)(2,1)} %proj.1), channel_id=1, source_target_pairs={{0,4},{1,5},{2,6},{3,7},{4,0},{5,1},{6,2},{7,3},{8,12},{9,13},{10,... | collective-permute-start | bytes 393224 | tf_op jit(solution)/shard_map/ppermute | solution.py:582
  7.6 11.5 %collective-permute-start.6 = (bf16[256,256]{1,0:T(8,128)(2,1)}, bf16[256,256]{1,0:T(8,128)(2,1)S(1)}, u32[]{:S(2)}, u32[]{:S(2)}) collective-permute-start(bf16[256,256]{1,0:T(8,128)(2,1)} %proj.1), channel_id=1, source_target_pairs={{0,6},{1,7},{2,4},{3,5},{4,2},{5,3},{6,0},{7,1},{8,14},{9,15},{10,... | collective-permute-start | bytes 393224 | tf_op jit(solution)/shard_map/ppermute | solution.py:582
  11.5 9.3 %collective-permute-start.7 = (bf16[128,512]{1,0:T(8,128)(2,1)S(1)}, bf16[128,512]{1,0:T(8,128)(2,1)S(1)}, u32[]{:S(2)}, u32[]{:S(2)}) collective-permute-start(bf16[128,512]{1,0:T(8,128)(2,1)S(1)} %half_of.2), channel_id=1, source_target_pairs={{0,2},{1,3},{2,0},{3,1},{4,6},{5,7},{6,4},{7,5},{8,10},{9,11},{10,... | collective-permute-start | bytes 393224 | tf_op jit(solution)/shard_map/ppermute | solution.py:582
  13.6 7.2 %collective-permute-start.8 = (bf16[128,512]{1,0:T(8,128)(2,1)S(1)}, bf16[128,512]{1,0:T(8,128)(2,1)S(1)}, u32[]{:S(2)}, u32[]{:S(2)}) collective-permute-start(bf16[128,512]{1,0:T(8,128)(2,1)S(1)} %half_of.3), channel_id=1, source_target_pairs={{0,4},{1,5},{2,6},{3,7},{4,0},{5,1},{6,2},{7,3},{8,12},{9,13},{10,... | collective-permute-start | bytes 393224 | tf_op jit(solution)/shard_map/ppermute | solution.py:582
  21.5 1.2 %collective-permute-start.9 = (f32[40,128]{1,0:T(8,128)S(1)}, f32[40,128]{1,0:T(8,128)S(1)}, u32[]{:S(2)}, u32[]{:S(2)}) collective-permute-start(f32[40,128]{1,0:T(8,128)S(1)} %get-tuple-element.47), channel_id=1, source_target_pairs={{0,1},{1,0},{2,3},{3,2},{4,5},{5,4},{6,7},{7,6},{8,9},{9,8},{10,11... | collective-permute-start | bytes 61448 | tf_op jit(solution)/shard_map/ppermute | solution.py:582
  22.7 4.7 %collective-permute-start.10 = (f32[40,128]{1,0:T(8,128)S(1)}, f32[40,128]{1,0:T(8,128)S(1)}, u32[]{:S(2)}, u32[]{:S(2)}) collective-permute-start(f32[40,128]{1,0:T(8,128)S(1)} %sum_arrays.1.refs_0_), channel_id=1, source_target_pairs={{0,16},{8,24},{16,0},{24,8},{1,17},{9,25},{17,1},{25,9},{2,18},{10... | collective-permute-start | bytes 61448 | tf_op jit(solution)/shard_map/ppermute | solution.py:582
  25.3 5.6 %collective-permute-start.11 = (f32[40,128]{1,0:T(8,128)S(1)}, f32[40,128]{1,0:T(8,128)S(1)}, u32[]{:S(2)}, u32[]{:S(2)}) collective-permute-start(f32[40,128]{1,0:T(8,128)S(1)} %sum_arrays.1.refs_0_), channel_id=1, source_target_pairs={{0,24},{8,16},{16,8},{24,0},{1,25},{9,17},{17,9},{25,1},{2,26},{10... | collective-permute-start | bytes 61448 | tf_op jit(solution)/shard_map/ppermute | solution.py:582
  26.7 4.2 %collective-permute-start.12 = (f32[40,128]{1,0:T(8,128)S(1)}, f32[40,128]{1,0:T(8,128)S(1)}, u32[]{:S(2)}, u32[]{:S(2)}) collective-permute-start(f32[40,128]{1,0:T(8,128)S(1)} %sum_arrays.1.refs_0_), channel_id=1, source_target_pairs={{0,8},{8,0},{16,24},{24,16},{1,9},{9,1},{17,25},{25,17},{2,10},{10... | collective-permute-start | bytes 61448 | tf_op jit(solution)/shard_map/ppermute | solution.py:582
  33.0 6.6 %collective-permute-start.18 = (bf16[144,512]{1,0:T(8,128)(2,1)S(1)}, bf16[144,512]{1,0:T(8,128)(2,1)S(1)}, u32[]{:S(2)}, u32[]{:S(2)}) collective-permute-start(bf16[144,512]{1,0:T(8,128)(2,1)S(1)} %get-tuple-element.63.refs_12_), channel_id=1, source_target_pairs={{0,2},{1,3},{2,0},{3,1},{4,6},{5,7},{6,4},{7,5},{8,10},{9,11},{10,... | collective-permute-start | bytes 442376 | tf_op jit(solution)/shard_map/ppermute | solution.py:582
  34.6 8.9 %collective-permute-start.19 = (bf16[144,512]{1,0:T(8,128)(2,1)S(1)}, bf16[144,512]{1,0:T(8,128)(2,1)S(1)}, u32[]{:S(2)}, u32[]{:S(2)}) collective-permute-start(bf16[144,512]{1,0:T(8,128)(2,1)S(1)} %get-tuple-element.64.refs_13_), channel_id=1, source_target_pairs={{0,4},{1,5},{2,6},{3,7},{4,0},{5,1},{6,2},{7,3},{8,12},{9,13},{10,... | collective-permute-start | bytes 442376 | tf_op jit(solution)/shard_map/ppermute | solution.py:582
  35.1 8.4 %collective-permute-start.20 = (bf16[144,512]{1,0:T(8,128)(2,1)S(1)}, bf16[144,512]{1,0:T(8,128)(2,1)S(1)}, u32[]{:S(2)}, u32[]{:S(2)}) collective-permute-start(bf16[144,512]{1,0:T(8,128)(2,1)S(1)} %get-tuple-element.65.refs_14_), channel_id=1, source_target_pairs={{0,6},{1,7},{2,4},{3,5},{4,2},{5,3},{6,0},{7,1},{8,14},{9,15},{10,... | collective-permute-start | bytes 442376 | tf_op jit(solution)/shard_map/ppermute | solution.py:582
  37.4 8.6 %collective-permute-start.13 = (bf16[144,512]{1,0:T(8,128)(2,1)S(1)}, bf16[144,512]{1,0:T(8,128)(2,1)S(1)}, u32[]{:S(2)}, u32[]{:S(2)}) collective-permute-start(bf16[144,512]{1,0:T(8,128)(2,1)S(1)} %get-tuple-element.66.refs_4_), channel_id=1, source_target_pairs={{0,2},{1,3},{2,0},{3,1},{4,6},{5,7},{6,4},{7,5},{8,10},{9,11},{10,... | collective-permute-start | bytes 442376 | tf_op jit(solution)/shard_map/ppermute | solution.py:582
  38.9 9.6 %collective-permute-start.14 = (bf16[144,512]{1,0:T(8,128)(2,1)S(1)}, bf16[144,512]{1,0:T(8,128)(2,1)S(1)}, u32[]{:S(2)}, u32[]{:S(2)}) collective-permute-start(bf16[144,512]{1,0:T(8,128)(2,1)S(1)} %get-tuple-element.67.refs_5_), channel_id=1, source_target_pairs={{0,4},{1,5},{2,6},{3,7},{4,0},{5,1},{6,2},{7,3},{8,12},{9,13},{10,... | collective-permute-start | bytes 442376 | tf_op jit(solution)/shard_map/ppermute | solution.py:582
  39.7 8.9 %collective-permute-start.15 = (bf16[144,512]{1,0:T(8,128)(2,1)S(1)}, bf16[144,512]{1,0:T(8,128)(2,1)S(1)}, u32[]{:S(2)}, u32[]{:S(2)}) collective-permute-start(bf16[144,512]{1,0:T(8,128)(2,1)S(1)} %get-tuple-element.68.refs_6_), channel_id=1, source_target_pairs={{0,6},{1,7},{2,4},{3,5},{4,2},{5,3},{6,0},{7,1},{8,14},{9,15},{10,... | collective-permute-start | bytes 442376 | tf_op jit(solution)/shard_map/ppermute | solution.py:582
  43.6 5.1 %collective-permute-start.21 = (bf16[64,512]{1,0:T(8,128)(2,1)S(1)}, bf16[64,512]{1,0:T(8,128)(2,1)S(1)}, u32[]{:S(2)}, u32[]{:S(2)}) collective-permute-start(bf16[64,512]{1,0:T(8,128)(2,1)S(1)} %get-tuple-element.71), channel_id=1, source_target_pairs={{0,8},{8,0},{16,24},{24,16},{1,9},{9,1},{17,25},{25,17},{2,10},{10... | collective-permute-start | bytes 196616 | tf_op jit(solution)/shard_map/ppermute | solution.py:582
  48.6 6.1 %collective-permute-start.16 = (bf16[128,512]{1,0:T(8,128)(2,1)S(1)}, bf16[128,512]{1,0:T(8,128)(2,1)S(1)}, u32[]{:S(2)}, u32[]{:S(2)}) collective-permute-start(bf16[128,512]{1,0:T(8,128)(2,1)S(1)} %get-tuple-element.69.mine), channel_id=1, source_target_pairs={{0,8},{8,0},{16,24},{24,16},{1,9},{9,1},{17,25},{25,17},{2,10},{10... | collective-permute-start | bytes 393224 | tf_op jit(solution)/shard_map/ppermute | solution.py:582
  48.7 6.2 %collective-permute-start.22 = (bf16[96,512]{1,0:T(8,128)(2,1)S(1)}, bf16[96,512]{1,0:T(8,128)(2,1)S(1)}, u32[]{:S(2)}, u32[]{:S(2)}) collective-permute-start(bf16[96,512]{1,0:T(8,128)(2,1)S(1)} %merge_slabs.4.mine.refs_0_), channel_id=1, source_target_pairs={{0,16},{8,24},{16,0},{24,8},{1,17},{9,25},{17,1},{25,9},{2,18},{10... | collective-permute-start | bytes 294920 | tf_op jit(solution)/shard_map/ppermute | solution.py:582
  54.7 6.5 %collective-permute-start.17 = (bf16[128,512]{1,0:T(8,128)(2,1)S(1)}, bf16[128,512]{1,0:T(8,128)(2,1)S(1)}, u32[]{:S(2)}, u32[]{:S(2)}) collective-permute-start(bf16[128,512]{1,0:T(8,128)(2,1)S(1)} %merge_slabs.3.refs_2_.last_mine), channel_id=1, source_target_pairs={{0,16},{8,24},{16,0},{24,8},{1,17},{9,25},{17,1},{25,9},{2,18},{10... | collective-permute-start | bytes 393224 | tf_op jit(solution)/shard_map/ppermute | solution.py:582
  55.0 6.8 %collective-permute-start.23 = (bf16[128,512]{1,0:T(8,128)(2,1)S(1)}, bf16[128,512]{1,0:T(8,128)(2,1)S(1)}, u32[]{:S(2)}, u32[]{:S(2)}) collective-permute-start(bf16[128,512]{1,0:T(8,128)(2,1)S(1)} %merge_slabs.5.mine), channel_id=1, source_target_pairs={{0,8},{8,0},{16,24},{24,16},{1,9},{9,1},{17,25},{25,17},{2,10},{10... | collective-permute-start | bytes 393224 | tf_op jit(solution)/shard_map/ppermute | solution.py:582
  57.4 1.2 %collective-permute-start.24 = (bf16[48,512]{1,0:T(8,128)(2,1)S(1)}, bf16[48,512]{1,0:T(8,128)(2,1)S(1)}, u32[]{:S(2)}, u32[]{:S(2)}) collective-permute-start(bf16[48,512]{1,0:T(8,128)(2,1)S(1)} %get-tuple-element.73.refs_0_), channel_id=1, source_target_pairs={{0,1},{1,0},{2,3},{3,2},{4,5},{5,4},{6,7},{7,6},{8,9},{9,8},{10,11... | collective-permute-start | bytes 147464 | tf_op jit(solution)/shard_map/ppermute | solution.py:582

commit v7 on v6

--- a/solution.py
+++ b/solution.py
@@ -451,7 +451,7 @@
 
 
 def collect_halves_kernel(start, rows, own, pooled, odd, *refs):
-    msgs, (keep, send, slab_ref) = refs[:-3], refs[-3:]
+    msgs, (keep, send, slab_ref) = [refs[(2, 0, 1).index(i)] for i in range(len(refs) - 3)], refs[-3:]
     width, half = own.shape[1], rows // 2
     total = own[start : start + rows]
     for msg in msgs:
@@ -486,7 +486,7 @@
         functools.partial(collect_halves_kernel, start, rows),
         [((half, width), BF), ((half, width), BF), ((slab_rows, width), BF)],
         "collect_terms",
-        *(own, pooled, odd, *msgs),
+        *(own, pooled, odd, *[msgs[i] for i in (2, 0, 1)]),
     )
     first = small_call(
         functools.partial(add_and_append_kernel, half, 1),
@@ -635,7 +635,7 @@
     total, tails = collect_grads(own, received[1], parts[1])
     if slabs == 4:
         merged = merge(parts[1][1], total, swap(total, "dp", 1))
-        mine, other = sum_by_halves(own, blocks[0][2], odd, received[0], parts[0], (), (merged,))
+        mine, other = sum_by_halves(own, blocks[0][2], odd, received[0], parts[0], (total,), (merged,))
         pieces = [mine, other, merged, swap(merged, "dp", 2)]
         order, above = [0, 2, 1, 3], parts[0][1] // 2
     else:

time: 63.3 us -> 62.9 us (level)
  transfers between devices with their start and end apart: 25 -> 25, of which waited for: 14 -> 16; matrix products, arithmetic and copies ran while one was open for 0% -> 0% of each run, Pallas kernels for 10% -> 10%
where the time goes in v7:
time: 62.9 us; the launch traced here: 62.7 us
  starting transfers between devices  28.8 us (46%)
  waiting for transfers between devices  22.5 us (36%)
  Pallas kernels  10.6 us (17%)
  between operations  0.77 us (1%)
    ppermute x25, starting transfers between devices, swap(): return lax.ppermute(x, axis, [(i, i ^ bit) for i in range(size)])  28.8 us
    ppermute x25, waiting for transfers between devices, swap(): return lax.ppermute(x, axis, [(i, i ^ bit) for i in range(size)])  22.5 us
    pallas_call x3, Pallas kernels, forward_call(): pl.pallas_call(kernel, in_specs=in_specs, out_specs=[vspec()] * len(shape...  5.42 us
    pallas_call x3, Pallas kernels, backward(): pl.pallas_call(functools.partial(backward_kernel, len(blocks), images, pa...  2.27 us
    pallas_call x9, Pallas kernels, small_call(): pl.pallas_call(kernel, in_specs=[vspec()] * len(arrays) + [pl.BlockSpec(m...  1.62 us
    pallas_call x1, Pallas kernels, hsic(): pl.pallas_call(functools.partial(hsic_kernel, slabs, images, groups), in_...  1.33 us
  transfers between devices with their start and end apart: 25, of which 16 were waited for; matrix products, arithmetic and copies ran while one was open for 0% of the time, Pallas kernels for 10%

profile of v7, /device:TPU:0, one launch (start us, length us, event | category | flops | bytes accessed | tf_op | source)
XLA Modules:
  0.0 62.7 jit_solution(9230129415279721585)
XLA Ops:
  0.6 0.5 collective-permute-start.1
  1.1 0.1 collective-permute-start
  1.2 2.9 %collective-permute-start.3 = (bf16[256,512]{1,0:T(8,128)(2,1)}, bf16[256,512]{1,0:T(8,128)(2,1)S(1)}, u32[]{:S(2)}, u32[]{:S(2)}) collective-permute-start(bf16[256,512]{1,0:T(8,128)(2,1)} %conv.1), channel_id=1, source_target_pairs={{0,4},{1,5},{2,6},{3,7},{4,0},{5,1},{6,2},{7,3},{8,12},{9,13},{10,... | collective-permute-start | bytes 786440 | tf_op jit(solution)/shard_map/ppermute | solution.py:582
  4.2 1.5 %collective-permute-start.2 = (bf16[256,512]{1,0:T(8,128)(2,1)}, bf16[256,512]{1,0:T(8,128)(2,1)S(1)}, u32[]{:S(2)}, u32[]{:S(2)}) collective-permute-start(bf16[256,512]{1,0:T(8,128)(2,1)} %conv.1), channel_id=1, source_target_pairs={{0,2},{1,3},{2,0},{3,1},{4,6},{5,7},{6,4},{7,5},{8,10},{9,11},{10,... | collective-permute-start | bytes 786440 | tf_op jit(solution)/shard_map/ppermute | solution.py:582
  5.7 0.5 collective-permute-start.4
  6.2 0.0 collective-permute-done.f_sib
  6.2 1.4 %collective-permute-start.5 = (bf16[256,256]{1,0:T(8,128)(2,1)}, bf16[256,256]{1,0:T(8,128)(2,1)S(1)}, u32[]{:S(2)}, u32[]{:S(2)}) collective-permute-start(bf16[256,256]{1,0:T(8,128)(2,1)} %proj.1), channel_id=1, source_target_pairs={{0,4},{1,5},{2,6},{3,7},{4,0},{5,1},{6,2},{7,3},{8,12},{9,13},{10,... | collective-permute-start | bytes 393224 | tf_op jit(solution)/shard_map/ppermute | solution.py:582
  7.6 0.0 collective-permute-done.1.s_sib
  7.6 1.6 %collective-permute-start.6 = (bf16[256,256]{1,0:T(8,128)(2,1)}, bf16[256,256]{1,0:T(8,128)(2,1)S(1)}, u32[]{:S(2)}, u32[]{:S(2)}) collective-permute-start(bf16[256,256]{1,0:T(8,128)(2,1)} %proj.1), channel_id=1, source_target_pairs={{0,6},{1,7},{2,4},{3,5},{4,2},{5,3},{6,0},{7,1},{8,14},{9,15},{10,... | collective-permute-start | bytes 393224 | tf_op jit(solution)/shard_map/ppermute | solution.py:582
  9.2 2.0 %forward_first.1 = (bf16[392,256]{1,0:T(8,128)(2,1)S(1)}, bf16[392,256]{1,0:T(8,128)(2,1)S(1)}, bf16[16,256]{1,0:T(8,128)(2,1)S(1)}, f32[16,256]{1,0:T(8,128)S(1...) custom-call(s32[1]{0:T(128)} %bitcast.1.index_ref, ...), custom_call_target="tpu_custom_call" | custom-call | flops 822083584 | bytes 802816 | tf_op jit(solution)/shard_map/forward_first/pallas_call | solution.py:171
  11.2 0.3 collective-permute-done.3.refs_1_.x
  11.5 2.1 %collective-permute-start.7 = (bf16[128,512]{1,0:T(8,128)(2,1)S(1)}, bf16[128,512]{1,0:T(8,128)(2,1)S(1)}, u32[]{:S(2)}, u32[]{:S(2)}) collective-permute-start(bf16[128,512]{1,0:T(8,128)(2,1)S(1)} %half_of.2), channel_id=1, source_target_pairs={{0,2},{1,3},{2,0},{3,1},{4,6},{5,7},{6,4},{7,5},{8,10},{9,11},{10,... | collective-permute-start | bytes 393224 | tf_op jit(solution)/shard_map/ppermute | solution.py:582
  13.6 0.0 collective-permute-done.2.refs_0_.x
  13.6 1.6 %collective-permute-start.8 = (bf16[128,512]{1,0:T(8,128)(2,1)S(1)}, bf16[128,512]{1,0:T(8,128)(2,1)S(1)}, u32[]{:S(2)}, u32[]{:S(2)}) collective-permute-start(bf16[128,512]{1,0:T(8,128)(2,1)S(1)} %half_of.3), channel_id=1, source_target_pairs={{0,4},{1,5},{2,6},{3,7},{4,0},{5,1},{6,2},{7,3},{8,12},{9,13},{10,... | collective-permute-start | bytes 393224 | tf_op jit(solution)/shard_map/ppermute | solution.py:582
  15.2 1.2 %collective-permute-done.4.refs_2_.refs_3_ = bf16[256,256]{1,0:T(8,128)(2,1)S(1)} collective-permute-done((bf16[256,256]{1,0:T(8,128)(2,1)}, bf16[256,256]{1,0:T(8,128)(2,1)S(1)}, u32[]{:S(2)}, u32[]{:S(2)}) %collective-permute-start.4) | collective-permute-done | bytes 131104 | tf_op jit(solution)/shard_map/ppermute | solution.py:582
  16.4 0.0 collective-permute-done.5.refs_3_.refs_7_
  16.4 2.7 %forward_middle.1 = (bf16[392,256]{1,0:T(8,128)(2,1)S(1)}, bf16[392,256]{1,0:T(8,128)(2,1)S(1)}, bf16[16,256]{1,0:T(8,128)(2,1)S(1)}, bf16[392,256]{1,0:T(8,128)...) custom-call(s32[1]{0:T(128)} %bitcast.1.index_ref, ...), custom_call_target="tpu_custom_call" | custom-call | flops 1644167168 | bytes 1605632 | tf_op jit(solution)/shard_map/forward_middle/pallas_call | solution.py:171
  19.1 0.0 collective-permute-done.6.proj.refs_11_
  19.1 1.7 %collective-permute-done.7.refs_0_ = bf16[128,512]{1,0:T(8,128)(2,1)S(1)} collective-permute-done((bf16[128,512]{1,0:T(8,128)(2,1)S(1)}, bf16[128,512]{1,0:T(8,128)(2,1)S(1)}, u32[]{:S(2)}, u32[]{:S(2)}) %collective-permute-start.7) | collective-permute-done | bytes 131104 | tf_op jit(solution)/shard_map/ppermute | solution.py:582
  20.8 0.0 collective-permute-done.8.refs_1_
  20.8 0.7 %forward_last.1 = (bf16[392,256]{1,0:T(8,128)(2,1)S(1)}, bf16[392,256]{1,0:T(8,128)(2,1)S(1)}, bf16[16,256]{1,0:T(8,128)(2,1)S(1)}, f32[40,128]{1,0:T(8,128)S(1)}, f32[40,128]{1,0:T(8,128)S(1)}) custom-call(bf16[392,512]{1,0:T(8,128)(2,1)S(1)} %get-tuple-element.40.f_own, bf16[392,512]{1,0:T(8,128)(2,1)S(1)} %collective-permute-done.f_sib, ...), custom_call_target="tpu_custom_call" | custom-call | flops 822083584 | bytes 802816 | tf_op jit(solution)/shard_map/forward_last/pallas_call | solution.py:171
  21.5 0.0 collective-permute-start.9
  21.5 1.2 %collective-permute-done.9.refs_1_ = f32[40,128]{1,0:T(8,128)S(1)} collective-permute-done((f32[40,128]{1,0:T(8,128)S(1)}, f32[40,128]{1,0:T(8,128)S(1)}, u32[]{:S(2)}, u32[]{:S(2)}) %collective-permute-start.9) | collective-permute-done | bytes 20512 | tf_op jit(solution)/shard_map/ppermute | solution.py:582
  22.7 2.6 %collective-permute-start.10 = (f32[40,128]{1,0:T(8,128)S(1)}, f32[40,128]{1,0:T(8,128)S(1)}, u32[]{:S(2)}, u32[]{:S(2)}) collective-permute-start(f32[40,128]{1,0:T(8,128)S(1)} %sum_arrays.1.refs_0_), channel_id=1, source_target_pairs={{0,16},{8,24},{16,0},{24,8},{1,17},{9,25},{17,1},{25,9},{2,18},{10... | collective-permute-start | bytes 61448 | tf_op jit(solution)/shard_map/ppermute | solution.py:582
  25.3 1.3 %collective-permute-start.11 = (f32[40,128]{1,0:T(8,128)S(1)}, f32[40,128]{1,0:T(8,128)S(1)}, u32[]{:S(2)}, u32[]{:S(2)}) collective-permute-start(f32[40,128]{1,0:T(8,128)S(1)} %sum_arrays.1.refs_0_), channel_id=1, source_target_pairs={{0,24},{8,16},{16,8},{24,0},{1,25},{9,17},{17,9},{25,1},{2,26},{10... | collective-permute-start | bytes 61448 | tf_op jit(solution)/shard_map/ppermute | solution.py:582
  26.7 0.2 collective-permute-start.12
  26.9 0.5 collective-permute-done.10.refs_1_
  27.4 3.5 %collective-permute-done.11.refs_2_ = f32[40,128]{1,0:T(8,128)S(1)} collective-permute-done((f32[40,128]{1,0:T(8,128)S(1)}, f32[40,128]{1,0:T(8,128)S(1)}, u32[]{:S(2)}, u32[]{:S(2)}) %collective-permute-start.11) | collective-permute-done | bytes 20512 | tf_op jit(solution)/shard_map/ppermute | solution.py:582
  30.9 0.0 collective-permute-done.12.refs_3_
  30.9 1.3 %hsic_groups.1 = (f32[4,16,256]{2,1,0:T(8,128)S(1)}, f32[1,1]{1,0:T(1,128)}, f32[8,128]{1,0:T(8,128)S(1)}) custom-call(s32[1]{0:T(128)} %bitcast.place_ref, f32[40,128]{1,0:T(8,128)S(1)} %sum_arrays.1.refs_0_, f32[40,128]{1,0:T(8,128)S(1)} %collective-permute-done.10.refs_1_, f32[40,128]{1,0:T(8,128)S(1)} %collective-permute-done.11.refs_2_, ...), custom_call_target="tpu_custom_call" | custom-call | flops 1000000000 | tf_op jit(solution)/shard_map/hsic_groups/pallas_call | solution.py:305
  32.3 0.8 %backward_blocks.3 = (bf16[144,512]{1,0:T(8,128)(2,1)S(1)}, bf16[144,512]{1,0:T(8,128)(2,1)S(1)}, bf16[144,512]{1,0:T(8,128)(2,1)S(1)}) custom-call(bf16[392,512]{1,0:T(8,128)(2,1)S(1)} %get-tuple-element.40.f_own, bf16[392,512]{1,0:T(8,128)(2,1)S(1)} %collective-permute-done.f_sib, f32[4,16,256]{2,1,0:T(8,128)S(1)} %get-tuple-element.48.ge_ref.own_ge, ...), custom_call_target="tpu_custom_call" | custom-call | flops 1233125376 | bytes 602112 | tf_op jit(solution)/shard_map/backward_blocks/pallas_call | solution.py:354
  33.0 1.5 %collective-permute-start.18 = (bf16[144,512]{1,0:T(8,128)(2,1)S(1)}, bf16[144,512]{1,0:T(8,128)(2,1)S(1)}, u32[]{:S(2)}, u32[]{:S(2)}) collective-permute-start(bf16[144,512]{1,0:T(8,128)(2,1)S(1)} %get-tuple-element.65.refs_14_), channel_id=1, source_target_pairs={{0,6},{1,7},{2,4},{3,5},{4,2},{5,3},{6,0},{7,1},{8,14},{9,15},{10,... | collective-permute-start | bytes 442376 | tf_op jit(solution)/shard_map/ppermute | solution.py:582
  34.5 0.5 collective-permute-start.19
  35.1 1.5 %collective-permute-start.20 = (bf16[144,512]{1,0:T(8,128)(2,1)S(1)}, bf16[144,512]{1,0:T(8,128)(2,1)S(1)}, u32[]{:S(2)}, u32[]{:S(2)}) collective-permute-start(bf16[144,512]{1,0:T(8,128)(2,1)S(1)} %get-tuple-element.64.refs_13_), channel_id=1, source_target_pairs={{0,4},{1,5},{2,6},{3,7},{4,0},{5,1},{6,2},{7,3},{8,12},{9,13},{10,... | collective-permute-start | bytes 442376 | tf_op jit(solution)/shard_map/ppermute | solution.py:582
  36.6 0.8 %backward_blocks.4 = (bf16[144,512]{1,0:T(8,128)(2,1)S(1)}, bf16[144,512]{1,0:T(8,128)(2,1)S(1)}, bf16[144,512]{1,0:T(8,128)(2,1)S(1)}) custom-call(bf16[392,512]{1,0:T(8,128)(2,1)S(1)} %get-tuple-element.40.f_own, bf16[392,512]{1,0:T(8,128)(2,1)S(1)} %collective-permute-done.f_sib, f32[4,16,256]{2,1,0:T(8,128)S(1)} %get-tuple-element.48.ge_ref.own_ge, ...), custom_call_target="tpu_custom_call" | custom-call | flops 1233125376 | bytes 602112 | tf_op jit(solution)/shard_map/backward_blocks/pallas_call | solution.py:354
  37.4 1.6 %collective-permute-start.13 = (bf16[144,512]{1,0:T(8,128)(2,1)S(1)}, bf16[144,512]{1,0:T(8,128)(2,1)S(1)}, u32[]{:S(2)}, u32[]{:S(2)}) collective-permute-start(bf16[144,512]{1,0:T(8,128)(2,1)S(1)} %get-tuple-element.66.refs_4_), channel_id=1, source_target_pairs={{0,2},{1,3},{2,0},{3,1},{4,6},{5,7},{6,4},{7,5},{8,10},{9,11},{10,... | collective-permute-start | bytes 442376 | tf_op jit(solution)/shard_map/ppermute | solution.py:582
  38.9 0.5 collective-permute-start.14
  39.5 1.3 %collective-permute-done.18.refs_0_ = bf16[144,512]{1,0:T(8,128)(2,1)S(1)} collective-permute-done((bf16[144,512]{1,0:T(8,128)(2,1)S(1)}, bf16[144,512]{1,0:T(8,128)(2,1)S(1)}, u32[]{:S(2)}, u32[]{:S(2)}) %collective-permute-start.18) | collective-permute-done | bytes 147488 | tf_op jit(solution)/shard_map/ppermute | solution.py:582
  40.8 1.4 %collective-permute-start.15 = (bf16[144,512]{1,0:T(8,128)(2,1)S(1)}, bf16[144,512]{1,0:T(8,128)(2,1)S(1)}, u32[]{:S(2)}, u32[]{:S(2)}) collective-permute-start(bf16[144,512]{1,0:T(8,128)(2,1)S(1)} %get-tuple-element.68.refs_6_), channel_id=1, source_target_pairs={{0,6},{1,7},{2,4},{3,5},{4,2},{5,3},{6,0},{7,1},{8,14},{9,15},{10,... | collective-permute-start | bytes 442376 | tf_op jit(solution)/shard_map/ppermute | solution.py:582
  42.2 0.7 %backward_blocks.5.own = f32[256,512]{1,0:T(8,128)S(1)} custom-call(bf16[392,512]{1,0:T(8,128)(2,1)S(1)} %get-tuple-element.40.f_own, bf16[392,512]{1,0:T(8,128)(2,1)S(1)} %collective-permute-done.f_sib, f32[4,16,256]{2,1,0:T(8,128)S(1)} %get-tuple-element.48.ge_ref.own_ge, bf16[392,256]{1,0:T(8,128)(2,1)S(1)} %get-tuple-element.50.refs_0_, ...), custom_call_target="tpu_custom_call" | custom-call | flops 822083584 | bytes 401408 | tf_op jit(solution)/shard_map/backward_blocks/pallas_call | solution.py:354
  42.9 0.1 collective-permute-done.19.refs_1_
  43.0 0.4 collective-permute-done.20.refs_2_
  43.4 0.1 collect_terms.3
  43.5 0.1 collective-permute-start.21
  43.5 1.9 %collective-permute-done.13.refs_0_ = bf16[144,512]{1,0:T(8,128)(2,1)S(1)} collective-permute-done((bf16[144,512]{1,0:T(8,128)(2,1)S(1)}, bf16[144,512]{1,0:T(8,128)(2,1)S(1)}, u32[]{:S(2)}, u32[]{:S(2)}) %collective-permute-start.13) | collective-permute-done | bytes 147488 | tf_op jit(solution)/shard_map/ppermute | solution.py:582
  45.4 1.0 %collective-permute-done.14.refs_1_ = bf16[144,512]{1,0:T(8,128)(2,1)S(1)} collective-permute-done((bf16[144,512]{1,0:T(8,128)(2,1)S(1)}, bf16[144,512]{1,0:T(8,128)(2,1)S(1)}, u32[]{:S(2)}, u32[]{:S(2)}) %collective-permute-start.14) | collective-permute-done | bytes 147488 | tf_op jit(solution)/shard_map/ppermute | solution.py:582
  46.4 1.6 %collective-permute-done.15.refs_2_ = bf16[144,512]{1,0:T(8,128)(2,1)S(1)} collective-permute-done((bf16[144,512]{1,0:T(8,128)(2,1)S(1)}, bf16[144,512]{1,0:T(8,128)(2,1)S(1)}, u32[]{:S(2)}, u32[]{:S(2)}) %collective-permute-start.15) | collective-permute-done | bytes 147488 | tf_op jit(solution)/shard_map/ppermute | solution.py:582
  48.0 0.1 collect_terms.2
  48.0 0.1 collective-permute-start.16
  48.1 0.0 collective-permute-done.21.other
  48.2 2.6 %collective-permute-start.22 = (bf16[96,512]{1,0:T(8,128)(2,1)S(1)}, bf16[96,512]{1,0:T(8,128)(2,1)S(1)}, u32[]{:S(2)}, u32[]{:S(2)}) collective-permute-start(bf16[96,512]{1,0:T(8,128)(2,1)S(1)} %merge_slabs.4.mine.refs_0_), channel_id=1, source_target_pairs={{0,16},{8,24},{16,0},{24,8},{1,17},{9,25},{17,1},{25,9},{2,18},{10... | collective-permute-start | bytes 294920 | tf_op jit(solution)/shard_map/ppermute | solution.py:582
  50.8 3.5 %collective-permute-done.16.other = bf16[128,512]{1,0:T(8,128)(2,1)S(1)} collective-permute-done((bf16[128,512]{1,0:T(8,128)(2,1)S(1)}, bf16[128,512]{1,0:T(8,128)(2,1)S(1)}, u32[]{:S(2)}, u32[]{:S(2)}) %collective-permute-start.16) | collective-permute-done | bytes 131104 | tf_op jit(solution)/shard_map/ppermute | solution.py:582
  54.4 0.1 collective-permute-start.17
  54.4 0.0 collective-permute-done.22.other.refs_1_
  54.5 2.5 %collective-permute-start.23 = (bf16[128,512]{1,0:T(8,128)(2,1)S(1)}, bf16[128,512]{1,0:T(8,128)(2,1)S(1)}, u32[]{:S(2)}, u32[]{:S(2)}) collective-permute-start(bf16[128,512]{1,0:T(8,128)(2,1)S(1)} %merge_slabs.5.mine), channel_id=1, source_target_pairs={{0,8},{8,0},{16,24},{24,16},{1,9},{9,1},{17,25},{25,17},{2,10},{10... | collective-permute-start | bytes 393224 | tf_op jit(solution)/shard_map/ppermute | solution.py:582
  57.0 0.0 collective-permute-start.24
  57.0 1.2 %collective-permute-done.24.refs_1_ = bf16[48,512]{1,0:T(8,128)(2,1)S(1)} collective-permute-done((bf16[48,512]{1,0:T(8,128)(2,1)S(1)}, bf16[48,512]{1,0:T(8,128)(2,1)S(1)}, u32[]{:S(2)}, u32[]{:S(2)}) %collective-permute-start.24) | collective-permute-done | bytes 49184 | tf_op jit(solution)/shard_map/ppermute | solution.py:582
  58.2 2.4 %collective-permute-done.17.last_other = bf16[128,512]{1,0:T(8,128)(2,1)S(1)} collective-permute-done((bf16[128,512]{1,0:T(8,128)(2,1)S(1)}, bf16[128,512]{1,0:T(8,128)(2,1)S(1)}, u32[]{:S(2)}, u32[]{:S(2)}) %collective-permute-start.17) | collective-permute-done | bytes 131104 | tf_op jit(solution)/shard_map/ppermute | solution.py:582
  60.6 0.7 %collective-permute-done.23.other = bf16[128,512]{1,0:T(8,128)(2,1)S(1)} collective-permute-done((bf16[128,512]{1,0:T(8,128)(2,1)S(1)}, bf16[128,512]{1,0:T(8,128)(2,1)S(1)}, u32[]{:S(2)}, u32[]{:S(2)}) %collective-permute-start.23) | collective-permute-done | bytes 131104 | tf_op jit(solution)/shard_map/ppermute | solution.py:582
  61.3 1.4 %last_sums.1 = (f32[256,512]{1,0:T(8,128)}, f32[256,256]{1,0:T(8,128)}) custom-call(f32[4,16,256]{2,1,0:T(8,128)S(1)} %get-tuple-element.48.ge_ref.own_ge, f32[8,128]{1,0:T(8,128)S(1)} %get-tuple-element.49.odd, bf16[128,512]{1,0:T(8,128)(2,1)S(1)} %merge_slabs.3.refs_2_.last_mine, bf16[128,512]{1,0:T(8,128)(2,1)S(1)} %collective-permute-done.17.last_other, ...), custom_call_target="tpu_custom_call" | custom-call | tf_op jit(solution)/shard_map/last_sums/pallas_call | solution.py:370
  (6 shorter events, 0.1 us)
Async XLA Ops:
  0.6 6.9 %collective-permute-start.1 = (bf16[392,2048]{1,0:T(8,128)(2,1)}, bf16[392,2048]{1,0:T(8,128)(2,1)}, u32[]{:S(2)}, u32[]{:S(2)}) collective-permute-start(bf16[392,2048]{1,0:T(8,128)(2,1)} %s_own.3), channel_id=1, source_target_pairs={{0,1},{1,0},{2,3},{3,2},{4,5},{5,4},{6,7},{7,6},{8,9},{9,8},{10,11... | collective-permute-start | bytes 4816904 | tf_op jit(solution)/shard_map/ppermute | solution.py:582
  1.1 5.1 %collective-permute-start = (bf16[392,512]{1,0:T(8,128)(2,1)}, bf16[392,512]{1,0:T(8,128)(2,1)S(1)}, u32[]{:S(2)}, u32[]{:S(2)}) collective-permute-start(bf16[392,512]{1,0:T(8,128)(2,1)} %f_own.1), channel_id=1, source_target_pairs={{0,1},{1,0},{2,3},{3,2},{4,5},{5,4},{6,7},{7,6},{8,9},{9,8},{10,11... | collective-permute-start | bytes 1204232 | tf_op jit(solution)/shard_map/ppermute | solution.py:582
  1.2 10.3 %collective-permute-start.3 = (bf16[256,512]{1,0:T(8,128)(2,1)}, bf16[256,512]{1,0:T(8,128)(2,1)S(1)}, u32[]{:S(2)}, u32[]{:S(2)}) collective-permute-start(bf16[256,512]{1,0:T(8,128)(2,1)} %conv.1), channel_id=1, source_target_pairs={{0,4},{1,5},{2,6},{3,7},{4,0},{5,1},{6,2},{7,3},{8,12},{9,13},{10,... | collective-permute-start | bytes 786440 | tf_op jit(solution)/shard_map/ppermute | solution.py:582
  4.2 9.4 %collective-permute-start.2 = (bf16[256,512]{1,0:T(8,128)(2,1)}, bf16[256,512]{1,0:T(8,128)(2,1)S(1)}, u32[]{:S(2)}, u32[]{:S(2)}) collective-permute-start(bf16[256,512]{1,0:T(8,128)(2,1)} %conv.1), channel_id=1, source_target_pairs={{0,2},{1,3},{2,0},{3,1},{4,6},{5,7},{6,4},{7,5},{8,10},{9,11},{10,... | collective-permute-start | bytes 786440 | tf_op jit(solution)/shard_map/ppermute | solution.py:582
  5.7 10.7 %collective-permute-start.4 = (bf16[256,256]{1,0:T(8,128)(2,1)}, bf16[256,256]{1,0:T(8,128)(2,1)S(1)}, u32[]{:S(2)}, u32[]{:S(2)}) collective-permute-start(bf16[256,256]{1,0:T(8,128)(2,1)} %proj.1), channel_id=1, source_target_pairs={{0,2},{1,3},{2,0},{3,1},{4,6},{5,7},{6,4},{7,5},{8,10},{9,11},{10,... | collective-permute-start | bytes 393224 | tf_op jit(solution)/shard_map/ppermute | solution.py:582
  6.2 10.2 %collective-permute-start.5 = (bf16[256,256]{1,0:T(8,128)(2,1)}, bf16[256,256]{1,0:T(8,128)(2,1)S(1)}, u32[]{:S(2)}, u32[]{:S(2)}) collective-permute-start(bf16[256,256]{1,0:T(8,128)(2,1)} %proj.1), channel_id=1, source_target_pairs={{0,4},{1,5},{2,6},{3,7},{4,0},{5,1},{6,2},{7,3},{8,12},{9,13},{10,... | collective-permute-start | bytes 393224 | tf_op jit(solution)/shard_map/ppermute | solution.py:582
  7.6 11.5 %collective-permute-start.6 = (bf16[256,256]{1,0:T(8,128)(2,1)}, bf16[256,256]{1,0:T(8,128)(2,1)S(1)}, u32[]{:S(2)}, u32[]{:S(2)}) collective-permute-start(bf16[256,256]{1,0:T(8,128)(2,1)} %proj.1), channel_id=1, source_target_pairs={{0,6},{1,7},{2,4},{3,5},{4,2},{5,3},{6,0},{7,1},{8,14},{9,15},{10,... | collective-permute-start | bytes 393224 | tf_op jit(solution)/shard_map/ppermute | solution.py:582
  11.5 9.3 %collective-permute-start.7 = (bf16[128,512]{1,0:T(8,128)(2,1)S(1)}, bf16[128,512]{1,0:T(8,128)(2,1)S(1)}, u32[]{:S(2)}, u32[]{:S(2)}) collective-permute-start(bf16[128,512]{1,0:T(8,128)(2,1)S(1)} %half_of.2), channel_id=1, source_target_pairs={{0,2},{1,3},{2,0},{3,1},{4,6},{5,7},{6,4},{7,5},{8,10},{9,11},{10,... | collective-permute-start | bytes 393224 | tf_op jit(solution)/shard_map/ppermute | solution.py:582
  13.6 7.2 %collective-permute-start.8 = (bf16[128,512]{1,0:T(8,128)(2,1)S(1)}, bf16[128,512]{1,0:T(8,128)(2,1)S(1)}, u32[]{:S(2)}, u32[]{:S(2)}) collective-permute-start(bf16[128,512]{1,0:T(8,128)(2,1)S(1)} %half_of.3), channel_id=1, source_target_pairs={{0,4},{1,5},{2,6},{3,7},{4,0},{5,1},{6,2},{7,3},{8,12},{9,13},{10,... | collective-permute-start | bytes 393224 | tf_op jit(solution)/shard_map/ppermute | solution.py:582
  21.5 1.2 %collective-permute-start.9 = (f32[40,128]{1,0:T(8,128)S(1)}, f32[40,128]{1,0:T(8,128)S(1)}, u32[]{:S(2)}, u32[]{:S(2)}) collective-permute-start(f32[40,128]{1,0:T(8,128)S(1)} %get-tuple-element.47), channel_id=1, source_target_pairs={{0,1},{1,0},{2,3},{3,2},{4,5},{5,4},{6,7},{7,6},{8,9},{9,8},{10,11... | collective-permute-start | bytes 61448 | tf_op jit(solution)/shard_map/ppermute | solution.py:582
  22.7 4.7 %collective-permute-start.10 = (f32[40,128]{1,0:T(8,128)S(1)}, f32[40,128]{1,0:T(8,128)S(1)}, u32[]{:S(2)}, u32[]{:S(2)}) collective-permute-start(f32[40,128]{1,0:T(8,128)S(1)} %sum_arrays.1.refs_0_), channel_id=1, source_target_pairs={{0,16},{8,24},{16,0},{24,8},{1,17},{9,25},{17,1},{25,9},{2,18},{10... | collective-permute-start | bytes 61448 | tf_op jit(solution)/shard_map/ppermute | solution.py:582
  25.3 5.6 %collective-permute-start.11 = (f32[40,128]{1,0:T(8,128)S(1)}, f32[40,128]{1,0:T(8,128)S(1)}, u32[]{:S(2)}, u32[]{:S(2)}) collective-permute-start(f32[40,128]{1,0:T(8,128)S(1)} %sum_arrays.1.refs_0_), channel_id=1, source_target_pairs={{0,24},{8,16},{16,8},{24,0},{1,25},{9,17},{17,9},{25,1},{2,26},{10... | collective-permute-start | bytes 61448 | tf_op jit(solution)/shard_map/ppermute | solution.py:582
  26.7 4.2 %collective-permute-start.12 = (f32[40,128]{1,0:T(8,128)S(1)}, f32[40,128]{1,0:T(8,128)S(1)}, u32[]{:S(2)}, u32[]{:S(2)}) collective-permute-start(f32[40,128]{1,0:T(8,128)S(1)} %sum_arrays.1.refs_0_), channel_id=1, source_target_pairs={{0,8},{8,0},{16,24},{24,16},{1,9},{9,1},{17,25},{25,17},{2,10},{10... | collective-permute-start | bytes 61448 | tf_op jit(solution)/shard_map/ppermute | solution.py:582
  33.0 7.8 %collective-permute-start.18 = (bf16[144,512]{1,0:T(8,128)(2,1)S(1)}, bf16[144,512]{1,0:T(8,128)(2,1)S(1)}, u32[]{:S(2)}, u32[]{:S(2)}) collective-permute-start(bf16[144,512]{1,0:T(8,128)(2,1)S(1)} %get-tuple-element.65.refs_14_), channel_id=1, source_target_pairs={{0,6},{1,7},{2,4},{3,5},{4,2},{5,3},{6,0},{7,1},{8,14},{9,15},{10,... | collective-permute-start | bytes 442376 | tf_op jit(solution)/shard_map/ppermute | solution.py:582
  34.5 8.5 %collective-permute-start.19 = (bf16[144,512]{1,0:T(8,128)(2,1)S(1)}, bf16[144,512]{1,0:T(8,128)(2,1)S(1)}, u32[]{:S(2)}, u32[]{:S(2)}) collective-permute-start(bf16[144,512]{1,0:T(8,128)(2,1)S(1)} %get-tuple-element.63.refs_12_), channel_id=1, source_target_pairs={{0,2},{1,3},{2,0},{3,1},{4,6},{5,7},{6,4},{7,5},{8,10},{9,11},{10,... | collective-permute-start | bytes 442376 | tf_op jit(solution)/shard_map/ppermute | solution.py:582
  35.1 8.3 %collective-permute-start.20 = (bf16[144,512]{1,0:T(8,128)(2,1)S(1)}, bf16[144,512]{1,0:T(8,128)(2,1)S(1)}, u32[]{:S(2)}, u32[]{:S(2)}) collective-permute-start(bf16[144,512]{1,0:T(8,128)(2,1)S(1)} %get-tuple-element.64.refs_13_), channel_id=1, source_target_pairs={{0,4},{1,5},{2,6},{3,7},{4,0},{5,1},{6,2},{7,3},{8,12},{9,13},{10,... | collective-permute-start | bytes 442376 | tf_op jit(solution)/shard_map/ppermute | solution.py:582
  37.4 8.0 %collective-permute-start.13 = (bf16[144,512]{1,0:T(8,128)(2,1)S(1)}, bf16[144,512]{1,0:T(8,128)(2,1)S(1)}, u32[]{:S(2)}, u32[]{:S(2)}) collective-permute-start(bf16[144,512]{1,0:T(8,128)(2,1)S(1)} %get-tuple-element.66.refs_4_), channel_id=1, source_target_pairs={{0,2},{1,3},{2,0},{3,1},{4,6},{5,7},{6,4},{7,5},{8,10},{9,11},{10,... | collective-permute-start | bytes 442376 | tf_op jit(solution)/shard_map/ppermute | solution.py:582
  38.9 7.5 %collective-permute-start.14 = (bf16[144,512]{1,0:T(8,128)(2,1)S(1)}, bf16[144,512]{1,0:T(8,128)(2,1)S(1)}, u32[]{:S(2)}, u32[]{:S(2)}) collective-permute-start(bf16[144,512]{1,0:T(8,128)(2,1)S(1)} %get-tuple-element.67.refs_5_), channel_id=1, source_target_pairs={{0,4},{1,5},{2,6},{3,7},{4,0},{5,1},{6,2},{7,3},{8,12},{9,13},{10,... | collective-permute-start | bytes 442376 | tf_op jit(solution)/shard_map/ppermute | solution.py:582
  40.8 7.2 %collective-permute-start.15 = (bf16[144,512]{1,0:T(8,128)(2,1)S(1)}, bf16[144,512]{1,0:T(8,128)(2,1)S(1)}, u32[]{:S(2)}, u32[]{:S(2)}) collective-permute-start(bf16[144,512]{1,0:T(8,128)(2,1)S(1)} %get-tuple-element.68.refs_6_), channel_id=1, source_target_pairs={{0,6},{1,7},{2,4},{3,5},{4,2},{5,3},{6,0},{7,1},{8,14},{9,15},{10,... | collective-permute-start | bytes 442376 | tf_op jit(solution)/shard_map/ppermute | solution.py:582
  43.5 4.7 %collective-permute-start.21 = (bf16[64,512]{1,0:T(8,128)(2,1)S(1)}, bf16[64,512]{1,0:T(8,128)(2,1)S(1)}, u32[]{:S(2)}, u32[]{:S(2)}) collective-permute-start(bf16[64,512]{1,0:T(8,128)(2,1)S(1)} %get-tuple-element.71), channel_id=1, source_target_pairs={{0,8},{8,0},{16,24},{24,16},{1,9},{9,1},{17,25},{25,17},{2,10},{10... | collective-permute-start | bytes 196616 | tf_op jit(solution)/shard_map/ppermute | solution.py:582
  48.0 6.3 %collective-permute-start.16 = (bf16[128,512]{1,0:T(8,128)(2,1)S(1)}, bf16[128,512]{1,0:T(8,128)(2,1)S(1)}, u32[]{:S(2)}, u32[]{:S(2)}) collective-permute-start(bf16[128,512]{1,0:T(8,128)(2,1)S(1)} %get-tuple-element.69.mine.refs_1_), channel_id=1, source_target_pairs={{0,8},{8,0},{16,24},{24,16},{1,9},{9,1},{17,25},{25,17},{2,10},{10... | collective-permute-start | bytes 393224 | tf_op jit(solution)/shard_map/ppermute | solution.py:582
  48.2 6.3 %collective-permute-start.22 = (bf16[96,512]{1,0:T(8,128)(2,1)S(1)}, bf16[96,512]{1,0:T(8,128)(2,1)S(1)}, u32[]{:S(2)}, u32[]{:S(2)}) collective-permute-start(bf16[96,512]{1,0:T(8,128)(2,1)S(1)} %merge_slabs.4.mine.refs_0_), channel_id=1, source_target_pairs={{0,16},{8,24},{16,0},{24,8},{1,17},{9,25},{17,1},{25,9},{2,18},{10... | collective-permute-start | bytes 294920 | tf_op jit(solution)/shard_map/ppermute | solution.py:582
  54.4 6.3 %collective-permute-start.17 = (bf16[128,512]{1,0:T(8,128)(2,1)S(1)}, bf16[128,512]{1,0:T(8,128)(2,1)S(1)}, u32[]{:S(2)}, u32[]{:S(2)}) collective-permute-start(bf16[128,512]{1,0:T(8,128)(2,1)S(1)} %merge_slabs.3.refs_2_.last_mine), channel_id=1, source_target_pairs={{0,16},{8,24},{16,0},{24,8},{1,17},{9,25},{17,1},{25,9},{2,18},{10... | collective-permute-start | bytes 393224 | tf_op jit(solution)/shard_map/ppermute | solution.py:582
  54.5 6.9 %collective-permute-start.23 = (bf16[128,512]{1,0:T(8,128)(2,1)S(1)}, bf16[128,512]{1,0:T(8,128)(2,1)S(1)}, u32[]{:S(2)}, u32[]{:S(2)}) collective-permute-start(bf16[128,512]{1,0:T(8,128)(2,1)S(1)} %merge_slabs.5.mine), channel_id=1, source_target_pairs={{0,8},{8,0},{16,24},{24,16},{1,9},{9,1},{17,25},{25,17},{2,10},{10... | collective-permute-start | bytes 393224 | tf_op jit(solution)/shard_map/ppermute | solution.py:582
  57.0 1.2 %collective-permute-start.24 = (bf16[48,512]{1,0:T(8,128)(2,1)S(1)}, bf16[48,512]{1,0:T(8,128)(2,1)S(1)}, u32[]{:S(2)}, u32[]{:S(2)}) collective-permute-start(bf16[48,512]{1,0:T(8,128)(2,1)S(1)} %get-tuple-element.73.refs_0_), channel_id=1, source_target_pairs={{0,1},{1,0},{2,3},{3,2},{4,5},{5,4},{6,7},{7,6},{8,9},{9,8},{10,11... | collective-permute-start | bytes 147464 | tf_op jit(solution)/shard_map/ppermute | solution.py:582

commit v8 on v7

--- a/solution.py
+++ b/solution.py
@@ -247,12 +247,10 @@
     return outs[:3], outs[3], outs[4]
 
 
-def group_terms(z, partner, groups):
+def group_terms(z, inner, partner, groups):
     count = z.shape[0]
-    z = z - jnp.mean(z, axis=0, keepdims=True)
     squares = jnp.sum(z * z, axis=1, keepdims=True)
     spread = 2.0 * jnp.mean(squares)
-    inner = lax.dot_general(z, z, NT, precision=lax.Precision.HIGHEST, preferred_element_type=F32)
     row = lax.broadcasted_iota(jnp.int32, (count, count), 0)
     col = lax.broadcasted_iota(jnp.int32, (count, count), 1)
     across = jnp.sum(jnp.where(row == col, squares, 0.0), axis=0, keepdims=True)
@@ -289,9 +287,14 @@
                 z_ref[g, at, t * 128 : (t + 1) * 128] = block[row : row + images]
         p_ref[at] = block[2 * tiles * images :]
     high_lane = lax.broadcasted_iota(jnp.int32, p_ref.shape, 1) >= 64
+    count = slabs * images
+    both = [z_ref[g] - jnp.mean(z_ref[g], axis=0, keepdims=True) for g in (0, 1)]
+    pair = jnp.concatenate(both, axis=0)
+    inner = lax.dot_general(pair, pair, NT, precision=lax.Precision.HIGHEST, preferred_element_type=F32)
     for g in (0, 1):
+        part = inner[g * count : (g + 1) * count, g * count : (g + 1) * count]
         partner = jnp.max(jnp.where(high_lane == (g == 1), p_ref[...], -1.0), axis=1, keepdims=True)
-        loss, grad = group_terms(z_ref[g], partner, groups)
+        loss, grad = group_terms(both[g], part, partner, groups)
         if g == 0:
             loss_ref[...] = loss
         g_ref[g] = grad

time: 62.9 us -> 62.6 us (level)
  no operation moved by 1% of the time
where the time goes in v8:
time: 62.6 us; the launch traced here: 62.5 us
  starting transfers between devices  28.8 us (46%)
  waiting for transfers between devices  22.5 us (36%)
  Pallas kernels  10.4 us (17%)
  between operations  0.77 us (1%)
    ppermute x25, starting transfers between devices, swap(): return lax.ppermute(x, axis, [(i, i ^ bit) for i in range(size)])  28.8 us
    ppermute x25, waiting for transfers between devices, swap(): return lax.ppermute(x, axis, [(i, i ^ bit) for i in range(size)])  22.5 us
    pallas_call x3, Pallas kernels, forward_call(): pl.pallas_call(kernel, in_specs=in_specs, out_specs=[vspec()] * len(shape...  5.42 us
    pallas_call x3, Pallas kernels, backward(): pl.pallas_call(functools.partial(backward_kernel, len(blocks), images, pa...  2.27 us
    pallas_call x9, Pallas kernels, small_call(): pl.pallas_call(kernel, in_specs=[vspec()] * len(arrays) + [pl.BlockSpec(m...  1.62 us
  transfers between devices with their start and end apart: 25, of which 16 were waited for; matrix products, arithmetic and copies ran while one was open for 0% of the time, Pallas kernels for 10%

profile of v8, /device:TPU:0, one launch (start us, length us, event | category | flops | bytes accessed | tf_op | source)
XLA Modules:
  0.0 62.5 jit_solution(9188503751360277596)
XLA Ops:
  0.6 0.5 collective-permute-start.1
  1.1 0.1 collective-permute-start
  1.2 2.9 %collective-permute-start.3 = (bf16[256,512]{1,0:T(8,128)(2,1)}, bf16[256,512]{1,0:T(8,128)(2,1)S(1)}, u32[]{:S(2)}, u32[]{:S(2)}) collective-permute-start(bf16[256,512]{1,0:T(8,128)(2,1)} %conv.1), channel_id=1, source_target_pairs={{0,4},{1,5},{2,6},{3,7},{4,0},{5,1},{6,2},{7,3},{8,12},{9,13},{10,... | collective-permute-start | bytes 786440 | tf_op jit(solution)/shard_map/ppermute | solution.py:585
  4.2 1.5 %collective-permute-start.2 = (bf16[256,512]{1,0:T(8,128)(2,1)}, bf16[256,512]{1,0:T(8,128)(2,1)S(1)}, u32[]{:S(2)}, u32[]{:S(2)}) collective-permute-start(bf16[256,512]{1,0:T(8,128)(2,1)} %conv.1), channel_id=1, source_target_pairs={{0,2},{1,3},{2,0},{3,1},{4,6},{5,7},{6,4},{7,5},{8,10},{9,11},{10,... | collective-permute-start | bytes 786440 | tf_op jit(solution)/shard_map/ppermute | solution.py:585
  5.7 0.5 collective-permute-start.4
  6.2 0.0 collective-permute-done.f_sib
  6.2 1.4 %collective-permute-start.5 = (bf16[256,256]{1,0:T(8,128)(2,1)}, bf16[256,256]{1,0:T(8,128)(2,1)S(1)}, u32[]{:S(2)}, u32[]{:S(2)}) collective-permute-start(bf16[256,256]{1,0:T(8,128)(2,1)} %proj.1), channel_id=1, source_target_pairs={{0,4},{1,5},{2,6},{3,7},{4,0},{5,1},{6,2},{7,3},{8,12},{9,13},{10,... | collective-permute-start | bytes 393224 | tf_op jit(solution)/shard_map/ppermute | solution.py:585
  7.6 0.0 collective-permute-done.1.s_sib
  7.6 1.6 %collective-permute-start.6 = (bf16[256,256]{1,0:T(8,128)(2,1)}, bf16[256,256]{1,0:T(8,128)(2,1)S(1)}, u32[]{:S(2)}, u32[]{:S(2)}) collective-permute-start(bf16[256,256]{1,0:T(8,128)(2,1)} %proj.1), channel_id=1, source_target_pairs={{0,6},{1,7},{2,4},{3,5},{4,2},{5,3},{6,0},{7,1},{8,14},{9,15},{10,... | collective-permute-start | bytes 393224 | tf_op jit(solution)/shard_map/ppermute | solution.py:585
  9.2 2.0 %forward_first.1 = (bf16[392,256]{1,0:T(8,128)(2,1)S(1)}, bf16[392,256]{1,0:T(8,128)(2,1)S(1)}, bf16[16,256]{1,0:T(8,128)(2,1)S(1)}, f32[16,256]{1,0:T(8,128)S(1...) custom-call(s32[1]{0:T(128)} %bitcast.1.index_ref, ...), custom_call_target="tpu_custom_call" | custom-call | flops 822083584 | bytes 802816 | tf_op jit(solution)/shard_map/forward_first/pallas_call | solution.py:171
  11.2 0.3 collective-permute-done.3.refs_1_.x
  11.5 2.1 %collective-permute-start.7 = (bf16[128,512]{1,0:T(8,128)(2,1)S(1)}, bf16[128,512]{1,0:T(8,128)(2,1)S(1)}, u32[]{:S(2)}, u32[]{:S(2)}) collective-permute-start(bf16[128,512]{1,0:T(8,128)(2,1)S(1)} %half_of.2), channel_id=1, source_target_pairs={{0,2},{1,3},{2,0},{3,1},{4,6},{5,7},{6,4},{7,5},{8,10},{9,11},{10,... | collective-permute-start | bytes 393224 | tf_op jit(solution)/shard_map/ppermute | solution.py:585
  13.6 0.0 collective-permute-done.2.refs_0_.x
  13.6 1.6 %collective-permute-start.8 = (bf16[128,512]{1,0:T(8,128)(2,1)S(1)}, bf16[128,512]{1,0:T(8,128)(2,1)S(1)}, u32[]{:S(2)}, u32[]{:S(2)}) collective-permute-start(bf16[128,512]{1,0:T(8,128)(2,1)S(1)} %half_of.3), channel_id=1, source_target_pairs={{0,4},{1,5},{2,6},{3,7},{4,0},{5,1},{6,2},{7,3},{8,12},{9,13},{10,... | collective-permute-start | bytes 393224 | tf_op jit(solution)/shard_map/ppermute | solution.py:585
  15.2 1.2 %collective-permute-done.4.refs_2_.refs_3_ = bf16[256,256]{1,0:T(8,128)(2,1)S(1)} collective-permute-done((bf16[256,256]{1,0:T(8,128)(2,1)}, bf16[256,256]{1,0:T(8,128)(2,1)S(1)}, u32[]{:S(2)}, u32[]{:S(2)}) %collective-permute-start.4) | collective-permute-done | bytes 131104 | tf_op jit(solution)/shard_map/ppermute | solution.py:585
  16.4 0.0 collective-permute-done.5.refs_3_.refs_7_
  16.4 2.7 %forward_middle.1 = (bf16[392,256]{1,0:T(8,128)(2,1)S(1)}, bf16[392,256]{1,0:T(8,128)(2,1)S(1)}, bf16[16,256]{1,0:T(8,128)(2,1)S(1)}, bf16[392,256]{1,0:T(8,128)...) custom-call(s32[1]{0:T(128)} %bitcast.1.index_ref, ...), custom_call_target="tpu_custom_call" | custom-call | flops 1644167168 | bytes 1605632 | tf_op jit(solution)/shard_map/forward_middle/pallas_call | solution.py:171
  19.1 0.0 collective-permute-done.6.proj.refs_11_
  19.1 1.7 %collective-permute-done.7.refs_0_ = bf16[128,512]{1,0:T(8,128)(2,1)S(1)} collective-permute-done((bf16[128,512]{1,0:T(8,128)(2,1)S(1)}, bf16[128,512]{1,0:T(8,128)(2,1)S(1)}, u32[]{:S(2)}, u32[]{:S(2)}) %collective-permute-start.7) | collective-permute-done | bytes 131104 | tf_op jit(solution)/shard_map/ppermute | solution.py:585
  20.8 0.0 collective-permute-done.8.refs_1_
  20.8 0.7 %forward_last.1 = (bf16[392,256]{1,0:T(8,128)(2,1)S(1)}, bf16[392,256]{1,0:T(8,128)(2,1)S(1)}, bf16[16,256]{1,0:T(8,128)(2,1)S(1)}, f32[40,128]{1,0:T(8,128)S(1)}, f32[40,128]{1,0:T(8,128)S(1)}) custom-call(bf16[392,512]{1,0:T(8,128)(2,1)S(1)} %get-tuple-element.40.f_own, bf16[392,512]{1,0:T(8,128)(2,1)S(1)} %collective-permute-done.f_sib, ...), custom_call_target="tpu_custom_call" | custom-call | flops 822083584 | bytes 802816 | tf_op jit(solution)/shard_map/forward_last/pallas_call | solution.py:171
  21.5 0.0 collective-permute-start.9
  21.5 1.2 %collective-permute-done.9.refs_1_ = f32[40,128]{1,0:T(8,128)S(1)} collective-permute-done((f32[40,128]{1,0:T(8,128)S(1)}, f32[40,128]{1,0:T(8,128)S(1)}, u32[]{:S(2)}, u32[]{:S(2)}) %collective-permute-start.9) | collective-permute-done | bytes 20512 | tf_op jit(solution)/shard_map/ppermute | solution.py:585
  22.7 2.6 %collective-permute-start.10 = (f32[40,128]{1,0:T(8,128)S(1)}, f32[40,128]{1,0:T(8,128)S(1)}, u32[]{:S(2)}, u32[]{:S(2)}) collective-permute-start(f32[40,128]{1,0:T(8,128)S(1)} %sum_arrays.1.refs_0_), channel_id=1, source_target_pairs={{0,16},{8,24},{16,0},{24,8},{1,17},{9,25},{17,1},{25,9},{2,18},{10... | collective-permute-start | bytes 61448 | tf_op jit(solution)/shard_map/ppermute | solution.py:585
  25.3 1.3 %collective-permute-start.11 = (f32[40,128]{1,0:T(8,128)S(1)}, f32[40,128]{1,0:T(8,128)S(1)}, u32[]{:S(2)}, u32[]{:S(2)}) collective-permute-start(f32[40,128]{1,0:T(8,128)S(1)} %sum_arrays.1.refs_0_), channel_id=1, source_target_pairs={{0,24},{8,16},{16,8},{24,0},{1,25},{9,17},{17,9},{25,1},{2,26},{10... | collective-permute-start | bytes 61448 | tf_op jit(solution)/shard_map/ppermute | solution.py:585
  26.7 0.2 collective-permute-start.12
  26.9 0.5 collective-permute-done.10.refs_1_
  27.4 3.5 %collective-permute-done.11.refs_2_ = f32[40,128]{1,0:T(8,128)S(1)} collective-permute-done((f32[40,128]{1,0:T(8,128)S(1)}, f32[40,128]{1,0:T(8,128)S(1)}, u32[]{:S(2)}, u32[]{:S(2)}) %collective-permute-start.11) | collective-permute-done | bytes 20512 | tf_op jit(solution)/shard_map/ppermute | solution.py:585
  30.9 0.0 collective-permute-done.12.refs_3_
  30.9 1.1 %hsic_groups.1 = (f32[4,16,256]{2,1,0:T(8,128)S(1)}, f32[1,1]{1,0:T(1,128)}, f32[8,128]{1,0:T(8,128)S(1)}) custom-call(s32[1]{0:T(128)} %bitcast.place_ref, f32[40,128]{1,0:T(8,128)S(1)} %sum_arrays.1.refs_0_, f32[40,128]{1,0:T(8,128)S(1)} %collective-permute-done.10.refs_1_, f32[40,128]{1,0:T(8,128)S(1)} %collective-permute-done.11.refs_2_, ...), custom_call_target="tpu_custom_call" | custom-call | flops 1000000000 | tf_op jit(solution)/shard_map/hsic_groups/pallas_call | solution.py:308
  32.0 0.8 %backward_blocks.3 = (bf16[144,512]{1,0:T(8,128)(2,1)S(1)}, bf16[144,512]{1,0:T(8,128)(2,1)S(1)}, bf16[144,512]{1,0:T(8,128)(2,1)S(1)}) custom-call(bf16[392,512]{1,0:T(8,128)(2,1)S(1)} %get-tuple-element.40.f_own, bf16[392,512]{1,0:T(8,128)(2,1)S(1)} %collective-permute-done.f_sib, f32[4,16,256]{2,1,0:T(8,128)S(1)} %get-tuple-element.48.ge_ref.own_ge, ...), custom_call_target="tpu_custom_call" | custom-call | flops 1233125376 | bytes 602112 | tf_op jit(solution)/shard_map/backward_blocks/pallas_call | solution.py:357
  32.8 1.5 %collective-permute-start.18 = (bf16[144,512]{1,0:T(8,128)(2,1)S(1)}, bf16[144,512]{1,0:T(8,128)(2,1)S(1)}, u32[]{:S(2)}, u32[]{:S(2)}) collective-permute-start(bf16[144,512]{1,0:T(8,128)(2,1)S(1)} %get-tuple-element.65.refs_14_), channel_id=1, source_target_pairs={{0,6},{1,7},{2,4},{3,5},{4,2},{5,3},{6,0},{7,1},{8,14},{9,15},{10,... | collective-permute-start | bytes 442376 | tf_op jit(solution)/shard_map/ppermute | solution.py:585
  34.3 0.5 collective-permute-start.19
  34.9 1.5 %collective-permute-start.20 = (bf16[144,512]{1,0:T(8,128)(2,1)S(1)}, bf16[144,512]{1,0:T(8,128)(2,1)S(1)}, u32[]{:S(2)}, u32[]{:S(2)}) collective-permute-start(bf16[144,512]{1,0:T(8,128)(2,1)S(1)} %get-tuple-element.64.refs_13_), channel_id=1, source_target_pairs={{0,4},{1,5},{2,6},{3,7},{4,0},{5,1},{6,2},{7,3},{8,12},{9,13},{10,... | collective-permute-start | bytes 442376 | tf_op jit(solution)/shard_map/ppermute | solution.py:585
  36.4 0.8 %backward_blocks.4 = (bf16[144,512]{1,0:T(8,128)(2,1)S(1)}, bf16[144,512]{1,0:T(8,128)(2,1)S(1)}, bf16[144,512]{1,0:T(8,128)(2,1)S(1)}) custom-call(bf16[392,512]{1,0:T(8,128)(2,1)S(1)} %get-tuple-element.40.f_own, bf16[392,512]{1,0:T(8,128)(2,1)S(1)} %collective-permute-done.f_sib, f32[4,16,256]{2,1,0:T(8,128)S(1)} %get-tuple-element.48.ge_ref.own_ge, ...), custom_call_target="tpu_custom_call" | custom-call | flops 1233125376 | bytes 602112 | tf_op jit(solution)/shard_map/backward_blocks/pallas_call | solution.py:357
  37.2 1.6 %collective-permute-start.13 = (bf16[144,512]{1,0:T(8,128)(2,1)S(1)}, bf16[144,512]{1,0:T(8,128)(2,1)S(1)}, u32[]{:S(2)}, u32[]{:S(2)}) collective-permute-start(bf16[144,512]{1,0:T(8,128)(2,1)S(1)} %get-tuple-element.66.refs_4_), channel_id=1, source_target_pairs={{0,2},{1,3},{2,0},{3,1},{4,6},{5,7},{6,4},{7,5},{8,10},{9,11},{10,... | collective-permute-start | bytes 442376 | tf_op jit(solution)/shard_map/ppermute | solution.py:585
  38.7 0.5 collective-permute-start.14
  39.2 1.3 %collective-permute-done.18.refs_0_ = bf16[144,512]{1,0:T(8,128)(2,1)S(1)} collective-permute-done((bf16[144,512]{1,0:T(8,128)(2,1)S(1)}, bf16[144,512]{1,0:T(8,128)(2,1)S(1)}, u32[]{:S(2)}, u32[]{:S(2)}) %collective-permute-start.18) | collective-permute-done | bytes 147488 | tf_op jit(solution)/shard_map/ppermute | solution.py:585
  40.6 1.4 %collective-permute-start.15 = (bf16[144,512]{1,0:T(8,128)(2,1)S(1)}, bf16[144,512]{1,0:T(8,128)(2,1)S(1)}, u32[]{:S(2)}, u32[]{:S(2)}) collective-permute-start(bf16[144,512]{1,0:T(8,128)(2,1)S(1)} %get-tuple-element.68.refs_6_), channel_id=1, source_target_pairs={{0,6},{1,7},{2,4},{3,5},{4,2},{5,3},{6,0},{7,1},{8,14},{9,15},{10,... | collective-permute-start | bytes 442376 | tf_op jit(solution)/shard_map/ppermute | solution.py:585
  42.0 0.7 %backward_blocks.5.own = f32[256,512]{1,0:T(8,128)S(1)} custom-call(bf16[392,512]{1,0:T(8,128)(2,1)S(1)} %get-tuple-element.40.f_own, bf16[392,512]{1,0:T(8,128)(2,1)S(1)} %collective-permute-done.f_sib, f32[4,16,256]{2,1,0:T(8,128)S(1)} %get-tuple-element.48.ge_ref.own_ge, bf16[392,256]{1,0:T(8,128)(2,1)S(1)} %get-tuple-element.50.refs_0_, ...), custom_call_target="tpu_custom_call" | custom-call | flops 822083584 | bytes 401408 | tf_op jit(solution)/shard_map/backward_blocks/pallas_call | solution.py:357
  42.7 0.1 collective-permute-done.19.refs_1_
  42.8 0.4 collective-permute-done.20.refs_2_
  43.2 0.1 collect_terms.3
  43.3 0.1 collective-permute-start.21
  43.3 1.9 %collective-permute-done.13.refs_0_ = bf16[144,512]{1,0:T(8,128)(2,1)S(1)} collective-permute-done((bf16[144,512]{1,0:T(8,128)(2,1)S(1)}, bf16[144,512]{1,0:T(8,128)(2,1)S(1)}, u32[]{:S(2)}, u32[]{:S(2)}) %collective-permute-start.13) | collective-permute-done | bytes 147488 | tf_op jit(solution)/shard_map/ppermute | solution.py:585
  45.2 1.0 %collective-permute-done.14.refs_1_ = bf16[144,512]{1,0:T(8,128)(2,1)S(1)} collective-permute-done((bf16[144,512]{1,0:T(8,128)(2,1)S(1)}, bf16[144,512]{1,0:T(8,128)(2,1)S(1)}, u32[]{:S(2)}, u32[]{:S(2)}) %collective-permute-start.14) | collective-permute-done | bytes 147488 | tf_op jit(solution)/shard_map/ppermute | solution.py:585
  46.2 1.6 %collective-permute-done.15.refs_2_ = bf16[144,512]{1,0:T(8,128)(2,1)S(1)} collective-permute-done((bf16[144,512]{1,0:T(8,128)(2,1)S(1)}, bf16[144,512]{1,0:T(8,128)(2,1)S(1)}, u32[]{:S(2)}, u32[]{:S(2)}) %collective-permute-start.15) | collective-permute-done | bytes 147488 | tf_op jit(solution)/shard_map/ppermute | solution.py:585
  47.8 0.1 collect_terms.2
  47.8 0.1 collective-permute-start.16
  47.9 0.0 collective-permute-done.21.other
  47.9 2.6 %collective-permute-start.22 = (bf16[96,512]{1,0:T(8,128)(2,1)S(1)}, bf16[96,512]{1,0:T(8,128)(2,1)S(1)}, u32[]{:S(2)}, u32[]{:S(2)}) collective-permute-start(bf16[96,512]{1,0:T(8,128)(2,1)S(1)} %merge_slabs.4.mine.refs_0_), channel_id=1, source_target_pairs={{0,16},{8,24},{16,0},{24,8},{1,17},{9,25},{17,1},{25,9},{2,18},{10... | collective-permute-start | bytes 294920 | tf_op jit(solution)/shard_map/ppermute | solution.py:585
  50.6 3.5 %collective-permute-done.16.other = bf16[128,512]{1,0:T(8,128)(2,1)S(1)} collective-permute-done((bf16[128,512]{1,0:T(8,128)(2,1)S(1)}, bf16[128,512]{1,0:T(8,128)(2,1)S(1)}, u32[]{:S(2)}, u32[]{:S(2)}) %collective-permute-start.16) | collective-permute-done | bytes 131104 | tf_op jit(solution)/shard_map/ppermute | solution.py:585
  54.1 0.1 collective-permute-start.17
  54.2 0.0 collective-permute-done.22.other.refs_1_
  54.2 2.5 %collective-permute-start.23 = (bf16[128,512]{1,0:T(8,128)(2,1)S(1)}, bf16[128,512]{1,0:T(8,128)(2,1)S(1)}, u32[]{:S(2)}, u32[]{:S(2)}) collective-permute-start(bf16[128,512]{1,0:T(8,128)(2,1)S(1)} %merge_slabs.5.mine), channel_id=1, source_target_pairs={{0,8},{8,0},{16,24},{24,16},{1,9},{9,1},{17,25},{25,17},{2,10},{10... | collective-permute-start | bytes 393224 | tf_op jit(solution)/shard_map/ppermute | solution.py:585
  56.8 0.0 collective-permute-start.24
  56.8 1.2 %collective-permute-done.24.refs_1_ = bf16[48,512]{1,0:T(8,128)(2,1)S(1)} collective-permute-done((bf16[48,512]{1,0:T(8,128)(2,1)S(1)}, bf16[48,512]{1,0:T(8,128)(2,1)S(1)}, u32[]{:S(2)}, u32[]{:S(2)}) %collective-permute-start.24) | collective-permute-done | bytes 49184 | tf_op jit(solution)/shard_map/ppermute | solution.py:585
  58.0 2.4 %collective-permute-done.17.last_other = bf16[128,512]{1,0:T(8,128)(2,1)S(1)} collective-permute-done((bf16[128,512]{1,0:T(8,128)(2,1)S(1)}, bf16[128,512]{1,0:T(8,128)(2,1)S(1)}, u32[]{:S(2)}, u32[]{:S(2)}) %collective-permute-start.17) | collective-permute-done | bytes 131104 | tf_op jit(solution)/shard_map/ppermute | solution.py:585
  60.4 0.7 %collective-permute-done.23.other = bf16[128,512]{1,0:T(8,128)(2,1)S(1)} collective-permute-done((bf16[128,512]{1,0:T(8,128)(2,1)S(1)}, bf16[128,512]{1,0:T(8,128)(2,1)S(1)}, u32[]{:S(2)}, u32[]{:S(2)}) %collective-permute-start.23) | collective-permute-done | bytes 131104 | tf_op jit(solution)/shard_map/ppermute | solution.py:585
  61.1 1.4 %last_sums.1 = (f32[256,512]{1,0:T(8,128)}, f32[256,256]{1,0:T(8,128)}) custom-call(f32[4,16,256]{2,1,0:T(8,128)S(1)} %get-tuple-element.48.ge_ref.own_ge, f32[8,128]{1,0:T(8,128)S(1)} %get-tuple-element.49.odd, bf16[128,512]{1,0:T(8,128)(2,1)S(1)} %merge_slabs.3.refs_2_.last_mine, bf16[128,512]{1,0:T(8,128)(2,1)S(1)} %collective-permute-done.17.last_other, ...), custom_call_target="tpu_custom_call" | custom-call | tf_op jit(solution)/shard_map/last_sums/pallas_call | solution.py:373
  (6 shorter events, 0.1 us)
Async XLA Ops:
  0.6 6.9 %collective-permute-start.1 = (bf16[392,2048]{1,0:T(8,128)(2,1)}, bf16[392,2048]{1,0:T(8,128)(2,1)}, u32[]{:S(2)}, u32[]{:S(2)}) collective-permute-start(bf16[392,2048]{1,0:T(8,128)(2,1)} %s_own.3), channel_id=1, source_target_pairs={{0,1},{1,0},{2,3},{3,2},{4,5},{5,4},{6,7},{7,6},{8,9},{9,8},{10,11... | collective-permute-start | bytes 4816904 | tf_op jit(solution)/shard_map/ppermute | solution.py:585
  1.1 5.1 %collective-permute-start = (bf16[392,512]{1,0:T(8,128)(2,1)}, bf16[392,512]{1,0:T(8,128)(2,1)S(1)}, u32[]{:S(2)}, u32[]{:S(2)}) collective-permute-start(bf16[392,512]{1,0:T(8,128)(2,1)} %f_own.1), channel_id=1, source_target_pairs={{0,1},{1,0},{2,3},{3,2},{4,5},{5,4},{6,7},{7,6},{8,9},{9,8},{10,11... | collective-permute-start | bytes 1204232 | tf_op jit(solution)/shard_map/ppermute | solution.py:585
  1.2 10.3 %collective-permute-start.3 = (bf16[256,512]{1,0:T(8,128)(2,1)}, bf16[256,512]{1,0:T(8,128)(2,1)S(1)}, u32[]{:S(2)}, u32[]{:S(2)}) collective-permute-start(bf16[256,512]{1,0:T(8,128)(2,1)} %conv.1), channel_id=1, source_target_pairs={{0,4},{1,5},{2,6},{3,7},{4,0},{5,1},{6,2},{7,3},{8,12},{9,13},{10,... | collective-permute-start | bytes 786440 | tf_op jit(solution)/shard_map/ppermute | solution.py:585
  4.2 9.4 %collective-permute-start.2 = (bf16[256,512]{1,0:T(8,128)(2,1)}, bf16[256,512]{1,0:T(8,128)(2,1)S(1)}, u32[]{:S(2)}, u32[]{:S(2)}) collective-permute-start(bf16[256,512]{1,0:T(8,128)(2,1)} %conv.1), channel_id=1, source_target_pairs={{0,2},{1,3},{2,0},{3,1},{4,6},{5,7},{6,4},{7,5},{8,10},{9,11},{10,... | collective-permute-start | bytes 786440 | tf_op jit(solution)/shard_map/ppermute | solution.py:585
  5.7 10.7 %collective-permute-start.4 = (bf16[256,256]{1,0:T(8,128)(2,1)}, bf16[256,256]{1,0:T(8,128)(2,1)S(1)}, u32[]{:S(2)}, u32[]{:S(2)}) collective-permute-start(bf16[256,256]{1,0:T(8,128)(2,1)} %proj.1), channel_id=1, source_target_pairs={{0,2},{1,3},{2,0},{3,1},{4,6},{5,7},{6,4},{7,5},{8,10},{9,11},{10,... | collective-permute-start | bytes 393224 | tf_op jit(solution)/shard_map/ppermute | solution.py:585
  6.2 10.2 %collective-permute-start.5 = (bf16[256,256]{1,0:T(8,128)(2,1)}, bf16[256,256]{1,0:T(8,128)(2,1)S(1)}, u32[]{:S(2)}, u32[]{:S(2)}) collective-permute-start(bf16[256,256]{1,0:T(8,128)(2,1)} %proj.1), channel_id=1, source_target_pairs={{0,4},{1,5},{2,6},{3,7},{4,0},{5,1},{6,2},{7,3},{8,12},{9,13},{10,... | collective-permute-start | bytes 393224 | tf_op jit(solution)/shard_map/ppermute | solution.py:585
  7.6 11.5 %collective-permute-start.6 = (bf16[256,256]{1,0:T(8,128)(2,1)}, bf16[256,256]{1,0:T(8,128)(2,1)S(1)}, u32[]{:S(2)}, u32[]{:S(2)}) collective-permute-start(bf16[256,256]{1,0:T(8,128)(2,1)} %proj.1), channel_id=1, source_target_pairs={{0,6},{1,7},{2,4},{3,5},{4,2},{5,3},{6,0},{7,1},{8,14},{9,15},{10,... | collective-permute-start | bytes 393224 | tf_op jit(solution)/shard_map/ppermute | solution.py:585
  11.5 9.3 %collective-permute-start.7 = (bf16[128,512]{1,0:T(8,128)(2,1)S(1)}, bf16[128,512]{1,0:T(8,128)(2,1)S(1)}, u32[]{:S(2)}, u32[]{:S(2)}) collective-permute-start(bf16[128,512]{1,0:T(8,128)(2,1)S(1)} %half_of.2), channel_id=1, source_target_pairs={{0,2},{1,3},{2,0},{3,1},{4,6},{5,7},{6,4},{7,5},{8,10},{9,11},{10,... | collective-permute-start | bytes 393224 | tf_op jit(solution)/shard_map/ppermute | solution.py:585
  13.6 7.2 %collective-permute-start.8 = (bf16[128,512]{1,0:T(8,128)(2,1)S(1)}, bf16[128,512]{1,0:T(8,128)(2,1)S(1)}, u32[]{:S(2)}, u32[]{:S(2)}) collective-permute-start(bf16[128,512]{1,0:T(8,128)(2,1)S(1)} %half_of.3), channel_id=1, source_target_pairs={{0,4},{1,5},{2,6},{3,7},{4,0},{5,1},{6,2},{7,3},{8,12},{9,13},{10,... | collective-permute-start | bytes 393224 | tf_op jit(solution)/shard_map/ppermute | solution.py:585
  21.5 1.2 %collective-permute-start.9 = (f32[40,128]{1,0:T(8,128)S(1)}, f32[40,128]{1,0:T(8,128)S(1)}, u32[]{:S(2)}, u32[]{:S(2)}) collective-permute-start(f32[40,128]{1,0:T(8,128)S(1)} %get-tuple-element.47), channel_id=1, source_target_pairs={{0,1},{1,0},{2,3},{3,2},{4,5},{5,4},{6,7},{7,6},{8,9},{9,8},{10,11... | collective-permute-start | bytes 61448 | tf_op jit(solution)/shard_map/ppermute | solution.py:585
  22.7 4.7 %collective-permute-start.10 = (f32[40,128]{1,0:T(8,128)S(1)}, f32[40,128]{1,0:T(8,128)S(1)}, u32[]{:S(2)}, u32[]{:S(2)}) collective-permute-start(f32[40,128]{1,0:T(8,128)S(1)} %sum_arrays.1.refs_0_), channel_id=1, source_target_pairs={{0,16},{8,24},{16,0},{24,8},{1,17},{9,25},{17,1},{25,9},{2,18},{10... | collective-permute-start | bytes 61448 | tf_op jit(solution)/shard_map/ppermute | solution.py:585
  25.3 5.6 %collective-permute-start.11 = (f32[40,128]{1,0:T(8,128)S(1)}, f32[40,128]{1,0:T(8,128)S(1)}, u32[]{:S(2)}, u32[]{:S(2)}) collective-permute-start(f32[40,128]{1,0:T(8,128)S(1)} %sum_arrays.1.refs_0_), channel_id=1, source_target_pairs={{0,24},{8,16},{16,8},{24,0},{1,25},{9,17},{17,9},{25,1},{2,26},{10... | collective-permute-start | bytes 61448 | tf_op jit(solution)/shard_map/ppermute | solution.py:585
  26.7 4.2 %collective-permute-start.12 = (f32[40,128]{1,0:T(8,128)S(1)}, f32[40,128]{1,0:T(8,128)S(1)}, u32[]{:S(2)}, u32[]{:S(2)}) collective-permute-start(f32[40,128]{1,0:T(8,128)S(1)} %sum_arrays.1.refs_0_), channel_id=1, source_target_pairs={{0,8},{8,0},{16,24},{24,16},{1,9},{9,1},{17,25},{25,17},{2,10},{10... | collective-permute-start | bytes 61448 | tf_op jit(solution)/shard_map/ppermute | solution.py:585
  32.8 7.8 %collective-permute-start.18 = (bf16[144,512]{1,0:T(8,128)(2,1)S(1)}, bf16[144,512]{1,0:T(8,128)(2,1)S(1)}, u32[]{:S(2)}, u32[]{:S(2)}) collective-permute-start(bf16[144,512]{1,0:T(8,128)(2,1)S(1)} %get-tuple-element.65.refs_14_), channel_id=1, source_target_pairs={{0,6},{1,7},{2,4},{3,5},{4,2},{5,3},{6,0},{7,1},{8,14},{9,15},{10,... | collective-permute-start | bytes 442376 | tf_op jit(solution)/shard_map/ppermute | solution.py:585
  34.3 8.4 %collective-permute-start.19 = (bf16[144,512]{1,0:T(8,128)(2,1)S(1)}, bf16[144,512]{1,0:T(8,128)(2,1)S(1)}, u32[]{:S(2)}, u32[]{:S(2)}) collective-permute-start(bf16[144,512]{1,0:T(8,128)(2,1)S(1)} %get-tuple-element.63.refs_12_), channel_id=1, source_target_pairs={{0,2},{1,3},{2,0},{3,1},{4,6},{5,7},{6,4},{7,5},{8,10},{9,11},{10,... | collective-permute-start | bytes 442376 | tf_op jit(solution)/shard_map/ppermute | solution.py:585
  34.9 8.3 %collective-permute-start.20 = (bf16[144,512]{1,0:T(8,128)(2,1)S(1)}, bf16[144,512]{1,0:T(8,128)(2,1)S(1)}, u32[]{:S(2)}, u32[]{:S(2)}) collective-permute-start(bf16[144,512]{1,0:T(8,128)(2,1)S(1)} %get-tuple-element.64.refs_13_), channel_id=1, source_target_pairs={{0,4},{1,5},{2,6},{3,7},{4,0},{5,1},{6,2},{7,3},{8,12},{9,13},{10,... | collective-permute-start | bytes 442376 | tf_op jit(solution)/shard_map/ppermute | solution.py:585
  37.2 8.0 %collective-permute-start.13 = (bf16[144,512]{1,0:T(8,128)(2,1)S(1)}, bf16[144,512]{1,0:T(8,128)(2,1)S(1)}, u32[]{:S(2)}, u32[]{:S(2)}) collective-permute-start(bf16[144,512]{1,0:T(8,128)(2,1)S(1)} %get-tuple-element.66.refs_4_), channel_id=1, source_target_pairs={{0,2},{1,3},{2,0},{3,1},{4,6},{5,7},{6,4},{7,5},{8,10},{9,11},{10,... | collective-permute-start | bytes 442376 | tf_op jit(solution)/shard_map/ppermute | solution.py:585
  38.7 7.4 %collective-permute-start.14 = (bf16[144,512]{1,0:T(8,128)(2,1)S(1)}, bf16[144,512]{1,0:T(8,128)(2,1)S(1)}, u32[]{:S(2)}, u32[]{:S(2)}) collective-permute-start(bf16[144,512]{1,0:T(8,128)(2,1)S(1)} %get-tuple-element.67.refs_5_), channel_id=1, source_target_pairs={{0,4},{1,5},{2,6},{3,7},{4,0},{5,1},{6,2},{7,3},{8,12},{9,13},{10,... | collective-permute-start | bytes 442376 | tf_op jit(solution)/shard_map/ppermute | solution.py:585
  40.6 7.2 %collective-permute-start.15 = (bf16[144,512]{1,0:T(8,128)(2,1)S(1)}, bf16[144,512]{1,0:T(8,128)(2,1)S(1)}, u32[]{:S(2)}, u32[]{:S(2)}) collective-permute-start(bf16[144,512]{1,0:T(8,128)(2,1)S(1)} %get-tuple-element.68.refs_6_), channel_id=1, source_target_pairs={{0,6},{1,7},{2,4},{3,5},{4,2},{5,3},{6,0},{7,1},{8,14},{9,15},{10,... | collective-permute-start | bytes 442376 | tf_op jit(solution)/shard_map/ppermute | solution.py:585
  43.3 4.6 %collective-permute-start.21 = (bf16[64,512]{1,0:T(8,128)(2,1)S(1)}, bf16[64,512]{1,0:T(8,128)(2,1)S(1)}, u32[]{:S(2)}, u32[]{:S(2)}) collective-permute-start(bf16[64,512]{1,0:T(8,128)(2,1)S(1)} %get-tuple-element.71), channel_id=1, source_target_pairs={{0,8},{8,0},{16,24},{24,16},{1,9},{9,1},{17,25},{25,17},{2,10},{10... | collective-permute-start | bytes 196616 | tf_op jit(solution)/shard_map/ppermute | solution.py:585
  47.8 6.3 %collective-permute-start.16 = (bf16[128,512]{1,0:T(8,128)(2,1)S(1)}, bf16[128,512]{1,0:T(8,128)(2,1)S(1)}, u32[]{:S(2)}, u32[]{:S(2)}) collective-permute-start(bf16[128,512]{1,0:T(8,128)(2,1)S(1)} %get-tuple-element.69.mine.refs_1_), channel_id=1, source_target_pairs={{0,8},{8,0},{16,24},{24,16},{1,9},{9,1},{17,25},{25,17},{2,10},{10... | collective-permute-start | bytes 393224 | tf_op jit(solution)/shard_map/ppermute | solution.py:585
  47.9 6.3 %collective-permute-start.22 = (bf16[96,512]{1,0:T(8,128)(2,1)S(1)}, bf16[96,512]{1,0:T(8,128)(2,1)S(1)}, u32[]{:S(2)}, u32[]{:S(2)}) collective-permute-start(bf16[96,512]{1,0:T(8,128)(2,1)S(1)} %merge_slabs.4.mine.refs_0_), channel_id=1, source_target_pairs={{0,16},{8,24},{16,0},{24,8},{1,17},{9,25},{17,1},{25,9},{2,18},{10... | collective-permute-start | bytes 294920 | tf_op jit(solution)/shard_map/ppermute | solution.py:585
  54.1 6.3 %collective-permute-start.17 = (bf16[128,512]{1,0:T(8,128)(2,1)S(1)}, bf16[128,512]{1,0:T(8,128)(2,1)S(1)}, u32[]{:S(2)}, u32[]{:S(2)}) collective-permute-start(bf16[128,512]{1,0:T(8,128)(2,1)S(1)} %merge_slabs.3.refs_2_.last_mine), channel_id=1, source_target_pairs={{0,16},{8,24},{16,0},{24,8},{1,17},{9,25},{17,1},{25,9},{2,18},{10... | collective-permute-start | bytes 393224 | tf_op jit(solution)/shard_map/ppermute | solution.py:585
  54.2 6.9 %collective-permute-start.23 = (bf16[128,512]{1,0:T(8,128)(2,1)S(1)}, bf16[128,512]{1,0:T(8,128)(2,1)S(1)}, u32[]{:S(2)}, u32[]{:S(2)}) collective-permute-start(bf16[128,512]{1,0:T(8,128)(2,1)S(1)} %merge_slabs.5.mine), channel_id=1, source_target_pairs={{0,8},{8,0},{16,24},{24,16},{1,9},{9,1},{17,25},{25,17},{2,10},{10... | collective-permute-start | bytes 393224 | tf_op jit(solution)/shard_map/ppermute | solution.py:585
  56.8 1.2 %collective-permute-start.24 = (bf16[48,512]{1,0:T(8,128)(2,1)S(1)}, bf16[48,512]{1,0:T(8,128)(2,1)S(1)}, u32[]{:S(2)}, u32[]{:S(2)}) collective-permute-start(bf16[48,512]{1,0:T(8,128)(2,1)S(1)} %get-tuple-element.73.refs_0_), channel_id=1, source_target_pairs={{0,1},{1,0},{2,3},{3,2},{4,5},{5,4},{6,7},{7,6},{8,9},{9,8},{10,11... | collective-permute-start | bytes 147464 | tf_op jit(solution)/shard_map/ppermute | solution.py:585

commit v9 on v8

--- a/solution.py
+++ b/solution.py
@@ -630,9 +630,11 @@
     parts = [(0, first_rows), (first_rows, count - first_rows)]
     terms, done = [], ()
     for part, extra in zip(parts, ("pooled", "embed")):
+        if terms:
+            (own,) = backward(feats, ge, blocks[:1], images, (0, count), None, done)
+            done = (own,)
         done = tuple(backward(feats, ge, blocks[1:], images, part, extra, done))
         terms.append(done)
-    (own,) = backward(feats, ge, blocks[:1], images, (0, count), None, done)
 
     received = [[swap(m, "fsdp", 2 * j) for j, m in enumerate(term, 1)] for term in terms]
     total, tails = collect_grads(own, received[1], parts[1])

time: 62.6 us -> 62.6 us (level)
  no operation moved by 1% of the time
where the time goes in v9:
time: 62.6 us; the launch traced here: 62.5 us
  starting transfers between devices  28.5 us (46%)
  waiting for transfers between devices  22.8 us (36%)
  Pallas kernels  10.4 us (17%)
  between operations  0.77 us (1%)
    ppermute x25, starting transfers between devices, swap(): return lax.ppermute(x, axis, [(i, i ^ bit) for i in range(size)])  28.5 us
    ppermute x25, waiting for transfers between devices, swap(): return lax.ppermute(x, axis, [(i, i ^ bit) for i in range(size)])  22.8 us
    pallas_call x3, Pallas kernels, forward_call(): pl.pallas_call(kernel, in_specs=in_specs, out_specs=[vspec()] * len(shape...  5.42 us
    pallas_call x3, Pallas kernels, backward(): pl.pallas_call(functools.partial(backward_kernel, len(blocks), images, pa...  2.27 us
    pallas_call x9, Pallas kernels, small_call(): pl.pallas_call(kernel, in_specs=[vspec()] * len(arrays) + [pl.BlockSpec(m...  1.64 us
  transfers between devices with their start and end apart: 25, of which 16 were waited for; matrix products, arithmetic and copies ran while one was open for 0% of the time, Pallas kernels for 10%

profile of v9, /device:TPU:0, one launch (start us, length us, event | category | flops | bytes accessed | tf_op | source)
XLA Modules:
  0.0 62.5 jit_solution(10938776805068631383)
XLA Ops:
  0.6 0.5 collective-permute-start.1
  1.1 0.1 collective-permute-start
  1.2 2.9 %collective-permute-start.3 = (bf16[256,512]{1,0:T(8,128)(2,1)}, bf16[256,512]{1,0:T(8,128)(2,1)S(1)}, u32[]{:S(2)}, u32[]{:S(2)}) collective-permute-start(bf16[256,512]{1,0:T(8,128)(2,1)} %conv.1), channel_id=1, source_target_pairs={{0,4},{1,5},{2,6},{3,7},{4,0},{5,1},{6,2},{7,3},{8,12},{9,13},{10,... | collective-permute-start | bytes 786440 | tf_op jit(solution)/shard_map/ppermute | solution.py:585
  4.2 1.5 %collective-permute-start.2 = (bf16[256,512]{1,0:T(8,128)(2,1)}, bf16[256,512]{1,0:T(8,128)(2,1)S(1)}, u32[]{:S(2)}, u32[]{:S(2)}) collective-permute-start(bf16[256,512]{1,0:T(8,128)(2,1)} %conv.1), channel_id=1, source_target_pairs={{0,2},{1,3},{2,0},{3,1},{4,6},{5,7},{6,4},{7,5},{8,10},{9,11},{10,... | collective-permute-start | bytes 786440 | tf_op jit(solution)/shard_map/ppermute | solution.py:585
  5.7 0.5 collective-permute-start.4
  6.2 0.0 collective-permute-done.f_sib
  6.2 1.4 %collective-permute-start.5 = (bf16[256,256]{1,0:T(8,128)(2,1)}, bf16[256,256]{1,0:T(8,128)(2,1)S(1)}, u32[]{:S(2)}, u32[]{:S(2)}) collective-permute-start(bf16[256,256]{1,0:T(8,128)(2,1)} %proj.1), channel_id=1, source_target_pairs={{0,4},{1,5},{2,6},{3,7},{4,0},{5,1},{6,2},{7,3},{8,12},{9,13},{10,... | collective-permute-start | bytes 393224 | tf_op jit(solution)/shard_map/ppermute | solution.py:585
  7.6 0.0 collective-permute-done.1.s_sib
  7.6 1.6 %collective-permute-start.6 = (bf16[256,256]{1,0:T(8,128)(2,1)}, bf16[256,256]{1,0:T(8,128)(2,1)S(1)}, u32[]{:S(2)}, u32[]{:S(2)}) collective-permute-start(bf16[256,256]{1,0:T(8,128)(2,1)} %proj.1), channel_id=1, source_target_pairs={{0,6},{1,7},{2,4},{3,5},{4,2},{5,3},{6,0},{7,1},{8,14},{9,15},{10,... | collective-permute-start | bytes 393224 | tf_op jit(solution)/shard_map/ppermute | solution.py:585
  9.2 2.0 %forward_first.1 = (bf16[392,256]{1,0:T(8,128)(2,1)S(1)}, bf16[392,256]{1,0:T(8,128)(2,1)S(1)}, bf16[16,256]{1,0:T(8,128)(2,1)S(1)}, f32[16,256]{1,0:T(8,128)S(1...) custom-call(s32[1]{0:T(128)} %bitcast.1.index_ref, ...), custom_call_target="tpu_custom_call" | custom-call | flops 822083584 | bytes 802816 | tf_op jit(solution)/shard_map/forward_first/pallas_call | solution.py:171
  11.2 0.3 collective-permute-done.3.refs_1_.x
  11.5 2.1 %collective-permute-start.7 = (bf16[128,512]{1,0:T(8,128)(2,1)S(1)}, bf16[128,512]{1,0:T(8,128)(2,1)S(1)}, u32[]{:S(2)}, u32[]{:S(2)}) collective-permute-start(bf16[128,512]{1,0:T(8,128)(2,1)S(1)} %half_of.2), channel_id=1, source_target_pairs={{0,2},{1,3},{2,0},{3,1},{4,6},{5,7},{6,4},{7,5},{8,10},{9,11},{10,... | collective-permute-start | bytes 393224 | tf_op jit(solution)/shard_map/ppermute | solution.py:585
  13.6 0.0 collective-permute-done.2.refs_0_.x
  13.6 1.6 %collective-permute-start.8 = (bf16[128,512]{1,0:T(8,128)(2,1)S(1)}, bf16[128,512]{1,0:T(8,128)(2,1)S(1)}, u32[]{:S(2)}, u32[]{:S(2)}) collective-permute-start(bf16[128,512]{1,0:T(8,128)(2,1)S(1)} %half_of.3), channel_id=1, source_target_pairs={{0,4},{1,5},{2,6},{3,7},{4,0},{5,1},{6,2},{7,3},{8,12},{9,13},{10,... | collective-permute-start | bytes 393224 | tf_op jit(solution)/shard_map/ppermute | solution.py:585
  15.2 1.2 %collective-permute-done.4.refs_2_.refs_3_ = bf16[256,256]{1,0:T(8,128)(2,1)S(1)} collective-permute-done((bf16[256,256]{1,0:T(8,128)(2,1)}, bf16[256,256]{1,0:T(8,128)(2,1)S(1)}, u32[]{:S(2)}, u32[]{:S(2)}) %collective-permute-start.4) | collective-permute-done | bytes 131104 | tf_op jit(solution)/shard_map/ppermute | solution.py:585
  16.4 0.0 collective-permute-done.5.refs_3_.refs_7_
  16.4 2.7 %forward_middle.1 = (bf16[392,256]{1,0:T(8,128)(2,1)S(1)}, bf16[392,256]{1,0:T(8,128)(2,1)S(1)}, bf16[16,256]{1,0:T(8,128)(2,1)S(1)}, bf16[392,256]{1,0:T(8,128)...) custom-call(s32[1]{0:T(128)} %bitcast.1.index_ref, ...), custom_call_target="tpu_custom_call" | custom-call | flops 1644167168 | bytes 1605632 | tf_op jit(solution)/shard_map/forward_middle/pallas_call | solution.py:171
  19.1 0.0 collective-permute-done.6.proj.refs_11_
  19.1 1.7 %collective-permute-done.7.refs_0_ = bf16[128,512]{1,0:T(8,128)(2,1)S(1)} collective-permute-done((bf16[128,512]{1,0:T(8,128)(2,1)S(1)}, bf16[128,512]{1,0:T(8,128)(2,1)S(1)}, u32[]{:S(2)}, u32[]{:S(2)}) %collective-permute-start.7) | collective-permute-done | bytes 131104 | tf_op jit(solution)/shard_map/ppermute | solution.py:585
  20.8 0.0 collective-permute-done.8.refs_1_
  20.8 0.7 %forward_last.1 = (bf16[392,256]{1,0:T(8,128)(2,1)S(1)}, bf16[392,256]{1,0:T(8,128)(2,1)S(1)}, bf16[16,256]{1,0:T(8,128)(2,1)S(1)}, f32[40,128]{1,0:T(8,128)S(1)}, f32[40,128]{1,0:T(8,128)S(1)}) custom-call(bf16[392,512]{1,0:T(8,128)(2,1)S(1)} %get-tuple-element.40.f_own, bf16[392,512]{1,0:T(8,128)(2,1)S(1)} %collective-permute-done.f_sib, ...), custom_call_target="tpu_custom_call" | custom-call | flops 822083584 | bytes 802816 | tf_op jit(solution)/shard_map/forward_last/pallas_call | solution.py:171
  21.5 0.0 collective-permute-start.9
  21.5 1.2 %collective-permute-done.9.refs_1_ = f32[40,128]{1,0:T(8,128)S(1)} collective-permute-done((f32[40,128]{1,0:T(8,128)S(1)}, f32[40,128]{1,0:T(8,128)S(1)}, u32[]{:S(2)}, u32[]{:S(2)}) %collective-permute-start.9) | collective-permute-done | bytes 20512 | tf_op jit(solution)/shard_map/ppermute | solution.py:585
  22.7 2.6 %collective-permute-start.10 = (f32[40,128]{1,0:T(8,128)S(1)}, f32[40,128]{1,0:T(8,128)S(1)}, u32[]{:S(2)}, u32[]{:S(2)}) collective-permute-start(f32[40,128]{1,0:T(8,128)S(1)} %sum_arrays.1.refs_0_), channel_id=1, source_target_pairs={{0,16},{8,24},{16,0},{24,8},{1,17},{9,25},{17,1},{25,9},{2,18},{10... | collective-permute-start | bytes 61448 | tf_op jit(solution)/shard_map/ppermute | solution.py:585
  25.3 1.3 %collective-permute-start.11 = (f32[40,128]{1,0:T(8,128)S(1)}, f32[40,128]{1,0:T(8,128)S(1)}, u32[]{:S(2)}, u32[]{:S(2)}) collective-permute-start(f32[40,128]{1,0:T(8,128)S(1)} %sum_arrays.1.refs_0_), channel_id=1, source_target_pairs={{0,24},{8,16},{16,8},{24,0},{1,25},{9,17},{17,9},{25,1},{2,26},{10... | collective-permute-start | bytes 61448 | tf_op jit(solution)/shard_map/ppermute | solution.py:585
  26.7 0.2 collective-permute-start.12
  26.9 0.5 collective-permute-done.10.refs_1_
  27.4 3.5 %collective-permute-done.11.refs_2_ = f32[40,128]{1,0:T(8,128)S(1)} collective-permute-done((f32[40,128]{1,0:T(8,128)S(1)}, f32[40,128]{1,0:T(8,128)S(1)}, u32[]{:S(2)}, u32[]{:S(2)}) %collective-permute-start.11) | collective-permute-done | bytes 20512 | tf_op jit(solution)/shard_map/ppermute | solution.py:585
  30.9 0.0 collective-permute-done.12.refs_3_
  30.9 1.1 %hsic_groups.1 = (f32[4,16,256]{2,1,0:T(8,128)S(1)}, f32[1,1]{1,0:T(1,128)}, f32[8,128]{1,0:T(8,128)S(1)}) custom-call(s32[1]{0:T(128)} %bitcast.place_ref, f32[40,128]{1,0:T(8,128)S(1)} %sum_arrays.1.refs_0_, f32[40,128]{1,0:T(8,128)S(1)} %collective-permute-done.10.refs_1_, f32[40,128]{1,0:T(8,128)S(1)} %collective-permute-done.11.refs_2_, ...), custom_call_target="tpu_custom_call" | custom-call | flops 1000000000 | tf_op jit(solution)/shard_map/hsic_groups/pallas_call | solution.py:308
  32.0 0.8 %backward_blocks.3 = (bf16[144,512]{1,0:T(8,128)(2,1)S(1)}, bf16[144,512]{1,0:T(8,128)(2,1)S(1)}, bf16[144,512]{1,0:T(8,128)(2,1)S(1)}) custom-call(bf16[392,512]{1,0:T(8,128)(2,1)S(1)} %get-tuple-element.40.f_own, bf16[392,512]{1,0:T(8,128)(2,1)S(1)} %collective-permute-done.f_sib, f32[4,16,256]{2,1,0:T(8,128)S(1)} %get-tuple-element.48.ge_ref.own_ge, ...), custom_call_target="tpu_custom_call" | custom-call | flops 1233125376 | bytes 602112 | tf_op jit(solution)/shard_map/backward_blocks/pallas_call | solution.py:357
  32.8 1.5 %collective-permute-start.18 = (bf16[144,512]{1,0:T(8,128)(2,1)S(1)}, bf16[144,512]{1,0:T(8,128)(2,1)S(1)}, u32[]{:S(2)}, u32[]{:S(2)}) collective-permute-start(bf16[144,512]{1,0:T(8,128)(2,1)S(1)} %get-tuple-element.65.refs_6_), channel_id=1, source_target_pairs={{0,6},{1,7},{2,4},{3,5},{4,2},{5,3},{6,0},{7,1},{8,14},{9,15},{10,... | collective-permute-start | bytes 442376 | tf_op jit(solution)/shard_map/ppermute | solution.py:585
  34.3 0.5 collective-permute-start.19
  34.9 1.5 %collective-permute-start.20 = (bf16[144,512]{1,0:T(8,128)(2,1)S(1)}, bf16[144,512]{1,0:T(8,128)(2,1)S(1)}, u32[]{:S(2)}, u32[]{:S(2)}) collective-permute-start(bf16[144,512]{1,0:T(8,128)(2,1)S(1)} %get-tuple-element.64.refs_5_), channel_id=1, source_target_pairs={{0,4},{1,5},{2,6},{3,7},{4,0},{5,1},{6,2},{7,3},{8,12},{9,13},{10,... | collective-permute-start | bytes 442376 | tf_op jit(solution)/shard_map/ppermute | solution.py:585
  36.4 0.7 %backward_blocks.4.refs_12_.own = f32[256,512]{1,0:T(8,128)S(1)} custom-call(bf16[392,512]{1,0:T(8,128)(2,1)S(1)} %get-tuple-element.40.f_own, bf16[392,512]{1,0:T(8,128)(2,1)S(1)} %collective-permute-done.f_sib, f32[4,16,256]{2,1,0:T(8,128)S(1)} %get-tuple-element.48.ge_ref.own_ge, bf16[392,256]{1,0:T(8,128)(2,1)S(1)} %get-tuple-element.50.refs_0_, ...), custom_call_target="tpu_custom_call" | custom-call | flops 822083584 | bytes 401408 | tf_op jit(solution)/shard_map/backward_blocks/pallas_call | solution.py:357
  37.1 0.8 %backward_blocks.5 = (bf16[144,512]{1,0:T(8,128)(2,1)S(1)}, bf16[144,512]{1,0:T(8,128)(2,1)S(1)}, bf16[144,512]{1,0:T(8,128)(2,1)S(1)}) custom-call(bf16[392,512]{1,0:T(8,128)(2,1)S(1)} %get-tuple-element.40.f_own, bf16[392,512]{1,0:T(8,128)(2,1)S(1)} %collective-permute-done.f_sib, f32[4,16,256]{2,1,0:T(8,128)S(1)} %get-tuple-element.48.ge_ref.own_ge, ...), custom_call_target="tpu_custom_call" | custom-call | flops 1233125376 | bytes 602112 | tf_op jit(solution)/shard_map/backward_blocks/pallas_call | solution.py:357
  37.9 1.5 %collective-permute-start.13 = (bf16[144,512]{1,0:T(8,128)(2,1)S(1)}, bf16[144,512]{1,0:T(8,128)(2,1)S(1)}, u32[]{:S(2)}, u32[]{:S(2)}) collective-permute-start(bf16[144,512]{1,0:T(8,128)(2,1)S(1)} %get-tuple-element.66), channel_id=1, source_target_pairs={{0,2},{1,3},{2,0},{3,1},{4,6},{5,7},{6,4},{7,5},{8,10},{9,11},{10,... | collective-permute-start | bytes 442376 | tf_op jit(solution)/shard_map/ppermute | solution.py:585
  39.4 0.5 collective-permute-start.14
  39.9 0.6 %collective-permute-done.18.refs_0_ = bf16[144,512]{1,0:T(8,128)(2,1)S(1)} collective-permute-done((bf16[144,512]{1,0:T(8,128)(2,1)S(1)}, bf16[144,512]{1,0:T(8,128)(2,1)S(1)}, u32[]{:S(2)}, u32[]{:S(2)}) %collective-permute-start.18) | collective-permute-done | bytes 147488 | tf_op jit(solution)/shard_map/ppermute | solution.py:585
  40.6 1.1 %collective-permute-start.15 = (bf16[144,512]{1,0:T(8,128)(2,1)S(1)}, bf16[144,512]{1,0:T(8,128)(2,1)S(1)}, u32[]{:S(2)}, u32[]{:S(2)}) collective-permute-start(bf16[144,512]{1,0:T(8,128)(2,1)S(1)} %get-tuple-element.68), channel_id=1, source_target_pairs={{0,6},{1,7},{2,4},{3,5},{4,2},{5,3},{6,0},{7,1},{8,14},{9,15},{10,... | collective-permute-start | bytes 442376 | tf_op jit(solution)/shard_map/ppermute | solution.py:585
  41.7 0.8 %collective-permute-done.19.refs_1_ = bf16[144,512]{1,0:T(8,128)(2,1)S(1)} collective-permute-done((bf16[144,512]{1,0:T(8,128)(2,1)S(1)}, bf16[144,512]{1,0:T(8,128)(2,1)S(1)}, u32[]{:S(2)}, u32[]{:S(2)}) %collective-permute-start.19) | collective-permute-done | bytes 147488 | tf_op jit(solution)/shard_map/ppermute | solution.py:585
  42.5 0.7 %collective-permute-done.20.refs_2_ = bf16[144,512]{1,0:T(8,128)(2,1)S(1)} collective-permute-done((bf16[144,512]{1,0:T(8,128)(2,1)S(1)}, bf16[144,512]{1,0:T(8,128)(2,1)S(1)}, u32[]{:S(2)}, u32[]{:S(2)}) %collective-permute-start.20) | collective-permute-done | bytes 147488 | tf_op jit(solution)/shard_map/ppermute | solution.py:585
  43.1 0.1 collect_terms.3
  43.2 0.1 collective-permute-start.21
  43.3 1.9 %collective-permute-done.13.refs_0_ = bf16[144,512]{1,0:T(8,128)(2,1)S(1)} collective-permute-done((bf16[144,512]{1,0:T(8,128)(2,1)S(1)}, bf16[144,512]{1,0:T(8,128)(2,1)S(1)}, u32[]{:S(2)}, u32[]{:S(2)}) %collective-permute-start.13) | collective-permute-done | bytes 147488 | tf_op jit(solution)/shard_map/ppermute | solution.py:585
  45.2 1.0 %collective-permute-done.14.refs_1_ = bf16[144,512]{1,0:T(8,128)(2,1)S(1)} collective-permute-done((bf16[144,512]{1,0:T(8,128)(2,1)S(1)}, bf16[144,512]{1,0:T(8,128)(2,1)S(1)}, u32[]{:S(2)}, u32[]{:S(2)}) %collective-permute-start.14) | collective-permute-done | bytes 147488 | tf_op jit(solution)/shard_map/ppermute | solution.py:585
  46.2 1.6 %collective-permute-done.15.refs_2_ = bf16[144,512]{1,0:T(8,128)(2,1)S(1)} collective-permute-done((bf16[144,512]{1,0:T(8,128)(2,1)S(1)}, bf16[144,512]{1,0:T(8,128)(2,1)S(1)}, u32[]{:S(2)}, u32[]{:S(2)}) %collective-permute-start.15) | collective-permute-done | bytes 147488 | tf_op jit(solution)/shard_map/ppermute | solution.py:585
  47.8 0.1 collect_terms.2
  47.8 0.1 collective-permute-start.16
  47.9 0.0 collective-permute-done.21.other
  48.0 2.6 %collective-permute-start.22 = (bf16[96,512]{1,0:T(8,128)(2,1)S(1)}, bf16[96,512]{1,0:T(8,128)(2,1)S(1)}, u32[]{:S(2)}, u32[]{:S(2)}) collective-permute-start(bf16[96,512]{1,0:T(8,128)(2,1)S(1)} %merge_slabs.4.mine.refs_0_), channel_id=1, source_target_pairs={{0,16},{8,24},{16,0},{24,8},{1,17},{9,25},{17,1},{25,9},{2,18},{10... | collective-permute-start | bytes 294920 | tf_op jit(solution)/shard_map/ppermute | solution.py:585
  50.6 3.5 %collective-permute-done.16.other = bf16[128,512]{1,0:T(8,128)(2,1)S(1)} collective-permute-done((bf16[128,512]{1,0:T(8,128)(2,1)S(1)}, bf16[128,512]{1,0:T(8,128)(2,1)S(1)}, u32[]{:S(2)}, u32[]{:S(2)}) %collective-permute-start.16) | collective-permute-done | bytes 131104 | tf_op jit(solution)/shard_map/ppermute | solution.py:585
  54.1 0.1 collective-permute-start.17
  54.2 0.0 collective-permute-done.22.other.refs_1_
  54.3 2.5 %collective-permute-start.23 = (bf16[128,512]{1,0:T(8,128)(2,1)S(1)}, bf16[128,512]{1,0:T(8,128)(2,1)S(1)}, u32[]{:S(2)}, u32[]{:S(2)}) collective-permute-start(bf16[128,512]{1,0:T(8,128)(2,1)S(1)} %merge_slabs.5.mine), channel_id=1, source_target_pairs={{0,8},{8,0},{16,24},{24,16},{1,9},{9,1},{17,25},{25,17},{2,10},{10... | collective-permute-start | bytes 393224 | tf_op jit(solution)/shard_map/ppermute | solution.py:585
  56.8 0.0 collective-permute-start.24
  56.8 1.2 %collective-permute-done.24.refs_1_ = bf16[48,512]{1,0:T(8,128)(2,1)S(1)} collective-permute-done((bf16[48,512]{1,0:T(8,128)(2,1)S(1)}, bf16[48,512]{1,0:T(8,128)(2,1)S(1)}, u32[]{:S(2)}, u32[]{:S(2)}) %collective-permute-start.24) | collective-permute-done | bytes 49184 | tf_op jit(solution)/shard_map/ppermute | solution.py:585
  58.0 2.4 %collective-permute-done.17.last_other = bf16[128,512]{1,0:T(8,128)(2,1)S(1)} collective-permute-done((bf16[128,512]{1,0:T(8,128)(2,1)S(1)}, bf16[128,512]{1,0:T(8,128)(2,1)S(1)}, u32[]{:S(2)}, u32[]{:S(2)}) %collective-permute-start.17) | collective-permute-done | bytes 131104 | tf_op jit(solution)/shard_map/ppermute | solution.py:585
  60.4 0.7 %collective-permute-done.23.other = bf16[128,512]{1,0:T(8,128)(2,1)S(1)} collective-permute-done((bf16[128,512]{1,0:T(8,128)(2,1)S(1)}, bf16[128,512]{1,0:T(8,128)(2,1)S(1)}, u32[]{:S(2)}, u32[]{:S(2)}) %collective-permute-start.23) | collective-permute-done | bytes 131104 | tf_op jit(solution)/shard_map/ppermute | solution.py:585
  61.1 1.4 %last_sums.1 = (f32[256,512]{1,0:T(8,128)}, f32[256,256]{1,0:T(8,128)}) custom-call(f32[4,16,256]{2,1,0:T(8,128)S(1)} %get-tuple-element.48.ge_ref.own_ge, f32[8,128]{1,0:T(8,128)S(1)} %get-tuple-element.49.odd, bf16[128,512]{1,0:T(8,128)(2,1)S(1)} %merge_slabs.3.refs_2_.last_mine, bf16[128,512]{1,0:T(8,128)(2,1)S(1)} %collective-permute-done.17.last_other, ...), custom_call_target="tpu_custom_call" | custom-call | tf_op jit(solution)/shard_map/last_sums/pallas_call | solution.py:373
  (6 shorter events, 0.1 us)
Async XLA Ops:
  0.6 6.9 %collective-permute-start.1 = (bf16[392,2048]{1,0:T(8,128)(2,1)}, bf16[392,2048]{1,0:T(8,128)(2,1)}, u32[]{:S(2)}, u32[]{:S(2)}) collective-permute-start(bf16[392,2048]{1,0:T(8,128)(2,1)} %s_own.3), channel_id=1, source_target_pairs={{0,1},{1,0},{2,3},{3,2},{4,5},{5,4},{6,7},{7,6},{8,9},{9,8},{10,11... | collective-permute-start | bytes 4816904 | tf_op jit(solution)/shard_map/ppermute | solution.py:585
  1.1 5.1 %collective-permute-start = (bf16[392,512]{1,0:T(8,128)(2,1)}, bf16[392,512]{1,0:T(8,128)(2,1)S(1)}, u32[]{:S(2)}, u32[]{:S(2)}) collective-permute-start(bf16[392,512]{1,0:T(8,128)(2,1)} %f_own.1), channel_id=1, source_target_pairs={{0,1},{1,0},{2,3},{3,2},{4,5},{5,4},{6,7},{7,6},{8,9},{9,8},{10,11... | collective-permute-start | bytes 1204232 | tf_op jit(solution)/shard_map/ppermute | solution.py:585
  1.2 10.3 %collective-permute-start.3 = (bf16[256,512]{1,0:T(8,128)(2,1)}, bf16[256,512]{1,0:T(8,128)(2,1)S(1)}, u32[]{:S(2)}, u32[]{:S(2)}) collective-permute-start(bf16[256,512]{1,0:T(8,128)(2,1)} %conv.1), channel_id=1, source_target_pairs={{0,4},{1,5},{2,6},{3,7},{4,0},{5,1},{6,2},{7,3},{8,12},{9,13},{10,... | collective-permute-start | bytes 786440 | tf_op jit(solution)/shard_map/ppermute | solution.py:585
  4.2 9.4 %collective-permute-start.2 = (bf16[256,512]{1,0:T(8,128)(2,1)}, bf16[256,512]{1,0:T(8,128)(2,1)S(1)}, u32[]{:S(2)}, u32[]{:S(2)}) collective-permute-start(bf16[256,512]{1,0:T(8,128)(2,1)} %conv.1), channel_id=1, source_target_pairs={{0,2},{1,3},{2,0},{3,1},{4,6},{5,7},{6,4},{7,5},{8,10},{9,11},{10,... | collective-permute-start | bytes 786440 | tf_op jit(solution)/shard_map/ppermute | solution.py:585
  5.7 10.7 %collective-permute-start.4 = (bf16[256,256]{1,0:T(8,128)(2,1)}, bf16[256,256]{1,0:T(8,128)(2,1)S(1)}, u32[]{:S(2)}, u32[]{:S(2)}) collective-permute-start(bf16[256,256]{1,0:T(8,128)(2,1)} %proj.1), channel_id=1, source_target_pairs={{0,2},{1,3},{2,0},{3,1},{4,6},{5,7},{6,4},{7,5},{8,10},{9,11},{10,... | collective-permute-start | bytes 393224 | tf_op jit(solution)/shard_map/ppermute | solution.py:585
  6.2 10.2 %collective-permute-start.5 = (bf16[256,256]{1,0:T(8,128)(2,1)}, bf16[256,256]{1,0:T(8,128)(2,1)S(1)}, u32[]{:S(2)}, u32[]{:S(2)}) collective-permute-start(bf16[256,256]{1,0:T(8,128)(2,1)} %proj.1), channel_id=1, source_target_pairs={{0,4},{1,5},{2,6},{3,7},{4,0},{5,1},{6,2},{7,3},{8,12},{9,13},{10,... | collective-permute-start | bytes 393224 | tf_op jit(solution)/shard_map/ppermute | solution.py:585
  7.6 11.5 %collective-permute-start.6 = (bf16[256,256]{1,0:T(8,128)(2,1)}, bf16[256,256]{1,0:T(8,128)(2,1)S(1)}, u32[]{:S(2)}, u32[]{:S(2)}) collective-permute-start(bf16[256,256]{1,0:T(8,128)(2,1)} %proj.1), channel_id=1, source_target_pairs={{0,6},{1,7},{2,4},{3,5},{4,2},{5,3},{6,0},{7,1},{8,14},{9,15},{10,... | collective-permute-start | bytes 393224 | tf_op jit(solution)/shard_map/ppermute | solution.py:585
  11.5 9.3 %collective-permute-start.7 = (bf16[128,512]{1,0:T(8,128)(2,1)S(1)}, bf16[128,512]{1,0:T(8,128)(2,1)S(1)}, u32[]{:S(2)}, u32[]{:S(2)}) collective-permute-start(bf16[128,512]{1,0:T(8,128)(2,1)S(1)} %half_of.2), channel_id=1, source_target_pairs={{0,2},{1,3},{2,0},{3,1},{4,6},{5,7},{6,4},{7,5},{8,10},{9,11},{10,... | collective-permute-start | bytes 393224 | tf_op jit(solution)/shard_map/ppermute | solution.py:585
  13.6 7.2 %collective-permute-start.8 = (bf16[128,512]{1,0:T(8,128)(2,1)S(1)}, bf16[128,512]{1,0:T(8,128)(2,1)S(1)}, u32[]{:S(2)}, u32[]{:S(2)}) collective-permute-start(bf16[128,512]{1,0:T(8,128)(2,1)S(1)} %half_of.3), channel_id=1, source_target_pairs={{0,4},{1,5},{2,6},{3,7},{4,0},{5,1},{6,2},{7,3},{8,12},{9,13},{10,... | collective-permute-start | bytes 393224 | tf_op jit(solution)/shard_map/ppermute | solution.py:585
  21.5 1.2 %collective-permute-start.9 = (f32[40,128]{1,0:T(8,128)S(1)}, f32[40,128]{1,0:T(8,128)S(1)}, u32[]{:S(2)}, u32[]{:S(2)}) collective-permute-start(f32[40,128]{1,0:T(8,128)S(1)} %get-tuple-element.47), channel_id=1, source_target_pairs={{0,1},{1,0},{2,3},{3,2},{4,5},{5,4},{6,7},{7,6},{8,9},{9,8},{10,11... | collective-permute-start | bytes 61448 | tf_op jit(solution)/shard_map/ppermute | solution.py:585
  22.7 4.7 %collective-permute-start.10 = (f32[40,128]{1,0:T(8,128)S(1)}, f32[40,128]{1,0:T(8,128)S(1)}, u32[]{:S(2)}, u32[]{:S(2)}) collective-permute-start(f32[40,128]{1,0:T(8,128)S(1)} %sum_arrays.1.refs_0_), channel_id=1, source_target_pairs={{0,16},{8,24},{16,0},{24,8},{1,17},{9,25},{17,1},{25,9},{2,18},{10... | collective-permute-start | bytes 61448 | tf_op jit(solution)/shard_map/ppermute | solution.py:585
  25.3 5.6 %collective-permute-start.11 = (f32[40,128]{1,0:T(8,128)S(1)}, f32[40,128]{1,0:T(8,128)S(1)}, u32[]{:S(2)}, u32[]{:S(2)}) collective-permute-start(f32[40,128]{1,0:T(8,128)S(1)} %sum_arrays.1.refs_0_), channel_id=1, source_target_pairs={{0,24},{8,16},{16,8},{24,0},{1,25},{9,17},{17,9},{25,1},{2,26},{10... | collective-permute-start | bytes 61448 | tf_op jit(solution)/shard_map/ppermute | solution.py:585
  26.7 4.2 %collective-permute-start.12 = (f32[40,128]{1,0:T(8,128)S(1)}, f32[40,128]{1,0:T(8,128)S(1)}, u32[]{:S(2)}, u32[]{:S(2)}) collective-permute-start(f32[40,128]{1,0:T(8,128)S(1)} %sum_arrays.1.refs_0_), channel_id=1, source_target_pairs={{0,8},{8,0},{16,24},{24,16},{1,9},{9,1},{17,25},{25,17},{2,10},{10... | collective-permute-start | bytes 61448 | tf_op jit(solution)/shard_map/ppermute | solution.py:585
  32.8 7.8 %collective-permute-start.18 = (bf16[144,512]{1,0:T(8,128)(2,1)S(1)}, bf16[144,512]{1,0:T(8,128)(2,1)S(1)}, u32[]{:S(2)}, u32[]{:S(2)}) collective-permute-start(bf16[144,512]{1,0:T(8,128)(2,1)S(1)} %get-tuple-element.65.refs_6_), channel_id=1, source_target_pairs={{0,6},{1,7},{2,4},{3,5},{4,2},{5,3},{6,0},{7,1},{8,14},{9,15},{10,... | collective-permute-start | bytes 442376 | tf_op jit(solution)/shard_map/ppermute | solution.py:585
  34.3 8.1 %collective-permute-start.19 = (bf16[144,512]{1,0:T(8,128)(2,1)S(1)}, bf16[144,512]{1,0:T(8,128)(2,1)S(1)}, u32[]{:S(2)}, u32[]{:S(2)}) collective-permute-start(bf16[144,512]{1,0:T(8,128)(2,1)S(1)} %get-tuple-element.63.refs_4_), channel_id=1, source_target_pairs={{0,2},{1,3},{2,0},{3,1},{4,6},{5,7},{6,4},{7,5},{8,10},{9,11},{10,... | collective-permute-start | bytes 442376 | tf_op jit(solution)/shard_map/ppermute | solution.py:585
  34.9 8.3 %collective-permute-start.20 = (bf16[144,512]{1,0:T(8,128)(2,1)S(1)}, bf16[144,512]{1,0:T(8,128)(2,1)S(1)}, u32[]{:S(2)}, u32[]{:S(2)}) collective-permute-start(bf16[144,512]{1,0:T(8,128)(2,1)S(1)} %get-tuple-element.64.refs_5_), channel_id=1, source_target_pairs={{0,4},{1,5},{2,6},{3,7},{4,0},{5,1},{6,2},{7,3},{8,12},{9,13},{10,... | collective-permute-start | bytes 442376 | tf_op jit(solution)/shard_map/ppermute | solution.py:585
  37.9 7.3 %collective-permute-start.13 = (bf16[144,512]{1,0:T(8,128)(2,1)S(1)}, bf16[144,512]{1,0:T(8,128)(2,1)S(1)}, u32[]{:S(2)}, u32[]{:S(2)}) collective-permute-start(bf16[144,512]{1,0:T(8,128)(2,1)S(1)} %get-tuple-element.66), channel_id=1, source_target_pairs={{0,2},{1,3},{2,0},{3,1},{4,6},{5,7},{6,4},{7,5},{8,10},{9,11},{10,... | collective-permute-start | bytes 442376 | tf_op jit(solution)/shard_map/ppermute | solution.py:585
  39.4 6.8 %collective-permute-start.14 = (bf16[144,512]{1,0:T(8,128)(2,1)S(1)}, bf16[144,512]{1,0:T(8,128)(2,1)S(1)}, u32[]{:S(2)}, u32[]{:S(2)}) collective-permute-start(bf16[144,512]{1,0:T(8,128)(2,1)S(1)} %get-tuple-element.67), channel_id=1, source_target_pairs={{0,4},{1,5},{2,6},{3,7},{4,0},{5,1},{6,2},{7,3},{8,12},{9,13},{10,... | collective-permute-start | bytes 442376 | tf_op jit(solution)/shard_map/ppermute | solution.py:585
  40.6 7.2 %collective-permute-start.15 = (bf16[144,512]{1,0:T(8,128)(2,1)S(1)}, bf16[144,512]{1,0:T(8,128)(2,1)S(1)}, u32[]{:S(2)}, u32[]{:S(2)}) collective-permute-start(bf16[144,512]{1,0:T(8,128)(2,1)S(1)} %get-tuple-element.68), channel_id=1, source_target_pairs={{0,6},{1,7},{2,4},{3,5},{4,2},{5,3},{6,0},{7,1},{8,14},{9,15},{10,... | collective-permute-start | bytes 442376 | tf_op jit(solution)/shard_map/ppermute | solution.py:585
  43.2 4.7 %collective-permute-start.21 = (bf16[64,512]{1,0:T(8,128)(2,1)S(1)}, bf16[64,512]{1,0:T(8,128)(2,1)S(1)}, u32[]{:S(2)}, u32[]{:S(2)}) collective-permute-start(bf16[64,512]{1,0:T(8,128)(2,1)S(1)} %get-tuple-element.71), channel_id=1, source_target_pairs={{0,8},{8,0},{16,24},{24,16},{1,9},{9,1},{17,25},{25,17},{2,10},{10... | collective-permute-start | bytes 196616 | tf_op jit(solution)/shard_map/ppermute | solution.py:585
  47.8 6.3 %collective-permute-start.16 = (bf16[128,512]{1,0:T(8,128)(2,1)S(1)}, bf16[128,512]{1,0:T(8,128)(2,1)S(1)}, u32[]{:S(2)}, u32[]{:S(2)}) collective-permute-start(bf16[128,512]{1,0:T(8,128)(2,1)S(1)} %get-tuple-element.69.mine.refs_1_), channel_id=1, source_target_pairs={{0,8},{8,0},{16,24},{24,16},{1,9},{9,1},{17,25},{25,17},{2,10},{10... | collective-permute-start | bytes 393224 | tf_op jit(solution)/shard_map/ppermute | solution.py:585
  48.0 6.3 %collective-permute-start.22 = (bf16[96,512]{1,0:T(8,128)(2,1)S(1)}, bf16[96,512]{1,0:T(8,128)(2,1)S(1)}, u32[]{:S(2)}, u32[]{:S(2)}) collective-permute-start(bf16[96,512]{1,0:T(8,128)(2,1)S(1)} %merge_slabs.4.mine.refs_0_), channel_id=1, source_target_pairs={{0,16},{8,24},{16,0},{24,8},{1,17},{9,25},{17,1},{25,9},{2,18},{10... | collective-permute-start | bytes 294920 | tf_op jit(solution)/shard_map/ppermute | solution.py:585
  54.1 6.3 %collective-permute-start.17 = (bf16[128,512]{1,0:T(8,128)(2,1)S(1)}, bf16[128,512]{1,0:T(8,128)(2,1)S(1)}, u32[]{:S(2)}, u32[]{:S(2)}) collective-permute-start(bf16[128,512]{1,0:T(8,128)(2,1)S(1)} %merge_slabs.3.refs_2_.last_mine), channel_id=1, source_target_pairs={{0,16},{8,24},{16,0},{24,8},{1,17},{9,25},{17,1},{25,9},{2,18},{10... | collective-permute-start | bytes 393224 | tf_op jit(solution)/shard_map/ppermute | solution.py:585
  54.3 6.9 %collective-permute-start.23 = (bf16[128,512]{1,0:T(8,128)(2,1)S(1)}, bf16[128,512]{1,0:T(8,128)(2,1)S(1)}, u32[]{:S(2)}, u32[]{:S(2)}) collective-permute-start(bf16[128,512]{1,0:T(8,128)(2,1)S(1)} %merge_slabs.5.mine), channel_id=1, source_target_pairs={{0,8},{8,0},{16,24},{24,16},{1,9},{9,1},{17,25},{25,17},{2,10},{10... | collective-permute-start | bytes 393224 | tf_op jit(solution)/shard_map/ppermute | solution.py:585
  56.8 1.2 %collective-permute-start.24 = (bf16[48,512]{1,0:T(8,128)(2,1)S(1)}, bf16[48,512]{1,0:T(8,128)(2,1)S(1)}, u32[]{:S(2)}, u32[]{:S(2)}) collective-permute-start(bf16[48,512]{1,0:T(8,128)(2,1)S(1)} %get-tuple-element.73.refs_0_), channel_id=1, source_target_pairs={{0,1},{1,0},{2,3},{3,2},{4,5},{5,4},{6,7},{7,6},{8,9},{9,8},{10,11... | collective-permute-start | bytes 147464 | tf_op jit(solution)/shard_map/ppermute | solution.py:585

commit v10 on v9

--- a/solution.py
+++ b/solution.py
@@ -572,12 +572,18 @@
 
 
 def last_sums_kernel(slabs, images, order, rows, own_ge, odd, last_mine, last_other, mine, other, *refs):
-    tails, (conv_out, proj_out) = refs[:-2], refs[-2:]
-    proj_sum(slabs, images, order, rows, own_ge, mine, other, tails, proj_out)
+    tails, (conv_out, proj_out, conv, proj, sems) = refs[:-5], refs[-5:]
     if slabs == 4:
-        final_halves(odd, mine, other, (last_mine, last_other), conv_out)
+        final_halves(odd, mine, other, (last_mine, last_other), conv)
     else:
-        final_whole((mine, other, last_mine, last_other), conv_out)
+        final_whole((mine, other, last_mine, last_other), conv)
+    conv_copy = pltpu.make_async_copy(conv, conv_out, sems.at[0])
+    conv_copy.start()
+    proj_sum(slabs, images, order, rows, own_ge, mine, other, tails, proj)
+    proj_copy = pltpu.make_async_copy(proj, proj_out, sems.at[1])
+    proj_copy.start()
+    conv_copy.wait()
+    proj_copy.wait()
 
 
 def swap(x, axis, bit):
@@ -651,12 +657,18 @@
                 piece = merge(part[1], piece, swap(piece, "dp", bit))
                 bit *= 2
             pieces += [piece, swap(piece, "dp", bit)]
-    grad_conv, grad_proj = small_call(
+    arrays = (ge, odd, pieces[2], pieces[3], pieces[0], pieces[1], tails, swap(tails, "fsdp", 1))
+    shapes = [(count, width), proj_weight.shape]
+    grad_conv, grad_proj = pl.pallas_call(
         functools.partial(last_sums_kernel, slabs, images, order, above),
-        [((count, width), F32), (proj_weight.shape, F32)],
-        "last_sums",
-        *(ge, odd, pieces[2], pieces[3], pieces[0], pieces[1], tails, swap(tails, "fsdp", 1)),
-    )
+        in_specs=[vspec()] * len(arrays),
+        out_specs=[pl.BlockSpec(memory_space=pl.ANY)] * 2,
+        out_shape=[jax.ShapeDtypeStruct(shape, F32) for shape in shapes],
+        scratch_shapes=[pltpu.VMEM(shape, F32) for shape in shapes] + [pltpu.SemaphoreType.DMA((2,))],
+        compiler_params=params(),
+        cost_estimate=pl.CostEstimate(flops=0, bytes_accessed=0, transcendentals=0),
+        name="last_sums",
+    )(*arrays)
     return grad_conv, grad_proj, loss.reshape(1)
 
 

time: 62.6 us -> 62.7 us (level)
    pallas_call x0 -> x1, Pallas kernels: none -> 1.4 us  [local(): pl.pallas_call(functools.partial(last_sums_kernel, slabs, images, order,...]
    pallas_call x9 -> x8, Pallas kernels: 1.64 us -> 0.26 us  [small_call(): pl.pallas_call(kernel, in_specs=[vspec()] * len(arrays) + [pl.BlockSpec(m...]
where the time goes in v10:
time: 62.7 us; the launch traced here: 62.5 us
  starting transfers between devices  28.5 us (45%)
  waiting for transfers between devices  22.8 us (36%)
  Pallas kernels  10.5 us (17%)
  between operations  0.77 us (1%)
    ppermute x25, starting transfers between devices, swap(): return lax.ppermute(x, axis, [(i, i ^ bit) for i in range(size)])  28.5 us
    ppermute x25, waiting for transfers between devices, swap(): return lax.ppermute(x, axis, [(i, i ^ bit) for i in range(size)])  22.8 us
    pallas_call x3, Pallas kernels, forward_call(): pl.pallas_call(kernel, in_specs=in_specs, out_specs=[vspec()] * len(shape...  5.42 us
    pallas_call x3, Pallas kernels, backward(): pl.pallas_call(functools.partial(backward_kernel, len(blocks), images, pa...  2.27 us
    pallas_call x1, Pallas kernels, local(): pl.pallas_call(functools.partial(last_sums_kernel, slabs, images, order,...  1.4 us
  transfers between devices with their start and end apart: 25, of which 16 were waited for; matrix products, arithmetic and copies ran while one was open for 0% of the time, Pallas kernels for 10%

profile of v10, /device:TPU:0, one launch (start us, length us, event | category | flops | bytes accessed | tf_op | source)
XLA Modules:
  0.0 62.5 jit_solution(6221646863840209196)
XLA Ops:
  0.6 0.5 collective-permute-start.1
  1.1 0.1 collective-permute-start
  1.2 2.9 %collective-permute-start.3 = (bf16[256,512]{1,0:T(8,128)(2,1)}, bf16[256,512]{1,0:T(8,128)(2,1)S(1)}, u32[]{:S(2)}, u32[]{:S(2)}) collective-permute-start(bf16[256,512]{1,0:T(8,128)(2,1)} %conv.1), channel_id=1, source_target_pairs={{0,4},{1,5},{2,6},{3,7},{4,0},{5,1},{6,2},{7,3},{8,12},{9,13},{10,... | collective-permute-start | bytes 786440 | tf_op jit(solution)/shard_map/ppermute | solution.py:591
  4.2 1.5 %collective-permute-start.2 = (bf16[256,512]{1,0:T(8,128)(2,1)}, bf16[256,512]{1,0:T(8,128)(2,1)S(1)}, u32[]{:S(2)}, u32[]{:S(2)}) collective-permute-start(bf16[256,512]{1,0:T(8,128)(2,1)} %conv.1), channel_id=1, source_target_pairs={{0,2},{1,3},{2,0},{3,1},{4,6},{5,7},{6,4},{7,5},{8,10},{9,11},{10,... | collective-permute-start | bytes 786440 | tf_op jit(solution)/shard_map/ppermute | solution.py:591
  5.7 0.5 collective-permute-start.4
  6.2 0.0 collective-permute-done.f_sib
  6.2 1.4 %collective-permute-start.5 = (bf16[256,256]{1,0:T(8,128)(2,1)}, bf16[256,256]{1,0:T(8,128)(2,1)S(1)}, u32[]{:S(2)}, u32[]{:S(2)}) collective-permute-start(bf16[256,256]{1,0:T(8,128)(2,1)} %proj.1), channel_id=1, source_target_pairs={{0,4},{1,5},{2,6},{3,7},{4,0},{5,1},{6,2},{7,3},{8,12},{9,13},{10,... | collective-permute-start | bytes 393224 | tf_op jit(solution)/shard_map/ppermute | solution.py:591
  7.6 0.0 collective-permute-done.1.s_sib
  7.6 1.6 %collective-permute-start.6 = (bf16[256,256]{1,0:T(8,128)(2,1)}, bf16[256,256]{1,0:T(8,128)(2,1)S(1)}, u32[]{:S(2)}, u32[]{:S(2)}) collective-permute-start(bf16[256,256]{1,0:T(8,128)(2,1)} %proj.1), channel_id=1, source_target_pairs={{0,6},{1,7},{2,4},{3,5},{4,2},{5,3},{6,0},{7,1},{8,14},{9,15},{10,... | collective-permute-start | bytes 393224 | tf_op jit(solution)/shard_map/ppermute | solution.py:591
  9.2 2.0 %forward_first.1 = (bf16[392,256]{1,0:T(8,128)(2,1)S(1)}, bf16[392,256]{1,0:T(8,128)(2,1)S(1)}, bf16[16,256]{1,0:T(8,128)(2,1)S(1)}, f32[16,256]{1,0:T(8,128)S(1...) custom-call(s32[1]{0:T(128)} %bitcast.1.index_ref, ...), custom_call_target="tpu_custom_call" | custom-call | flops 822083584 | bytes 802816 | tf_op jit(solution)/shard_map/forward_first/pallas_call | solution.py:171
  11.2 0.3 collective-permute-done.3.refs_1_.x
  11.5 2.1 %collective-permute-start.7 = (bf16[128,512]{1,0:T(8,128)(2,1)S(1)}, bf16[128,512]{1,0:T(8,128)(2,1)S(1)}, u32[]{:S(2)}, u32[]{:S(2)}) collective-permute-start(bf16[128,512]{1,0:T(8,128)(2,1)S(1)} %half_of.2), channel_id=1, source_target_pairs={{0,2},{1,3},{2,0},{3,1},{4,6},{5,7},{6,4},{7,5},{8,10},{9,11},{10,... | collective-permute-start | bytes 393224 | tf_op jit(solution)/shard_map/ppermute | solution.py:591
  13.6 0.0 collective-permute-done.2.refs_0_.x
  13.6 1.6 %collective-permute-start.8 = (bf16[128,512]{1,0:T(8,128)(2,1)S(1)}, bf16[128,512]{1,0:T(8,128)(2,1)S(1)}, u32[]{:S(2)}, u32[]{:S(2)}) collective-permute-start(bf16[128,512]{1,0:T(8,128)(2,1)S(1)} %half_of.3), channel_id=1, source_target_pairs={{0,4},{1,5},{2,6},{3,7},{4,0},{5,1},{6,2},{7,3},{8,12},{9,13},{10,... | collective-permute-start | bytes 393224 | tf_op jit(solution)/shard_map/ppermute | solution.py:591
  15.2 1.2 %collective-permute-done.4.refs_2_.refs_3_ = bf16[256,256]{1,0:T(8,128)(2,1)S(1)} collective-permute-done((bf16[256,256]{1,0:T(8,128)(2,1)}, bf16[256,256]{1,0:T(8,128)(2,1)S(1)}, u32[]{:S(2)}, u32[]{:S(2)}) %collective-permute-start.4) | collective-permute-done | bytes 131104 | tf_op jit(solution)/shard_map/ppermute | solution.py:591
  16.4 0.0 collective-permute-done.5.refs_3_.refs_7_
  16.4 2.7 %forward_middle.1 = (bf16[392,256]{1,0:T(8,128)(2,1)S(1)}, bf16[392,256]{1,0:T(8,128)(2,1)S(1)}, bf16[16,256]{1,0:T(8,128)(2,1)S(1)}, bf16[392,256]{1,0:T(8,128)...) custom-call(s32[1]{0:T(128)} %bitcast.1.index_ref, ...), custom_call_target="tpu_custom_call" | custom-call | flops 1644167168 | bytes 1605632 | tf_op jit(solution)/shard_map/forward_middle/pallas_call | solution.py:171
  19.1 0.0 collective-permute-done.6.proj.refs_11_
  19.1 1.7 %collective-permute-done.7.refs_0_ = bf16[128,512]{1,0:T(8,128)(2,1)S(1)} collective-permute-done((bf16[128,512]{1,0:T(8,128)(2,1)S(1)}, bf16[128,512]{1,0:T(8,128)(2,1)S(1)}, u32[]{:S(2)}, u32[]{:S(2)}) %collective-permute-start.7) | collective-permute-done | bytes 131104 | tf_op jit(solution)/shard_map/ppermute | solution.py:591
  20.8 0.0 collective-permute-done.8.refs_1_
  20.8 0.7 %forward_last.1 = (bf16[392,256]{1,0:T(8,128)(2,1)S(1)}, bf16[392,256]{1,0:T(8,128)(2,1)S(1)}, bf16[16,256]{1,0:T(8,128)(2,1)S(1)}, f32[40,128]{1,0:T(8,128)S(1)}, f32[40,128]{1,0:T(8,128)S(1)}) custom-call(bf16[392,512]{1,0:T(8,128)(2,1)S(1)} %get-tuple-element.40.f_own, bf16[392,512]{1,0:T(8,128)(2,1)S(1)} %collective-permute-done.f_sib, ...), custom_call_target="tpu_custom_call" | custom-call | flops 822083584 | bytes 802816 | tf_op jit(solution)/shard_map/forward_last/pallas_call | solution.py:171
  21.5 0.0 collective-permute-start.9
  21.5 1.2 %collective-permute-done.9.refs_1_ = f32[40,128]{1,0:T(8,128)S(1)} collective-permute-done((f32[40,128]{1,0:T(8,128)S(1)}, f32[40,128]{1,0:T(8,128)S(1)}, u32[]{:S(2)}, u32[]{:S(2)}) %collective-permute-start.9) | collective-permute-done | bytes 20512 | tf_op jit(solution)/shard_map/ppermute | solution.py:591
  22.7 2.6 %collective-permute-start.10 = (f32[40,128]{1,0:T(8,128)S(1)}, f32[40,128]{1,0:T(8,128)S(1)}, u32[]{:S(2)}, u32[]{:S(2)}) collective-permute-start(f32[40,128]{1,0:T(8,128)S(1)} %sum_arrays.1.refs_0_), channel_id=1, source_target_pairs={{0,16},{8,24},{16,0},{24,8},{1,17},{9,25},{17,1},{25,9},{2,18},{10... | collective-permute-start | bytes 61448 | tf_op jit(solution)/shard_map/ppermute | solution.py:591
  25.3 1.3 %collective-permute-start.11 = (f32[40,128]{1,0:T(8,128)S(1)}, f32[40,128]{1,0:T(8,128)S(1)}, u32[]{:S(2)}, u32[]{:S(2)}) collective-permute-start(f32[40,128]{1,0:T(8,128)S(1)} %sum_arrays.1.refs_0_), channel_id=1, source_target_pairs={{0,24},{8,16},{16,8},{24,0},{1,25},{9,17},{17,9},{25,1},{2,26},{10... | collective-permute-start | bytes 61448 | tf_op jit(solution)/shard_map/ppermute | solution.py:591
  26.7 0.2 collective-permute-start.12
  26.9 0.5 collective-permute-done.10.refs_1_
  27.4 3.5 %collective-permute-done.11.refs_2_ = f32[40,128]{1,0:T(8,128)S(1)} collective-permute-done((f32[40,128]{1,0:T(8,128)S(1)}, f32[40,128]{1,0:T(8,128)S(1)}, u32[]{:S(2)}, u32[]{:S(2)}) %collective-permute-start.11) | collective-permute-done | bytes 20512 | tf_op jit(solution)/shard_map/ppermute | solution.py:591
  30.9 0.0 collective-permute-done.12.refs_3_
  30.9 1.1 %hsic_groups.1 = (f32[4,16,256]{2,1,0:T(8,128)S(1)}, f32[1,1]{1,0:T(1,128)}, f32[8,128]{1,0:T(8,128)S(1)}) custom-call(s32[1]{0:T(128)} %bitcast.place_ref, f32[40,128]{1,0:T(8,128)S(1)} %sum_arrays.1.refs_0_, f32[40,128]{1,0:T(8,128)S(1)} %collective-permute-done.10.refs_1_, f32[40,128]{1,0:T(8,128)S(1)} %collective-permute-done.11.refs_2_, ...), custom_call_target="tpu_custom_call" | custom-call | flops 1000000000 | tf_op jit(solution)/shard_map/hsic_groups/pallas_call | solution.py:308
  32.0 0.8 %backward_blocks.3 = (bf16[144,512]{1,0:T(8,128)(2,1)S(1)}, bf16[144,512]{1,0:T(8,128)(2,1)S(1)}, bf16[144,512]{1,0:T(8,128)(2,1)S(1)}) custom-call(bf16[392,512]{1,0:T(8,128)(2,1)S(1)} %get-tuple-element.40.f_own, bf16[392,512]{1,0:T(8,128)(2,1)S(1)} %collective-permute-done.f_sib, f32[4,16,256]{2,1,0:T(8,128)S(1)} %get-tuple-element.48.ge_ref.own_ge, ...), custom_call_target="tpu_custom_call" | custom-call | flops 1233125376 | bytes 602112 | tf_op jit(solution)/shard_map/backward_blocks/pallas_call | solution.py:357
  32.8 1.5 %collective-permute-start.18 = (bf16[144,512]{1,0:T(8,128)(2,1)S(1)}, bf16[144,512]{1,0:T(8,128)(2,1)S(1)}, u32[]{:S(2)}, u32[]{:S(2)}) collective-permute-start(bf16[144,512]{1,0:T(8,128)(2,1)S(1)} %get-tuple-element.65.refs_6_), channel_id=1, source_target_pairs={{0,6},{1,7},{2,4},{3,5},{4,2},{5,3},{6,0},{7,1},{8,14},{9,15},{10,... | collective-permute-start | bytes 442376 | tf_op jit(solution)/shard_map/ppermute | solution.py:591
  34.3 0.5 collective-permute-start.19
  34.9 1.5 %collective-permute-start.20 = (bf16[144,512]{1,0:T(8,128)(2,1)S(1)}, bf16[144,512]{1,0:T(8,128)(2,1)S(1)}, u32[]{:S(2)}, u32[]{:S(2)}) collective-permute-start(bf16[144,512]{1,0:T(8,128)(2,1)S(1)} %get-tuple-element.64.refs_5_), channel_id=1, source_target_pairs={{0,4},{1,5},{2,6},{3,7},{4,0},{5,1},{6,2},{7,3},{8,12},{9,13},{10,... | collective-permute-start | bytes 442376 | tf_op jit(solution)/shard_map/ppermute | solution.py:591
  36.4 0.7 %backward_blocks.4.refs_12_.own = f32[256,512]{1,0:T(8,128)S(1)} custom-call(bf16[392,512]{1,0:T(8,128)(2,1)S(1)} %get-tuple-element.40.f_own, bf16[392,512]{1,0:T(8,128)(2,1)S(1)} %collective-permute-done.f_sib, f32[4,16,256]{2,1,0:T(8,128)S(1)} %get-tuple-element.48.ge_ref.own_ge, bf16[392,256]{1,0:T(8,128)(2,1)S(1)} %get-tuple-element.50.refs_0_, ...), custom_call_target="tpu_custom_call" | custom-call | flops 822083584 | bytes 401408 | tf_op jit(solution)/shard_map/backward_blocks/pallas_call | solution.py:357
  37.1 0.8 %backward_blocks.5 = (bf16[144,512]{1,0:T(8,128)(2,1)S(1)}, bf16[144,512]{1,0:T(8,128)(2,1)S(1)}, bf16[144,512]{1,0:T(8,128)(2,1)S(1)}) custom-call(bf16[392,512]{1,0:T(8,128)(2,1)S(1)} %get-tuple-element.40.f_own, bf16[392,512]{1,0:T(8,128)(2,1)S(1)} %collective-permute-done.f_sib, f32[4,16,256]{2,1,0:T(8,128)S(1)} %get-tuple-element.48.ge_ref.own_ge, ...), custom_call_target="tpu_custom_call" | custom-call | flops 1233125376 | bytes 602112 | tf_op jit(solution)/shard_map/backward_blocks/pallas_call | solution.py:357
  37.9 1.5 %collective-permute-start.13 = (bf16[144,512]{1,0:T(8,128)(2,1)S(1)}, bf16[144,512]{1,0:T(8,128)(2,1)S(1)}, u32[]{:S(2)}, u32[]{:S(2)}) collective-permute-start(bf16[144,512]{1,0:T(8,128)(2,1)S(1)} %get-tuple-element.66), channel_id=1, source_target_pairs={{0,2},{1,3},{2,0},{3,1},{4,6},{5,7},{6,4},{7,5},{8,10},{9,11},{10,... | collective-permute-start | bytes 442376 | tf_op jit(solution)/shard_map/ppermute | solution.py:591
  39.4 0.5 collective-permute-start.14
  39.9 0.6 %collective-permute-done.18.refs_0_ = bf16[144,512]{1,0:T(8,128)(2,1)S(1)} collective-permute-done((bf16[144,512]{1,0:T(8,128)(2,1)S(1)}, bf16[144,512]{1,0:T(8,128)(2,1)S(1)}, u32[]{:S(2)}, u32[]{:S(2)}) %collective-permute-start.18) | collective-permute-done | bytes 147488 | tf_op jit(solution)/shard_map/ppermute | solution.py:591
  40.6 1.1 %collective-permute-start.15 = (bf16[144,512]{1,0:T(8,128)(2,1)S(1)}, bf16[144,512]{1,0:T(8,128)(2,1)S(1)}, u32[]{:S(2)}, u32[]{:S(2)}) collective-permute-start(bf16[144,512]{1,0:T(8,128)(2,1)S(1)} %get-tuple-element.68), channel_id=1, source_target_pairs={{0,6},{1,7},{2,4},{3,5},{4,2},{5,3},{6,0},{7,1},{8,14},{9,15},{10,... | collective-permute-start | bytes 442376 | tf_op jit(solution)/shard_map/ppermute | solution.py:591
  41.7 0.8 %collective-permute-done.19.refs_1_ = bf16[144,512]{1,0:T(8,128)(2,1)S(1)} collective-permute-done((bf16[144,512]{1,0:T(8,128)(2,1)S(1)}, bf16[144,512]{1,0:T(8,128)(2,1)S(1)}, u32[]{:S(2)}, u32[]{:S(2)}) %collective-permute-start.19) | collective-permute-done | bytes 147488 | tf_op jit(solution)/shard_map/ppermute | solution.py:591
  42.5 0.7 %collective-permute-done.20.refs_2_ = bf16[144,512]{1,0:T(8,128)(2,1)S(1)} collective-permute-done((bf16[144,512]{1,0:T(8,128)(2,1)S(1)}, bf16[144,512]{1,0:T(8,128)(2,1)S(1)}, u32[]{:S(2)}, u32[]{:S(2)}) %collective-permute-start.20) | collective-permute-done | bytes 147488 | tf_op jit(solution)/shard_map/ppermute | solution.py:591
  43.1 0.1 collect_terms.3
  43.2 0.1 collective-permute-start.21
  43.3 1.9 %collective-permute-done.13.refs_0_ = bf16[144,512]{1,0:T(8,128)(2,1)S(1)} collective-permute-done((bf16[144,512]{1,0:T(8,128)(2,1)S(1)}, bf16[144,512]{1,0:T(8,128)(2,1)S(1)}, u32[]{:S(2)}, u32[]{:S(2)}) %collective-permute-start.13) | collective-permute-done | bytes 147488 | tf_op jit(solution)/shard_map/ppermute | solution.py:591
  45.2 1.0 %collective-permute-done.14.refs_1_ = bf16[144,512]{1,0:T(8,128)(2,1)S(1)} collective-permute-done((bf16[144,512]{1,0:T(8,128)(2,1)S(1)}, bf16[144,512]{1,0:T(8,128)(2,1)S(1)}, u32[]{:S(2)}, u32[]{:S(2)}) %collective-permute-start.14) | collective-permute-done | bytes 147488 | tf_op jit(solution)/shard_map/ppermute | solution.py:591
  46.2 1.6 %collective-permute-done.15.refs_2_ = bf16[144,512]{1,0:T(8,128)(2,1)S(1)} collective-permute-done((bf16[144,512]{1,0:T(8,128)(2,1)S(1)}, bf16[144,512]{1,0:T(8,128)(2,1)S(1)}, u32[]{:S(2)}, u32[]{:S(2)}) %collective-permute-start.15) | collective-permute-done | bytes 147488 | tf_op jit(solution)/shard_map/ppermute | solution.py:591
  47.8 0.1 collect_terms.2
  47.8 0.1 collective-permute-start.16
  47.9 0.0 collective-permute-done.21.other
  48.0 2.6 %collective-permute-start.22 = (bf16[96,512]{1,0:T(8,128)(2,1)S(1)}, bf16[96,512]{1,0:T(8,128)(2,1)S(1)}, u32[]{:S(2)}, u32[]{:S(2)}) collective-permute-start(bf16[96,512]{1,0:T(8,128)(2,1)S(1)} %merge_slabs.4.mine.refs_0_), channel_id=1, source_target_pairs={{0,16},{8,24},{16,0},{24,8},{1,17},{9,25},{17,1},{25,9},{2,18},{10... | collective-permute-start | bytes 294920 | tf_op jit(solution)/shard_map/ppermute | solution.py:591
  50.6 3.5 %collective-permute-done.16.other = bf16[128,512]{1,0:T(8,128)(2,1)S(1)} collective-permute-done((bf16[128,512]{1,0:T(8,128)(2,1)S(1)}, bf16[128,512]{1,0:T(8,128)(2,1)S(1)}, u32[]{:S(2)}, u32[]{:S(2)}) %collective-permute-start.16) | collective-permute-done | bytes 131104 | tf_op jit(solution)/shard_map/ppermute | solution.py:591
  54.1 0.1 collective-permute-start.17
  54.2 0.0 collective-permute-done.22.other.refs_1_
  54.3 2.5 %collective-permute-start.23 = (bf16[128,512]{1,0:T(8,128)(2,1)S(1)}, bf16[128,512]{1,0:T(8,128)(2,1)S(1)}, u32[]{:S(2)}, u32[]{:S(2)}) collective-permute-start(bf16[128,512]{1,0:T(8,128)(2,1)S(1)} %merge_slabs.5.mine), channel_id=1, source_target_pairs={{0,8},{8,0},{16,24},{24,16},{1,9},{9,1},{17,25},{25,17},{2,10},{10... | collective-permute-start | bytes 393224 | tf_op jit(solution)/shard_map/ppermute | solution.py:591
  56.8 0.0 collective-permute-start.24
  56.8 1.2 %collective-permute-done.24.refs_1_ = bf16[48,512]{1,0:T(8,128)(2,1)S(1)} collective-permute-done((bf16[48,512]{1,0:T(8,128)(2,1)S(1)}, bf16[48,512]{1,0:T(8,128)(2,1)S(1)}, u32[]{:S(2)}, u32[]{:S(2)}) %collective-permute-start.24) | collective-permute-done | bytes 49184 | tf_op jit(solution)/shard_map/ppermute | solution.py:591
  58.0 2.4 %collective-permute-done.17.last_other = bf16[128,512]{1,0:T(8,128)(2,1)S(1)} collective-permute-done((bf16[128,512]{1,0:T(8,128)(2,1)S(1)}, bf16[128,512]{1,0:T(8,128)(2,1)S(1)}, u32[]{:S(2)}, u32[]{:S(2)}) %collective-permute-start.17) | collective-permute-done | bytes 131104 | tf_op jit(solution)/shard_map/ppermute | solution.py:591
  60.4 0.7 %collective-permute-done.23.other = bf16[128,512]{1,0:T(8,128)(2,1)S(1)} collective-permute-done((bf16[128,512]{1,0:T(8,128)(2,1)S(1)}, bf16[128,512]{1,0:T(8,128)(2,1)S(1)}, u32[]{:S(2)}, u32[]{:S(2)}) %collective-permute-start.23) | collective-permute-done | bytes 131104 | tf_op jit(solution)/shard_map/ppermute | solution.py:591
  61.1 1.4 %last_sums.1 = (f32[256,512]{1,0:T(8,128)}, f32[256,256]{1,0:T(8,128)}) custom-call(f32[4,16,256]{2,1,0:T(8,128)S(1)} %get-tuple-element.48.ge_ref.own_ge, f32[8,128]{1,0:T(8,128)S(1)} %get-tuple-element.49.odd, bf16[128,512]{1,0:T(8,128)(2,1)S(1)} %merge_slabs.3.refs_2_.last_mine, bf16[128,512]{1,0:T(8,128)(2,1)S(1)} %collective-permute-done.17.last_other, ...), custom_call_target="tpu_custom_call" | custom-call | tf_op jit(solution)/shard_map/last_sums/pallas_call | solution.py:662
  (6 shorter events, 0.1 us)
Async XLA Ops:
  0.6 6.9 %collective-permute-start.1 = (bf16[392,2048]{1,0:T(8,128)(2,1)}, bf16[392,2048]{1,0:T(8,128)(2,1)}, u32[]{:S(2)}, u32[]{:S(2)}) collective-permute-start(bf16[392,2048]{1,0:T(8,128)(2,1)} %s_own.3), channel_id=1, source_target_pairs={{0,1},{1,0},{2,3},{3,2},{4,5},{5,4},{6,7},{7,6},{8,9},{9,8},{10,11... | collective-permute-start | bytes 4816904 | tf_op jit(solution)/shard_map/ppermute | solution.py:591
  1.1 5.1 %collective-permute-start = (bf16[392,512]{1,0:T(8,128)(2,1)}, bf16[392,512]{1,0:T(8,128)(2,1)S(1)}, u32[]{:S(2)}, u32[]{:S(2)}) collective-permute-start(bf16[392,512]{1,0:T(8,128)(2,1)} %f_own.1), channel_id=1, source_target_pairs={{0,1},{1,0},{2,3},{3,2},{4,5},{5,4},{6,7},{7,6},{8,9},{9,8},{10,11... | collective-permute-start | bytes 1204232 | tf_op jit(solution)/shard_map/ppermute | solution.py:591
  1.2 10.3 %collective-permute-start.3 = (bf16[256,512]{1,0:T(8,128)(2,1)}, bf16[256,512]{1,0:T(8,128)(2,1)S(1)}, u32[]{:S(2)}, u32[]{:S(2)}) collective-permute-start(bf16[256,512]{1,0:T(8,128)(2,1)} %conv.1), channel_id=1, source_target_pairs={{0,4},{1,5},{2,6},{3,7},{4,0},{5,1},{6,2},{7,3},{8,12},{9,13},{10,... | collective-permute-start | bytes 786440 | tf_op jit(solution)/shard_map/ppermute | solution.py:591
  4.2 9.4 %collective-permute-start.2 = (bf16[256,512]{1,0:T(8,128)(2,1)}, bf16[256,512]{1,0:T(8,128)(2,1)S(1)}, u32[]{:S(2)}, u32[]{:S(2)}) collective-permute-start(bf16[256,512]{1,0:T(8,128)(2,1)} %conv.1), channel_id=1, source_target_pairs={{0,2},{1,3},{2,0},{3,1},{4,6},{5,7},{6,4},{7,5},{8,10},{9,11},{10,... | collective-permute-start | bytes 786440 | tf_op jit(solution)/shard_map/ppermute | solution.py:591
  5.7 10.7 %collective-permute-start.4 = (bf16[256,256]{1,0:T(8,128)(2,1)}, bf16[256,256]{1,0:T(8,128)(2,1)S(1)}, u32[]{:S(2)}, u32[]{:S(2)}) collective-permute-start(bf16[256,256]{1,0:T(8,128)(2,1)} %proj.1), channel_id=1, source_target_pairs={{0,2},{1,3},{2,0},{3,1},{4,6},{5,7},{6,4},{7,5},{8,10},{9,11},{10,... | collective-permute-start | bytes 393224 | tf_op jit(solution)/shard_map/ppermute | solution.py:591
  6.2 10.2 %collective-permute-start.5 = (bf16[256,256]{1,0:T(8,128)(2,1)}, bf16[256,256]{1,0:T(8,128)(2,1)S(1)}, u32[]{:S(2)}, u32[]{:S(2)}) collective-permute-start(bf16[256,256]{1,0:T(8,128)(2,1)} %proj.1), channel_id=1, source_target_pairs={{0,4},{1,5},{2,6},{3,7},{4,0},{5,1},{6,2},{7,3},{8,12},{9,13},{10,... | collective-permute-start | bytes 393224 | tf_op jit(solution)/shard_map/ppermute | solution.py:591
  7.6 11.5 %collective-permute-start.6 = (bf16[256,256]{1,0:T(8,128)(2,1)}, bf16[256,256]{1,0:T(8,128)(2,1)S(1)}, u32[]{:S(2)}, u32[]{:S(2)}) collective-permute-start(bf16[256,256]{1,0:T(8,128)(2,1)} %proj.1), channel_id=1, source_target_pairs={{0,6},{1,7},{2,4},{3,5},{4,2},{5,3},{6,0},{7,1},{8,14},{9,15},{10,... | collective-permute-start | bytes 393224 | tf_op jit(solution)/shard_map/ppermute | solution.py:591
  11.5 9.3 %collective-permute-start.7 = (bf16[128,512]{1,0:T(8,128)(2,1)S(1)}, bf16[128,512]{1,0:T(8,128)(2,1)S(1)}, u32[]{:S(2)}, u32[]{:S(2)}) collective-permute-start(bf16[128,512]{1,0:T(8,128)(2,1)S(1)} %half_of.2), channel_id=1, source_target_pairs={{0,2},{1,3},{2,0},{3,1},{4,6},{5,7},{6,4},{7,5},{8,10},{9,11},{10,... | collective-permute-start | bytes 393224 | tf_op jit(solution)/shard_map/ppermute | solution.py:591
  13.6 7.2 %collective-permute-start.8 = (bf16[128,512]{1,0:T(8,128)(2,1)S(1)}, bf16[128,512]{1,0:T(8,128)(2,1)S(1)}, u32[]{:S(2)}, u32[]{:S(2)}) collective-permute-start(bf16[128,512]{1,0:T(8,128)(2,1)S(1)} %half_of.3), channel_id=1, source_target_pairs={{0,4},{1,5},{2,6},{3,7},{4,0},{5,1},{6,2},{7,3},{8,12},{9,13},{10,... | collective-permute-start | bytes 393224 | tf_op jit(solution)/shard_map/ppermute | solution.py:591
  21.5 1.2 %collective-permute-start.9 = (f32[40,128]{1,0:T(8,128)S(1)}, f32[40,128]{1,0:T(8,128)S(1)}, u32[]{:S(2)}, u32[]{:S(2)}) collective-permute-start(f32[40,128]{1,0:T(8,128)S(1)} %get-tuple-element.47), channel_id=1, source_target_pairs={{0,1},{1,0},{2,3},{3,2},{4,5},{5,4},{6,7},{7,6},{8,9},{9,8},{10,11... | collective-permute-start | bytes 61448 | tf_op jit(solution)/shard_map/ppermute | solution.py:591
  22.7 4.7 %collective-permute-start.10 = (f32[40,128]{1,0:T(8,128)S(1)}, f32[40,128]{1,0:T(8,128)S(1)}, u32[]{:S(2)}, u32[]{:S(2)}) collective-permute-start(f32[40,128]{1,0:T(8,128)S(1)} %sum_arrays.1.refs_0_), channel_id=1, source_target_pairs={{0,16},{8,24},{16,0},{24,8},{1,17},{9,25},{17,1},{25,9},{2,18},{10... | collective-permute-start | bytes 61448 | tf_op jit(solution)/shard_map/ppermute | solution.py:591
  25.3 5.6 %collective-permute-start.11 = (f32[40,128]{1,0:T(8,128)S(1)}, f32[40,128]{1,0:T(8,128)S(1)}, u32[]{:S(2)}, u32[]{:S(2)}) collective-permute-start(f32[40,128]{1,0:T(8,128)S(1)} %sum_arrays.1.refs_0_), channel_id=1, source_target_pairs={{0,24},{8,16},{16,8},{24,0},{1,25},{9,17},{17,9},{25,1},{2,26},{10... | collective-permute-start | bytes 61448 | tf_op jit(solution)/shard_map/ppermute | solution.py:591
  26.7 4.2 %collective-permute-start.12 = (f32[40,128]{1,0:T(8,128)S(1)}, f32[40,128]{1,0:T(8,128)S(1)}, u32[]{:S(2)}, u32[]{:S(2)}) collective-permute-start(f32[40,128]{1,0:T(8,128)S(1)} %sum_arrays.1.refs_0_), channel_id=1, source_target_pairs={{0,8},{8,0},{16,24},{24,16},{1,9},{9,1},{17,25},{25,17},{2,10},{10... | collective-permute-start | bytes 61448 | tf_op jit(solution)/shard_map/ppermute | solution.py:591
  32.8 7.8 %collective-permute-start.18 = (bf16[144,512]{1,0:T(8,128)(2,1)S(1)}, bf16[144,512]{1,0:T(8,128)(2,1)S(1)}, u32[]{:S(2)}, u32[]{:S(2)}) collective-permute-start(bf16[144,512]{1,0:T(8,128)(2,1)S(1)} %get-tuple-element.65.refs_6_), channel_id=1, source_target_pairs={{0,6},{1,7},{2,4},{3,5},{4,2},{5,3},{6,0},{7,1},{8,14},{9,15},{10,... | collective-permute-start | bytes 442376 | tf_op jit(solution)/shard_map/ppermute | solution.py:591
  34.3 8.1 %collective-permute-start.19 = (bf16[144,512]{1,0:T(8,128)(2,1)S(1)}, bf16[144,512]{1,0:T(8,128)(2,1)S(1)}, u32[]{:S(2)}, u32[]{:S(2)}) collective-permute-start(bf16[144,512]{1,0:T(8,128)(2,1)S(1)} %get-tuple-element.63.refs_4_), channel_id=1, source_target_pairs={{0,2},{1,3},{2,0},{3,1},{4,6},{5,7},{6,4},{7,5},{8,10},{9,11},{10,... | collective-permute-start | bytes 442376 | tf_op jit(solution)/shard_map/ppermute | solution.py:591
  34.9 8.3 %collective-permute-start.20 = (bf16[144,512]{1,0:T(8,128)(2,1)S(1)}, bf16[144,512]{1,0:T(8,128)(2,1)S(1)}, u32[]{:S(2)}, u32[]{:S(2)}) collective-permute-start(bf16[144,512]{1,0:T(8,128)(2,1)S(1)} %get-tuple-element.64.refs_5_), channel_id=1, source_target_pairs={{0,4},{1,5},{2,6},{3,7},{4,0},{5,1},{6,2},{7,3},{8,12},{9,13},{10,... | collective-permute-start | bytes 442376 | tf_op jit(solution)/shard_map/ppermute | solution.py:591
  37.9 7.3 %collective-permute-start.13 = (bf16[144,512]{1,0:T(8,128)(2,1)S(1)}, bf16[144,512]{1,0:T(8,128)(2,1)S(1)}, u32[]{:S(2)}, u32[]{:S(2)}) collective-permute-start(bf16[144,512]{1,0:T(8,128)(2,1)S(1)} %get-tuple-element.66), channel_id=1, source_target_pairs={{0,2},{1,3},{2,0},{3,1},{4,6},{5,7},{6,4},{7,5},{8,10},{9,11},{10,... | collective-permute-start | bytes 442376 | tf_op jit(solution)/shard_map/ppermute | solution.py:591
  39.4 6.8 %collective-permute-start.14 = (bf16[144,512]{1,0:T(8,128)(2,1)S(1)}, bf16[144,512]{1,0:T(8,128)(2,1)S(1)}, u32[]{:S(2)}, u32[]{:S(2)}) collective-permute-start(bf16[144,512]{1,0:T(8,128)(2,1)S(1)} %get-tuple-element.67), channel_id=1, source_target_pairs={{0,4},{1,5},{2,6},{3,7},{4,0},{5,1},{6,2},{7,3},{8,12},{9,13},{10,... | collective-permute-start | bytes 442376 | tf_op jit(solution)/shard_map/ppermute | solution.py:591
  40.6 7.2 %collective-permute-start.15 = (bf16[144,512]{1,0:T(8,128)(2,1)S(1)}, bf16[144,512]{1,0:T(8,128)(2,1)S(1)}, u32[]{:S(2)}, u32[]{:S(2)}) collective-permute-start(bf16[144,512]{1,0:T(8,128)(2,1)S(1)} %get-tuple-element.68), channel_id=1, source_target_pairs={{0,6},{1,7},{2,4},{3,5},{4,2},{5,3},{6,0},{7,1},{8,14},{9,15},{10,... | collective-permute-start | bytes 442376 | tf_op jit(solution)/shard_map/ppermute | solution.py:591
  43.2 4.7 %collective-permute-start.21 = (bf16[64,512]{1,0:T(8,128)(2,1)S(1)}, bf16[64,512]{1,0:T(8,128)(2,1)S(1)}, u32[]{:S(2)}, u32[]{:S(2)}) collective-permute-start(bf16[64,512]{1,0:T(8,128)(2,1)S(1)} %get-tuple-element.71), channel_id=1, source_target_pairs={{0,8},{8,0},{16,24},{24,16},{1,9},{9,1},{17,25},{25,17},{2,10},{10... | collective-permute-start | bytes 196616 | tf_op jit(solution)/shard_map/ppermute | solution.py:591
  47.8 6.3 %collective-permute-start.16 = (bf16[128,512]{1,0:T(8,128)(2,1)S(1)}, bf16[128,512]{1,0:T(8,128)(2,1)S(1)}, u32[]{:S(2)}, u32[]{:S(2)}) collective-permute-start(bf16[128,512]{1,0:T(8,128)(2,1)S(1)} %get-tuple-element.69.mine.refs_1_), channel_id=1, source_target_pairs={{0,8},{8,0},{16,24},{24,16},{1,9},{9,1},{17,25},{25,17},{2,10},{10... | collective-permute-start | bytes 393224 | tf_op jit(solution)/shard_map/ppermute | solution.py:591
  48.0 6.3 %collective-permute-start.22 = (bf16[96,512]{1,0:T(8,128)(2,1)S(1)}, bf16[96,512]{1,0:T(8,128)(2,1)S(1)}, u32[]{:S(2)}, u32[]{:S(2)}) collective-permute-start(bf16[96,512]{1,0:T(8,128)(2,1)S(1)} %merge_slabs.4.mine.refs_0_), channel_id=1, source_target_pairs={{0,16},{8,24},{16,0},{24,8},{1,17},{9,25},{17,1},{25,9},{2,18},{10... | collective-permute-start | bytes 294920 | tf_op jit(solution)/shard_map/ppermute | solution.py:591
  54.1 6.3 %collective-permute-start.17 = (bf16[128,512]{1,0:T(8,128)(2,1)S(1)}, bf16[128,512]{1,0:T(8,128)(2,1)S(1)}, u32[]{:S(2)}, u32[]{:S(2)}) collective-permute-start(bf16[128,512]{1,0:T(8,128)(2,1)S(1)} %merge_slabs.3.refs_2_.last_mine), channel_id=1, source_target_pairs={{0,16},{8,24},{16,0},{24,8},{1,17},{9,25},{17,1},{25,9},{2,18},{10... | collective-permute-start | bytes 393224 | tf_op jit(solution)/shard_map/ppermute | solution.py:591
  54.3 6.9 %collective-permute-start.23 = (bf16[128,512]{1,0:T(8,128)(2,1)S(1)}, bf16[128,512]{1,0:T(8,128)(2,1)S(1)}, u32[]{:S(2)}, u32[]{:S(2)}) collective-permute-start(bf16[128,512]{1,0:T(8,128)(2,1)S(1)} %merge_slabs.5.mine), channel_id=1, source_target_pairs={{0,8},{8,0},{16,24},{24,16},{1,9},{9,1},{17,25},{25,17},{2,10},{10... | collective-permute-start | bytes 393224 | tf_op jit(solution)/shard_map/ppermute | solution.py:591
  56.8 1.2 %collective-permute-start.24 = (bf16[48,512]{1,0:T(8,128)(2,1)S(1)}, bf16[48,512]{1,0:T(8,128)(2,1)S(1)}, u32[]{:S(2)}, u32[]{:S(2)}) collective-permute-start(bf16[48,512]{1,0:T(8,128)(2,1)S(1)} %get-tuple-element.73.refs_0_), channel_id=1, source_target_pairs={{0,1},{1,0},{2,3},{3,2},{4,5},{5,4},{6,7},{7,6},{8,9},{9,8},{10,11... | collective-permute-start | bytes 147464 | tf_op jit(solution)/shard_map/ppermute | solution.py:591
